TPU v7x, 32 devices: a whole 2x2x4 slice. The times are simulated.
32 devices in a mesh: groups: 2 (over y), expert: 4 (over z), dp: 2 (over x), mp: 2 (over core).
Axes of the slice: x: 2, y: 2, z: 4, core: 2. Of those that a mesh axis runs over, the one named last changes fastest.
Arguments:
- hidden: bfloat16 [1024, 2048], P(('groups', 'expert', 'dp'), 'mp'), parts along dimension 0, may hold values from -6 to 6
- queries: bfloat16 [1024, 2048], P(('groups', 'expert', 'dp'), 'mp'), parts along dimension 0, may hold values from -6 to 120
- memory: bfloat16 [1024, 2, 2048], P(('groups', 'expert', 'dp'), None, 'mp'), parts along dimension 0, may hold values from -6 to 40.5
- target_pair: int32 [1024], P(('groups', 'expert', 'dp')), parts along dimension 0, may hold values from 0 to 15, as said below
- source_pair: int32 [1024], P(('groups', 'expert', 'dp')), parts along dimension 0, may hold values from 0 to 15, as said below
- routes: int32 [1024, 2], P(('groups', 'expert', 'dp')), parts along dimension 0, may hold values from 0 to 3, all different within a row; in each aligned block of 64 rows (0 to 63, 64 to 127, ...) at most 40 rows name the same one
- route_weight: float32 [1024, 2], P(('groups', 'expert', 'dp')), parts along dimension 0, may hold values from 0.1 to 1
- norm_gain: float32 [2048], replicated, may hold values from 0.5 to 1.5
- norm_bias: float32 [2048], replicated, may hold values from -3 to 3
- expert_in: bfloat16 [4, 2048, 8192], P('expert', None, ('dp', 'mp')), may hold values from -0.125 to 0.125
- expert_out: bfloat16 [4, 8192, 2048], P('expert', ('dp', 'mp')), may hold values from -0.0625 to 0.0625
Outputs:
- mixed: bfloat16 [1024, 2048], P(('groups', 'expert', 'dp'), 'mp'), parts along dimension 0
There are 2 independent parts, one for each index of `groups`. A program takes and returns all parts, laid end to end along the dimension named above; an argument that names none is the same for every part. Nothing has to cross between parts.
Inputs may be any that keep to these rules, and one draw needn't show every extreme that they name: `target_pair`: within each batch pair numbers run over 0 to 15; each pair's target tokens form one contiguous run on one index of expert and dp, which holds the tokens of 4 pairs. `source_pair`: within each batch, memory rows read by expert index and then row carry pair numbers that never fall, and every pair has at least one row. `routes`: among the rows of one device no expert is named more than 40 times.
All inputs are finite; a program needn't handle non-finite values.
Results may differ from a plain program's by a relative error of at most 0.008.
Values may be sent and summed in bfloat16 or wider, within the bound.
No kernel may reach another device: no remote copies, remote signals or barrier semaphores. Data moves between devices by JAX's collectives and lax.ppermute only.
A program may use at most 128 MiB of HBM per device.

v0:
```python
import math

import jax
import jax.numpy as jnp
from jax import lax
from jax.sharding import PartitionSpec as P

HEAD = 128


EPSILON = 1e-05
NEGATIVE = -1e30


def shards(
    hidden,
    queries,
    memory,
    target_pair,
    source_pair,
    routes,
    route_weight,
    norm_gain,
    norm_bias,
    expert_in,
    expert_out,
):
    tok_rows = hidden.shape[0]
    local_heads = queries.shape[1] // HEAD
    scale = 1.0 / math.sqrt(HEAD)
    query_heads = queries.reshape(tok_rows, local_heads, HEAD)
    running = jnp.full((local_heads, tok_rows), NEGATIVE, jnp.float32)
    rows = lax.all_gather(memory, "expert", axis=0, tiled=True)
    row_pairs = lax.all_gather(source_pair, "expert", axis=0, tiled=True)
    count = rows.shape[0]
    keys = rows[:, 0, :].reshape(count, local_heads, HEAD)
    values = rows[:, 1, :].reshape(count, local_heads, HEAD)
    score = (
        jnp.einsum("thd,rhd->htr", query_heads, keys, preferred_element_type=jnp.float32) * scale
    )
    match = (target_pair[:, None] == row_pairs[None, :])[None]
    masked = jnp.where(match, score, NEGATIVE)
    newest = jnp.maximum(running, jnp.max(masked, axis=-1))
    weight = jnp.where(match, jnp.exp(masked - newest[:, :, None]), 0.0)
    total = jnp.sum(weight, axis=-1)
    summed = jnp.einsum(
        "htr,rhd->htd", weight.astype(jnp.bfloat16), values, preferred_element_type=jnp.float32
    )
    running, total, summed = (newest, total, summed)
    context = jnp.transpose(summed / total[:, :, None], (1, 0, 2)).reshape(
        tok_rows, local_heads * HEAD
    )
    attended = (hidden.astype(jnp.float32) + context).astype(jnp.bfloat16)
    full_rows = lax.all_gather(attended, "mp", axis=1, tiled=True)
    width = full_rows.shape[1]
    experts_all = lax.axis_size("expert")
    batches = lax.axis_size("dp")
    cap = 2 * tok_rows // experts_all * 5 // 4
    flat = routes.reshape(-1)
    named = (flat[:, None] == jnp.arange(experts_all, dtype=jnp.int32)[None, :]).astype(jnp.int32)
    slot = jnp.sum((jnp.cumsum(named, axis=0) - named) * named, axis=1)
    dest = flat * cap + slot
    place = dest[:, None] == jnp.arange(experts_all * cap, dtype=jnp.int32)[None, :]
    per_token = jnp.sum(place.reshape(tok_rows, 2, experts_all * cap).astype(jnp.bfloat16), axis=1)
    outgoing = lax.dot_general(
        per_token, full_rows, (((0,), (0,)), ((), ())), preferred_element_type=jnp.float32
    ).astype(jnp.bfloat16)
    copies = jnp.broadcast_to(
        outgoing.reshape(experts_all, 1, cap, width), (experts_all, batches, cap, width)
    ).reshape(experts_all * batches * cap, width)
    arrived = lax.all_to_all(copies, ("expert", "dp"), split_axis=0, concat_axis=0, tiled=True)
    values = arrived.astype(jnp.float32)
    center = jnp.mean(values, axis=-1, keepdims=True)
    spread = jnp.mean(jnp.square(values - center), axis=-1, keepdims=True)
    normed = ((values - center) * lax.rsqrt(spread + EPSILON) * norm_gain + norm_bias).astype(
        jnp.bfloat16
    )
    active = jax.nn.relu(jnp.dot(normed, expert_in[0], preferred_element_type=jnp.float32)).astype(
        jnp.bfloat16
    )
    partial_value = jnp.dot(active, expert_out[0], preferred_element_type=jnp.float32).astype(
        jnp.bfloat16
    )
    returned = lax.all_to_all(
        partial_value, ("expert", "dp"), split_axis=0, concat_axis=0, tiled=True
    )
    expert_sum = jnp.sum(
        returned.reshape(experts_all, batches, cap, width).astype(jnp.float32), axis=1
    )
    picked = jnp.dot(
        place.astype(jnp.float32),
        expert_sum.reshape(experts_all * cap, width),
        precision=lax.Precision.HIGHEST,
    )
    blended = jnp.sum(picked.reshape(tok_rows, 2, width) * route_weight[:, :, None], axis=1)
    share = lax.psum_scatter(
        blended.astype(jnp.bfloat16), "mp", scatter_dimension=1, tiled=True
    ).astype(jnp.float32)
    return (attended.astype(jnp.float32) + share).astype(jnp.bfloat16)


def solution(mesh):
    return jax.shard_map(
        shards,
        mesh=mesh,
        in_specs=(
            P(("groups", "expert", "dp"), "mp"),
            P(("groups", "expert", "dp"), "mp"),
            P(("groups", "expert", "dp"), None, "mp"),
            P(("groups", "expert", "dp")),
            P(("groups", "expert", "dp")),
            P(("groups", "expert", "dp"), None),
            P(("groups", "expert", "dp"), None),
            P(),
            P(),
            P("expert", None, ("dp", "mp")),
            P("expert", ("dp", "mp"), None),
        ),
        out_specs=P(("groups", "expert", "dp"), "mp"),
        check_vma=False,
    )
```

profile of v0, /device:TPU:0, one launch (start us, length us, event | category | flops | bytes accessed | tf_op | source)
XLA Modules:
  0.0 148.1 jit_solution(10495505063601206719)
XLA Ops:
  6.5 0.7 all-gather.2.cloned.1.call-update
  7.3 0.8 copy.53
  8.9 1.3 dynamic-slice
  10.8 0.9 dynamic-update-slice
  11.7 9.9 %all-reduce = s32[256]{0:T(256)S(1)} all-reduce(s32[256]{0:T(256)S(1)} %dynamic-update-slice), channel_id=1, replica_groups=mesh['groups'=2,'expert'=4,'dp'=2,'mp'=2] {'expert'}, use_global_device_ids=true, to_apply=%add | all-reduce | flops 256 | bytes 2048
  21.6 0.7 multiply_add_fusion
  22.3 0.7 broadcast_compare_fusion
  23.1 16.5 %all-gather.2.cloned.1.call-done = bf16[256,2,1024]{2,1,0:T(2,128)(2,1)} async-done(((bf16[64,2,1024]{2,1,0:T(2,128)(2,1)}), bf16[256,2,1024]{2,1,0:T(2,128)(2,1)}) %all-gather.2.cloned.1.call-update) | async-done | bytes 1048592 | tf_op jit(solution)/shard_map/all_gather | solution.py:33
  39.6 3.2 %fusion.42 = (bf16[256,1,1024]{2,1,0:T(2,128)(2,1)S(1)}, bf16[256,1,1024]{2,1,0:T(2,128)(2,1)S(1)}) fusion(bf16[256,2,1024]{2,1,0:T(2,128)(2,1)} %all-gather.2.cloned.1.call-done), kind=kLoop, calls=%fused_computation.51 | loop fusion | bytes 2097152 | tf_op jit(solution)/shard_map/slice | solution.py:36
  42.8 0.9 copy.57
  43.8 0.3 fusion.43
  44.1 0.9 copy.58
  45.0 0.3 fusion.25
  45.3 0.3 fusion.22
  45.7 2.0 %all_gather.11 = bf16[64,2048]{1,0:T(8,128)(2,1)S(1)} all-gather(bf16[64,1024]{1,0:T(8,128)(2,1)S(1)} %fusion.28), channel_id=1, replica_groups=mesh['groups'=2,'expert'=4,'dp'=2,'mp'=2] {'mp'}, dimensions={1}, use_global_device_ids=true | all-gather | bytes 393216 | tf_op jit(solution)/shard_map/all_gather | solution.py:54
  47.7 0.3 convolution_convert_fusion
  48.2 35.7 %all_to_all.18 = bf16[8,40,2048]{2,1,0:T(8,128)(2,1)S(1)} all-to-all(bf16[8,40,2048]{2,1,0:T(8,128)(2,1)S(1)} %bitcast.59), channel_id=1, replica_groups=mesh['groups'=2,'expert'=4,'dp'=2,'mp'=2] {'expert','dp'}, dimensions={0} | all-to-all | bytes 2621440 | tf_op jit(solution)/shard_map/all_to_all | solution.py:71
  84.2 0.5 fusion.15
  84.7 0.6 fusion.18
  85.2 11.3 %fusion.12 = bf16[320,2048]{1,0:T(8,128)(2,1)S(1)} fusion(bf16[1,2048,2048]{2,1,0:T(8,128)(2,1)} %param.21, bf16[320,2048]{1,0:T(8,128)(2,1)S(1)} %bitcast.62, bf16[1,2048,2048]{2,1,0:T(8,128)(2,1)} %param.20), kind=kOutput, calls=%fused_computation.10 | convolution fusion | flops 5370675200 | bytes 19398656 | tf_op jit(solution)/shard_map/dot_general | solution.py:81
  96.6 34.5 %all_to_all.19 = bf16[8,40,2048]{2,1,0:T(8,128)(2,1)S(1)} all-to-all(bf16[8,40,2048]{2,1,0:T(8,128)(2,1)S(1)} %bitcast.63), channel_id=1, replica_groups=mesh['groups'=2,'expert'=4,'dp'=2,'mp'=2] {'expert','dp'}, dimensions={0} | all-to-all | bytes 2621440 | tf_op jit(solution)/shard_map/all_to_all | solution.py:84
  131.4 1.5 fusion.19
  132.9 6.8 %reduce-scatter.2.cloned.1.call-done = bf16[64,1024]{1,0:T(8,128)(2,1)} async-done(((bf16[64,2048]{1,0:T(8,128)(2,1)}), bf16[64,1024]{1,0:T(8,128)(2,1)}) %reduce-scatter.2.cloned.1.call-update) | async-done | bytes 131088 | tf_op jit(solution)/shard_map/reduce_scatter | solution.py:96
  139.6 1.6 %add_convert_fusion = bf16[64,1024]{1,0:T(8,128)(2,1)} fusion(bf16[64,1024]{1,0:T(8,128)(2,1)} %reduce-scatter.2.cloned.1.call-done, bf16[64,1024]{1,0:T(8,128)(2,1)S(1)} %fusion.28), kind=kLoop, calls=%fused_computation.29 | loop fusion | flops 262144 | bytes 393216 | tf_op jit(solution)/shard_map/convert_element_type | solution.py:99
  (28 shorter events, 1.6 us)
Async XLA Ops:
  6.5 37.2 %copy-start = (bf16[64,1024]{1,0:T(8,128)(2,1)S(1)}, bf16[64,1024]{1,0:T(8,128)(2,1)}, u32[]{:S(2)}) copy-start(bf16[64,1024]{1,0:T(8,128)(2,1)} %param.12) | copy-start | bytes 393220
  6.5 33.1 %all-gather.2.cloned.1.call-start = ((), (), s32[]{:S(2)}) async-start(), calls=%async_computation.3 | async-start | bytes 1310720 | tf_op jit(solution)/shard_map/all_gather | solution.py:33
  7.3 132.4 %reduce-scatter.2.cloned.1.call-start = ((), (), s32[]{:S(2)}) async-start(), calls=%async_computation.4 | async-start | bytes 393216 | tf_op jit(solution)/shard_map/reduce_scatter | solution.py:96
  43.8 1.9 %copy-start.1 = (bf16[64,1024]{1,0:T(8,128)(2,1)S(1)}, bf16[64,1024]{1,0:T(8,128)(2,1)}, u32[]{:S(2)}) copy-start(bf16[64,1024]{1,0:T(8,128)(2,1)} %param.11) | copy-start | bytes 393220
  48.2 36.5 %copy-start.2 = (f32[2048]{0:T(1024)S(1)}, f32[2048]{0:T(1024)}, u32[]{:S(2)}) copy-start(f32[2048]{0:T(1024)} %param.19) | copy-start | bytes 24580
  48.2 36.4 %copy-start.3 = (f32[2048]{0:T(1024)S(1)}, f32[2048]{0:T(1024)}, u32[]{:S(2)}) copy-start(f32[2048]{0:T(1024)} %param.18) | copy-start | bytes 24580
  96.6 34.8 %copy-start.4 = (f32[64,2]{0,1:T(2,128)S(1)}, f32[64,2]{0,1:T(2,128)}, u32[]{:S(2)}) copy-start(f32[64,2]{0,1:T(2,128)} %param.17) | copy-start | bytes 1540
Sparse Core Ops, SparseCore 0:
  8.9 30.6 all-gather.1
  133.0 6.6 reduce-scatter.1
where the time goes:
time: 148 us
  blocking collectives  82.1 us (55%)
  waiting for transfers between devices  24 us (16%)
  between operations  14.3 us (10%)
  matrix products  13.8 us (9%)
  local copies, waits for them, and re-layouts  8.49 us (6%)
  other arithmetic  5.38 us (4%)
    all_to_all x1, blocking collectives, shards(): lax.all_to_all(copies, ('expert', 'dp'), split_axis=0, concat_axis=0, til...  35.7 us
    all_to_all x1, blocking collectives, shards(): lax.all_to_all(partial_value, ('expert', 'dp'), split_axis=0, concat_axis...  34.5 us
    all_gather x1, waiting for transfers between devices, shards(): rows = lax.all_gather(memory, 'expert', axis=0, tiled=True)  16.5 us
    dot_general x1, matrix products, shards(): jnp.dot(active, expert_out[0], preferred_element_type=jnp.float32)  11.3 us
    unnamed x1, blocking collectives  9.89 us
    reduce_scatter x1, waiting for transfers between devices, shards(): lax.psum_scatter(blended.astype(jnp.bfloat16), 'mp', scatter_dimension=1,...  6.77 us
    unnamed x16, local copies, waits for them, and re-layouts  4.74 us
    slice x1, local copies, waits for them, and re-layouts, shards(): keys = rows[:, 0, :].reshape(count, local_heads, HEAD)  3.25 us
  transfers between devices with their start and end apart: 2, of which 2 were waited for; matrix products, arithmetic and copies ran while one was open for 3% of the time, Pallas kernels for 0%

commit v1 on v0

--- a/solution.py
+++ b/solution.py
@@ -1,15 +1,355 @@
+import functools
 import math
 
 import jax
 import jax.numpy as jnp
 from jax import lax
+from jax.experimental import pallas as pl
+from jax.experimental.pallas import tpu as pltpu
 from jax.sharding import PartitionSpec as P
 
 HEAD = 128
-
-
 EPSILON = 1e-05
 NEGATIVE = -1e30
+META = 16
+VMEM_LIMIT = 12 * 1024 * 1024
+
+BF16 = jnp.bfloat16
+F32 = jnp.float32
+IN_VMEM = pl.BlockSpec(memory_space=pltpu.VMEM)
+IN_SMEM = pl.BlockSpec(memory_space=pltpu.SMEM)
+IN_HBM = pl.BlockSpec(memory_space=pl.ANY)
+
+
+def struct(rows, columns, dtype=BF16):
+    return jax.ShapeDtypeStruct((rows, columns), dtype)
+
+
+def call(kernel, outs, specs, scratch=(), flops=0, moved=0):
+    return pl.pallas_call(
+        kernel,
+        out_shape=outs,
+        in_specs=specs,
+        out_specs=[IN_VMEM] * len(outs),
+        scratch_shapes=scratch,
+        compiler_params=pltpu.CompilerParams(vmem_limit_bytes=VMEM_LIMIT),
+        cost_estimate=pl.CostEstimate(flops=flops, bytes_accessed=moved, transcendentals=0),
+    )
+
+
+def dot(a, b):
+    return lax.dot_general(a, b, (((1,), (0,)), ((), ())), preferred_element_type=F32)
+
+
+def dot_nt(a, b):
+    return lax.dot_general(a, b, (((1,), (1,)), ((), ())), preferred_element_type=F32)
+
+
+def iota(shape, dimension):
+    return lax.broadcasted_iota(jnp.int32, shape, dimension)
+
+
+def wrapped(value, size):
+    return jnp.where(value >= size, value - size, value)
+
+
+def columns_at(start, width):
+    return pl.ds(pl.multiple_of(start * width, width), width)
+
+
+def pack_kernel(experts, at_ref, q_ref, m_ref, h_ref, tp_ref, sp_ref, r_ref, *outs):
+    rows, width = q_ref.shape[0], outs[0].shape[1]
+    here = at_ref[0]
+    row = iota((META, rows), 0)
+    kinds = jnp.where(
+        row == 0,
+        tp_ref[...],
+        jnp.where(
+            row == 1,
+            sp_ref[...],
+            jnp.where(row == 2, r_ref[0:1, :], jnp.where(row == 3, r_ref[1:2, :], 0)),
+        ),
+    )
+    kinds = kinds.astype(F32).astype(BF16)
+    for step, out in enumerate(outs):
+        cols = columns_at(wrapped(here + step, experts), width)
+        out[0:rows, :] = q_ref[:, cols]
+        out[rows : 2 * rows, :] = m_ref[:, 0, cols]
+        out[2 * rows : 3 * rows, :] = m_ref[:, 1, cols]
+        out[3 * rows : 4 * rows, :] = h_ref[:, cols]
+        moved = (iota((rows, width), 1) == iota((rows, width), 0) + step * rows).astype(BF16)
+        out[4 * rows :, :] = dot(kinds, moved).astype(BF16)
+
+
+def prefetch_kernel(w1_ref, w2_ref, after_ref, o1_ref, o2_ref, sems):
+    parts = sems.shape[1]
+    size = w1_ref.shape[0] // parts
+    copies = []
+    for k, (src, dst) in enumerate(((w1_ref, o1_ref), (w2_ref, o2_ref))):
+        for part in range(parts):
+            rows = pl.ds(part * size, size)
+            copies.append(pltpu.make_async_copy(src.at[rows], dst.at[rows], sems.at[k, part]))
+    for copy in copies:
+        copy.start()
+    for copy in copies:
+        copy.wait()
+
+
+def attend_kernel(experts, rows, cap, at_ref, *refs):
+    messages, compact, attended = refs[:experts], refs[experts : 2 * experts], refs[2 * experts :]
+    width = messages[0].shape[1]
+    count = experts * rows
+    here = at_ref[0]
+    meta = sum(m[4 * rows :, :].astype(F32) for m in messages)
+    same = (iota((count, count), 0) == iota((count, count), 1)).astype(BF16)
+    columns = dot_nt(same, meta.astype(BF16))
+    match = columns[:, 0:1] == meta[1:2, :]
+    scale = 1.0 / math.sqrt(HEAD)
+    parts = []
+    for head in range(width // HEAD):
+        lanes = slice(head * HEAD, (head + 1) * HEAD)
+
+        def stacked(kind):
+            return jnp.concatenate(
+                [m[kind * rows : (kind + 1) * rows, lanes] for m in messages], axis=0
+            )
+
+        score = dot_nt(stacked(0), stacked(1)) * scale
+        masked = jnp.where(match, score, NEGATIVE)
+        largest = jnp.max(masked, axis=-1, keepdims=True)
+        weight = jnp.where(match, jnp.exp(masked - largest), 0.0)
+        total = jnp.sum(weight, axis=-1, keepdims=True)
+        context = dot(weight.astype(BF16), stacked(2)) / total
+        parts.append((stacked(3).astype(F32) + context).astype(BF16))
+    states = jnp.concatenate(parts, axis=1)
+    for block, out in enumerate(attended):
+        out[...] = states[block * rows : (block + 1) * rows, :]
+    first, second = meta[2:3, :].astype(jnp.int32), meta[3:4, :].astype(jnp.int32)
+    expert = wrapped(here + iota((META, count), 0), experts)
+    named = ((first == expert) | (second == expert)) & (iota((META, count), 0) < experts)
+    before = (iota((count, count), 0) < iota((count, count), 1)) & (
+        iota((count, count), 0) // rows == iota((count, count), 1) // rows
+    )
+    slot = dot(named.astype(BF16), before.astype(BF16)).astype(jnp.int32)
+    source = here - iota((META, count), 1) // rows
+    source = jnp.where(source < 0, source + experts, source)
+    spot = jnp.where(named, source * cap + slot, -1)
+    for step, out in enumerate(compact):
+        place = iota((experts * cap, count), 0) == spot[step : step + 1, :]
+        out[...] = dot(place.astype(BF16), states).astype(BF16)
+
+
+def first_kernel(experts, tile, at_ref, *refs):
+    mine, other = refs[:experts], refs[experts : 2 * experts]
+    gain_ref, bias_ref, w_ref, out_ref, x_ref, n_ref = refs[2 * experts :]
+    width = mine[0].shape[1]
+    here, half = at_ref[0], at_ref[1]
+    for step in range(experts):
+        source = here - step
+        source = jnp.where(source < 0, source + experts, source)
+        x_ref[:, columns_at(half * experts + source, width)] = mine[step][...]
+        x_ref[:, columns_at((1 - half) * experts + source, width)] = other[step][...]
+    values = x_ref[...].astype(F32)
+    center = jnp.mean(values, axis=-1, keepdims=True)
+    shifted = values - center
+    spread = jnp.mean(jnp.square(shifted), axis=-1, keepdims=True)
+    normed = shifted * lax.rsqrt(spread + EPSILON) * gain_ref[...] + bias_ref[...]
+    n_ref[...] = normed.astype(BF16)
+
+    @pl.loop(0, w_ref.shape[1] // tile)
+    def _(at):
+        cols = columns_at(at, tile)
+        out_ref[:, cols] = jnp.maximum(dot(n_ref[...], w_ref[:, cols]), 0.0).astype(BF16)
+
+
+def second_kernel(tile, at_ref, a_ref, w_ref, sent_ref, kept_ref):
+    half = at_ref[1]
+    tiles = sent_ref.shape[1] // tile
+
+    @pl.loop(0, tiles)
+    def _(at):
+        cols = columns_at(at, tile)
+        sent_ref[:, cols] = dot(
+            a_ref[...], w_ref[:, columns_at((1 - half) * tiles + at, tile)]
+        ).astype(BF16)
+
+    @pl.loop(0, tiles)
+    def _(at):
+        cols = columns_at(at, tile)
+        kept_ref[:, cols] = dot(
+            a_ref[...], w_ref[:, columns_at(half * tiles + at, tile)]
+        ).astype(BF16)
+
+
+def split_kernel(experts, at_ref, kept_ref, got_ref, *refs):
+    outs, total = refs[:experts], refs[experts]
+    cap = outs[0].shape[0]
+    total[...] = kept_ref[...].astype(F32) + got_ref[...].astype(F32)
+    for step, out in enumerate(outs):
+        target = wrapped(at_ref[0] + step, experts)
+        out[...] = total[pl.ds(pl.multiple_of(target * cap, 8), cap), :].astype(out.dtype)
+
+
+def mix_kernel(experts, at_ref, weight_ref, *refs):
+    returned, states = refs[:experts], refs[experts : 2 * experts]
+    out_ref, total = refs[2 * experts :]
+    width = states[0].shape[1]
+    share = jnp.zeros(total.shape, F32)
+    for step in range(experts):
+        weight = weight_ref[step]
+        high = weight.astype(BF16)
+        rest = weight - high.astype(F32)
+        middle = rest.astype(BF16)
+        low = (rest - middle.astype(F32)).astype(BF16)
+        rows = returned[step][...]
+        share = share + (dot(high, rows) + (dot(middle, rows) + dot(low, rows)))
+    total[...] = share
+    for step in range(experts):
+        cols = columns_at(wrapped(at_ref[0] + step, experts), width)
+        out_ref[:, cols] = (states[step][...].astype(F32) + total[:, cols]).astype(BF16)
+
+
+def head_shards(
+    hidden,
+    queries,
+    memory,
+    target_pair,
+    source_pair,
+    routes,
+    route_weight,
+    norm_gain,
+    norm_bias,
+    expert_in,
+    expert_out,
+):
+    rows, columns = hidden.shape
+    experts = lax.axis_size("expert")
+    width = columns // experts
+    cap = 2 * rows // experts * 5 // 4
+    model = 2 * columns
+    hidden_units = expert_in.shape[2]
+    here, half = lax.axis_index("expert"), lax.axis_index("mp")
+    at = jnp.stack([here, half]).astype(jnp.int32)
+
+    def along(array, step):
+        if step % experts == 0:
+            return array
+        pairs = [(i, (i + step) % experts) for i in range(experts)]
+        return lax.ppermute(array, "expert", pairs)
+
+    def swap(array, axis):
+        return lax.ppermute(array, axis, [(0, 1), (1, 0)])
+
+    packed = call(
+        functools.partial(pack_kernel, experts),
+        [struct(4 * rows + META, width)] * experts,
+        [IN_SMEM] + [IN_VMEM] * 6,
+        moved=16 * rows * columns,
+    )(
+        at,
+        queries,
+        memory,
+        hidden,
+        target_pair.reshape(1, rows),
+        source_pair.reshape(1, rows),
+        routes.T,
+    )
+    messages = [along(packed[step], step) for step in range(experts)]
+
+    w_in, w_out = pl.pallas_call(
+        prefetch_kernel,
+        out_shape=[
+            pltpu.VMEM((model, hidden_units), BF16),
+            pltpu.VMEM((hidden_units, model), BF16),
+        ],
+        in_specs=[IN_HBM, IN_HBM, IN_HBM],
+        out_specs=[IN_VMEM, IN_VMEM],
+        scratch_shapes=[pltpu.SemaphoreType.DMA((2, 4))],
+        compiler_params=pltpu.CompilerParams(vmem_limit_bytes=VMEM_LIMIT),
+        cost_estimate=pl.CostEstimate(
+            flops=0, bytes_accessed=8 * model * hidden_units, transcendentals=0
+        ),
+    )(expert_in[0], expert_out[0], packed[0])
+
+    named = jnp.any(routes[:, :, None] == jnp.arange(experts)[None, None, :], axis=1)
+    named = named.astype(jnp.int32)
+    slots = jnp.cumsum(named, axis=0) - named
+    chosen = (here - jnp.arange(experts)) % experts
+    slot = jnp.take(slots.T, chosen, axis=0)
+    weight = jnp.sum(
+        jnp.where(routes[None, :, :] == chosen[:, None, None], route_weight[None, :, :], 0.0),
+        axis=2,
+    )
+    weights = jnp.where(
+        slot[:, :, None] == jnp.arange(cap)[None, None, :], weight[:, :, None], 0.0
+    )
+
+    attended = call(
+        functools.partial(attend_kernel, experts, rows, cap),
+        [struct(experts * cap, width)] * experts + [struct(rows, width)] * experts,
+        [IN_SMEM] + [IN_VMEM] * experts,
+        flops=8 * experts * experts * rows * rows * width,
+        moved=16 * rows * columns,
+    )(at, *messages)
+    compact, states = attended[:experts], attended[experts:]
+
+    own = [along(compact[step], step) for step in range(experts)]
+    far = [swap(block, "dp") for block in own]
+
+    def first(blocks):
+        count = experts * cap
+        return call(
+            functools.partial(first_kernel, experts, 512),
+            [struct(count, hidden_units)],
+            [IN_SMEM] + [IN_VMEM] * (2 * experts + 3),
+            scratch=[pltpu.VMEM((count, model), BF16)] * 2,
+            flops=2 * count * model * hidden_units,
+            moved=2 * model * hidden_units,
+        )(
+            at,
+            *blocks,
+            *[swap(block, "mp") for block in blocks],
+            norm_gain.reshape(1, model),
+            norm_bias.reshape(1, model),
+            pltpu.with_memory_space_constraint(w_in, pltpu.VMEM),
+        )[0]
+
+    def second(active):
+        count = experts * cap
+        sent, kept = call(
+            functools.partial(second_kernel, 512),
+            [struct(count, columns)] * 2,
+            [IN_SMEM, IN_VMEM, IN_VMEM],
+            flops=2 * count * model * hidden_units,
+            moved=2 * model * hidden_units,
+        )(at, active, pltpu.with_memory_space_constraint(w_out, pltpu.VMEM))
+        return kept, swap(sent, "mp")
+
+    def split(kept, got, dtype):
+        return call(
+            functools.partial(split_kernel, experts),
+            [struct(cap, columns, dtype)] * experts,
+            [IN_SMEM, IN_VMEM, IN_VMEM],
+            scratch=[pltpu.VMEM((experts * cap, columns), F32)],
+            moved=8 * experts * cap * columns,
+        )(at, kept, got)
+
+    active_own = first(own)
+    active_far = first(far)
+    gone = [swap(block, "dp") for block in split(*second(active_far), BF16)]
+    mine = split(*second(active_own), F32)
+    summed = [(block + came.astype(F32)).astype(BF16) for block, came in zip(mine, gone)]
+    returned = [along(summed[step], step) for step in range(experts)]
+    home = [along(states[step], -step) for step in range(experts)]
+
+    return call(
+        functools.partial(mix_kernel, experts),
+        [struct(rows, columns)],
+        [IN_SMEM] + [IN_VMEM] * (2 * experts + 1),
+        scratch=[pltpu.VMEM((rows, columns), F32)],
+        flops=6 * rows * experts * cap * columns,
+        moved=4 * rows * columns,
+    )(at, weights, *returned, *home)[0]
 
 
 def shards(
@@ -99,9 +439,24 @@
     return (attended.astype(jnp.float32) + share).astype(jnp.bfloat16)
 
 
+def layer(hidden, queries, memory, *rest):
+    experts = lax.axis_size("expert")
+    rows, columns = hidden.shape
+    heads = columns // HEAD
+    by_heads = (
+        lax.axis_size("mp") == 2
+        and lax.axis_size("dp") == 2
+        and heads % experts == 0
+        and memory.shape[0] == rows
+        and experts * rows <= columns // experts
+        and experts <= META
+    )
+    return (head_shards if by_heads else shards)(hidden, queries, memory, *rest)
+
+
 def solution(mesh):
     return jax.shard_map(
-        shards,
+        layer,
         mesh=mesh,
         in_specs=(
             P(("groups", "expert", "dp"), "mp"),

time: 148 us -> 83 us (0.56)
  blocking collectives: 82.1 us -> 0 us
  starting transfers between devices: 0.04 us -> 35 us
  Pallas kernels: 0 us -> 18.8 us
  between operations: 14.3 us -> 0.21 us
  matrix products: 13.8 us -> 0 us
  waiting for transfers between devices: 24 us -> 15.9 us
  other arithmetic: 5.38 us -> 0.59 us
  local copies, waits for them, and re-layouts: 8.49 us -> 12.3 us
    all_to_all x2 -> x0, blocking collectives: 70.2 us -> none  [the longest x1 35.7 us: shards(): lax.all_to_all(copies, ('expert', 'dp'), split_axis=0, concat_axis=0, til...]
    ppermute x0 -> x30, starting transfers between devices: none -> 35 us  [the longest x12 22.7 us: along(): return lax.ppermute(array, 'expert', pairs)]
    pallas_call x0 -> x10, Pallas kernels: none -> 18.8 us  [the longest x2 6.33 us: first(): call(functools.partial(first_kernel, experts, 512), [struct(count, hidden...]
    all_gather x1 -> x0, waiting for transfers between devices: 16.5 us -> none  [shards(): rows = lax.all_gather(memory, 'expert', axis=0, tiled=True)]
    ppermute x0 -> x30, waiting for transfers between devices: none -> 15.9 us  [the longest x12 13 us: along(): return lax.ppermute(array, 'expert', pairs)]
    dot_general x5 -> x0, matrix products: 13.8 us -> none  [the longest x1 11.3 us: shards(): jnp.dot(active, expert_out[0], preferred_element_type=jnp.float32)]
    unnamed x1 -> x0, blocking collectives: 9.89 us -> none
    unnamed x16 -> x24, local copies, waits for them, and re-layouts: 4.74 us -> 11.5 us
  transfers between devices with their start and end apart: 2 -> 30, of which waited for: 2 -> 10; matrix products, arithmetic and copies ran while one was open for 3% -> 2% of each run, Pallas kernels for 0% -> 17%
where the time goes in v1:
time: 83 us; the launch traced here: 82.7 us
  starting transfers between devices  35 us (42%)
  Pallas kernels  18.8 us (23%)
  waiting for transfers between devices  15.9 us (19%)
  local copies, waits for them, and re-layouts  12.3 us (15%)
    ppermute x12, starting transfers between devices, along(): return lax.ppermute(array, 'expert', pairs)  22.7 us
    ppermute x12, waiting for transfers between devices, along(): return lax.ppermute(array, 'expert', pairs)  13 us
    ppermute x18, starting transfers between devices, swap(): return lax.ppermute(array, axis, [(0, 1), (1, 0)])  12.2 us
    unnamed x24, local copies, waits for them, and re-layouts  11.5 us
    pallas_call x2, Pallas kernels, first(): call(functools.partial(first_kernel, experts, 512), [struct(count, hidden...  6.33 us
    pallas_call x2, Pallas kernels, second(): call(functools.partial(second_kernel, 512), [struct(count, columns)] * 2,...  5.33 us
    ppermute x18, waiting for transfers between devices, swap(): return lax.ppermute(array, axis, [(0, 1), (1, 0)])  2.86 us
    pallas_call x1, Pallas kernels, head_shards(): call(functools.partial(mix_kernel, experts), [struct(rows, columns)], [IN...  1.76 us
  transfers between devices with their start and end apart: 30, of which 10 were waited for; matrix products, arithmetic and copies ran while one was open for 2% of the time, Pallas kernels for 17%

profile of v1, /device:TPU:0, one launch (start us, length us, event | category | flops | bytes accessed | tf_op | source)
XLA Modules:
  0.0 82.7 jit_solution(70268559344513464)
XLA Ops:
  6.2 3.0 %collective-permute-start = (bf16[272,256]{1,0:T(8,128)(2,1)S(1)}, bf16[272,256]{1,0:T(8,128)(2,1)S(1)}, u32[]{:S(2)}, u32[]{:S(2)}) collective-permute-start(bf16[272,256]{1,0:T(8,128)(2,1)S(1)} %get-tuple-element.32), channel_id=1, source_target_pairs={{0,4},{4,8},{8,12},{12,0},{1,5},{5,9},{9,13},{13,1},{2,6},{6,10},{... | collective-permute-start | bytes 417800 | tf_op jit(solution)/shard_map/ppermute | solution.py:238
  9.3 2.6 %collective-permute-start.1 = (bf16[272,256]{1,0:T(8,128)(2,1)S(1)}, bf16[272,256]{1,0:T(8,128)(2,1)S(1)}, u32[]{:S(2)}, u32[]{:S(2)}) collective-permute-start(bf16[272,256]{1,0:T(8,128)(2,1)S(1)} %get-tuple-element.33), channel_id=1, source_target_pairs={{0,8},{4,12},{8,0},{12,4},{1,9},{5,13},{9,1},{13,5},{2,10},{6,14},... | collective-permute-start | bytes 417800 | tf_op jit(solution)/shard_map/ppermute | solution.py:238
  14.1 1.8 %collective-permute-done.refs_1_ = bf16[272,256]{1,0:T(8,128)(2,1)S(1)} collective-permute-done((bf16[272,256]{1,0:T(8,128)(2,1)S(1)}, bf16[272,256]{1,0:T(8,128)(2,1)S(1)}, u32[]{:S(2)}, u32[]{:S(2)}) %collective-permute-start) | collective-permute-done | bytes 139296 | tf_op jit(solution)/shard_map/ppermute | solution.py:238
  15.9 5.1 %collective-permute-done.1.refs_2_ = bf16[272,256]{1,0:T(8,128)(2,1)S(1)} collective-permute-done((bf16[272,256]{1,0:T(8,128)(2,1)S(1)}, bf16[272,256]{1,0:T(8,128)(2,1)S(1)}, u32[]{:S(2)}, u32[]{:S(2)}) %collective-permute-start.1) | collective-permute-done | bytes 139296 | tf_op jit(solution)/shard_map/ppermute | solution.py:238
  22.4 3.5 %collective-permute-start.3 = (bf16[160,256]{1,0:T(8,128)(2,1)S(1)}, bf16[160,256]{1,0:T(8,128)(2,1)S(1)}, u32[]{:S(2)}, u32[]{:S(2)}) collective-permute-start(bf16[160,256]{1,0:T(8,128)(2,1)S(1)} %get-tuple-element.36), channel_id=1, source_target_pairs={{0,4},{4,8},{8,12},{12,0},{1,5},{5,9},{9,13},{13,1},{2,6},{6,10},{... | collective-permute-start | bytes 245768 | tf_op jit(solution)/shard_map/ppermute | solution.py:238
  25.9 1.6 %collective-permute-start.4 = (bf16[160,256]{1,0:T(8,128)(2,1)S(1)}, bf16[160,256]{1,0:T(8,128)(2,1)S(1)}, u32[]{:S(2)}, u32[]{:S(2)}) collective-permute-start(bf16[160,256]{1,0:T(8,128)(2,1)S(1)} %get-tuple-element.37), channel_id=1, source_target_pairs={{0,8},{4,12},{8,0},{12,4},{1,9},{5,13},{9,1},{13,5},{2,10},{6,14},... | collective-permute-start | bytes 245768 | tf_op jit(solution)/shard_map/ppermute | solution.py:238
  28.4 1.6 %collective-permute-start.11 = (bf16[160,256]{1,0:T(8,128)(2,1)S(1)}, bf16[160,256]{1,0:T(8,128)(2,1)S(1)}, u32[]{:S(2)}, u32[]{:S(2)}) collective-permute-start(bf16[160,256]{1,0:T(8,128)(2,1)S(1)} %get-tuple-element.35.refs_0_), channel_id=1, source_target_pairs={{0,2},{2,0},{1,3},{3,1},{4,6},{6,4},{5,7},{7,5},{8,10},{10,8},{9,1... | collective-permute-start | bytes 245768 | tf_op jit(solution)/shard_map/ppermute | solution.py:241
  30.0 1.5 %collective-permute-start.12 = (bf16[160,256]{1,0:T(8,128)(2,1)S(1)}, bf16[160,256]{1,0:T(8,128)(2,1)S(1)}, u32[]{:S(2)}, u32[]{:S(2)}) collective-permute-start(bf16[160,256]{1,0:T(8,128)(2,1)S(1)} %collective-permute-done.3.refs_1_), channel_id=1, source_target_pairs={{0,2},{2,0},{1,3},{3,1},{4,6},{6,4},{5,7},{7,5},{8,10},{10,8},{9,1... | collective-permute-start | bytes 245768 | tf_op jit(solution)/shard_map/ppermute | solution.py:241
  31.5 1.5 %collective-permute-done.4.refs_2_ = bf16[160,256]{1,0:T(8,128)(2,1)S(1)} collective-permute-done((bf16[160,256]{1,0:T(8,128)(2,1)S(1)}, bf16[160,256]{1,0:T(8,128)(2,1)S(1)}, u32[]{:S(2)}, u32[]{:S(2)}) %collective-permute-start.4) | collective-permute-done | bytes 81952 | tf_op jit(solution)/shard_map/ppermute | solution.py:238
  33.0 1.5 %collective-permute-start.13 = (bf16[160,256]{1,0:T(8,128)(2,1)S(1)}, bf16[160,256]{1,0:T(8,128)(2,1)S(1)}, u32[]{:S(2)}, u32[]{:S(2)}) collective-permute-start(bf16[160,256]{1,0:T(8,128)(2,1)S(1)} %collective-permute-done.4.refs_2_), channel_id=1, source_target_pairs={{0,2},{2,0},{1,3},{3,1},{4,6},{6,4},{5,7},{7,5},{8,10},{10,8},{9,1... | collective-permute-start | bytes 245768 | tf_op jit(solution)/shard_map/ppermute | solution.py:241
  35.1 3.4 %copy-done = bf16[1,2048,2048]{2,1,0:T(8,128)(2,1)S(1)} copy-done((bf16[1,2048,2048]{2,1,0:T(8,128)(2,1)S(1)}, bf16[1,2048,2048]{2,1,0:T(8,128)(2,1)}, u32[]{:S(2)}) %copy-start) | copy-done | bytes 8388632
  38.5 3.4 %copy-done.1 = bf16[1,2048,2048]{2,1,0:T(8,128)(2,1)S(1)} copy-done((bf16[1,2048,2048]{2,1,0:T(8,128)(2,1)S(1)}, bf16[1,2048,2048]{2,1,0:T(8,128)(2,1)}, u32[]{:S(2)}) %copy-start.1) | copy-done | bytes 8388632
  45.3 3.2 %shard_map.115.a_ref = bf16[160,2048]{1,0:T(8,128)(2,1)S(1)} custom-call(s32[2]{0:T(128)S(1)} %pad_add_fusion.at_ref, bf16[160,256]{1,0:T(8,128)(2,1)S(1)} %collective-permute-done.11.refs_0_, bf16[160,256]{1,0:T(8,128)(2,1)S(1)} %collective-permute-done.12.refs_1_, bf16[160,256]{1,0:T(8,128)(2,1)S(1)} %collective-permute-done.13.refs_2_, ...), custom_call_target="tpu_custom_call" | custom-call | flops 1342177280 | bytes 8388608 | tf_op jit(solution)/shard_map/pallas_call | solution.py:301
  48.5 2.7 %shard_map.116 = (bf16[160,1024]{1,0:T(8,128)(2,1)S(1)}, bf16[160,1024]{1,0:T(8,128)(2,1)S(1)}) custom-call(s32[2]{0:T(128)S(1)} %pad_add_fusion.at_ref, bf16[160,2048]{1,0:T(8,128)(2,1)S(1)} %shard_map.115.a_ref, bf16[2048,2048]{1,0:T(8,128)(2,1)S(1)} %get-tuple-element.40.w_ref), custom_call_target="tpu_custom_call" | custom-call | flops 1342177280 | bytes 8388608 | tf_op jit(solution)/shard_map/pallas_call | solution.py:319
  51.5 3.2 %shard_map.112.a_ref = bf16[160,2048]{1,0:T(8,128)(2,1)S(1)} custom-call(s32[2]{0:T(128)S(1)} %pad_add_fusion.at_ref, bf16[160,256]{1,0:T(8,128)(2,1)S(1)} %get-tuple-element.35.refs_0_, bf16[160,256]{1,0:T(8,128)(2,1)S(1)} %collective-permute-done.3.refs_1_, bf16[160,256]{1,0:T(8,128)(2,1)S(1)} %collective-permute-done.4.refs_2_, ...), custom_call_target="tpu_custom_call" | custom-call | flops 1342177280 | bytes 8388608 | tf_op jit(solution)/shard_map/pallas_call | solution.py:301
  54.6 2.7 %shard_map.113 = (bf16[160,1024]{1,0:T(8,128)(2,1)S(1)}, bf16[160,1024]{1,0:T(8,128)(2,1)S(1)}) custom-call(s32[2]{0:T(128)S(1)} %pad_add_fusion.at_ref, bf16[160,2048]{1,0:T(8,128)(2,1)S(1)} %shard_map.112.a_ref, bf16[2048,2048]{1,0:T(8,128)(2,1)S(1)} %get-tuple-element.40.w_ref), custom_call_target="tpu_custom_call" | custom-call | flops 1342177280 | bytes 8388608 | tf_op jit(solution)/shard_map/pallas_call | solution.py:319
  58.4 1.6 %collective-permute-start.25 = (bf16[40,1024]{1,0:T(8,128)(2,1)S(1)}, bf16[40,1024]{1,0:T(8,128)(2,1)S(1)}, u32[]{:S(2)}, u32[]{:S(2)}) collective-permute-start(bf16[40,1024]{1,0:T(8,128)(2,1)S(1)} %get-tuple-element.52), channel_id=1, source_target_pairs={{0,2},{2,0},{1,3},{3,1},{4,6},{6,4},{5,7},{7,5},{8,10},{10,8},{9,1... | collective-permute-start | bytes 245768 | tf_op jit(solution)/shard_map/ppermute | solution.py:241
  60.1 3.2 %collective-permute-start.27 = (bf16[64,256]{1,0:T(8,128)(2,1)S(1)}, bf16[64,256]{1,0:T(8,128)(2,1)S(1)}, u32[]{:S(2)}, u32[]{:S(2)}) collective-permute-start(bf16[64,256]{1,0:T(8,128)(2,1)S(1)} %get-tuple-element.54), channel_id=1, source_target_pairs={{0,12},{4,0},{8,4},{12,8},{1,13},{5,1},{9,5},{13,9},{2,14},{6,2},{... | collective-permute-start | bytes 98312 | tf_op jit(solution)/shard_map/ppermute | solution.py:238
  65.2 1.5 %collective-permute-start.21 = (bf16[40,1024]{1,0:T(8,128)(2,1)S(1)}, bf16[40,1024]{1,0:T(8,128)(2,1)S(1)}, u32[]{:S(2)}, u32[]{:S(2)}) collective-permute-start(bf16[40,1024]{1,0:T(8,128)(2,1)S(1)} %get-tuple-element.48), channel_id=1, source_target_pairs={{0,2},{2,0},{1,3},{3,1},{4,6},{6,4},{5,7},{7,5},{8,10},{10,8},{9,1... | collective-permute-start | bytes 245768 | tf_op jit(solution)/shard_map/ppermute | solution.py:241
  66.7 2.6 %collective-permute-done.23 = bf16[40,1024]{1,0:T(8,128)(2,1)S(1)} collective-permute-done((bf16[40,1024]{1,0:T(8,128)(2,1)S(1)}, bf16[40,1024]{1,0:T(8,128)(2,1)S(1)}, u32[]{:S(2)}, u32[]{:S(2)}) %collective-permute-start.23) | collective-permute-done | bytes 81952 | tf_op jit(solution)/shard_map/ppermute | solution.py:241
  70.3 3.2 %collective-permute-start.26 = (bf16[40,1024]{1,0:T(8,128)(2,1)S(1)}, bf16[40,1024]{1,0:T(8,128)(2,1)S(1)}, u32[]{:S(2)}, u32[]{:S(2)}) collective-permute-start(bf16[40,1024]{1,0:T(8,128)(2,1)S(1)} %add_convert_fusion), channel_id=1, source_target_pairs={{0,12},{4,0},{8,4},{12,8},{1,13},{5,1},{9,5},{13,9},{2,14},{6,2},{... | collective-permute-start | bytes 245768 | tf_op jit(solution)/shard_map/ppermute | solution.py:238
  74.7 1.8 %collective-permute-start.22 = (bf16[40,1024]{1,0:T(8,128)(2,1)S(1)}, bf16[40,1024]{1,0:T(8,128)(2,1)S(1)}, u32[]{:S(2)}, u32[]{:S(2)}) collective-permute-start(bf16[40,1024]{1,0:T(8,128)(2,1)S(1)} %add_convert_fusion.2), channel_id=1, source_target_pairs={{0,4},{4,8},{8,12},{12,0},{1,5},{5,9},{9,13},{13,1},{2,6},{6,10},{... | collective-permute-start | bytes 245768 | tf_op jit(solution)/shard_map/ppermute | solution.py:238
  76.6 3.0 %collective-permute-done.24.refs_2_ = bf16[40,1024]{1,0:T(8,128)(2,1)S(1)} collective-permute-done((bf16[40,1024]{1,0:T(8,128)(2,1)S(1)}, bf16[40,1024]{1,0:T(8,128)(2,1)S(1)}, u32[]{:S(2)}, u32[]{:S(2)}) %collective-permute-start.24) | collective-permute-done | bytes 81952 | tf_op jit(solution)/shard_map/ppermute | solution.py:238
  80.9 1.8 %shard_map.118 = bf16[64,1024]{1,0:T(8,128)(2,1)} custom-call(s32[2]{0:T(128)S(1)} %pad_add_fusion.at_ref, f32[4,64,40]{2,1,0:T(8,128)S(1)} %fusion.weight_ref, bf16[40,1024]{1,0:T(8,128)(2,1)S(1)} %add_convert_fusion.3.refs_0_, bf16[40,1024]{1,0:T(8,128)(2,1)S(1)} %collective-permute-done.22.refs_1_, bf16[40,1024]{1,0:T(8,128)(2,1)S(1)} %collective-permute-done.24.refs_2_, ...), custom_call_target="tpu_custom_call" | custom-call | flops 62914560 | bytes 262144 | tf_op jit(solution)/shard_map/pallas_call | solution.py:345
  (89 shorter events, 21.8 us)
Async XLA Ops:
  6.2 9.7 %collective-permute-start = (bf16[272,256]{1,0:T(8,128)(2,1)S(1)}, bf16[272,256]{1,0:T(8,128)(2,1)S(1)}, u32[]{:S(2)}, u32[]{:S(2)}) collective-permute-start(bf16[272,256]{1,0:T(8,128)(2,1)S(1)} %get-tuple-element.32), channel_id=1, source_target_pairs={{0,4},{4,8},{8,12},{12,0},{1,5},{5,9},{9,13},{13,1},{2,6},{6,10},{... | collective-permute-start | bytes 417800 | tf_op jit(solution)/shard_map/ppermute | solution.py:238
  9.3 11.8 %collective-permute-start.1 = (bf16[272,256]{1,0:T(8,128)(2,1)S(1)}, bf16[272,256]{1,0:T(8,128)(2,1)S(1)}, u32[]{:S(2)}, u32[]{:S(2)}) collective-permute-start(bf16[272,256]{1,0:T(8,128)(2,1)S(1)} %get-tuple-element.33), channel_id=1, source_target_pairs={{0,8},{4,12},{8,0},{12,4},{1,9},{5,13},{9,1},{13,5},{2,10},{6,14},... | collective-permute-start | bytes 417800 | tf_op jit(solution)/shard_map/ppermute | solution.py:238
  11.8 9.2 %collective-permute-start.2 = (bf16[272,256]{1,0:T(8,128)(2,1)S(1)}, bf16[272,256]{1,0:T(8,128)(2,1)S(1)}, u32[]{:S(2)}, u32[]{:S(2)}) collective-permute-start(bf16[272,256]{1,0:T(8,128)(2,1)S(1)} %get-tuple-element.34), channel_id=1, source_target_pairs={{0,12},{4,0},{8,4},{12,8},{1,13},{5,1},{9,5},{13,9},{2,14},{6,2},{... | collective-permute-start | bytes 417800 | tf_op jit(solution)/shard_map/ppermute | solution.py:238
  22.4 7.6 %collective-permute-start.3 = (bf16[160,256]{1,0:T(8,128)(2,1)S(1)}, bf16[160,256]{1,0:T(8,128)(2,1)S(1)}, u32[]{:S(2)}, u32[]{:S(2)}) collective-permute-start(bf16[160,256]{1,0:T(8,128)(2,1)S(1)} %get-tuple-element.36), channel_id=1, source_target_pairs={{0,4},{4,8},{8,12},{12,0},{1,5},{5,9},{9,13},{13,1},{2,6},{6,10},{... | collective-permute-start | bytes 245768 | tf_op jit(solution)/shard_map/ppermute | solution.py:238
  25.9 7.1 %collective-permute-start.4 = (bf16[160,256]{1,0:T(8,128)(2,1)S(1)}, bf16[160,256]{1,0:T(8,128)(2,1)S(1)}, u32[]{:S(2)}, u32[]{:S(2)}) collective-permute-start(bf16[160,256]{1,0:T(8,128)(2,1)S(1)} %get-tuple-element.37), channel_id=1, source_target_pairs={{0,8},{4,12},{8,0},{12,4},{1,9},{5,13},{9,1},{13,5},{2,10},{6,14},... | collective-permute-start | bytes 245768 | tf_op jit(solution)/shard_map/ppermute | solution.py:238
  27.5 7.0 %collective-permute-start.5 = (bf16[160,256]{1,0:T(8,128)(2,1)S(1)}, bf16[160,256]{1,0:T(8,128)(2,1)S(1)}, u32[]{:S(2)}, u32[]{:S(2)}) collective-permute-start(bf16[160,256]{1,0:T(8,128)(2,1)S(1)} %get-tuple-element.38), channel_id=1, source_target_pairs={{0,12},{4,0},{8,4},{12,8},{1,13},{5,1},{9,5},{13,9},{2,14},{6,2},{... | collective-permute-start | bytes 245768 | tf_op jit(solution)/shard_map/ppermute | solution.py:238
  28.4 14.8 %collective-permute-start.11 = (bf16[160,256]{1,0:T(8,128)(2,1)S(1)}, bf16[160,256]{1,0:T(8,128)(2,1)S(1)}, u32[]{:S(2)}, u32[]{:S(2)}) collective-permute-start(bf16[160,256]{1,0:T(8,128)(2,1)S(1)} %get-tuple-element.35.refs_0_), channel_id=1, source_target_pairs={{0,2},{2,0},{1,3},{3,1},{4,6},{6,4},{5,7},{7,5},{8,10},{10,8},{9,1... | collective-permute-start | bytes 245768 | tf_op jit(solution)/shard_map/ppermute | solution.py:241
  30.0 13.2 %collective-permute-start.12 = (bf16[160,256]{1,0:T(8,128)(2,1)S(1)}, bf16[160,256]{1,0:T(8,128)(2,1)S(1)}, u32[]{:S(2)}, u32[]{:S(2)}) collective-permute-start(bf16[160,256]{1,0:T(8,128)(2,1)S(1)} %collective-permute-done.3.refs_1_), channel_id=1, source_target_pairs={{0,2},{2,0},{1,3},{3,1},{4,6},{6,4},{5,7},{7,5},{8,10},{10,8},{9,1... | collective-permute-start | bytes 245768 | tf_op jit(solution)/shard_map/ppermute | solution.py:241
  33.0 10.7 %collective-permute-start.13 = (bf16[160,256]{1,0:T(8,128)(2,1)S(1)}, bf16[160,256]{1,0:T(8,128)(2,1)S(1)}, u32[]{:S(2)}, u32[]{:S(2)}) collective-permute-start(bf16[160,256]{1,0:T(8,128)(2,1)S(1)} %collective-permute-done.4.refs_2_), channel_id=1, source_target_pairs={{0,2},{2,0},{1,3},{3,1},{4,6},{6,4},{5,7},{7,5},{8,10},{10,8},{9,1... | collective-permute-start | bytes 245768 | tf_op jit(solution)/shard_map/ppermute | solution.py:241
  34.5 9.3 %collective-permute-start.14 = (bf16[160,256]{1,0:T(8,128)(2,1)S(1)}, bf16[160,256]{1,0:T(8,128)(2,1)S(1)}, u32[]{:S(2)}, u32[]{:S(2)}) collective-permute-start(bf16[160,256]{1,0:T(8,128)(2,1)S(1)} %collective-permute-done.5.refs_3_), channel_id=1, source_target_pairs={{0,2},{2,0},{1,3},{3,1},{4,6},{6,4},{5,7},{7,5},{8,10},{10,8},{9,1... | collective-permute-start | bytes 245768 | tf_op jit(solution)/shard_map/ppermute | solution.py:241
  44.2 7.2 %collective-permute-start.6 = (bf16[160,256]{1,0:T(8,128)(2,1)S(1)}, bf16[160,256]{1,0:T(8,128)(2,1)S(1)}, u32[]{:S(2)}, u32[]{:S(2)}) collective-permute-start(bf16[160,256]{1,0:T(8,128)(2,1)S(1)} %get-tuple-element.35.refs_0_), channel_id=1, source_target_pairs={{0,1},{1,0},{2,3},{3,2},{4,5},{5,4},{6,7},{7,6},{8,9},{9,8},{10,11... | collective-permute-start | bytes 245768 | tf_op jit(solution)/shard_map/ppermute | solution.py:241
  44.5 7.0 %collective-permute-start.7 = (bf16[160,256]{1,0:T(8,128)(2,1)S(1)}, bf16[160,256]{1,0:T(8,128)(2,1)S(1)}, u32[]{:S(2)}, u32[]{:S(2)}) collective-permute-start(bf16[160,256]{1,0:T(8,128)(2,1)S(1)} %collective-permute-done.3.refs_1_), channel_id=1, source_target_pairs={{0,1},{1,0},{2,3},{3,2},{4,5},{5,4},{6,7},{7,6},{8,9},{9,8},{10,11... | collective-permute-start | bytes 245768 | tf_op jit(solution)/shard_map/ppermute | solution.py:241
  44.8 6.7 %collective-permute-start.8 = (bf16[160,256]{1,0:T(8,128)(2,1)S(1)}, bf16[160,256]{1,0:T(8,128)(2,1)S(1)}, u32[]{:S(2)}, u32[]{:S(2)}) collective-permute-start(bf16[160,256]{1,0:T(8,128)(2,1)S(1)} %collective-permute-done.4.refs_2_), channel_id=1, source_target_pairs={{0,1},{1,0},{2,3},{3,2},{4,5},{5,4},{6,7},{7,6},{8,9},{9,8},{10,11... | collective-permute-start | bytes 245768 | tf_op jit(solution)/shard_map/ppermute | solution.py:241
  45.0 6.5 %collective-permute-start.9 = (bf16[160,256]{1,0:T(8,128)(2,1)S(1)}, bf16[160,256]{1,0:T(8,128)(2,1)S(1)}, u32[]{:S(2)}, u32[]{:S(2)}) collective-permute-start(bf16[160,256]{1,0:T(8,128)(2,1)S(1)} %collective-permute-done.5.refs_3_), channel_id=1, source_target_pairs={{0,1},{1,0},{2,3},{3,2},{4,5},{5,4},{6,7},{7,6},{8,9},{9,8},{10,11... | collective-permute-start | bytes 245768 | tf_op jit(solution)/shard_map/ppermute | solution.py:241
  51.1 6.6 %collective-permute-start.19 = (bf16[160,1024]{1,0:T(8,128)(2,1)S(1)}, bf16[160,1024]{1,0:T(8,128)(2,1)S(1)}, u32[]{:S(2)}, u32[]{:S(2)}) collective-permute-start(bf16[160,1024]{1,0:T(8,128)(2,1)S(1)} %get-tuple-element.45), channel_id=1, source_target_pairs={{0,1},{1,0},{2,3},{3,2},{4,5},{5,4},{6,7},{7,6},{8,9},{9,8},{10,11... | collective-permute-start | bytes 983048 | tf_op jit(solution)/shard_map/ppermute | solution.py:241
  57.3 6.6 %collective-permute-start.10 = (bf16[160,1024]{1,0:T(8,128)(2,1)S(1)}, bf16[160,1024]{1,0:T(8,128)(2,1)S(1)}, u32[]{:S(2)}, u32[]{:S(2)}) collective-permute-start(bf16[160,1024]{1,0:T(8,128)(2,1)S(1)} %get-tuple-element.42), channel_id=1, source_target_pairs={{0,1},{1,0},{2,3},{3,2},{4,5},{5,4},{6,7},{7,6},{8,9},{9,8},{10,11... | collective-permute-start | bytes 983048 | tf_op jit(solution)/shard_map/ppermute | solution.py:241
  58.4 6.8 %collective-permute-start.25 = (bf16[40,1024]{1,0:T(8,128)(2,1)S(1)}, bf16[40,1024]{1,0:T(8,128)(2,1)S(1)}, u32[]{:S(2)}, u32[]{:S(2)}) collective-permute-start(bf16[40,1024]{1,0:T(8,128)(2,1)S(1)} %get-tuple-element.52), channel_id=1, source_target_pairs={{0,2},{2,0},{1,3},{3,1},{4,6},{6,4},{5,7},{7,5},{8,10},{10,8},{9,1... | collective-permute-start | bytes 245768 | tf_op jit(solution)/shard_map/ppermute | solution.py:241
  60.1 13.4 %collective-permute-start.27 = (bf16[64,256]{1,0:T(8,128)(2,1)S(1)}, bf16[64,256]{1,0:T(8,128)(2,1)S(1)}, u32[]{:S(2)}, u32[]{:S(2)}) collective-permute-start(bf16[64,256]{1,0:T(8,128)(2,1)S(1)} %get-tuple-element.54), channel_id=1, source_target_pairs={{0,12},{4,0},{8,4},{12,8},{1,13},{5,1},{9,5},{13,9},{2,14},{6,2},{... | collective-permute-start | bytes 98312 | tf_op jit(solution)/shard_map/ppermute | solution.py:238
  63.3 13.2 %collective-permute-start.28 = (bf16[64,256]{1,0:T(8,128)(2,1)S(1)}, bf16[64,256]{1,0:T(8,128)(2,1)S(1)}, u32[]{:S(2)}, u32[]{:S(2)}) collective-permute-start(bf16[64,256]{1,0:T(8,128)(2,1)S(1)} %get-tuple-element.55), channel_id=1, source_target_pairs={{0,8},{4,12},{8,0},{12,4},{1,9},{5,13},{9,1},{13,5},{2,10},{6,14},... | collective-permute-start | bytes 98312 | tf_op jit(solution)/shard_map/ppermute | solution.py:238
  63.3 13.2 %collective-permute-start.29 = (bf16[64,256]{1,0:T(8,128)(2,1)S(1)}, bf16[64,256]{1,0:T(8,128)(2,1)S(1)}, u32[]{:S(2)}, u32[]{:S(2)}) collective-permute-start(bf16[64,256]{1,0:T(8,128)(2,1)S(1)} %get-tuple-element.56), channel_id=1, source_target_pairs={{0,4},{4,8},{8,12},{12,0},{1,5},{5,9},{9,13},{13,1},{2,6},{6,10},{... | collective-permute-start | bytes 98312 | tf_op jit(solution)/shard_map/ppermute | solution.py:238
  69.3 5.3 %collective-permute-start.20 = (bf16[40,1024]{1,0:T(8,128)(2,1)S(1)}, bf16[40,1024]{1,0:T(8,128)(2,1)S(1)}, u32[]{:S(2)}, u32[]{:S(2)}) collective-permute-start(bf16[40,1024]{1,0:T(8,128)(2,1)S(1)} %get-tuple-element.46), channel_id=1, source_target_pairs={{0,2},{2,0},{1,3},{3,1},{4,6},{6,4},{5,7},{7,5},{8,10},{10,8},{9,1... | collective-permute-start | bytes 245768 | tf_op jit(solution)/shard_map/ppermute | solution.py:241
  70.3 6.3 %collective-permute-start.26 = (bf16[40,1024]{1,0:T(8,128)(2,1)S(1)}, bf16[40,1024]{1,0:T(8,128)(2,1)S(1)}, u32[]{:S(2)}, u32[]{:S(2)}) collective-permute-start(bf16[40,1024]{1,0:T(8,128)(2,1)S(1)} %add_convert_fusion), channel_id=1, source_target_pairs={{0,12},{4,0},{8,4},{12,8},{1,13},{5,1},{9,5},{13,9},{2,14},{6,2},{... | collective-permute-start | bytes 245768 | tf_op jit(solution)/shard_map/ppermute | solution.py:238
  73.6 6.1 %collective-permute-start.24 = (bf16[40,1024]{1,0:T(8,128)(2,1)S(1)}, bf16[40,1024]{1,0:T(8,128)(2,1)S(1)}, u32[]{:S(2)}, u32[]{:S(2)}) collective-permute-start(bf16[40,1024]{1,0:T(8,128)(2,1)S(1)} %add_convert_fusion.1), channel_id=1, source_target_pairs={{0,8},{4,12},{8,0},{12,4},{1,9},{5,13},{9,1},{13,5},{2,10},{6,14},... | collective-permute-start | bytes 245768 | tf_op jit(solution)/shard_map/ppermute | solution.py:238
  74.7 6.2 %collective-permute-start.22 = (bf16[40,1024]{1,0:T(8,128)(2,1)S(1)}, bf16[40,1024]{1,0:T(8,128)(2,1)S(1)}, u32[]{:S(2)}, u32[]{:S(2)}) collective-permute-start(bf16[40,1024]{1,0:T(8,128)(2,1)S(1)} %add_convert_fusion.2), channel_id=1, source_target_pairs={{0,4},{4,8},{8,12},{12,0},{1,5},{5,9},{9,13},{13,1},{2,6},{6,10},{... | collective-permute-start | bytes 245768 | tf_op jit(solution)/shard_map/ppermute | solution.py:238
  (18 other events, 46.7 us)

commit v2 on v1

--- a/solution.py
+++ b/solution.py
@@ -18,7 +18,7 @@
 F32 = jnp.float32
 IN_VMEM = pl.BlockSpec(memory_space=pltpu.VMEM)
 IN_SMEM = pl.BlockSpec(memory_space=pltpu.SMEM)
-IN_HBM = pl.BlockSpec(memory_space=pl.ANY)
+IN_HBM = pl.BlockSpec(memory_space=pltpu.HBM)
 
 
 def struct(rows, columns, dtype=BF16):
@@ -45,40 +45,81 @@
     return lax.dot_general(a, b, (((1,), (1,)), ((), ())), preferred_element_type=F32)
 
 
+def dot_tn(a, b):
+    return lax.dot_general(a, b, (((0,), (0,)), ((), ())), preferred_element_type=F32)
+
+
 def iota(shape, dimension):
     return lax.broadcasted_iota(jnp.int32, shape, dimension)
 
 
-def wrapped(value, size):
-    return jnp.where(value >= size, value - size, value)
+def in_hbm(array):
+    return pltpu.with_memory_space_constraint(array, pltpu.HBM)
+
+
+def in_vmem(array):
+    return pltpu.with_memory_space_constraint(array, pltpu.VMEM)
 
 
 def columns_at(start, width):
     return pl.ds(pl.multiple_of(start * width, width), width)
 
 
-def pack_kernel(experts, at_ref, q_ref, m_ref, h_ref, tp_ref, sp_ref, r_ref, *outs):
-    rows, width = q_ref.shape[0], outs[0].shape[1]
+def thirds(array):
+    high = array.astype(BF16).astype(F32)
+    middle = (array - high).astype(BF16).astype(F32)
+    low = (array - high - middle).astype(BF16).astype(F32)
+    return [high, middle, low]
+
+
+def pack_kernel(experts, at_ref, q_hbm, m_hbm, h_hbm, tp_hbm, sp_hbm, r_hbm, rw_hbm, *refs):
+    outs = refs[:experts]
+    m_ref, tp_ref, sp_ref, r_ref, rw_ref, sems, small_sems = refs[experts:]
+    rows, width = q_hbm.shape[0], outs[0].shape[1]
     here = at_ref[0]
+    small = [
+        pltpu.make_async_copy(src, dst, small_sems.at[k])
+        for k, (src, dst) in enumerate(
+            ((tp_hbm, tp_ref), (sp_hbm, sp_ref), (r_hbm, r_ref), (rw_hbm, rw_ref))
+        )
+    ]
+    large = []
+    for step, out in enumerate(outs):
+        cols = columns_at(here ^ step, width)
+        large.append(
+            (
+                pltpu.make_async_copy(m_hbm.at[:, :, cols], m_ref.at[step], sems.at[0, step]),
+                pltpu.make_async_copy(q_hbm.at[:, cols], out.at[pl.ds(0, rows)], sems.at[1, step]),
+                pltpu.make_async_copy(
+                    h_hbm.at[:, cols], out.at[pl.ds(3 * rows, rows)], sems.at[2, step]
+                ),
+            )
+        )
+    for copy in small:
+        copy.start()
+    for copies in large:
+        for copy in copies:
+            copy.start()
+    for copy in small:
+        copy.wait()
     row = iota((META, rows), 0)
-    kinds = jnp.where(
-        row == 0,
-        tp_ref[...],
-        jnp.where(
-            row == 1,
-            sp_ref[...],
-            jnp.where(row == 2, r_ref[0:1, :], jnp.where(row == 3, r_ref[1:2, :], 0)),
-        ),
-    )
-    kinds = kinds.astype(F32).astype(BF16)
+    lines = [tp_ref[...], sp_ref[...], r_ref[0:1, :], r_ref[1:2, :]]
+    lines = [line.astype(F32) for line in lines]
+    lines += thirds(rw_ref[0:1, :]) + thirds(rw_ref[1:2, :])
+    kinds = jnp.zeros((META, rows), F32)
+    for k, line in enumerate(lines):
+        kinds = jnp.where(row == k, line, kinds)
+    kinds = kinds.astype(BF16)
     for step, out in enumerate(outs):
-        cols = columns_at(wrapped(here + step, experts), width)
-        out[0:rows, :] = q_ref[:, cols]
-        out[rows : 2 * rows, :] = m_ref[:, 0, cols]
-        out[2 * rows : 3 * rows, :] = m_ref[:, 1, cols]
-        out[3 * rows : 4 * rows, :] = h_ref[:, cols]
         moved = (iota((rows, width), 1) == iota((rows, width), 0) + step * rows).astype(BF16)
         out[4 * rows :, :] = dot(kinds, moved).astype(BF16)
+    for step, out in enumerate(outs):
+        large[step][0].wait()
+        out[rows : 2 * rows, :] = m_ref[step, :, 0, :]
+        out[2 * rows : 3 * rows, :] = m_ref[step, :, 1, :]
+    for copies in large:
+        copies[1].wait()
+        copies[2].wait()
 
 
 def prefetch_kernel(w1_ref, w2_ref, after_ref, o1_ref, o2_ref, sems):
@@ -95,8 +136,8 @@
         copy.wait()
 
 
-def attend_kernel(experts, rows, cap, at_ref, *refs):
-    messages, compact, attended = refs[:experts], refs[experts : 2 * experts], refs[2 * experts :]
+def attend_kernel(experts, rows, cap, at_ref, w1_ref, w2_ref, *refs):
+    messages, compact = refs[:experts], refs[experts:]
     width = messages[0].shape[1]
     count = experts * rows
     here = at_ref[0]
@@ -122,21 +163,27 @@
         context = dot(weight.astype(BF16), stacked(2)) / total
         parts.append((stacked(3).astype(F32) + context).astype(BF16))
     states = jnp.concatenate(parts, axis=1)
-    for block, out in enumerate(attended):
-        out[...] = states[block * rows : (block + 1) * rows, :]
     first, second = meta[2:3, :].astype(jnp.int32), meta[3:4, :].astype(jnp.int32)
-    expert = wrapped(here + iota((META, count), 0), experts)
+    expert = here ^ iota((META, count), 0)
     named = ((first == expert) | (second == expert)) & (iota((META, count), 0) < experts)
     before = (iota((count, count), 0) < iota((count, count), 1)) & (
         iota((count, count), 0) // rows == iota((count, count), 1) // rows
     )
     slot = dot(named.astype(BF16), before.astype(BF16)).astype(jnp.int32)
-    source = here - iota((META, count), 1) // rows
-    source = jnp.where(source < 0, source + experts, source)
+    source = here ^ (iota((META, count), 1) // rows)
     spot = jnp.where(named, source * cap + slot, -1)
     for step, out in enumerate(compact):
         place = iota((experts * cap, count), 0) == spot[step : step + 1, :]
-        out[...] = dot(place.astype(BF16), states).astype(BF16)
+        place = place.astype(BF16)
+        out[0 : experts * cap, :] = dot(place, states).astype(BF16)
+        leads = first == (here ^ step)
+        values = [jnp.where(leads, meta[4 + k : 5 + k, :], meta[7 + k : 8 + k, :]) for k in range(3)]
+        values.append(leads.astype(F32))
+        lines = jnp.zeros((META, count), F32)
+        for k, value in enumerate(values):
+            lines = jnp.where(iota((META, count), 0) == k, value, lines)
+        out[experts * cap :, :] = jnp.zeros((META, width), BF16)
+        out[experts * cap :, 0 : experts * cap] = dot_nt(lines.astype(BF16), place).astype(BF16)
 
 
 def first_kernel(experts, tile, at_ref, *refs):
@@ -145,68 +192,89 @@
     width = mine[0].shape[1]
     here, half = at_ref[0], at_ref[1]
     for step in range(experts):
-        source = here - step
-        source = jnp.where(source < 0, source + experts, source)
-        x_ref[:, columns_at(half * experts + source, width)] = mine[step][...]
-        x_ref[:, columns_at((1 - half) * experts + source, width)] = other[step][...]
-    values = x_ref[...].astype(F32)
-    center = jnp.mean(values, axis=-1, keepdims=True)
-    shifted = values - center
-    spread = jnp.mean(jnp.square(shifted), axis=-1, keepdims=True)
-    normed = shifted * lax.rsqrt(spread + EPSILON) * gain_ref[...] + bias_ref[...]
-    n_ref[...] = normed.astype(BF16)
-
-    @pl.loop(0, w_ref.shape[1] // tile)
-    def _(at):
-        cols = columns_at(at, tile)
+        source = here ^ step
+        x_ref[:, columns_at(half * experts + source, width)] = mine[step][0 : x_ref.shape[0], :]
+        x_ref[:, columns_at((1 - half) * experts + source, width)] = other[step][0 : x_ref.shape[0], :]
+    for at in range(0, x_ref.shape[0], META):
+        block = slice(at, at + META)
+        values = x_ref[block, :].astype(F32)
+        center = jnp.mean(values, axis=-1, keepdims=True)
+        shifted = values - center
+        spread = jnp.mean(jnp.square(shifted), axis=-1, keepdims=True)
+        normed = shifted * lax.rsqrt(spread + EPSILON) * gain_ref[...] + bias_ref[...]
+        n_ref[block, :] = normed.astype(BF16)
+    for at in range(0, w_ref.shape[1], tile):
+        cols = slice(at, at + tile)
         out_ref[:, cols] = jnp.maximum(dot(n_ref[...], w_ref[:, cols]), 0.0).astype(BF16)
 
 
 def second_kernel(tile, at_ref, a_ref, w_ref, sent_ref, kept_ref):
-    half = at_ref[1]
-    tiles = sent_ref.shape[1] // tile
-
-    @pl.loop(0, tiles)
-    def _(at):
-        cols = columns_at(at, tile)
-        sent_ref[:, cols] = dot(
-            a_ref[...], w_ref[:, columns_at((1 - half) * tiles + at, tile)]
-        ).astype(BF16)
-
-    @pl.loop(0, tiles)
-    def _(at):
-        cols = columns_at(at, tile)
-        kept_ref[:, cols] = dot(
-            a_ref[...], w_ref[:, columns_at(half * tiles + at, tile)]
-        ).astype(BF16)
-
-
-def split_kernel(experts, at_ref, kept_ref, got_ref, *refs):
-    outs, total = refs[:experts], refs[experts]
-    cap = outs[0].shape[0]
+    columns = sent_ref.shape[1]
+    lower = at_ref[1] == 0
+    for at in range(0, columns, tile):
+        low = dot(a_ref[...], w_ref[:, at : at + tile])
+        high = dot(a_ref[...], w_ref[:, columns + at : columns + at + tile])
+        sent_ref[:, at : at + tile] = jnp.where(lower, high, low).astype(BF16)
+        kept_ref[:, at : at + tile] = jnp.where(lower, low, high).astype(BF16)
+
+
+def away_kernel(experts, order, at_ref, kept_ref, got_ref, *refs):
+    outs, total = refs[:-1], refs[-1]
     total[...] = kept_ref[...].astype(F32) + got_ref[...].astype(F32)
-    for step, out in enumerate(outs):
-        target = wrapped(at_ref[0] + step, experts)
-        out[...] = total[pl.ds(pl.multiple_of(target * cap, 8), cap), :].astype(out.dtype)
-
-
-def mix_kernel(experts, at_ref, weight_ref, *refs):
-    returned, states = refs[:experts], refs[experts : 2 * experts]
-    out_ref, total = refs[2 * experts :]
-    width = states[0].shape[1]
-    share = jnp.zeros(total.shape, F32)
+    cap = total.shape[0] // experts
+    each = experts // len(outs)
+    for k, step in enumerate(order):
+        rows = pl.ds(pl.multiple_of((at_ref[0] ^ step) * cap, 8), cap)
+        at = k % each * cap
+        outs[k // each][at : at + cap, :] = total[rows, :].astype(BF16)
+
+
+def base_kernel(experts, at_ref, kept_ref, got_ref, *refs):
+    blocks, bases, factors = refs[:experts], refs[experts : 2 * experts], refs[2 * experts : -3]
+    total, states, columns = refs[-3:]
+    count = total.shape[0]
+    cap = count // experts
+    width = blocks[0].shape[1]
+    lines = blocks[0][count:, 0:count]
+    same = (iota((count, count), 0) == iota((count, count), 1)).astype(BF16)
+    columns[:, 0:META] = dot_nt(same, lines)
+    weight = columns[:, 0:1] + columns[:, 1:2] + columns[:, 2:3]
+    leads = columns[:, 3:4]
     for step in range(experts):
-        weight = weight_ref[step]
-        high = weight.astype(BF16)
-        rest = weight - high.astype(F32)
-        middle = rest.astype(BF16)
-        low = (rest - middle.astype(F32)).astype(BF16)
-        rows = returned[step][...]
-        share = share + (dot(high, rows) + (dot(middle, rows) + dot(low, rows)))
-    total[...] = share
+        states[:, columns_at(at_ref[0] ^ step, width)] = blocks[step][0:count, :].astype(F32)
+    total[...] = (kept_ref[...].astype(F32) + got_ref[...].astype(F32)) * weight + (
+        leads * states[...]
+    )
+    columns[...] = jnp.broadcast_to(weight, columns.shape)
     for step in range(experts):
-        cols = columns_at(wrapped(at_ref[0] + step, experts), width)
-        out_ref[:, cols] = (states[step][...].astype(F32) + total[:, cols]).astype(BF16)
+        rows = pl.ds(pl.multiple_of((at_ref[0] ^ step) * cap, 8), cap)
+        bases[step][...] = total[rows, :]
+        factors[step][...] = columns[rows, :]
+
+
+def join_kernel(came_ref, *refs):
+    count = len(refs) // 3
+    cap = refs[0].shape[0]
+    for k in range(count):
+        base_ref, factor_ref, out_ref = refs[k], refs[count + k], refs[2 * count + k]
+        came = came_ref[k * cap : (k + 1) * cap, :].astype(F32)
+        out_ref[...] = (base_ref[...] + factor_ref[:, 0:1] * came).astype(BF16)
+
+
+def mix_kernel(experts, cap, at_ref, routes_ref, *refs):
+    returned, out_ref = refs[:experts], refs[experts]
+    rows = out_ref.shape[0]
+    expert = at_ref[0] ^ iota((META, rows), 0)
+    named = (routes_ref[0:1, :] == expert) | (routes_ref[1:2, :] == expert)
+    named = named & (iota((META, rows), 0) < experts)
+    before = (iota((rows, rows), 0) < iota((rows, rows), 1)).astype(BF16)
+    slot = dot(named.astype(BF16), before).astype(jnp.int32)
+    slot = jnp.where(named, slot, -1)
+    share = jnp.zeros(out_ref.shape, F32)
+    for step in range(experts):
+        place = (iota((cap, rows), 0) == slot[step : step + 1, :]).astype(BF16)
+        share = share + dot_tn(place, returned[step][...])
+    out_ref[...] = share.astype(BF16)
 
 
 def head_shards(
@@ -232,10 +300,9 @@
     at = jnp.stack([here, half]).astype(jnp.int32)
 
     def along(array, step):
-        if step % experts == 0:
+        if step == 0:
             return array
-        pairs = [(i, (i + step) % experts) for i in range(experts)]
-        return lax.ppermute(array, "expert", pairs)
+        return lax.ppermute(array, "expert", [(i, i ^ step) for i in range(experts)])
 
     def swap(array, axis):
         return lax.ppermute(array, axis, [(0, 1), (1, 0)])
@@ -243,18 +310,30 @@
     packed = call(
         functools.partial(pack_kernel, experts),
         [struct(4 * rows + META, width)] * experts,
-        [IN_SMEM] + [IN_VMEM] * 6,
+        [IN_SMEM] + [IN_HBM] * 7,
+        scratch=[
+            pltpu.VMEM((experts, rows, 2, width), BF16),
+            pltpu.VMEM((1, rows), jnp.int32),
+            pltpu.VMEM((1, rows), jnp.int32),
+            pltpu.VMEM((2, rows), jnp.int32),
+            pltpu.VMEM((2, rows), F32),
+            pltpu.SemaphoreType.DMA((3, experts)),
+            pltpu.SemaphoreType.DMA((4,)),
+        ],
         moved=16 * rows * columns,
     )(
         at,
-        queries,
-        memory,
-        hidden,
-        target_pair.reshape(1, rows),
-        source_pair.reshape(1, rows),
-        routes.T,
-    )
-    messages = [along(packed[step], step) for step in range(experts)]
+        in_hbm(queries),
+        in_hbm(memory),
+        in_hbm(hidden),
+        in_hbm(target_pair.reshape(1, rows)),
+        in_hbm(source_pair.reshape(1, rows)),
+        in_hbm(routes.T),
+        in_hbm(route_weight.T),
+    )
+    order = list(range(experts // 2, experts)) + list(reversed(range(experts // 2)))
+    messages = {step: along(packed[step], step) for step in order}
+    messages = [messages[step] for step in range(experts)]
 
     w_in, w_out = pl.pallas_call(
         prefetch_kernel,
@@ -262,41 +341,33 @@
             pltpu.VMEM((model, hidden_units), BF16),
             pltpu.VMEM((hidden_units, model), BF16),
         ],
-        in_specs=[IN_HBM, IN_HBM, IN_HBM],
+        in_specs=[IN_HBM, IN_HBM, IN_VMEM],
         out_specs=[IN_VMEM, IN_VMEM],
         scratch_shapes=[pltpu.SemaphoreType.DMA((2, 4))],
         compiler_params=pltpu.CompilerParams(vmem_limit_bytes=VMEM_LIMIT),
         cost_estimate=pl.CostEstimate(
             flops=0, bytes_accessed=8 * model * hidden_units, transcendentals=0
         ),
-    )(expert_in[0], expert_out[0], packed[0])
-
-    named = jnp.any(routes[:, :, None] == jnp.arange(experts)[None, None, :], axis=1)
-    named = named.astype(jnp.int32)
-    slots = jnp.cumsum(named, axis=0) - named
-    chosen = (here - jnp.arange(experts)) % experts
-    slot = jnp.take(slots.T, chosen, axis=0)
-    weight = jnp.sum(
-        jnp.where(routes[None, :, :] == chosen[:, None, None], route_weight[None, :, :], 0.0),
-        axis=2,
-    )
-    weights = jnp.where(
-        slot[:, :, None] == jnp.arange(cap)[None, None, :], weight[:, :, None], 0.0
-    )
-
-    attended = call(
+    )(in_hbm(expert_in[0]), in_hbm(expert_out[0]), packed[0])
+
+    compact = call(
         functools.partial(attend_kernel, experts, rows, cap),
-        [struct(experts * cap, width)] * experts + [struct(rows, width)] * experts,
-        [IN_SMEM] + [IN_VMEM] * experts,
+        [struct(experts * cap + META, width)] * experts,
+        [IN_SMEM] + [IN_VMEM] * (2 + experts),
         flops=8 * experts * experts * rows * rows * width,
         moved=16 * rows * columns,
-    )(at, *messages)
-    compact, states = attended[:experts], attended[experts:]
-
-    own = [along(compact[step], step) for step in range(experts)]
-    far = [swap(block, "dp") for block in own]
-
-    def first(blocks):
+    )(at, in_vmem(w_in), in_vmem(w_out), *messages)
+
+    far = {0: swap(compact[0], "dp")}
+    own = {0: compact[0]}
+    early, late = order[: experts // 2], order[experts // 2 : -1]
+    own.update({step: along(compact[step], step) for step in early})
+    held, far[0] = lax.optimization_barrier(([compact[step] for step in late], far[0]))
+    own.update({step: along(block, step) for step, block in zip(late, held)})
+    far.update({step: swap(own[step], "dp") for step in order[:-1]})
+    own_other = {step: swap(own[step], "mp") for step in own}
+
+    def first(blocks, others):
         count = experts * cap
         return call(
             functools.partial(first_kernel, experts, 512),
@@ -307,11 +378,11 @@
             moved=2 * model * hidden_units,
         )(
             at,
-            *blocks,
-            *[swap(block, "mp") for block in blocks],
+            *[blocks[step] for step in range(experts)],
+            *[others[step] for step in range(experts)],
             norm_gain.reshape(1, model),
             norm_bias.reshape(1, model),
-            pltpu.with_memory_space_constraint(w_in, pltpu.VMEM),
+            in_vmem(w_in),
         )[0]
 
     def second(active):
@@ -322,34 +393,46 @@
             [IN_SMEM, IN_VMEM, IN_VMEM],
             flops=2 * count * model * hidden_units,
             moved=2 * model * hidden_units,
-        )(at, active, pltpu.with_memory_space_constraint(w_out, pltpu.VMEM))
+        )(at, active, in_vmem(w_out))
         return kept, swap(sent, "mp")
 
-    def split(kept, got, dtype):
-        return call(
-            functools.partial(split_kernel, experts),
-            [struct(cap, columns, dtype)] * experts,
-            [IN_SMEM, IN_VMEM, IN_VMEM],
-            scratch=[pltpu.VMEM((experts * cap, columns), F32)],
-            moved=8 * experts * cap * columns,
-        )(at, kept, got)
-
-    active_own = first(own)
-    active_far = first(far)
-    gone = [swap(block, "dp") for block in split(*second(active_far), BF16)]
-    mine = split(*second(active_own), F32)
-    summed = [(block + came.astype(F32)).astype(BF16) for block, came in zip(mine, gone)]
-    returned = [along(summed[step], step) for step in range(experts)]
-    home = [along(states[step], -step) for step in range(experts)]
+    kept, got = second(first(own, own_other))
+    far, kept = lax.optimization_barrier((far, kept))
+    far_other = {step: swap(far[step], "mp") for step in order}
+    parts = call(
+        functools.partial(away_kernel, experts, order),
+        [struct(2 * cap, columns)] * (experts // 2),
+        [IN_SMEM, IN_VMEM, IN_VMEM],
+        scratch=[pltpu.VMEM((experts * cap, columns), F32)],
+        moved=8 * experts * cap * columns,
+    )(at, *second(first(far, far_other)))
+    came = [swap(part, "dp") for part in parts]
+    based = call(
+        functools.partial(base_kernel, experts),
+        [struct(cap, columns, F32)] * experts + [struct(cap, HEAD, F32)] * experts,
+        [IN_SMEM] + [IN_VMEM] * (2 + experts),
+        scratch=[pltpu.VMEM((experts * cap, columns), F32)] * 2
+        + [pltpu.VMEM((experts * cap, HEAD), F32)],
+        moved=16 * experts * cap * columns,
+    )(at, kept, got, *[own[step] for step in range(experts)])
+    returned = {}
+    for k, part in enumerate(came):
+        steps = order[2 * k : 2 * k + 2]
+        joined = call(
+            join_kernel,
+            [struct(cap, columns)] * 2,
+            [IN_VMEM] * 5,
+            moved=32 * cap * columns,
+        )(part, *[based[step] for step in steps], *[based[experts + step] for step in steps])
+        returned.update({step: along(block, step) for step, block in zip(steps, joined)})
 
     return call(
-        functools.partial(mix_kernel, experts),
+        functools.partial(mix_kernel, experts, cap),
         [struct(rows, columns)],
-        [IN_SMEM] + [IN_VMEM] * (2 * experts + 1),
-        scratch=[pltpu.VMEM((rows, columns), F32)],
-        flops=6 * rows * experts * cap * columns,
+        [IN_SMEM] + [IN_VMEM] * (experts + 1),
+        flops=2 * rows * experts * cap * columns,
         moved=4 * rows * columns,
-    )(at, weights, *returned, *home)[0]
+    )(at, routes.T, *[returned[step] for step in range(experts)])[0]
 
 
 def shards(
@@ -450,6 +533,7 @@
         and memory.shape[0] == rows
         and experts * rows <= columns // experts
         and experts <= META
+        and experts & (experts - 1) == 0
     )
     return (head_shards if by_heads else shards)(hidden, queries, memory, *rest)
 

time: 83 us -> 68.1 us (0.82)
  starting transfers between devices: 35 us -> 22.4 us
  local copies, waits for them, and re-layouts: 12.3 us -> 0.01 us
  waiting for transfers between devices: 15.9 us -> 22.9 us
  Pallas kernels: 18.8 us -> 22.4 us
    unnamed x24 -> x6, local copies, waits for them, and re-layouts: 11.5 us -> 0.01 us
    ppermute x12 -> x9, starting transfers between devices: 22.7 us -> 14.5 us  [along(): lax.ppermute(array, 'expert', [(i, i ^ step) for i in range(experts)])]
    ppermute x18 -> x16, waiting for transfers between devices: 2.86 us -> 7.62 us  [swap(): return lax.ppermute(array, axis, [(0, 1), (1, 0)])]
    pallas_call x1, Pallas kernels: 1.2 us -> 5.92 us  [head_shards(): pl.pallas_call(prefetch_kernel, out_shape=[pltpu.VMEM((model, hidden_unit...]
    ppermute x18 -> x16, starting transfers between devices: 12.2 us -> 7.99 us  [swap(): return lax.ppermute(array, axis, [(0, 1), (1, 0)])]
    ppermute x12 -> x9, waiting for transfers between devices: 13 us -> 15.3 us  [along(): lax.ppermute(array, 'expert', [(i, i ^ step) for i in range(experts)])]
    pallas_call x2, Pallas kernels: 6.33 us -> 4.99 us  [first(): call(functools.partial(first_kernel, experts, 512), [struct(count, hidden...]
    pallas_call x2, Pallas kernels: 5.33 us -> 4.2 us  [second(): call(functools.partial(second_kernel, 512), [struct(count, columns)] * 2,...]
  transfers between devices with their start and end apart: 30 -> 25, of which waited for: 10 -> 14; matrix products, arithmetic and copies ran while one was open for 2% -> 0% of each run, Pallas kernels for 17% -> 18%
where the time goes in v2:
time: 68.1 us; the launch traced here: 68 us
  waiting for transfers between devices  22.9 us (34%)
  Pallas kernels  22.4 us (33%)
  starting transfers between devices  22.4 us (33%)
    ppermute x9, waiting for transfers between devices, along(): lax.ppermute(array, 'expert', [(i, i ^ step) for i in range(experts)])  15.3 us
    ppermute x9, starting transfers between devices, along(): lax.ppermute(array, 'expert', [(i, i ^ step) for i in range(experts)])  14.5 us
    ppermute x16, starting transfers between devices, swap(): return lax.ppermute(array, axis, [(0, 1), (1, 0)])  7.99 us
    ppermute x16, waiting for transfers between devices, swap(): return lax.ppermute(array, axis, [(0, 1), (1, 0)])  7.62 us
    pallas_call x1, Pallas kernels, head_shards(): pl.pallas_call(prefetch_kernel, out_shape=[pltpu.VMEM((model, hidden_unit...  5.92 us
    pallas_call x2, Pallas kernels, first(): call(functools.partial(first_kernel, experts, 512), [struct(count, hidden...  4.99 us
    pallas_call x2, Pallas kernels, second(): call(functools.partial(second_kernel, 512), [struct(count, columns)] * 2,...  4.2 us
    pallas_call x1, Pallas kernels, head_shards(): call(functools.partial(pack_kernel, experts), [struct(4 * rows + META, wi...  2.35 us
  transfers between devices with their start and end apart: 25, of which 14 were waited for; matrix products, arithmetic and copies ran while one was open for 0% of the time, Pallas kernels for 18%

profile of v2, /device:TPU:0, one launch (start us, length us, event | category | flops | bytes accessed | tf_op | source)
XLA Modules:
  0.0 68.0 jit_solution(8067456154388263396)
XLA Ops:
  0.1 2.4 %shard_map.109 = (bf16[272,256]{1,0:T(8,128)(2,1)S(1)}, bf16[272,256]{1,0:T(8,128)(2,1)S(1)}, bf16[272,256]{1,0:T(8,128)(2,1)S(1)}, bf16[272,256]{1,0:T(8,128)(2,1)S(1)}) custom-call(s32[2]{0:T(128)S(1)} %pad_add_fusion.at_ref, bf16[64,1024]{1,0:T(8,128)(2,1)} %q_hbm.1, bf16[64,2,1024]{2,1,0:T(2,128)(2,1)} %m_hbm.1, bf16[64,1024]{1,0:T(8,128)(2,1)} %h_hbm.1, ...), custom_call_target="tpu_custom_call" | custom-call | bytes 1048576 | tf_op jit(solution)/shard_map/pallas_call | solution.py:310
  2.4 3.1 %collective-permute-start = (bf16[272,256]{1,0:T(8,128)(2,1)S(1)}, bf16[272,256]{1,0:T(8,128)(2,1)S(1)}, u32[]{:S(2)}, u32[]{:S(2)}) collective-permute-start(bf16[272,256]{1,0:T(8,128)(2,1)S(1)} %get-tuple-element.43), channel_id=1, source_target_pairs={{0,4},{4,0},{8,12},{12,8},{1,5},{5,1},{9,13},{13,9},{2,6},{6,2},{1... | collective-permute-start | bytes 417800 | tf_op jit(solution)/shard_map/ppermute | solution.py:305
  5.5 2.6 %collective-permute-start.1 = (bf16[272,256]{1,0:T(8,128)(2,1)S(1)}, bf16[272,256]{1,0:T(8,128)(2,1)S(1)}, u32[]{:S(2)}, u32[]{:S(2)}) collective-permute-start(bf16[272,256]{1,0:T(8,128)(2,1)S(1)} %get-tuple-element.44), channel_id=1, source_target_pairs={{0,8},{4,12},{8,0},{12,4},{1,9},{5,13},{9,1},{13,5},{2,10},{6,14},... | collective-permute-start | bytes 417800 | tf_op jit(solution)/shard_map/ppermute | solution.py:305
  8.1 5.9 %shard_map.110 = (bf16[2048,2048]{1,0:T(8,128)(2,1)S(1)}, bf16[2048,2048]{1,0:T(8,128)(2,1)S(1)}) custom-call(bf16[2048,2048]{1,0:T(8,128)(2,1)} %bitcast.16, bf16[2048,2048]{1,0:T(8,128)(2,1)} %bitcast.17, bf16[272,256]{1,0:T(8,128)(2,1)S(1)} %get-tuple-element.40.after_ref.refs_0_), custom_call_target="tpu_custom_call" | custom-call | bytes 33554432 | tf_op jit(solution)/shard_map/pallas_call | solution.py:338
  14.1 4.9 %collective-permute-done.1.refs_2_ = bf16[272,256]{1,0:T(8,128)(2,1)S(1)} collective-permute-done((bf16[272,256]{1,0:T(8,128)(2,1)S(1)}, bf16[272,256]{1,0:T(8,128)(2,1)S(1)}, u32[]{:S(2)}, u32[]{:S(2)}) %collective-permute-start.1) | collective-permute-done | bytes 139296 | tf_op jit(solution)/shard_map/ppermute | solution.py:305
  19.0 1.4 %shard_map.111 = (bf16[176,256]{1,0:T(8,128)(2,1)S(1)}, bf16[176,256]{1,0:T(8,128)(2,1)S(1)}, bf16[176,256]{1,0:T(8,128)(2,1)S(1)}, bf16[176,256]{1,0:T(8,128)(2,1)S(1)}) custom-call(s32[2]{0:T(128)S(1)} %pad_add_fusion.at_ref, bf16[2048,2048]{1,0:T(8,128)(2,1)S(1)} %get-tuple-element.41.w1_ref.refs_10_, ...), custom_call_target="tpu_custom_call" | custom-call | flops 134217728 | bytes 1048576 | tf_op jit(solution)/shard_map/pallas_call | solution.py:353
  20.5 1.6 %collective-permute-start.3 = (bf16[176,256]{1,0:T(8,128)(2,1)S(1)}, bf16[176,256]{1,0:T(8,128)(2,1)S(1)}, u32[]{:S(2)}, u32[]{:S(2)}) collective-permute-start(bf16[176,256]{1,0:T(8,128)(2,1)S(1)} %get-tuple-element.47.refs_0_), channel_id=1, source_target_pairs={{0,2},{2,0},{1,3},{3,1},{4,6},{6,4},{5,7},{7,5},{8,10},{10,8},{9,1... | collective-permute-start | bytes 270344 | tf_op jit(solution)/shard_map/ppermute | solution.py:308
  22.0 3.1 %collective-permute-start.6 = (bf16[176,256]{1,0:T(8,128)(2,1)S(1)}, bf16[176,256]{1,0:T(8,128)(2,1)S(1)}, u32[]{:S(2)}, u32[]{:S(2)}) collective-permute-start(bf16[176,256]{1,0:T(8,128)(2,1)S(1)} %get-tuple-element.50), channel_id=1, source_target_pairs={{0,8},{4,12},{8,0},{12,4},{1,9},{5,13},{9,1},{13,5},{2,10},{6,14},... | collective-permute-start | bytes 270344 | tf_op jit(solution)/shard_map/ppermute | solution.py:305
  25.1 1.4 %collective-permute-start.8 = (bf16[176,256]{1,0:T(8,128)(2,1)S(1)}, bf16[176,256]{1,0:T(8,128)(2,1)S(1)}, u32[]{:S(2)}, u32[]{:S(2)}) collective-permute-start(bf16[176,256]{1,0:T(8,128)(2,1)S(1)} %get-tuple-element.51), channel_id=1, source_target_pairs={{0,12},{4,8},{8,4},{12,0},{1,13},{5,9},{9,5},{13,1},{2,14},{6,10},... | collective-permute-start | bytes 270344 | tf_op jit(solution)/shard_map/ppermute | solution.py:305
  27.2 3.2 %collective-permute-done.6.refs_2_ = bf16[176,256]{1,0:T(8,128)(2,1)S(1)} collective-permute-done((bf16[176,256]{1,0:T(8,128)(2,1)S(1)}, bf16[176,256]{1,0:T(8,128)(2,1)S(1)}, u32[]{:S(2)}, u32[]{:S(2)}) %collective-permute-start.6) | collective-permute-done | bytes 90144 | tf_op jit(solution)/shard_map/ppermute | solution.py:305
  30.4 1.5 %collective-permute-done.8.refs_3_ = bf16[176,256]{1,0:T(8,128)(2,1)S(1)} collective-permute-done((bf16[176,256]{1,0:T(8,128)(2,1)S(1)}, bf16[176,256]{1,0:T(8,128)(2,1)S(1)}, u32[]{:S(2)}, u32[]{:S(2)}) %collective-permute-start.8) | collective-permute-done | bytes 90144 | tf_op jit(solution)/shard_map/ppermute | solution.py:305
  33.0 1.5 %collective-permute-start.9 = (bf16[176,256]{1,0:T(8,128)(2,1)S(1)}, bf16[176,256]{1,0:T(8,128)(2,1)S(1)}, u32[]{:S(2)}, u32[]{:S(2)}) collective-permute-start(bf16[176,256]{1,0:T(8,128)(2,1)S(1)} %collective-permute-done.8.refs_3_), channel_id=1, source_target_pairs={{0,2},{2,0},{1,3},{3,1},{4,6},{6,4},{5,7},{7,5},{8,10},{10,8},{9,1... | collective-permute-start | bytes 270344 | tf_op jit(solution)/shard_map/ppermute | solution.py:308
  35.0 2.5 %shard_map.112.a_ref = bf16[160,2048]{1,0:T(8,128)(2,1)S(1)} custom-call(s32[2]{0:T(128)S(1)} %pad_add_fusion.at_ref, bf16[176,256]{1,0:T(8,128)(2,1)S(1)} %get-tuple-element.47.refs_0_, bf16[176,256]{1,0:T(8,128)(2,1)S(1)} %collective-permute-done.4.refs_1_, bf16[176,256]{1,0:T(8,128)(2,1)S(1)} %collective-permute-done.6.refs_2_, ...), custom_call_target="tpu_custom_call" | custom-call | flops 1342177280 | bytes 8388608 | tf_op jit(solution)/shard_map/pallas_call | solution.py:372
  37.5 2.1 %shard_map.113 = (bf16[160,1024]{1,0:T(8,128)(2,1)S(1)}, bf16[160,1024]{1,0:T(8,128)(2,1)S(1)}) custom-call(s32[2]{0:T(128)S(1)} %pad_add_fusion.at_ref, bf16[160,2048]{1,0:T(8,128)(2,1)S(1)} %shard_map.112.a_ref, bf16[2048,2048]{1,0:T(8,128)(2,1)S(1)} %get-tuple-element.42.w2_ref.w_ref), custom_call_target="tpu_custom_call" | custom-call | flops 1342177280 | bytes 8388608 | tf_op jit(solution)/shard_map/pallas_call | solution.py:390
  39.8 1.4 %collective-permute-done.5.refs_1_ = bf16[176,256]{1,0:T(8,128)(2,1)S(1)} collective-permute-done((bf16[176,256]{1,0:T(8,128)(2,1)S(1)}, bf16[176,256]{1,0:T(8,128)(2,1)S(1)}, u32[]{:S(2)}, u32[]{:S(2)}) %collective-permute-start.5) | collective-permute-done | bytes 90144 | tf_op jit(solution)/shard_map/ppermute | solution.py:308
  43.1 2.5 %shard_map.114.a_ref = bf16[160,2048]{1,0:T(8,128)(2,1)S(1)} custom-call(s32[2]{0:T(128)S(1)} %pad_add_fusion.at_ref, bf16[176,256]{1,0:T(8,128)(2,1)S(1)} %collective-permute-done.3.refs_0_, bf16[176,256]{1,0:T(8,128)(2,1)S(1)} %collective-permute-done.5.refs_1_, bf16[176,256]{1,0:T(8,128)(2,1)S(1)} %collective-permute-done.7.refs_2_, ...), custom_call_target="tpu_custom_call" | custom-call | flops 1342177280 | bytes 8388608 | tf_op jit(solution)/shard_map/pallas_call | solution.py:372
  45.6 2.1 %shard_map.115 = (bf16[160,1024]{1,0:T(8,128)(2,1)S(1)}, bf16[160,1024]{1,0:T(8,128)(2,1)S(1)}) custom-call(s32[2]{0:T(128)S(1)} %pad_add_fusion.at_ref, bf16[160,2048]{1,0:T(8,128)(2,1)S(1)} %shard_map.114.a_ref, bf16[2048,2048]{1,0:T(8,128)(2,1)S(1)} %get-tuple-element.42.w2_ref.w_ref), custom_call_target="tpu_custom_call" | custom-call | flops 1342177280 | bytes 8388608 | tf_op jit(solution)/shard_map/pallas_call | solution.py:390
  48.3 1.1 %collective-permute-done.18.got_ref = bf16[160,1024]{1,0:T(8,128)(2,1)S(1)} collective-permute-done((bf16[160,1024]{1,0:T(8,128)(2,1)S(1)}, bf16[160,1024]{1,0:T(8,128)(2,1)S(1)}, u32[]{:S(2)}, u32[]{:S(2)}) %collective-permute-start.18) | collective-permute-done | bytes 327712 | tf_op jit(solution)/shard_map/ppermute | solution.py:308
  50.7 1.5 %collective-permute-start.19 = (bf16[80,1024]{1,0:T(8,128)(2,1)S(1)}, bf16[80,1024]{1,0:T(8,128)(2,1)S(1)}, u32[]{:S(2)}, u32[]{:S(2)}) collective-permute-start(bf16[80,1024]{1,0:T(8,128)(2,1)S(1)} %get-tuple-element.59), channel_id=1, source_target_pairs={{0,2},{2,0},{1,3},{3,1},{4,6},{6,4},{5,7},{7,5},{8,10},{10,8},{9,1... | collective-permute-start | bytes 491528 | tf_op jit(solution)/shard_map/ppermute | solution.py:308
  53.2 4.0 %collective-permute-done.22.came_ref = bf16[80,1024]{1,0:T(8,128)(2,1)S(1)} collective-permute-done((bf16[80,1024]{1,0:T(8,128)(2,1)S(1)}, bf16[80,1024]{1,0:T(8,128)(2,1)S(1)}, u32[]{:S(2)}, u32[]{:S(2)}) %collective-permute-start.22) | collective-permute-done | bytes 163872 | tf_op jit(solution)/shard_map/ppermute | solution.py:308
  57.3 1.1 %collective-permute-start.23 = (bf16[40,1024]{1,0:T(8,128)(2,1)S(1)}, bf16[40,1024]{1,0:T(8,128)(2,1)S(1)}, u32[]{:S(2)}, u32[]{:S(2)}) collective-permute-start(bf16[40,1024]{1,0:T(8,128)(2,1)S(1)} %get-tuple-element.73), channel_id=1, source_target_pairs={{0,8},{4,12},{8,0},{12,4},{1,9},{5,13},{9,1},{13,5},{2,10},{6,14},... | collective-permute-start | bytes 245768 | tf_op jit(solution)/shard_map/ppermute | solution.py:305
  58.4 2.0 %collective-permute-start.24 = (bf16[40,1024]{1,0:T(8,128)(2,1)S(1)}, bf16[40,1024]{1,0:T(8,128)(2,1)S(1)}, u32[]{:S(2)}, u32[]{:S(2)}) collective-permute-start(bf16[40,1024]{1,0:T(8,128)(2,1)S(1)} %get-tuple-element.74), channel_id=1, source_target_pairs={{0,12},{4,8},{8,4},{12,0},{1,13},{5,9},{9,5},{13,1},{2,14},{6,10},... | collective-permute-start | bytes 245768 | tf_op jit(solution)/shard_map/ppermute | solution.py:305
  61.1 5.0 %collective-permute-done.23.refs_2_ = bf16[40,1024]{1,0:T(8,128)(2,1)S(1)} collective-permute-done((bf16[40,1024]{1,0:T(8,128)(2,1)S(1)}, bf16[40,1024]{1,0:T(8,128)(2,1)S(1)}, u32[]{:S(2)}, u32[]{:S(2)}) %collective-permute-start.23) | collective-permute-done | bytes 81952 | tf_op jit(solution)/shard_map/ppermute | solution.py:305
  66.3 1.7 %shard_map.120 = bf16[64,1024]{1,0:T(8,128)(2,1)} custom-call(s32[2]{0:T(128)S(1)} %pad_add_fusion.at_ref, s32[2,64]{1,0:T(2,128)S(1)} %bitcast.15, bf16[40,1024]{1,0:T(8,128)(2,1)S(1)} %get-tuple-element.66.refs_0_, bf16[40,1024]{1,0:T(8,128)(2,1)S(1)} %collective-permute-done.21.refs_1_, bf16[40,1024]{1,0:T(8,128)(2,1)S(1)} %collective-permute-done.23.refs_2_, ...), custom_call_target="tpu_custom_call" | custom-call | flops 20971520 | bytes 262144 | tf_op jit(solution)/shard_map/pallas_call | solution.py:429
  (45 shorter events, 8.4 us)
Async XLA Ops:
  2.4 11.6 %collective-permute-start = (bf16[272,256]{1,0:T(8,128)(2,1)S(1)}, bf16[272,256]{1,0:T(8,128)(2,1)S(1)}, u32[]{:S(2)}, u32[]{:S(2)}) collective-permute-start(bf16[272,256]{1,0:T(8,128)(2,1)S(1)} %get-tuple-element.43), channel_id=1, source_target_pairs={{0,4},{4,0},{8,12},{12,8},{1,5},{5,1},{9,13},{13,9},{2,6},{6,2},{1... | collective-permute-start | bytes 417800 | tf_op jit(solution)/shard_map/ppermute | solution.py:305
  5.5 13.5 %collective-permute-start.1 = (bf16[272,256]{1,0:T(8,128)(2,1)S(1)}, bf16[272,256]{1,0:T(8,128)(2,1)S(1)}, u32[]{:S(2)}, u32[]{:S(2)}) collective-permute-start(bf16[272,256]{1,0:T(8,128)(2,1)S(1)} %get-tuple-element.44), channel_id=1, source_target_pairs={{0,8},{4,12},{8,0},{12,4},{1,9},{5,13},{9,1},{13,5},{2,10},{6,14},... | collective-permute-start | bytes 417800 | tf_op jit(solution)/shard_map/ppermute | solution.py:305
  8.1 10.9 %collective-permute-start.2 = (bf16[272,256]{1,0:T(8,128)(2,1)S(1)}, bf16[272,256]{1,0:T(8,128)(2,1)S(1)}, u32[]{:S(2)}, u32[]{:S(2)}) collective-permute-start(bf16[272,256]{1,0:T(8,128)(2,1)S(1)} %get-tuple-element.45), channel_id=1, source_target_pairs={{0,12},{4,8},{8,4},{12,0},{1,13},{5,9},{9,5},{13,1},{2,14},{6,10},... | collective-permute-start | bytes 417800 | tf_op jit(solution)/shard_map/ppermute | solution.py:305
  20.5 6.0 %collective-permute-start.3 = (bf16[176,256]{1,0:T(8,128)(2,1)S(1)}, bf16[176,256]{1,0:T(8,128)(2,1)S(1)}, u32[]{:S(2)}, u32[]{:S(2)}) collective-permute-start(bf16[176,256]{1,0:T(8,128)(2,1)S(1)} %get-tuple-element.47.refs_0_), channel_id=1, source_target_pairs={{0,2},{2,0},{1,3},{3,1},{4,6},{6,4},{5,7},{7,5},{8,10},{10,8},{9,1... | collective-permute-start | bytes 270344 | tf_op jit(solution)/shard_map/ppermute | solution.py:308
  22.0 8.4 %collective-permute-start.6 = (bf16[176,256]{1,0:T(8,128)(2,1)S(1)}, bf16[176,256]{1,0:T(8,128)(2,1)S(1)}, u32[]{:S(2)}, u32[]{:S(2)}) collective-permute-start(bf16[176,256]{1,0:T(8,128)(2,1)S(1)} %get-tuple-element.50), channel_id=1, source_target_pairs={{0,8},{4,12},{8,0},{12,4},{1,9},{5,13},{9,1},{13,5},{2,10},{6,14},... | collective-permute-start | bytes 270344 | tf_op jit(solution)/shard_map/ppermute | solution.py:305
  25.1 6.8 %collective-permute-start.8 = (bf16[176,256]{1,0:T(8,128)(2,1)S(1)}, bf16[176,256]{1,0:T(8,128)(2,1)S(1)}, u32[]{:S(2)}, u32[]{:S(2)}) collective-permute-start(bf16[176,256]{1,0:T(8,128)(2,1)S(1)} %get-tuple-element.51), channel_id=1, source_target_pairs={{0,12},{4,8},{8,4},{12,0},{1,13},{5,9},{9,5},{13,1},{2,14},{6,10},... | collective-permute-start | bytes 270344 | tf_op jit(solution)/shard_map/ppermute | solution.py:305
  26.5 5.8 %collective-permute-start.4 = (bf16[176,256]{1,0:T(8,128)(2,1)S(1)}, bf16[176,256]{1,0:T(8,128)(2,1)S(1)}, u32[]{:S(2)}, u32[]{:S(2)}) collective-permute-start(bf16[176,256]{1,0:T(8,128)(2,1)S(1)} %get-tuple-element.49), channel_id=1, source_target_pairs={{0,4},{4,0},{8,12},{12,8},{1,5},{5,1},{9,13},{13,9},{2,6},{6,2},{1... | collective-permute-start | bytes 270344 | tf_op jit(solution)/shard_map/ppermute | solution.py:305
  27.2 5.8 %collective-permute-start.10 = (bf16[176,256]{1,0:T(8,128)(2,1)S(1)}, bf16[176,256]{1,0:T(8,128)(2,1)S(1)}, u32[]{:S(2)}, u32[]{:S(2)}) collective-permute-start(bf16[176,256]{1,0:T(8,128)(2,1)S(1)} %get-tuple-element.47.refs_0_), channel_id=1, source_target_pairs={{0,1},{1,0},{2,3},{3,2},{4,5},{5,4},{6,7},{7,6},{8,9},{9,8},{10,11... | collective-permute-start | bytes 270344 | tf_op jit(solution)/shard_map/ppermute | solution.py:308
  30.4 4.1 %collective-permute-start.12 = (bf16[176,256]{1,0:T(8,128)(2,1)S(1)}, bf16[176,256]{1,0:T(8,128)(2,1)S(1)}, u32[]{:S(2)}, u32[]{:S(2)}) collective-permute-start(bf16[176,256]{1,0:T(8,128)(2,1)S(1)} %collective-permute-done.6.refs_2_), channel_id=1, source_target_pairs={{0,1},{1,0},{2,3},{3,2},{4,5},{5,4},{6,7},{7,6},{8,9},{9,8},{10,11... | collective-permute-start | bytes 270344 | tf_op jit(solution)/shard_map/ppermute | solution.py:308
  31.9 3.1 %collective-permute-start.13 = (bf16[176,256]{1,0:T(8,128)(2,1)S(1)}, bf16[176,256]{1,0:T(8,128)(2,1)S(1)}, u32[]{:S(2)}, u32[]{:S(2)}) collective-permute-start(bf16[176,256]{1,0:T(8,128)(2,1)S(1)} %collective-permute-done.8.refs_3_), channel_id=1, source_target_pairs={{0,1},{1,0},{2,3},{3,2},{4,5},{5,4},{6,7},{7,6},{8,9},{9,8},{10,11... | collective-permute-start | bytes 270344 | tf_op jit(solution)/shard_map/ppermute | solution.py:308
  32.3 2.7 %collective-permute-start.11 = (bf16[176,256]{1,0:T(8,128)(2,1)S(1)}, bf16[176,256]{1,0:T(8,128)(2,1)S(1)}, u32[]{:S(2)}, u32[]{:S(2)}) collective-permute-start(bf16[176,256]{1,0:T(8,128)(2,1)S(1)} %collective-permute-done.4.refs_1_), channel_id=1, source_target_pairs={{0,1},{1,0},{2,3},{3,2},{4,5},{5,4},{6,7},{7,6},{8,9},{9,8},{10,11... | collective-permute-start | bytes 270344 | tf_op jit(solution)/shard_map/ppermute | solution.py:308
  32.4 7.2 %collective-permute-start.7 = (bf16[176,256]{1,0:T(8,128)(2,1)S(1)}, bf16[176,256]{1,0:T(8,128)(2,1)S(1)}, u32[]{:S(2)}, u32[]{:S(2)}) collective-permute-start(bf16[176,256]{1,0:T(8,128)(2,1)S(1)} %collective-permute-done.6.refs_2_), channel_id=1, source_target_pairs={{0,2},{2,0},{1,3},{3,1},{4,6},{6,4},{5,7},{7,5},{8,10},{10,8},{9,1... | collective-permute-start | bytes 270344 | tf_op jit(solution)/shard_map/ppermute | solution.py:308
  33.0 6.8 %collective-permute-start.9 = (bf16[176,256]{1,0:T(8,128)(2,1)S(1)}, bf16[176,256]{1,0:T(8,128)(2,1)S(1)}, u32[]{:S(2)}, u32[]{:S(2)}) collective-permute-start(bf16[176,256]{1,0:T(8,128)(2,1)S(1)} %collective-permute-done.8.refs_3_), channel_id=1, source_target_pairs={{0,2},{2,0},{1,3},{3,1},{4,6},{6,4},{5,7},{7,5},{8,10},{10,8},{9,1... | collective-permute-start | bytes 270344 | tf_op jit(solution)/shard_map/ppermute | solution.py:308
  34.5 6.7 %collective-permute-start.5 = (bf16[176,256]{1,0:T(8,128)(2,1)S(1)}, bf16[176,256]{1,0:T(8,128)(2,1)S(1)}, u32[]{:S(2)}, u32[]{:S(2)}) collective-permute-start(bf16[176,256]{1,0:T(8,128)(2,1)S(1)} %collective-permute-done.4.refs_1_), channel_id=1, source_target_pairs={{0,2},{2,0},{1,3},{3,1},{4,6},{6,4},{5,7},{7,5},{8,10},{10,8},{9,1... | collective-permute-start | bytes 270344 | tf_op jit(solution)/shard_map/ppermute | solution.py:308
  41.2 1.3 %collective-permute-start.14 = (bf16[176,256]{1,0:T(8,128)(2,1)S(1)}, bf16[176,256]{1,0:T(8,128)(2,1)S(1)}, u32[]{:S(2)}, u32[]{:S(2)}) collective-permute-start(bf16[176,256]{1,0:T(8,128)(2,1)S(1)} %collective-permute-done.3.refs_0_), channel_id=1, source_target_pairs={{0,1},{1,0},{2,3},{3,2},{4,5},{5,4},{6,7},{7,6},{8,9},{9,8},{10,11... | collective-permute-start | bytes 270344 | tf_op jit(solution)/shard_map/ppermute | solution.py:308
  41.2 1.4 %collective-permute-start.15 = (bf16[176,256]{1,0:T(8,128)(2,1)S(1)}, bf16[176,256]{1,0:T(8,128)(2,1)S(1)}, u32[]{:S(2)}, u32[]{:S(2)}) collective-permute-start(bf16[176,256]{1,0:T(8,128)(2,1)S(1)} %collective-permute-done.5.refs_1_), channel_id=1, source_target_pairs={{0,1},{1,0},{2,3},{3,2},{4,5},{5,4},{6,7},{7,6},{8,9},{9,8},{10,11... | collective-permute-start | bytes 270344 | tf_op jit(solution)/shard_map/ppermute | solution.py:308
  41.7 1.4 %collective-permute-start.17 = (bf16[176,256]{1,0:T(8,128)(2,1)S(1)}, bf16[176,256]{1,0:T(8,128)(2,1)S(1)}, u32[]{:S(2)}, u32[]{:S(2)}) collective-permute-start(bf16[176,256]{1,0:T(8,128)(2,1)S(1)} %collective-permute-done.9.refs_3_), channel_id=1, source_target_pairs={{0,1},{1,0},{2,3},{3,2},{4,5},{5,4},{6,7},{7,6},{8,9},{9,8},{10,11... | collective-permute-start | bytes 270344 | tf_op jit(solution)/shard_map/ppermute | solution.py:308
  47.7 1.7 %collective-permute-start.18 = (bf16[160,1024]{1,0:T(8,128)(2,1)S(1)}, bf16[160,1024]{1,0:T(8,128)(2,1)S(1)}, u32[]{:S(2)}, u32[]{:S(2)}) collective-permute-start(bf16[160,1024]{1,0:T(8,128)(2,1)S(1)} %get-tuple-element.58), channel_id=1, source_target_pairs={{0,1},{1,0},{2,3},{3,2},{4,5},{5,4},{6,7},{7,6},{8,9},{9,8},{10,11... | collective-permute-start | bytes 983048 | tf_op jit(solution)/shard_map/ppermute | solution.py:308
  48.2 4.1 %collective-permute-start.20 = (bf16[160,1024]{1,0:T(8,128)(2,1)S(1)}, bf16[160,1024]{1,0:T(8,128)(2,1)S(1)}, u32[]{:S(2)}, u32[]{:S(2)}) collective-permute-start(bf16[160,1024]{1,0:T(8,128)(2,1)S(1)} %get-tuple-element.61), channel_id=1, source_target_pairs={{0,1},{1,0},{2,3},{3,2},{4,5},{5,4},{6,7},{7,6},{8,9},{9,8},{10,11... | collective-permute-start | bytes 983048 | tf_op jit(solution)/shard_map/ppermute | solution.py:308
  50.1 7.1 %collective-permute-start.22 = (bf16[80,1024]{1,0:T(8,128)(2,1)S(1)}, bf16[80,1024]{1,0:T(8,128)(2,1)S(1)}, u32[]{:S(2)}, u32[]{:S(2)}) collective-permute-start(bf16[80,1024]{1,0:T(8,128)(2,1)S(1)} %get-tuple-element.68), channel_id=1, source_target_pairs={{0,2},{2,0},{1,3},{3,1},{4,6},{6,4},{5,7},{7,5},{8,10},{10,8},{9,1... | collective-permute-start | bytes 491528 | tf_op jit(solution)/shard_map/ppermute | solution.py:308
  50.7 9.6 %collective-permute-start.19 = (bf16[80,1024]{1,0:T(8,128)(2,1)S(1)}, bf16[80,1024]{1,0:T(8,128)(2,1)S(1)}, u32[]{:S(2)}, u32[]{:S(2)}) collective-permute-start(bf16[80,1024]{1,0:T(8,128)(2,1)S(1)} %get-tuple-element.59), channel_id=1, source_target_pairs={{0,2},{2,0},{1,3},{3,1},{4,6},{6,4},{5,7},{7,5},{8,10},{10,8},{9,1... | collective-permute-start | bytes 491528 | tf_op jit(solution)/shard_map/ppermute | solution.py:308
  57.3 8.7 %collective-permute-start.23 = (bf16[40,1024]{1,0:T(8,128)(2,1)S(1)}, bf16[40,1024]{1,0:T(8,128)(2,1)S(1)}, u32[]{:S(2)}, u32[]{:S(2)}) collective-permute-start(bf16[40,1024]{1,0:T(8,128)(2,1)S(1)} %get-tuple-element.73), channel_id=1, source_target_pairs={{0,8},{4,12},{8,0},{12,4},{1,9},{5,13},{9,1},{13,5},{2,10},{6,14},... | collective-permute-start | bytes 245768 | tf_op jit(solution)/shard_map/ppermute | solution.py:305
  58.4 7.6 %collective-permute-start.24 = (bf16[40,1024]{1,0:T(8,128)(2,1)S(1)}, bf16[40,1024]{1,0:T(8,128)(2,1)S(1)}, u32[]{:S(2)}, u32[]{:S(2)}) collective-permute-start(bf16[40,1024]{1,0:T(8,128)(2,1)S(1)} %get-tuple-element.74), channel_id=1, source_target_pairs={{0,12},{4,8},{8,4},{12,0},{1,13},{5,9},{9,5},{13,1},{2,14},{6,10},... | collective-permute-start | bytes 245768 | tf_op jit(solution)/shard_map/ppermute | solution.py:305
  60.5 5.8 %collective-permute-start.21 = (bf16[40,1024]{1,0:T(8,128)(2,1)S(1)}, bf16[40,1024]{1,0:T(8,128)(2,1)S(1)}, u32[]{:S(2)}, u32[]{:S(2)}) collective-permute-start(bf16[40,1024]{1,0:T(8,128)(2,1)S(1)} %get-tuple-element.67), channel_id=1, source_target_pairs={{0,4},{4,0},{8,12},{12,8},{1,5},{5,1},{9,13},{13,9},{2,6},{6,2},{1... | collective-permute-start | bytes 245768 | tf_op jit(solution)/shard_map/ppermute | solution.py:305
  (4 other events, 58.5 us)

commit v3 on v2

v3 whole, which is shorter than its diff:
```python
import functools
import math

import jax
import jax.numpy as jnp
from jax import lax
from jax.experimental import pallas as pl
from jax.experimental.pallas import tpu as pltpu
from jax.sharding import PartitionSpec as P

HEAD = 128
EPSILON = 1e-05
NEGATIVE = -1e30
META = 16
LATER = 16 * 1024 * 1024
ORDER = (2, 3, 1, 0)
VMEM_LIMIT = 12 * 1024 * 1024

BF16 = jnp.bfloat16
F32 = jnp.float32
IN_VMEM = pl.BlockSpec(memory_space=pltpu.VMEM)
IN_ANY = pl.BlockSpec(memory_space=pl.ANY)
IN_HBM = pl.BlockSpec(memory_space=pltpu.HBM)


def struct(rows, columns, dtype=BF16):
    return jax.ShapeDtypeStruct((rows, columns), dtype)


def call(kernel, outs, specs, scratch=(), flops=0, moved=0):
    return pl.pallas_call(
        kernel,
        out_shape=outs,
        in_specs=specs,
        out_specs=[IN_VMEM] * len(outs),
        scratch_shapes=scratch,
        compiler_params=pltpu.CompilerParams(vmem_limit_bytes=VMEM_LIMIT),
        cost_estimate=pl.CostEstimate(flops=flops, bytes_accessed=moved, transcendentals=0),
    )


def dot(a, b):
    return lax.dot_general(a, b, (((1,), (0,)), ((), ())), preferred_element_type=F32)


def dot_nt(a, b):
    return lax.dot_general(a, b, (((1,), (1,)), ((), ())), preferred_element_type=F32)


def dot_tn(a, b):
    return lax.dot_general(a, b, (((0,), (0,)), ((), ())), preferred_element_type=F32)


def iota(shape, dimension):
    return lax.broadcasted_iota(jnp.int32, shape, dimension)


def in_hbm(array):
    return pltpu.with_memory_space_constraint(array, pltpu.HBM)


def in_vmem(array):
    return pltpu.with_memory_space_constraint(array, pltpu.VMEM)


def columns_at(start, width):
    return pl.ds(pl.multiple_of(start * width, width), width)


def thirds(array):
    high = array.astype(BF16).astype(F32)
    middle = (array - high).astype(BF16).astype(F32)
    low = (array - high - middle).astype(BF16).astype(F32)
    return [high, middle, low]


def pack_kernel(steps, q_hbm, m_hbm, h_hbm, tp_hbm, sp_hbm, r_hbm, rw_hbm, *refs):
    outs, refs = refs[-7 - len(steps) : -7], refs[-7:]
    m_ref, tp_ref, sp_ref, r_ref, rw_ref, sems, small_sems = refs
    rows, width = q_hbm.shape[0], outs[0].shape[1]
    here = lax.axis_index("expert")
    small = [
        pltpu.make_async_copy(src, dst, small_sems.at[k])
        for k, (src, dst) in enumerate(
            ((tp_hbm, tp_ref), (sp_hbm, sp_ref), (r_hbm, r_ref), (rw_hbm, rw_ref))
        )
    ]
    large = []
    for k, (step, out) in enumerate(zip(steps, outs)):
        cols = columns_at(here ^ step, width)
        large.append(
            (
                pltpu.make_async_copy(m_hbm.at[:, :, cols], m_ref.at[k], sems.at[0, k]),
                pltpu.make_async_copy(q_hbm.at[:, cols], out.at[pl.ds(0, rows)], sems.at[1, k]),
                pltpu.make_async_copy(
                    h_hbm.at[:, cols], out.at[pl.ds(3 * rows, rows)], sems.at[2, k]
                ),
            )
        )
    for copy in small:
        copy.start()
    for copies in large:
        for copy in copies:
            copy.start()
    for copy in small:
        copy.wait()
    row = iota((META, rows), 0)
    lines = [tp_ref[...], sp_ref[...], r_ref[0:1, :], r_ref[1:2, :]]
    lines = [line.astype(F32) for line in lines]
    lines += thirds(rw_ref[0:1, :]) + thirds(rw_ref[1:2, :])
    kinds = jnp.zeros((META, rows), F32)
    for k, line in enumerate(lines):
        kinds = jnp.where(row == k, line, kinds)
    kinds = kinds.astype(BF16)
    for step, out in zip(steps, outs):
        moved = (iota((rows, width), 1) == iota((rows, width), 0) + step * rows).astype(BF16)
        out[4 * rows :, :] = dot(kinds, moved).astype(BF16)
    for k, out in enumerate(outs):
        large[k][0].wait()
        out[rows : 2 * rows, :] = m_ref[k, :, 0, :]
        out[2 * rows : 3 * rows, :] = m_ref[k, :, 1, :]
    for copies in large:
        copies[1].wait()
        copies[2].wait()


def prefetch_kernel(experts, w1_hbm, w2_hbm, gain_hbm, bias_hbm, after_ref, *refs):
    w1_ref, w2_ref, gain_ref, bias_ref, sems, small_sems = refs
    here, half = lax.axis_index("expert"), lax.axis_index("mp")
    size = w1_ref.shape[0] // (2 * experts)
    copies = []
    for part in range(2 * experts):
        core = half if part < experts else 1 - half
        source = columns_at(core * experts + (here ^ ORDER[part % experts]), size)
        target = pl.ds(part * size, size)
        copies += [
            pltpu.make_async_copy(w1_hbm.at[source], w1_ref.at[target], sems.at[0, part]),
            pltpu.make_async_copy(w2_hbm.at[target], w2_ref.at[target], sems.at[1, part]),
            pltpu.make_async_copy(
                gain_hbm.at[:, source], gain_ref.at[:, target], small_sems.at[0, part]
            ),
            pltpu.make_async_copy(
                bias_hbm.at[:, source], bias_ref.at[:, target], small_sems.at[1, part]
            ),
        ]
    for copy in copies:
        copy.start()
    for copy in copies:
        copy.wait()


def attend_kernel(experts, rows, cap, w1_ref, w2_ref, *refs):
    arrived, compact = dict(zip(ORDER, refs[:experts])), refs[experts:]
    messages = [arrived[step] for step in range(experts)]
    width = messages[0].shape[1]
    count = experts * rows
    here = lax.axis_index("expert")
    meta = sum(m[4 * rows :, :].astype(F32) for m in messages)
    same = (iota((count, count), 0) == iota((count, count), 1)).astype(BF16)
    columns = dot_nt(same, meta.astype(BF16))
    match = columns[:, 0:1] == meta[1:2, :]
    scale = 1.0 / math.sqrt(HEAD)
    parts = []
    for head in range(width // HEAD):
        lanes = slice(head * HEAD, (head + 1) * HEAD)

        def stacked(kind):
            return jnp.concatenate(
                [m[kind * rows : (kind + 1) * rows, lanes] for m in messages], axis=0
            )

        score = dot_nt(stacked(0), stacked(1)) * scale
        masked = jnp.where(match, score, NEGATIVE)
        largest = jnp.max(masked, axis=-1, keepdims=True)
        weight = jnp.where(match, jnp.exp(masked - largest), 0.0)
        total = jnp.sum(weight, axis=-1, keepdims=True)
        context = dot(weight.astype(BF16), stacked(2)) / total
        parts.append((stacked(3).astype(F32) + context).astype(BF16))
    states = jnp.concatenate(parts, axis=1)
    first, second = meta[2:3, :].astype(jnp.int32), meta[3:4, :].astype(jnp.int32)
    expert = here ^ iota((META, count), 0)
    named = ((first == expert) | (second == expert)) & (iota((META, count), 0) < experts)
    before = (iota((count, count), 0) < iota((count, count), 1)) & (
        iota((count, count), 0) // rows == iota((count, count), 1) // rows
    )
    slot = dot(named.astype(BF16), before.astype(BF16)).astype(jnp.int32)
    block = (iota((META, count), 1) // rows) ^ iota((META, count), 0)
    spot = jnp.where(named, block * cap + slot, -1)
    for step, out in zip(ORDER, compact):
        place = iota((experts * cap, count), 0) == spot[step : step + 1, :]
        place = place.astype(BF16)
        out[0 : experts * cap, :] = dot(place, states).astype(BF16)
        leads = first == (here ^ step)
        values = [jnp.where(leads, meta[4 + k : 5 + k, :], meta[7 + k : 8 + k, :]) for k in range(3)]
        values.append(leads.astype(F32))
        lines = jnp.zeros((META, count), F32)
        for k, value in enumerate(values):
            lines = jnp.where(iota((META, count), 0) == k, value, lines)
        out[experts * cap :, :] = jnp.zeros((META, width), BF16)
        out[experts * cap :, 0 : experts * cap] = dot_nt(lines.astype(BF16), place).astype(BF16)


def trim_kernel(block_ref, out_ref):
    out_ref[...] = block_ref[0 : out_ref.shape[0], :]


def first_kernel(tile, *refs):
    blocks, (gain_ref, bias_ref, w_ref, out_ref, n_ref) = refs[:-5], refs[-5:]
    width, model = blocks[0].shape[1], n_ref.shape[1]
    for at in range(0, n_ref.shape[0], META):
        rows = slice(at, at + META)
        values = [block[rows, :].astype(F32) for block in blocks]
        center = jnp.sum(sum(values), axis=-1, keepdims=True) * (1.0 / model)
        shifted = [value - center for value in values]
        spread = sum(value * value for value in shifted)
        spread = jnp.sum(spread, axis=-1, keepdims=True) * (1.0 / model)
        scale = lax.rsqrt(spread + EPSILON)
        for k, value in enumerate(shifted):
            cols = slice(k * width, (k + 1) * width)
            normed = value * scale * gain_ref[:, cols] + bias_ref[:, cols]
            n_ref[rows, cols] = normed.astype(BF16)
    for at in range(0, w_ref.shape[1], tile):
        cols = slice(at, at + tile)
        out_ref[:, cols] = jnp.maximum(dot(n_ref[...], w_ref[:, cols]), 0.0).astype(BF16)


def second_kernel(tile, a_ref, w_ref, kept_ref, *sent):
    columns, rows = kept_ref.shape[1], sent[0].shape[0]
    lower = lax.axis_index("mp") == 0
    for at in range(0, columns, tile):
        low = dot(a_ref[...], w_ref[:, at : at + tile])
        high = dot(a_ref[...], w_ref[:, columns + at : columns + at + tile])
        kept_ref[:, at : at + tile] = jnp.where(lower, low, high).astype(BF16)
        other = jnp.where(lower, high, low).astype(BF16)
        for k, out_ref in enumerate(sent):
            out_ref[:, at : at + tile] = other[k * rows : (k + 1) * rows, :]


def row_factors(lines_ref, count):
    same = (iota((count, count), 0) == iota((count, count), 1)).astype(BF16)
    columns = dot_nt(same, lines_ref[count:, 0:count])
    return columns[:, 0:1] + columns[:, 1:2] + columns[:, 2:3], columns[:, 3:4]


def plain_kernel(kept_ref, got_ref, out_ref):
    rows = slice(kept_ref.shape[0] - out_ref.shape[0], kept_ref.shape[0])
    out_ref[...] = (kept_ref[rows, :].astype(F32) + got_ref[rows, :].astype(F32)).astype(BF16)


def gather_states(blocks, states, rows):
    here = lax.axis_index("expert")
    width = blocks[0].shape[1]
    for step, block in zip(ORDER, blocks):
        states[:, columns_at(here ^ step, width)] = block[rows, :].astype(F32)


def base_kernel(experts, kept_ref, *refs):
    got, blocks, refs = refs[:2], refs[2 : 2 + experts], refs[2 + experts :]
    bases, factors, states = refs[:2], refs[2:4], refs[4]
    count = kept_ref.shape[0]
    cap = count // experts
    weight, leads = row_factors(blocks[-1], count)
    gather_states(blocks, states, slice(2 * cap, 4 * cap))
    for k in range(2):
        rows, half = slice((2 + k) * cap, (3 + k) * cap), slice(k * cap, (k + 1) * cap)
        total = kept_ref[rows, :].astype(F32) + got[k][...].astype(F32)
        bases[k][...] = total * weight[rows, :] + leads[rows, :] * states[half, :]
        factors[k][...] = jnp.broadcast_to(weight[rows, :], (cap, HEAD))


def tail_kernel(experts, kept_ref, *refs):
    got, blocks, refs = refs[:2], refs[2 : 2 + experts], refs[2 + experts :]
    far_kept_ref, far_got_ref, lines_ref, _, near0, near1, far0, far1, states = refs
    count = kept_ref.shape[0]
    cap = count // experts
    weight, leads = row_factors(blocks[-1], count)
    far_weight, _ = row_factors(lines_ref, count)
    gather_states(blocks, states, slice(0, 2 * cap))
    for k, (near, far) in enumerate(((near0, far0), (near1, far1))):
        rows = slice(k * cap, (k + 1) * cap)
        total = kept_ref[rows, :].astype(F32) + got[k][...].astype(F32)
        total = total * weight[rows, :] + leads[rows, :] * states[rows, :]
        near[...] = total.astype(BF16)
        total = far_kept_ref[rows, :].astype(F32) + far_got_ref[rows, :].astype(F32)
        far[...] = (total * far_weight[rows, :]).astype(BF16)


def join_kernel(came_ref, *refs):
    count = len(refs) // 3
    cap = refs[0].shape[0]
    for k in range(count):
        base_ref, factor_ref, out_ref = refs[k], refs[count + k], refs[2 * count + k]
        came = came_ref[k * cap : (k + 1) * cap, :].astype(F32)
        out_ref[...] = (base_ref[...] + factor_ref[:, 0:1] * came).astype(BF16)


def mix_kernel(experts, cap, tile, steps, routes_ref, *refs):
    returned, refs = refs[: len(steps)], refs[len(steps) :]
    out_ref = refs[-1]
    rows = out_ref.shape[0]
    expert = lax.axis_index("expert") ^ iota((META, rows), 0)
    named = (routes_ref[0:1, :] == expert) | (routes_ref[1:2, :] == expert)
    named = named & (iota((META, rows), 0) < experts)
    before = (iota((rows, rows), 0) < iota((rows, rows), 1)).astype(BF16)
    slot = jnp.where(named, dot(named.astype(BF16), before), -1.0)
    same = (iota((rows, rows), 0) == iota((rows, rows), 1)).astype(BF16)
    slot = dot_nt(same, slot.astype(BF16)).astype(jnp.int32)
    place = {
        step: (iota((rows, cap), 1) == slot[:, step : step + 1]).astype(BF16) for step in set(steps)
    }
    for at in range(0, out_ref.shape[1], tile):
        cols = slice(at, at + tile)
        share = refs[0][:, cols] if len(refs) > 1 else jnp.zeros((rows, tile), F32)
        for step, block in zip(steps, returned):
            share = share + dot(place[step], block[:, cols])
        out_ref[:, cols] = share.astype(out_ref.dtype)


def head_shards(
    hidden,
    queries,
    memory,
    target_pair,
    source_pair,
    routes,
    route_weight,
    norm_gain,
    norm_bias,
    expert_in,
    expert_out,
):
    rows, columns = hidden.shape
    experts = lax.axis_size("expert")
    width = columns // experts
    cap = 2 * rows // experts * 5 // 4
    model = 2 * columns
    hidden_units = expert_in.shape[2]

    def along(array, step):
        if step == 0:
            return array
        return lax.ppermute(array, "expert", [(i, i ^ step) for i in range(experts)])

    def swap(array, axis):
        return lax.ppermute(array, axis, [(0, 1), (1, 0)])

    def across(array):
        pairs = [(2 * i + j, 2 * (i ^ 1) + 1 - j) for i in range(experts) for j in range(2)]
        return lax.ppermute(array, ("expert", "dp"), pairs)

    def pack(steps, *after):
        return call(
            functools.partial(pack_kernel, steps),
            [struct(4 * rows + META, width)] * len(steps),
            [IN_HBM] * 7 + [IN_ANY] * len(after),
            scratch=[
                pltpu.VMEM((len(steps), rows, 2, width), BF16),
                pltpu.VMEM((1, rows), jnp.int32),
                pltpu.VMEM((1, rows), jnp.int32),
                pltpu.VMEM((2, rows), jnp.int32),
                pltpu.VMEM((2, rows), F32),
                pltpu.SemaphoreType.DMA((3, len(steps))),
                pltpu.SemaphoreType.DMA((4,)),
            ],
            moved=LATER if after else 0,
        )(
            in_hbm(queries),
            in_hbm(memory),
            in_hbm(hidden),
            in_hbm(target_pair.reshape(1, rows)),
            in_hbm(source_pair.reshape(1, rows)),
            in_hbm(routes.T),
            in_hbm(route_weight.T),
            *after,
        )

    packed = {}
    for steps in ((2,), (1,), (3, 0)):
        packed.update(zip(steps, pack(steps, *list(packed.values())[-1:])))
    messages = [along(packed[step], step) for step in ORDER]

    w_in, w_out, gain, bias = pl.pallas_call(
        functools.partial(prefetch_kernel, experts),
        out_shape=[
            pltpu.VMEM((model, hidden_units), BF16),
            pltpu.VMEM((hidden_units, model), BF16),
            pltpu.VMEM((1, model), F32),
            pltpu.VMEM((1, model), F32),
        ],
        in_specs=[IN_HBM] * 4 + [IN_ANY],
        out_specs=[IN_VMEM] * 4,
        scratch_shapes=[pltpu.SemaphoreType.DMA((2, 2 * experts))] * 2,
        compiler_params=pltpu.CompilerParams(vmem_limit_bytes=VMEM_LIMIT),
        cost_estimate=pl.CostEstimate(
            flops=0, bytes_accessed=8 * model * hidden_units, transcendentals=0
        ),
    )(
        in_hbm(expert_in[0]),
        in_hbm(expert_out[0]),
        in_hbm(norm_gain.reshape(1, model)),
        in_hbm(norm_bias.reshape(1, model)),
        packed[0],
    )

    compact = call(
        functools.partial(attend_kernel, experts, rows, cap),
        [struct(experts * cap + META, width)] * experts,
        [IN_VMEM] * (2 + experts),
        flops=8 * experts * experts * rows * rows * width,
        moved=16 * rows * columns,
    )(in_vmem(w_in), in_vmem(w_out), *messages)

    own = {step: along(block, step) for step, block in zip(ORDER, compact)}
    count = experts * cap

    def trim(block):
        return call(trim_kernel, [struct(count, width)], [IN_VMEM])(block)[0]

    trimmed = {step: trim(own[step]) for step in ORDER}
    far = {step: swap(own[step], "dp") for step in (2, 3)}
    far[1] = across(compact[2])
    far[0] = swap(compact[3], "dp")
    own_other = {step: swap(trimmed[step], "mp") for step in ORDER}

    def first(blocks, others, known):
        return call(
            functools.partial(first_kernel, 512),
            [struct(count, hidden_units)],
            [IN_VMEM] * (2 * experts + 3),
            scratch=[pltpu.VMEM((count, model), BF16)],
            flops=known * 2 * count * model * hidden_units,
            moved=known * 2 * model * hidden_units,
        )(
            *[blocks[step] for step in ORDER],
            *[others[step] for step in ORDER],
            in_vmem(gain),
            in_vmem(bias),
            in_vmem(w_in),
        )[0]

    def second(active, parts, known):
        kept, *sent = call(
            functools.partial(second_kernel, 512),
            [struct(count, columns)] + [struct(count // parts, columns)] * parts,
            [IN_VMEM, IN_VMEM],
            flops=known * 2 * count * model * hidden_units,
            moved=known * 2 * model * hidden_units,
        )(active, in_vmem(w_out))
        return kept, [swap(part, "mp") for part in sent]

    own_other[0], far[0], far[1] = lax.optimization_barrier((own_other[0], far[0], far[1]))
    active = first(own, own_other, 0)
    *late, active = lax.optimization_barrier((*[far[step] for step in ORDER], active))
    far = dict(zip(ORDER, late))
    far_other = {step: swap(far[step], "mp") for step in ORDER}
    mine, (theirs,) = second(first(far, far_other, 1), 1, 1)
    kept, got = second(active, experts, 0)
    arrived = [own[step] for step in ORDER]
    based = call(
        functools.partial(base_kernel, experts),
        [struct(cap, columns, F32)] * 2 + [struct(cap, HEAD, F32)] * 2,
        [IN_VMEM] * (3 + experts),
        scratch=[pltpu.VMEM((2 * cap, columns), F32)],
    )(kept, *got[2:], *arrived)
    plain = call(plain_kernel, [struct(2 * cap, columns)], [IN_VMEM] * 2)(mine, theirs)[0]
    joined = call(join_kernel, [struct(cap, columns)] * 2, [IN_VMEM] * 5)(swap(plain, "dp"), *based)
    near0, near1, away0, away1 = call(
        functools.partial(tail_kernel, experts),
        [struct(cap, columns)] * 4,
        [IN_VMEM] * (6 + experts) + [IN_ANY],
        scratch=[pltpu.VMEM((2 * cap, columns), F32)],
        moved=LATER,
    )(kept, *got[:2], *arrived, mine, theirs, far[0], joined[0])
    def mix(steps, blocks, dtype, *before):
        return call(
            functools.partial(mix_kernel, experts, cap, 512, steps),
            [struct(rows, columns, dtype)],
            [IN_VMEM] * (1 + len(blocks) + len(before)),
        )(routes.T, *blocks, *before)[0]

    share = mix((2, 3), [along(joined[0], 2), along(joined[1], 3)], F32)
    direct = [along(near1, 1), near0, across(away1), swap(away0, "dp")]
    return mix((1, 0, 1, 0), direct, BF16, share)


def shards(
    hidden,
    queries,
    memory,
    target_pair,
    source_pair,
    routes,
    route_weight,
    norm_gain,
    norm_bias,
    expert_in,
    expert_out,
):
    tok_rows = hidden.shape[0]
    local_heads = queries.shape[1] // HEAD
    scale = 1.0 / math.sqrt(HEAD)
    query_heads = queries.reshape(tok_rows, local_heads, HEAD)
    running = jnp.full((local_heads, tok_rows), NEGATIVE, jnp.float32)
    rows = lax.all_gather(memory, "expert", axis=0, tiled=True)
    row_pairs = lax.all_gather(source_pair, "expert", axis=0, tiled=True)
    count = rows.shape[0]
    keys = rows[:, 0, :].reshape(count, local_heads, HEAD)
    values = rows[:, 1, :].reshape(count, local_heads, HEAD)
    score = (
        jnp.einsum("thd,rhd->htr", query_heads, keys, preferred_element_type=jnp.float32) * scale
    )
    match = (target_pair[:, None] == row_pairs[None, :])[None]
    masked = jnp.where(match, score, NEGATIVE)
    newest = jnp.maximum(running, jnp.max(masked, axis=-1))
    weight = jnp.where(match, jnp.exp(masked - newest[:, :, None]), 0.0)
    total = jnp.sum(weight, axis=-1)
    summed = jnp.einsum(
        "htr,rhd->htd", weight.astype(jnp.bfloat16), values, preferred_element_type=jnp.float32
    )
    running, total, summed = (newest, total, summed)
    context = jnp.transpose(summed / total[:, :, None], (1, 0, 2)).reshape(
        tok_rows, local_heads * HEAD
    )
    attended = (hidden.astype(jnp.float32) + context).astype(jnp.bfloat16)
    full_rows = lax.all_gather(attended, "mp", axis=1, tiled=True)
    width = full_rows.shape[1]
    experts_all = lax.axis_size("expert")
    batches = lax.axis_size("dp")
    cap = 2 * tok_rows // experts_all * 5 // 4
    flat = routes.reshape(-1)
    named = (flat[:, None] == jnp.arange(experts_all, dtype=jnp.int32)[None, :]).astype(jnp.int32)
    slot = jnp.sum((jnp.cumsum(named, axis=0) - named) * named, axis=1)
    dest = flat * cap + slot
    place = dest[:, None] == jnp.arange(experts_all * cap, dtype=jnp.int32)[None, :]
    per_token = jnp.sum(place.reshape(tok_rows, 2, experts_all * cap).astype(jnp.bfloat16), axis=1)
    outgoing = lax.dot_general(
        per_token, full_rows, (((0,), (0,)), ((), ())), preferred_element_type=jnp.float32
    ).astype(jnp.bfloat16)
    copies = jnp.broadcast_to(
        outgoing.reshape(experts_all, 1, cap, width), (experts_all, batches, cap, width)
    ).reshape(experts_all * batches * cap, width)
    arrived = lax.all_to_all(copies, ("expert", "dp"), split_axis=0, concat_axis=0, tiled=True)
    values = arrived.astype(jnp.float32)
    center = jnp.mean(values, axis=-1, keepdims=True)
    spread = jnp.mean(jnp.square(values - center), axis=-1, keepdims=True)
    normed = ((values - center) * lax.rsqrt(spread + EPSILON) * norm_gain + norm_bias).astype(
        jnp.bfloat16
    )
    active = jax.nn.relu(jnp.dot(normed, expert_in[0], preferred_element_type=jnp.float32)).astype(
        jnp.bfloat16
    )
    partial_value = jnp.dot(active, expert_out[0], preferred_element_type=jnp.float32).astype(
        jnp.bfloat16
    )
    returned = lax.all_to_all(
        partial_value, ("expert", "dp"), split_axis=0, concat_axis=0, tiled=True
    )
    expert_sum = jnp.sum(
        returned.reshape(experts_all, batches, cap, width).astype(jnp.float32), axis=1
    )
    picked = jnp.dot(
        place.astype(jnp.float32),
        expert_sum.reshape(experts_all * cap, width),
        precision=lax.Precision.HIGHEST,
    )
    blended = jnp.sum(picked.reshape(tok_rows, 2, width) * route_weight[:, :, None], axis=1)
    share = lax.psum_scatter(
        blended.astype(jnp.bfloat16), "mp", scatter_dimension=1, tiled=True
    ).astype(jnp.float32)
    return (attended.astype(jnp.float32) + share).astype(jnp.bfloat16)


def layer(hidden, queries, memory, *rest):
    experts = lax.axis_size("expert")
    rows, columns = hidden.shape
    heads = columns // HEAD
    by_heads = (
        lax.axis_size("mp") == 2
        and lax.axis_size("dp") == 2
        and heads % experts == 0
        and memory.shape[0] == rows
        and experts * rows <= columns // experts
        and experts == 4
    )
    return (head_shards if by_heads else shards)(hidden, queries, memory, *rest)


def solution(mesh):
    return jax.shard_map(
        layer,
        mesh=mesh,
        in_specs=(
            P(("groups", "expert", "dp"), "mp"),
            P(("groups", "expert", "dp"), "mp"),
            P(("groups", "expert", "dp"), None, "mp"),
            P(("groups", "expert", "dp")),
            P(("groups", "expert", "dp")),
            P(("groups", "expert", "dp"), None),
            P(("groups", "expert", "dp"), None),
            P(),
            P(),
            P("expert", None, ("dp", "mp")),
            P("expert", ("dp", "mp"), None),
        ),
        out_specs=P(("groups", "expert", "dp"), "mp"),
        check_vma=False,
    )
```

time: 68.1 us -> 63 us (0.925)
  waiting for transfers between devices: 22.9 us -> 15.8 us
  starting transfers between devices: 22.4 us -> 26.7 us
  Pallas kernels: 22.4 us -> 20.1 us
    ppermute x9, waiting for transfers between devices: 15.3 us -> 7.85 us  [along(): lax.ppermute(array, 'expert', [(i, i ^ step) for i in range(experts)])]
    ppermute x0 -> x2, starting transfers between devices: none -> 3.55 us  [across(): return lax.ppermute(array, ('expert', 'dp'), pairs)]
    ppermute x0 -> x2, waiting for transfers between devices: none -> 1.35 us  [across(): return lax.ppermute(array, ('expert', 'dp'), pairs)]
    pallas_call x10 -> x17, Pallas kernels: 20 us -> 18.9 us  [the longest x1 6.21 us: head_shards(): pl.pallas_call(functools.partial(prefetch_kernel, experts), out_shape=[pl...]
    ppermute x16 -> x18, waiting for transfers between devices: 7.62 us -> 6.57 us  [swap(): return lax.ppermute(array, axis, [(0, 1), (1, 0)])]
    ppermute x9, starting transfers between devices: 14.5 us -> 15.2 us  [along(): lax.ppermute(array, 'expert', [(i, i ^ step) for i in range(experts)])]
    ppermute x16 -> x18, starting transfers between devices: 7.99 us -> 7.9 us  [swap(): return lax.ppermute(array, axis, [(0, 1), (1, 0)])]
  transfers between devices with their start and end apart: 25 -> 29, of which waited for: 14 -> 19; matrix products, arithmetic and copies ran while one was open for 0% -> 0% of each run, Pallas kernels for 18% -> 21%
where the time goes in v3:
time: 63 us; the launch traced here: 62.7 us
  starting transfers between devices  26.7 us (42%)
  Pallas kernels  20.1 us (32%)
  waiting for transfers between devices  15.8 us (25%)
    ppermute x9, starting transfers between devices, along(): lax.ppermute(array, 'expert', [(i, i ^ step) for i in range(experts)])  15.2 us
    ppermute x18, starting transfers between devices, swap(): return lax.ppermute(array, axis, [(0, 1), (1, 0)])  7.9 us
    ppermute x9, waiting for transfers between devices, along(): lax.ppermute(array, 'expert', [(i, i ^ step) for i in range(experts)])  7.85 us
    ppermute x18, waiting for transfers between devices, swap(): return lax.ppermute(array, axis, [(0, 1), (1, 0)])  6.57 us
    pallas_call x1, Pallas kernels, head_shards(): pl.pallas_call(functools.partial(prefetch_kernel, experts), out_shape=[pl...  6.21 us
    pallas_call x2, Pallas kernels, first(): call(functools.partial(first_kernel, 512), [struct(count, hidden_units)],...  3.74 us
    pallas_call x3, Pallas kernels, pack(): call(functools.partial(pack_kernel, steps), [struct(4 * rows + META, widt...  3.58 us
    ppermute x2, starting transfers between devices, across(): return lax.ppermute(array, ('expert', 'dp'), pairs)  3.55 us
  transfers between devices with their start and end apart: 29, of which 19 were waited for; matrix products, arithmetic and copies ran while one was open for 0% of the time, Pallas kernels for 21%

profile of v3, /device:TPU:0, one launch (start us, length us, event | category | flops | bytes accessed | tf_op | source)
XLA Modules:
  0.0 62.7 jit_solution(12649526244655793058)
XLA Ops:
  0.0 1.1 %shard_map.109.refs_0_ = bf16[272,256]{1,0:T(8,128)(2,1)S(1)} custom-call(bf16[64,1024]{1,0:T(8,128)(2,1)} %q_hbm.5, bf16[64,2,1024]{2,1,0:T(2,128)(2,1)} %m_hbm.5, bf16[64,1024]{1,0:T(8,128)(2,1)} %h_hbm.5, s32[1,64]{1,0:T(1,128)} %bitcast.20, s32[1,64]{1,0:T(1,128)} %bitcast.23, s32[2,64]{1,0:T(2,128)} %bitcast.8, f32[2,64]{1,0:T(2,128)} %bitcast.15), custom_call_target="tpu_custom_call" | custom-call | tf_op jit(solution)/shard_map/pallas_call | solution.py:352
  1.1 4.1 %collective-permute-start = (bf16[272,256]{1,0:T(8,128)(2,1)S(1)}, bf16[272,256]{1,0:T(8,128)(2,1)S(1)}, u32[]{:S(2)}, u32[]{:S(2)}) collective-permute-start(bf16[272,256]{1,0:T(8,128)(2,1)S(1)} %shard_map.109.refs_0_), channel_id=1, source_target_pairs={{0,8},{4,12},{8,0},{12,4},{1,9},{5,13},{9,1},{13,5},{2,10},{6,14},... | collective-permute-start | bytes 417800 | tf_op jit(solution)/shard_map/ppermute | solution.py:342
  5.2 1.1 %shard_map.110.refs_0_ = bf16[272,256]{1,0:T(8,128)(2,1)S(1)} custom-call(bf16[64,1024]{1,0:T(8,128)(2,1)} %q_hbm.5, bf16[64,2,1024]{2,1,0:T(2,128)(2,1)} %m_hbm.5, bf16[64,1024]{1,0:T(8,128)(2,1)} %h_hbm.5, s32[1,64]{1,0:T(1,128)} %bitcast.21, s32[1,64]{1,0:T(1,128)} %bitcast.24, s32[2,64]{1,0:T(2,128)} %bitcast.9, f32[2,64]{1,0:T(2,128)} %bitcast.16, ...), custom_call_target="tpu_custom_call" | custom-call | bytes 16777216 | tf_op jit(solution)/shard_map/pallas_call | solution.py:352
  6.3 1.6 %collective-permute-start.2 = (bf16[272,256]{1,0:T(8,128)(2,1)S(1)}, bf16[272,256]{1,0:T(8,128)(2,1)S(1)}, u32[]{:S(2)}, u32[]{:S(2)}) collective-permute-start(bf16[272,256]{1,0:T(8,128)(2,1)S(1)} %shard_map.110.refs_0_), channel_id=1, source_target_pairs={{0,4},{4,0},{8,12},{12,8},{1,5},{5,1},{9,13},{13,9},{2,6},{6,2},{1... | collective-permute-start | bytes 417800 | tf_op jit(solution)/shard_map/ppermute | solution.py:342
  8.0 1.4 %shard_map.111 = (bf16[272,256]{1,0:T(8,128)(2,1)S(1)}, bf16[272,256]{1,0:T(8,128)(2,1)S(1)}) custom-call(bf16[64,1024]{1,0:T(8,128)(2,1)} %q_hbm.5, bf16[64,2,1024]{2,1,0:T(2,128)(2,1)} %m_hbm.5, bf16[64,1024]{1,0:T(8,128)(2,1)} %h_hbm.5, s32[1,64]{1,0:T(1,128)} %bitcast.22, s32[1,64]{1,0:T(1,128)} %bitcast.25, s32[2,64]{1,0:T(2,128)} %bitcast.10, ...), custom_call_target="tpu_custom_call" | custom-call | bytes 16777216 | tf_op jit(solution)/shard_map/pallas_call | solution.py:352
  9.4 6.2 %shard_map.112 = (bf16[2048,2048]{1,0:T(8,128)(2,1)S(1)}, bf16[2048,2048]{1,0:T(8,128)(2,1)S(1)}, f32[1,2048]{1,0:T(1,128)S(1)}, f32[1,2048]{1,0:T(1,128)S(1)}) custom-call(bf16[2048,2048]{1,0:T(8,128)(2,1)} %bitcast.13, bf16[2048,2048]{1,0:T(8,128)(2,1)} %bitcast.14, f32[1,2048]{1,0:T(1,128)} %bitcast.18, f32[1,2048]{1,0:T(1,128)} %bitcast.19, ...), custom_call_target="tpu_custom_call" | custom-call | bytes 33554432 | tf_op jit(solution)/shard_map/pallas_call | solution.py:382
  16.3 0.9 %shard_map.113 = (bf16[176,256]{1,0:T(8,128)(2,1)S(1)}, bf16[176,256]{1,0:T(8,128)(2,1)S(1)}, bf16[176,256]{1,0:T(8,128)(2,1)S(1)}, bf16[176,256]{1,0:T(8,128)(2,1)S(1)}) custom-call(bf16[2048,2048]{1,0:T(8,128)(2,1)S(1)} %get-tuple-element.41.w1_ref.refs_10_, bf16[2048,2048]{1,0:T(8,128)(2,1)S(1)} %get-tuple-element.42.w2_ref.w_ref, ...), custom_call_target="tpu_custom_call" | custom-call | flops 134217728 | bytes 1048576 | tf_op jit(solution)/shard_map/pallas_call | solution.py:405
  17.3 4.2 %collective-permute-start.3 = (bf16[176,256]{1,0:T(8,128)(2,1)S(1)}, bf16[176,256]{1,0:T(8,128)(2,1)S(1)}, u32[]{:S(2)}, u32[]{:S(2)}) collective-permute-start(bf16[176,256]{1,0:T(8,128)(2,1)S(1)} %get-tuple-element.44), channel_id=1, source_target_pairs={{0,8},{4,12},{8,0},{12,4},{1,9},{5,13},{9,1},{13,5},{2,10},{6,14},... | collective-permute-start | bytes 270344 | tf_op jit(solution)/shard_map/ppermute | solution.py:342
  22.2 2.8 %collective-permute-start.9 = (bf16[176,256]{1,0:T(8,128)(2,1)S(1)}, bf16[176,256]{1,0:T(8,128)(2,1)S(1)}, u32[]{:S(2)}, u32[]{:S(2)}) collective-permute-start(bf16[176,256]{1,0:T(8,128)(2,1)S(1)} %get-tuple-element.47), channel_id=1, source_target_pairs={{0,6},{2,4},{4,2},{6,0},{8,14},{10,12},{12,10},{14,8},{1,7},{3,5},... | collective-permute-start | bytes 270344 | tf_op jit(solution)/shard_map/ppermute | solution.py:349
  25.5 2.7 %collective-permute-done.3.block_ref.refs_0_.refs_2_ = bf16[176,256]{1,0:T(8,128)(2,1)S(1)} collective-permute-done((bf16[176,256]{1,0:T(8,128)(2,1)S(1)}, bf16[176,256]{1,0:T(8,128)(2,1)S(1)}, u32[]{:S(2)}, u32[]{:S(2)}) %collective-permute-start.3) | collective-permute-done | bytes 90144 | tf_op jit(solution)/shard_map/ppermute | solution.py:342
  28.8 1.5 %collective-permute-start.4 = (bf16[176,256]{1,0:T(8,128)(2,1)S(1)}, bf16[176,256]{1,0:T(8,128)(2,1)S(1)}, u32[]{:S(2)}, u32[]{:S(2)}) collective-permute-start(bf16[176,256]{1,0:T(8,128)(2,1)S(1)} %collective-permute-done.3.block_ref.refs_0_.refs_2_), channel_id=1, source_target_pairs={{0,2},{2,0},{1,3},{3,1},{4,6},{6,4},{5,7},{7,5},{8,10},{10,8},{9,1... | collective-permute-start | bytes 270344 | tf_op jit(solution)/shard_map/ppermute | solution.py:345
  30.3 1.4 %collective-permute-start.6 = (bf16[176,256]{1,0:T(8,128)(2,1)S(1)}, bf16[176,256]{1,0:T(8,128)(2,1)S(1)}, u32[]{:S(2)}, u32[]{:S(2)}) collective-permute-start(bf16[176,256]{1,0:T(8,128)(2,1)S(1)} %collective-permute-done.5.block_ref.refs_1_.refs_3_), channel_id=1, source_target_pairs={{0,2},{2,0},{1,3},{3,1},{4,6},{6,4},{5,7},{7,5},{8,10},{10,8},{9,1... | collective-permute-start | bytes 270344 | tf_op jit(solution)/shard_map/ppermute | solution.py:345
  33.9 1.9 %shard_map.118.a_ref = bf16[160,2048]{1,0:T(8,128)(2,1)S(1)} custom-call(bf16[176,256]{1,0:T(8,128)(2,1)S(1)} %collective-permute-done.3.block_ref.refs_0_.refs_2_, bf16[176,256]{1,0:T(8,128)(2,1)S(1)} %collective-permute-done.5.block_ref.refs_1_.refs_3_, bf16[176,256]{1,0:T(8,128)(2,1)S(1)} %collective-permute-done.10.block_ref.refs_2_.refs_4_, ...), custom_call_target="tpu_custom_call" | custom-call | tf_op jit(solution)/shard_map/pallas_call | solution.py:426
  38.2 1.9 %shard_map.120.a_ref = bf16[160,2048]{1,0:T(8,128)(2,1)S(1)} custom-call(bf16[176,256]{1,0:T(8,128)(2,1)S(1)} %collective-permute-done.4.refs_0_, bf16[176,256]{1,0:T(8,128)(2,1)S(1)} %collective-permute-done.6.refs_1_, bf16[176,256]{1,0:T(8,128)(2,1)S(1)} %collective-permute-done.9.refs_2_, bf16[176,256]{1,0:T(8,128)(2,1)S(1)} %collective-permute-done.8.refs_3_.refs_8_, ...), custom_call_target="tpu_custom_call" | custom-call | flops 1342177280 | bytes 8388608 | tf_op jit(solution)/shard_map/pallas_call | solution.py:426
  40.1 1.5 %shard_map.121 = (bf16[160,1024]{1,0:T(8,128)(2,1)S(1)}, bf16[160,1024]{1,0:T(8,128)(2,1)S(1)}) custom-call(bf16[160,2048]{1,0:T(8,128)(2,1)S(1)} %shard_map.120.a_ref, bf16[2048,2048]{1,0:T(8,128)(2,1)S(1)} %get-tuple-element.42.w2_ref.w_ref), custom_call_target="tpu_custom_call" | custom-call | flops 1342177280 | bytes 8388608 | tf_op jit(solution)/shard_map/pallas_call | solution.py:442
  42.1 1.3 %collective-permute-done.20.got_ref.refs_7_ = bf16[160,1024]{1,0:T(8,128)(2,1)S(1)} collective-permute-done((bf16[160,1024]{1,0:T(8,128)(2,1)S(1)}, bf16[160,1024]{1,0:T(8,128)(2,1)S(1)}, u32[]{:S(2)}, u32[]{:S(2)}) %collective-permute-start.20) | collective-permute-done | bytes 327712 | tf_op jit(solution)/shard_map/ppermute | solution.py:345
  44.0 1.5 %shard_map.119 = (bf16[160,1024]{1,0:T(8,128)(2,1)S(1)}, bf16[40,1024]{1,0:T(8,128)(2,1)S(1)}, bf16[40,1024]{1,0:T(8,128)(2,1)S(1)}, bf16[40,1024]{1,0:T(8,128)(2,1)S(1)}, bf16[40,1024]{1,0:T(8,128)(2,1)S(1)}) custom-call(bf16[160,2048]{1,0:T(8,128)(2,1)S(1)} %shard_map.118.a_ref, bf16[2048,2048]{1,0:T(8,128)(2,1)S(1)} %get-tuple-element.42.w2_ref.w_ref), custom_call_target="tpu_custom_call" | custom-call | tf_op jit(solution)/shard_map/pallas_call | solution.py:442
  47.3 2.6 %collective-permute-done.21.came_ref = bf16[80,1024]{1,0:T(8,128)(2,1)S(1)} collective-permute-done((bf16[80,1024]{1,0:T(8,128)(2,1)S(1)}, bf16[80,1024]{1,0:T(8,128)(2,1)S(1)}, u32[]{:S(2)}, u32[]{:S(2)}) %collective-permute-start.21) | collective-permute-done | bytes 163872 | tf_op jit(solution)/shard_map/ppermute | solution.py:345
  50.0 2.2 %collective-permute-start.28 = (bf16[40,1024]{1,0:T(8,128)(2,1)S(1)}, bf16[40,1024]{1,0:T(8,128)(2,1)S(1)}, u32[]{:S(2)}, u32[]{:S(2)}) collective-permute-start(bf16[40,1024]{1,0:T(8,128)(2,1)S(1)} %get-tuple-element.74), channel_id=1, source_target_pairs={{0,12},{4,8},{8,4},{12,0},{1,13},{5,9},{9,5},{13,1},{2,14},{6,10},... | collective-permute-start | bytes 245768 | tf_op jit(solution)/shard_map/ppermute | solution.py:342
  52.8 2.1 %collective-permute-start.24 = (bf16[40,1024]{1,0:T(8,128)(2,1)S(1)}, bf16[40,1024]{1,0:T(8,128)(2,1)S(1)}, u32[]{:S(2)}, u32[]{:S(2)}) collective-permute-start(bf16[40,1024]{1,0:T(8,128)(2,1)S(1)} %get-tuple-element.70), channel_id=1, source_target_pairs={{0,4},{4,0},{8,12},{12,8},{1,5},{5,1},{9,13},{13,9},{2,6},{6,2},{1... | collective-permute-start | bytes 245768 | tf_op jit(solution)/shard_map/ppermute | solution.py:342
  54.9 0.8 %collective-permute-start.25 = (bf16[40,1024]{1,0:T(8,128)(2,1)S(1)}, bf16[40,1024]{1,0:T(8,128)(2,1)S(1)}, u32[]{:S(2)}, u32[]{:S(2)}) collective-permute-start(bf16[40,1024]{1,0:T(8,128)(2,1)S(1)} %get-tuple-element.72), channel_id=1, source_target_pairs={{0,6},{2,4},{4,2},{6,0},{8,14},{10,12},{12,10},{14,8},{1,7},{3,5},... | collective-permute-start | bytes 245768 | tf_op jit(solution)/shard_map/ppermute | solution.py:349
  55.7 0.7 %collective-permute-start.26 = (bf16[40,1024]{1,0:T(8,128)(2,1)S(1)}, bf16[40,1024]{1,0:T(8,128)(2,1)S(1)}, u32[]{:S(2)}, u32[]{:S(2)}) collective-permute-start(bf16[40,1024]{1,0:T(8,128)(2,1)S(1)} %get-tuple-element.73), channel_id=1, source_target_pairs={{0,2},{2,0},{1,3},{3,1},{4,6},{6,4},{5,7},{7,5},{8,10},{10,8},{9,1... | collective-permute-start | bytes 245768 | tf_op jit(solution)/shard_map/ppermute | solution.py:345
  56.9 3.3 %collective-permute-done.27.refs_0_ = bf16[40,1024]{1,0:T(8,128)(2,1)S(1)} collective-permute-done((bf16[40,1024]{1,0:T(8,128)(2,1)S(1)}, bf16[40,1024]{1,0:T(8,128)(2,1)S(1)}, u32[]{:S(2)}, u32[]{:S(2)}) %collective-permute-start.27) | collective-permute-done | bytes 81952 | tf_op jit(solution)/shard_map/ppermute | solution.py:342
  61.5 1.2 %shard_map.127 = bf16[64,1024]{1,0:T(8,128)(2,1)} custom-call(s32[2,64]{1,0:T(2,128)S(1)} %bitcast.12, bf16[40,1024]{1,0:T(8,128)(2,1)S(1)} %collective-permute-done.24.refs_0_, bf16[40,1024]{1,0:T(8,128)(2,1)S(1)} %get-tuple-element.71.refs_1_, bf16[40,1024]{1,0:T(8,128)(2,1)S(1)} %collective-permute-done.25.refs_2_, ...), custom_call_target="tpu_custom_call" | custom-call | tf_op jit(solution)/shard_map/pallas_call | solution.py:475
  (55 shorter events, 12.4 us)
Async XLA Ops:
  1.1 14.5 %collective-permute-start = (bf16[272,256]{1,0:T(8,128)(2,1)S(1)}, bf16[272,256]{1,0:T(8,128)(2,1)S(1)}, u32[]{:S(2)}, u32[]{:S(2)}) collective-permute-start(bf16[272,256]{1,0:T(8,128)(2,1)S(1)} %shard_map.109.refs_0_), channel_id=1, source_target_pairs={{0,8},{4,12},{8,0},{12,4},{1,9},{5,13},{9,1},{13,5},{2,10},{6,14},... | collective-permute-start | bytes 417800 | tf_op jit(solution)/shard_map/ppermute | solution.py:342
  6.3 9.3 %collective-permute-start.2 = (bf16[272,256]{1,0:T(8,128)(2,1)S(1)}, bf16[272,256]{1,0:T(8,128)(2,1)S(1)}, u32[]{:S(2)}, u32[]{:S(2)}) collective-permute-start(bf16[272,256]{1,0:T(8,128)(2,1)S(1)} %shard_map.110.refs_0_), channel_id=1, source_target_pairs={{0,4},{4,0},{8,12},{12,8},{1,5},{5,1},{9,13},{13,9},{2,6},{6,2},{1... | collective-permute-start | bytes 417800 | tf_op jit(solution)/shard_map/ppermute | solution.py:342
  9.4 7.0 %collective-permute-start.1 = (bf16[272,256]{1,0:T(8,128)(2,1)S(1)}, bf16[272,256]{1,0:T(8,128)(2,1)S(1)}, u32[]{:S(2)}, u32[]{:S(2)}) collective-permute-start(bf16[272,256]{1,0:T(8,128)(2,1)S(1)} %get-tuple-element.43), channel_id=1, source_target_pairs={{0,12},{4,8},{8,4},{12,0},{1,13},{5,9},{9,5},{13,1},{2,14},{6,10},... | collective-permute-start | bytes 417800 | tf_op jit(solution)/shard_map/ppermute | solution.py:342
  17.3 10.8 %collective-permute-start.3 = (bf16[176,256]{1,0:T(8,128)(2,1)S(1)}, bf16[176,256]{1,0:T(8,128)(2,1)S(1)}, u32[]{:S(2)}, u32[]{:S(2)}) collective-permute-start(bf16[176,256]{1,0:T(8,128)(2,1)S(1)} %get-tuple-element.44), channel_id=1, source_target_pairs={{0,8},{4,12},{8,0},{12,4},{1,9},{5,13},{9,1},{13,5},{2,10},{6,14},... | collective-permute-start | bytes 270344 | tf_op jit(solution)/shard_map/ppermute | solution.py:342
  21.5 7.3 %collective-permute-start.5 = (bf16[176,256]{1,0:T(8,128)(2,1)S(1)}, bf16[176,256]{1,0:T(8,128)(2,1)S(1)}, u32[]{:S(2)}, u32[]{:S(2)}) collective-permute-start(bf16[176,256]{1,0:T(8,128)(2,1)S(1)} %get-tuple-element.45), channel_id=1, source_target_pairs={{0,12},{4,8},{8,4},{12,0},{1,13},{5,9},{9,5},{13,1},{2,14},{6,10},... | collective-permute-start | bytes 270344 | tf_op jit(solution)/shard_map/ppermute | solution.py:342
  22.0 8.4 %collective-permute-start.10 = (bf16[176,256]{1,0:T(8,128)(2,1)S(1)}, bf16[176,256]{1,0:T(8,128)(2,1)S(1)}, u32[]{:S(2)}, u32[]{:S(2)}) collective-permute-start(bf16[176,256]{1,0:T(8,128)(2,1)S(1)} %get-tuple-element.47), channel_id=1, source_target_pairs={{0,4},{4,0},{8,12},{12,8},{1,5},{5,1},{9,13},{13,9},{2,6},{6,2},{1... | collective-permute-start | bytes 270344 | tf_op jit(solution)/shard_map/ppermute | solution.py:342
  22.2 10.3 %collective-permute-start.9 = (bf16[176,256]{1,0:T(8,128)(2,1)S(1)}, bf16[176,256]{1,0:T(8,128)(2,1)S(1)}, u32[]{:S(2)}, u32[]{:S(2)}) collective-permute-start(bf16[176,256]{1,0:T(8,128)(2,1)S(1)} %get-tuple-element.47), channel_id=1, source_target_pairs={{0,6},{2,4},{4,2},{6,0},{8,14},{10,12},{12,10},{14,8},{1,7},{3,5},... | collective-permute-start | bytes 270344 | tf_op jit(solution)/shard_map/ppermute | solution.py:349
  24.9 7.6 %collective-permute-start.8 = (bf16[176,256]{1,0:T(8,128)(2,1)S(1)}, bf16[176,256]{1,0:T(8,128)(2,1)S(1)}, u32[]{:S(2)}, u32[]{:S(2)}) collective-permute-start(bf16[176,256]{1,0:T(8,128)(2,1)S(1)} %get-tuple-element.46.block_ref.refs_3_.refs_5_), channel_id=1, source_target_pairs={{0,2},{2,0},{1,3},{3,1},{4,6},{6,4},{5,7},{7,5},{8,10},{10,8},{9,1... | collective-permute-start | bytes 270344 | tf_op jit(solution)/shard_map/ppermute | solution.py:345
  28.1 3.7 %collective-permute-start.7 = (bf16[160,256]{1,0:T(8,128)(2,1)S(1)}, bf16[160,256]{1,0:T(8,128)(2,1)S(1)}, u32[]{:S(2)}, u32[]{:S(2)}) collective-permute-start(bf16[160,256]{1,0:T(8,128)(2,1)S(1)} %shard_map.114), channel_id=1, source_target_pairs={{0,1},{1,0},{2,3},{3,2},{4,5},{5,4},{6,7},{7,6},{8,9},{9,8},{10,11... | collective-permute-start | bytes 245768 | tf_op jit(solution)/shard_map/ppermute | solution.py:345
  28.8 7.0 %collective-permute-start.4 = (bf16[176,256]{1,0:T(8,128)(2,1)S(1)}, bf16[176,256]{1,0:T(8,128)(2,1)S(1)}, u32[]{:S(2)}, u32[]{:S(2)}) collective-permute-start(bf16[176,256]{1,0:T(8,128)(2,1)S(1)} %collective-permute-done.3.block_ref.refs_0_.refs_2_), channel_id=1, source_target_pairs={{0,2},{2,0},{1,3},{3,1},{4,6},{6,4},{5,7},{7,5},{8,10},{10,8},{9,1... | collective-permute-start | bytes 270344 | tf_op jit(solution)/shard_map/ppermute | solution.py:345
  30.3 5.9 %collective-permute-start.6 = (bf16[176,256]{1,0:T(8,128)(2,1)S(1)}, bf16[176,256]{1,0:T(8,128)(2,1)S(1)}, u32[]{:S(2)}, u32[]{:S(2)}) collective-permute-start(bf16[176,256]{1,0:T(8,128)(2,1)S(1)} %collective-permute-done.5.block_ref.refs_1_.refs_3_), channel_id=1, source_target_pairs={{0,2},{2,0},{1,3},{3,1},{4,6},{6,4},{5,7},{7,5},{8,10},{10,8},{9,1... | collective-permute-start | bytes 270344 | tf_op jit(solution)/shard_map/ppermute | solution.py:345
  32.5 1.4 %collective-permute-start.13 = (bf16[160,256]{1,0:T(8,128)(2,1)S(1)}, bf16[160,256]{1,0:T(8,128)(2,1)S(1)}, u32[]{:S(2)}, u32[]{:S(2)}) collective-permute-start(bf16[160,256]{1,0:T(8,128)(2,1)S(1)} %shard_map.117), channel_id=1, source_target_pairs={{0,1},{1,0},{2,3},{3,2},{4,5},{5,4},{6,7},{7,6},{8,9},{9,8},{10,11... | collective-permute-start | bytes 245768 | tf_op jit(solution)/shard_map/ppermute | solution.py:345
  36.3 1.4 %collective-permute-start.17 = (bf16[176,256]{1,0:T(8,128)(2,1)S(1)}, bf16[176,256]{1,0:T(8,128)(2,1)S(1)}, u32[]{:S(2)}, u32[]{:S(2)}) collective-permute-start(bf16[176,256]{1,0:T(8,128)(2,1)S(1)} %collective-permute-done.6.refs_1_), channel_id=1, source_target_pairs={{0,1},{1,0},{2,3},{3,2},{4,5},{5,4},{6,7},{7,6},{8,9},{9,8},{10,11... | collective-permute-start | bytes 270344 | tf_op jit(solution)/shard_map/ppermute | solution.py:345
  36.8 1.4 %collective-permute-start.19 = (bf16[176,256]{1,0:T(8,128)(2,1)S(1)}, bf16[176,256]{1,0:T(8,128)(2,1)S(1)}, u32[]{:S(2)}, u32[]{:S(2)}) collective-permute-start(bf16[176,256]{1,0:T(8,128)(2,1)S(1)} %collective-permute-done.8.refs_3_.refs_8_), channel_id=1, source_target_pairs={{0,1},{1,0},{2,3},{3,2},{4,5},{5,4},{6,7},{7,6},{8,9},{9,8},{10,11... | collective-permute-start | bytes 270344 | tf_op jit(solution)/shard_map/ppermute | solution.py:345
  41.6 1.7 %collective-permute-start.20 = (bf16[160,1024]{1,0:T(8,128)(2,1)S(1)}, bf16[160,1024]{1,0:T(8,128)(2,1)S(1)}, u32[]{:S(2)}, u32[]{:S(2)}) collective-permute-start(bf16[160,1024]{1,0:T(8,128)(2,1)S(1)} %get-tuple-element.62), channel_id=1, source_target_pairs={{0,1},{1,0},{2,3},{3,2},{4,5},{5,4},{6,7},{7,6},{8,9},{9,8},{10,11... | collective-permute-start | bytes 983048 | tf_op jit(solution)/shard_map/ppermute | solution.py:345
  43.4 6.5 %collective-permute-start.21 = (bf16[80,1024]{1,0:T(8,128)(2,1)S(1)}, bf16[80,1024]{1,0:T(8,128)(2,1)S(1)}, u32[]{:S(2)}, u32[]{:S(2)}) collective-permute-start(bf16[80,1024]{1,0:T(8,128)(2,1)S(1)} %shard_map.122), channel_id=1, source_target_pairs={{0,2},{2,0},{1,3},{3,1},{4,6},{6,4},{5,7},{7,5},{8,10},{10,8},{9,1... | collective-permute-start | bytes 491528 | tf_op jit(solution)/shard_map/ppermute | solution.py:345
  45.7 1.4 %collective-permute-start.23 = (bf16[40,1024]{1,0:T(8,128)(2,1)S(1)}, bf16[40,1024]{1,0:T(8,128)(2,1)S(1)}, u32[]{:S(2)}, u32[]{:S(2)}) collective-permute-start(bf16[40,1024]{1,0:T(8,128)(2,1)S(1)} %get-tuple-element.64), channel_id=1, source_target_pairs={{0,1},{1,0},{2,3},{3,2},{4,5},{5,4},{6,7},{7,6},{8,9},{9,8},{10,11... | collective-permute-start | bytes 245768 | tf_op jit(solution)/shard_map/ppermute | solution.py:345
  46.1 6.4 %collective-permute-start.14 = (bf16[40,1024]{1,0:T(8,128)(2,1)S(1)}, bf16[40,1024]{1,0:T(8,128)(2,1)S(1)}, u32[]{:S(2)}, u32[]{:S(2)}) collective-permute-start(bf16[40,1024]{1,0:T(8,128)(2,1)S(1)} %get-tuple-element.55), channel_id=1, source_target_pairs={{0,1},{1,0},{2,3},{3,2},{4,5},{5,4},{6,7},{7,6},{8,9},{9,8},{10,11... | collective-permute-start | bytes 245768 | tf_op jit(solution)/shard_map/ppermute | solution.py:345
  46.2 6.3 %collective-permute-start.15 = (bf16[40,1024]{1,0:T(8,128)(2,1)S(1)}, bf16[40,1024]{1,0:T(8,128)(2,1)S(1)}, u32[]{:S(2)}, u32[]{:S(2)}) collective-permute-start(bf16[40,1024]{1,0:T(8,128)(2,1)S(1)} %get-tuple-element.56), channel_id=1, source_target_pairs={{0,1},{1,0},{2,3},{3,2},{4,5},{5,4},{6,7},{7,6},{8,9},{9,8},{10,11... | collective-permute-start | bytes 245768 | tf_op jit(solution)/shard_map/ppermute | solution.py:345
  50.0 6.8 %collective-permute-start.28 = (bf16[40,1024]{1,0:T(8,128)(2,1)S(1)}, bf16[40,1024]{1,0:T(8,128)(2,1)S(1)}, u32[]{:S(2)}, u32[]{:S(2)}) collective-permute-start(bf16[40,1024]{1,0:T(8,128)(2,1)S(1)} %get-tuple-element.74), channel_id=1, source_target_pairs={{0,12},{4,8},{8,4},{12,0},{1,13},{5,9},{9,5},{13,1},{2,14},{6,10},... | collective-permute-start | bytes 245768 | tf_op jit(solution)/shard_map/ppermute | solution.py:342
  52.3 7.9 %collective-permute-start.27 = (bf16[40,1024]{1,0:T(8,128)(2,1)S(1)}, bf16[40,1024]{1,0:T(8,128)(2,1)S(1)}, u32[]{:S(2)}, u32[]{:S(2)}) collective-permute-start(bf16[40,1024]{1,0:T(8,128)(2,1)S(1)} %get-tuple-element.69.refs_9_), channel_id=1, source_target_pairs={{0,8},{4,12},{8,0},{12,4},{1,9},{5,13},{9,1},{13,5},{2,10},{6,14},... | collective-permute-start | bytes 245768 | tf_op jit(solution)/shard_map/ppermute | solution.py:342
  52.8 7.9 %collective-permute-start.24 = (bf16[40,1024]{1,0:T(8,128)(2,1)S(1)}, bf16[40,1024]{1,0:T(8,128)(2,1)S(1)}, u32[]{:S(2)}, u32[]{:S(2)}) collective-permute-start(bf16[40,1024]{1,0:T(8,128)(2,1)S(1)} %get-tuple-element.70), channel_id=1, source_target_pairs={{0,4},{4,0},{8,12},{12,8},{1,5},{5,1},{9,13},{13,9},{2,6},{6,2},{1... | collective-permute-start | bytes 245768 | tf_op jit(solution)/shard_map/ppermute | solution.py:342
  54.9 6.6 %collective-permute-start.25 = (bf16[40,1024]{1,0:T(8,128)(2,1)S(1)}, bf16[40,1024]{1,0:T(8,128)(2,1)S(1)}, u32[]{:S(2)}, u32[]{:S(2)}) collective-permute-start(bf16[40,1024]{1,0:T(8,128)(2,1)S(1)} %get-tuple-element.72), channel_id=1, source_target_pairs={{0,6},{2,4},{4,2},{6,0},{8,14},{10,12},{12,10},{14,8},{1,7},{3,5},... | collective-permute-start | bytes 245768 | tf_op jit(solution)/shard_map/ppermute | solution.py:349
  55.7 5.8 %collective-permute-start.26 = (bf16[40,1024]{1,0:T(8,128)(2,1)S(1)}, bf16[40,1024]{1,0:T(8,128)(2,1)S(1)}, u32[]{:S(2)}, u32[]{:S(2)}) collective-permute-start(bf16[40,1024]{1,0:T(8,128)(2,1)S(1)} %get-tuple-element.73), channel_id=1, source_target_pairs={{0,2},{2,0},{1,3},{3,1},{4,6},{6,4},{5,7},{7,5},{8,10},{10,8},{9,1... | collective-permute-start | bytes 245768 | tf_op jit(solution)/shard_map/ppermute | solution.py:345
  (6 other events, 25.1 us)

commit v4 on v3

--- a/solution.py
+++ b/solution.py
@@ -13,6 +13,7 @@
 NEGATIVE = -1e30
 META = 16
 LATER = 16 * 1024 * 1024
+MIB = 1024 * 1024
 ORDER = (2, 3, 1, 0)
 VMEM_LIMIT = 12 * 1024 * 1024
 
@@ -200,16 +201,29 @@
         out[experts * cap :, 0 : experts * cap] = dot_nt(lines.astype(BF16), place).astype(BF16)
 
 
+def copy_kernel(block_ref, out_ref):
+    out_ref[...] = block_ref[...]
+
+
 def trim_kernel(block_ref, out_ref):
     out_ref[...] = block_ref[0 : out_ref.shape[0], :]
 
 
+def pair_kernel(left_ref, right_ref, out_ref):
+    rows, width = slice(0, out_ref.shape[0]), left_ref.shape[1]
+    out_ref[:, 0:width] = left_ref[rows, :]
+    out_ref[:, width:] = right_ref[rows, :]
+
+
 def first_kernel(tile, *refs):
     blocks, (gain_ref, bias_ref, w_ref, out_ref, n_ref) = refs[:-5], refs[-5:]
-    width, model = blocks[0].shape[1], n_ref.shape[1]
+    width, model = min(block.shape[1] for block in blocks), n_ref.shape[1]
+    pieces = [
+        (block, slice(at, at + width)) for block in blocks for at in range(0, block.shape[1], width)
+    ]
     for at in range(0, n_ref.shape[0], META):
         rows = slice(at, at + META)
-        values = [block[rows, :].astype(F32) for block in blocks]
+        values = [block[rows, cols].astype(F32) for block, cols in pieces]
         center = jnp.sum(sum(values), axis=-1, keepdims=True) * (1.0 / model)
         shifted = [value - center for value in values]
         spread = sum(value * value for value in shifted)
@@ -236,15 +250,28 @@
             out_ref[:, at : at + tile] = other[k * rows : (k + 1) * rows, :]
 
 
+def half_kernel(tile, other, a_ref, w_ref, *outs):
+    columns, rows = outs[0].shape[1], outs[0].shape[0]
+    half = lax.axis_index("mp")
+    half = 1 - half if other else half
+    for at in range(columns // tile):
+        part = dot(a_ref[...], w_ref[:, columns_at(half * (columns // tile) + at, tile)])
+        for k, out_ref in enumerate(outs):
+            out_ref[:, at * tile : (at + 1) * tile] = part[k * rows : (k + 1) * rows, :].astype(BF16)
+
+
 def row_factors(lines_ref, count):
     same = (iota((count, count), 0) == iota((count, count), 1)).astype(BF16)
     columns = dot_nt(same, lines_ref[count:, 0:count])
     return columns[:, 0:1] + columns[:, 1:2] + columns[:, 2:3], columns[:, 3:4]
 
 
-def plain_kernel(kept_ref, got_ref, out_ref):
-    rows = slice(kept_ref.shape[0] - out_ref.shape[0], kept_ref.shape[0])
-    out_ref[...] = (kept_ref[rows, :].astype(F32) + got_ref[rows, :].astype(F32)).astype(BF16)
+def plain_kernel(kept_ref, got_ref, *outs):
+    cap = outs[0].shape[0]
+    for k, out_ref in enumerate(outs):
+        rows, half = slice((2 + k) * cap, (3 + k) * cap), slice(k * cap, (k + 1) * cap)
+        total = kept_ref[rows, :].astype(F32) + got_ref[half, :].astype(F32)
+        out_ref[...] = total.astype(BF16)
 
 
 def gather_states(blocks, states, rows):
@@ -255,7 +282,7 @@
 
 
 def base_kernel(experts, kept_ref, *refs):
-    got, blocks, refs = refs[:2], refs[2 : 2 + experts], refs[2 + experts :]
+    got_ref, blocks, refs = refs[0], refs[1 : 1 + experts], refs[1 + experts :]
     bases, factors, states = refs[:2], refs[2:4], refs[4]
     count = kept_ref.shape[0]
     cap = count // experts
@@ -263,13 +290,13 @@
     gather_states(blocks, states, slice(2 * cap, 4 * cap))
     for k in range(2):
         rows, half = slice((2 + k) * cap, (3 + k) * cap), slice(k * cap, (k + 1) * cap)
-        total = kept_ref[rows, :].astype(F32) + got[k][...].astype(F32)
+        total = kept_ref[rows, :].astype(F32) + got_ref[half, :].astype(F32)
         bases[k][...] = total * weight[rows, :] + leads[rows, :] * states[half, :]
         factors[k][...] = jnp.broadcast_to(weight[rows, :], (cap, HEAD))
 
 
 def tail_kernel(experts, kept_ref, *refs):
-    got, blocks, refs = refs[:2], refs[2 : 2 + experts], refs[2 + experts :]
+    got_ref, blocks, refs = refs[0], refs[1 : 1 + experts], refs[1 + experts :]
     far_kept_ref, far_got_ref, lines_ref, _, near0, near1, far0, far1, states = refs
     count = kept_ref.shape[0]
     cap = count // experts
@@ -278,20 +305,16 @@
     gather_states(blocks, states, slice(0, 2 * cap))
     for k, (near, far) in enumerate(((near0, far0), (near1, far1))):
         rows = slice(k * cap, (k + 1) * cap)
-        total = kept_ref[rows, :].astype(F32) + got[k][...].astype(F32)
+        total = kept_ref[rows, :].astype(F32) + got_ref[rows, :].astype(F32)
         total = total * weight[rows, :] + leads[rows, :] * states[rows, :]
         near[...] = total.astype(BF16)
         total = far_kept_ref[rows, :].astype(F32) + far_got_ref[rows, :].astype(F32)
         far[...] = (total * far_weight[rows, :]).astype(BF16)
 
 
-def join_kernel(came_ref, *refs):
-    count = len(refs) // 3
-    cap = refs[0].shape[0]
-    for k in range(count):
-        base_ref, factor_ref, out_ref = refs[k], refs[count + k], refs[2 * count + k]
-        came = came_ref[k * cap : (k + 1) * cap, :].astype(F32)
-        out_ref[...] = (base_ref[...] + factor_ref[:, 0:1] * came).astype(BF16)
+def join_kernel(came_ref, base_ref, factor_ref, out_ref):
+    total = base_ref[...] + factor_ref[:, 0:1] * came_ref[...].astype(F32)
+    out_ref[...] = total.astype(BF16)
 
 
 def mix_kernel(experts, cap, tile, steps, routes_ref, *refs):
@@ -410,67 +433,86 @@
         moved=16 * rows * columns,
     )(in_vmem(w_in), in_vmem(w_out), *messages)
 
-    own = {step: along(block, step) for step, block in zip(ORDER, compact)}
+    def ahead(block, mib):
+        return call(copy_kernel, [struct(*block.shape)], [IN_VMEM], moved=mib * MIB)(block)[0]
+
+    compact = dict(zip(ORDER, compact))
+    own = {step: along(compact[step], step) for step in ORDER}
     count = experts * cap
 
     def trim(block):
         return call(trim_kernel, [struct(count, width)], [IN_VMEM])(block)[0]
 
-    trimmed = {step: trim(own[step]) for step in ORDER}
-    far = {step: swap(own[step], "dp") for step in (2, 3)}
-    far[1] = across(compact[2])
-    far[0] = swap(compact[3], "dp")
-    own_other = {step: swap(trimmed[step], "mp") for step in ORDER}
-
-    def first(blocks, others, known):
+    def first(blocks, known):
         return call(
             functools.partial(first_kernel, 512),
             [struct(count, hidden_units)],
-            [IN_VMEM] * (2 * experts + 3),
+            [IN_VMEM] * (len(blocks) + 3),
             scratch=[pltpu.VMEM((count, model), BF16)],
             flops=known * 2 * count * model * hidden_units,
             moved=known * 2 * model * hidden_units,
-        )(
-            *[blocks[step] for step in ORDER],
-            *[others[step] for step in ORDER],
-            in_vmem(gain),
-            in_vmem(bias),
-            in_vmem(w_in),
-        )[0]
-
-    def second(active, parts, known):
-        kept, *sent = call(
-            functools.partial(second_kernel, 512),
-            [struct(count, columns)] + [struct(count // parts, columns)] * parts,
+        )(*blocks, in_vmem(gain), in_vmem(bias), in_vmem(w_in))[0]
+
+    def pair(left, right):
+        return call(pair_kernel, [struct(count, 2 * width)], [IN_VMEM] * 2)(left, right)[0]
+
+    trimmed = [trim(own[step]) for step in ORDER]
+    far1, far0 = across(compact[1]), swap(compact[0], "dp")
+    near = pair(own[2], own[3])
+    far = swap(near, "dp")
+    trimmed[2], far1, far0 = lax.optimization_barrier((trimmed[2], far1, far0))
+    near_other = [swap(block, "mp") for block in trimmed]
+    far1_other, far0_other = swap(far1, "mp"), swap(far0, "mp")
+    active = first([near, own[1], own[0], *near_other], 0)
+    far, active = lax.optimization_barrier((far, active))
+    far_other = swap(far, "mp")
+    kept, *sent = call(
+        functools.partial(second_kernel, 512),
+        [struct(count, columns)] + [struct(count // 2, columns)] * 2,
+        [IN_VMEM, IN_VMEM],
+    )(active, in_vmem(w_out))
+    got = [swap(part, "mp") for part in sent]
+    far_other, kept = lax.optimization_barrier((far_other, kept))
+
+    active = first([far, far1, far0, far_other, far1_other, far0_other], 1)
+    active, *got = lax.optimization_barrier((active, *got))
+
+    def half(active, other, parts):
+        return call(
+            functools.partial(half_kernel, 512, other),
+            [struct(count // parts, columns)] * parts,
             [IN_VMEM, IN_VMEM],
-            flops=known * 2 * count * model * hidden_units,
-            moved=known * 2 * model * hidden_units,
+            flops=count * model * hidden_units,
+            moved=model * hidden_units,
         )(active, in_vmem(w_out))
-        return kept, [swap(part, "mp") for part in sent]
-
-    own_other[0], far[0], far[1] = lax.optimization_barrier((own_other[0], far[0], far[1]))
-    active = first(own, own_other, 0)
-    *late, active = lax.optimization_barrier((*[far[step] for step in ORDER], active))
-    far = dict(zip(ORDER, late))
-    far_other = {step: swap(far[step], "mp") for step in ORDER}
-    mine, (theirs,) = second(first(far, far_other, 1), 1, 1)
-    kept, got = second(active, experts, 0)
+
+    theirs = [swap(part, "mp") for part in half(active, True, 2)]
+    mine = half(active, False, 1)[0]
     arrived = [own[step] for step in ORDER]
-    based = call(
+    base2, base3, factor2, factor3 = call(
         functools.partial(base_kernel, experts),
         [struct(cap, columns, F32)] * 2 + [struct(cap, HEAD, F32)] * 2,
-        [IN_VMEM] * (3 + experts),
+        [IN_VMEM] * (2 + experts),
         scratch=[pltpu.VMEM((2 * cap, columns), F32)],
-    )(kept, *got[2:], *arrived)
-    plain = call(plain_kernel, [struct(2 * cap, columns)], [IN_VMEM] * 2)(mine, theirs)[0]
-    joined = call(join_kernel, [struct(cap, columns)] * 2, [IN_VMEM] * 5)(swap(plain, "dp"), *based)
+    )(kept, got[1], *arrived)
+    theirs[1], base2 = lax.optimization_barrier((theirs[1], base2))
+    plain2, plain3 = call(plain_kernel, [struct(cap, columns)] * 2, [IN_VMEM] * 2)(mine, theirs[1])
+
+    def join(came, base, factor, mib):
+        return call(join_kernel, [struct(cap, columns)], [IN_VMEM] * 3, moved=mib * MIB)(
+            came, base, factor
+        )[0]
+
+    joined2 = join(swap(plain2, "dp"), base2, factor2, 4)
+    joined3 = join(swap(plain3, "dp"), base3, factor3, 0)
     near0, near1, away0, away1 = call(
         functools.partial(tail_kernel, experts),
         [struct(cap, columns)] * 4,
-        [IN_VMEM] * (6 + experts) + [IN_ANY],
+        [IN_VMEM] * (5 + experts) + [IN_ANY],
         scratch=[pltpu.VMEM((2 * cap, columns), F32)],
-        moved=LATER,
-    )(kept, *got[:2], *arrived, mine, theirs, far[0], joined[0])
+        moved=2 * LATER,
+    )(kept, got[0], *arrived, mine, theirs[0], far0, plain3)
+
     def mix(steps, blocks, dtype, *before):
         return call(
             functools.partial(mix_kernel, experts, cap, 512, steps),
@@ -478,9 +520,9 @@
             [IN_VMEM] * (1 + len(blocks) + len(before)),
         )(routes.T, *blocks, *before)[0]
 
-    share = mix((2, 3), [along(joined[0], 2), along(joined[1], 3)], F32)
     direct = [along(near1, 1), near0, across(away1), swap(away0, "dp")]
-    return mix((1, 0, 1, 0), direct, BF16, share)
+    share = mix((1, 0, 1, 0), direct, F32)
+    return mix((2, 3), [along(joined2, 2), along(joined3, 3)], BF16, share)
 
 
 def shards(

time: 63 us -> 59.6 us (0.946)
  waiting for transfers between devices: 15.8 us -> 8.99 us
  starting transfers between devices: 26.7 us -> 29.7 us
    ppermute x18 -> x16, waiting for transfers between devices: 6.57 us -> 0.95 us  [swap(): return lax.ppermute(array, axis, [(0, 1), (1, 0)])]
    ppermute x9, starting transfers between devices: 15.2 us -> 16.7 us  [along(): lax.ppermute(array, 'expert', [(i, i ^ step) for i in range(experts)])]
    ppermute x9, waiting for transfers between devices: 7.85 us -> 6.55 us  [along(): lax.ppermute(array, 'expert', [(i, i ^ step) for i in range(experts)])]
    ppermute x18 -> x16, starting transfers between devices: 7.9 us -> 8.81 us  [swap(): return lax.ppermute(array, axis, [(0, 1), (1, 0)])]
    pallas_call x4 -> x7, Pallas kernels: 3.22 us -> 3.51 us  [the longest x2 1.74 us: half(): call(functools.partial(half_kernel, 512, other), [struct(count // parts,...]
  transfers between devices with their start and end apart: 29 -> 27, of which waited for: 19 -> 7; matrix products, arithmetic and copies ran while one was open for 0% -> 0% of each run, Pallas kernels for 21% -> 27%
where the time goes in v4:
time: 59.6 us; the launch traced here: 59.3 us
  starting transfers between devices  29.7 us (50%)
  Pallas kernels  20.4 us (34%)
  waiting for transfers between devices  8.99 us (15%)
    ppermute x9, starting transfers between devices, along(): lax.ppermute(array, 'expert', [(i, i ^ step) for i in range(experts)])  16.7 us
    ppermute x16, starting transfers between devices, swap(): return lax.ppermute(array, axis, [(0, 1), (1, 0)])  8.81 us
    ppermute x9, waiting for transfers between devices, along(): lax.ppermute(array, 'expert', [(i, i ^ step) for i in range(experts)])  6.55 us
    pallas_call x1, Pallas kernels, head_shards(): pl.pallas_call(functools.partial(prefetch_kernel, experts), out_shape=[pl...  6.21 us
    ppermute x2, starting transfers between devices, across(): return lax.ppermute(array, ('expert', 'dp'), pairs)  4.18 us
    pallas_call x2, Pallas kernels, first(): call(functools.partial(first_kernel, 512), [struct(count, hidden_units)],...  3.75 us
    pallas_call x3, Pallas kernels, pack(): call(functools.partial(pack_kernel, steps), [struct(4 * rows + META, widt...  3.58 us
    pallas_call x2, Pallas kernels, mix(): call(functools.partial(mix_kernel, experts, cap, 512, steps), [struct(row...  1.76 us
  transfers between devices with their start and end apart: 27, of which 7 were waited for; matrix products, arithmetic and copies ran while one was open for 0% of the time, Pallas kernels for 27%

profile of v4, /device:TPU:0, one launch (start us, length us, event | category | flops | bytes accessed | tf_op | source)
XLA Modules:
  0.0 59.3 jit_solution(16077219525771925570)
XLA Ops:
  0.0 1.1 %shard_map.109.refs_0_ = bf16[272,256]{1,0:T(8,128)(2,1)S(1)} custom-call(bf16[64,1024]{1,0:T(8,128)(2,1)} %q_hbm.5, bf16[64,2,1024]{2,1,0:T(2,128)(2,1)} %m_hbm.5, bf16[64,1024]{1,0:T(8,128)(2,1)} %h_hbm.5, s32[1,64]{1,0:T(1,128)} %bitcast.20, s32[1,64]{1,0:T(1,128)} %bitcast.23, s32[2,64]{1,0:T(2,128)} %bitcast.8, f32[2,64]{1,0:T(2,128)} %bitcast.15), custom_call_target="tpu_custom_call" | custom-call | tf_op jit(solution)/shard_map/pallas_call | solution.py:375
  1.1 4.1 %collective-permute-start = (bf16[272,256]{1,0:T(8,128)(2,1)S(1)}, bf16[272,256]{1,0:T(8,128)(2,1)S(1)}, u32[]{:S(2)}, u32[]{:S(2)}) collective-permute-start(bf16[272,256]{1,0:T(8,128)(2,1)S(1)} %shard_map.109.refs_0_), channel_id=1, source_target_pairs={{0,8},{4,12},{8,0},{12,4},{1,9},{5,13},{9,1},{13,5},{2,10},{6,14},... | collective-permute-start | bytes 417800 | tf_op jit(solution)/shard_map/ppermute | solution.py:365
  5.2 1.1 %shard_map.110.refs_0_ = bf16[272,256]{1,0:T(8,128)(2,1)S(1)} custom-call(bf16[64,1024]{1,0:T(8,128)(2,1)} %q_hbm.5, bf16[64,2,1024]{2,1,0:T(2,128)(2,1)} %m_hbm.5, bf16[64,1024]{1,0:T(8,128)(2,1)} %h_hbm.5, s32[1,64]{1,0:T(1,128)} %bitcast.21, s32[1,64]{1,0:T(1,128)} %bitcast.24, s32[2,64]{1,0:T(2,128)} %bitcast.9, f32[2,64]{1,0:T(2,128)} %bitcast.16, ...), custom_call_target="tpu_custom_call" | custom-call | bytes 16777216 | tf_op jit(solution)/shard_map/pallas_call | solution.py:375
  6.3 1.6 %collective-permute-start.2 = (bf16[272,256]{1,0:T(8,128)(2,1)S(1)}, bf16[272,256]{1,0:T(8,128)(2,1)S(1)}, u32[]{:S(2)}, u32[]{:S(2)}) collective-permute-start(bf16[272,256]{1,0:T(8,128)(2,1)S(1)} %shard_map.110.refs_0_), channel_id=1, source_target_pairs={{0,4},{4,0},{8,12},{12,8},{1,5},{5,1},{9,13},{13,9},{2,6},{6,2},{1... | collective-permute-start | bytes 417800 | tf_op jit(solution)/shard_map/ppermute | solution.py:365
  8.0 1.4 %shard_map.111 = (bf16[272,256]{1,0:T(8,128)(2,1)S(1)}, bf16[272,256]{1,0:T(8,128)(2,1)S(1)}) custom-call(bf16[64,1024]{1,0:T(8,128)(2,1)} %q_hbm.5, bf16[64,2,1024]{2,1,0:T(2,128)(2,1)} %m_hbm.5, bf16[64,1024]{1,0:T(8,128)(2,1)} %h_hbm.5, s32[1,64]{1,0:T(1,128)} %bitcast.22, s32[1,64]{1,0:T(1,128)} %bitcast.25, s32[2,64]{1,0:T(2,128)} %bitcast.10, ...), custom_call_target="tpu_custom_call" | custom-call | bytes 16777216 | tf_op jit(solution)/shard_map/pallas_call | solution.py:375
  9.4 6.2 %shard_map.112 = (bf16[2048,2048]{1,0:T(8,128)(2,1)S(1)}, bf16[2048,2048]{1,0:T(8,128)(2,1)S(1)}, f32[1,2048]{1,0:T(1,128)S(1)}, f32[1,2048]{1,0:T(1,128)S(1)}) custom-call(bf16[2048,2048]{1,0:T(8,128)(2,1)} %bitcast.13, bf16[2048,2048]{1,0:T(8,128)(2,1)} %bitcast.14, f32[1,2048]{1,0:T(1,128)} %bitcast.18, f32[1,2048]{1,0:T(1,128)} %bitcast.19, ...), custom_call_target="tpu_custom_call" | custom-call | bytes 33554432 | tf_op jit(solution)/shard_map/pallas_call | solution.py:405
  16.3 0.9 %shard_map.113 = (bf16[176,256]{1,0:T(8,128)(2,1)S(1)}, bf16[176,256]{1,0:T(8,128)(2,1)S(1)}, bf16[176,256]{1,0:T(8,128)(2,1)S(1)}, bf16[176,256]{1,0:T(8,128)(2,1)S(1)}) custom-call(bf16[2048,2048]{1,0:T(8,128)(2,1)S(1)} %get-tuple-element.43.w1_ref.refs_9_.refs_8_, bf16[2048,2048]{1,0:T(8,128)(2,1)S(1)} %get-tuple-element.44.w2_ref.w_ref, ...), custom_call_target="tpu_custom_call" | custom-call | flops 134217728 | bytes 1048576 | tf_op jit(solution)/shard_map/pallas_call | solution.py:428
  17.3 4.2 %collective-permute-start.3 = (bf16[176,256]{1,0:T(8,128)(2,1)S(1)}, bf16[176,256]{1,0:T(8,128)(2,1)S(1)}, u32[]{:S(2)}, u32[]{:S(2)}) collective-permute-start(bf16[176,256]{1,0:T(8,128)(2,1)S(1)} %get-tuple-element.46), channel_id=1, source_target_pairs={{0,8},{4,12},{8,0},{12,4},{1,9},{5,13},{9,1},{13,5},{2,10},{6,14},... | collective-permute-start | bytes 270344 | tf_op jit(solution)/shard_map/ppermute | solution.py:365
  22.2 2.8 %collective-permute-start.9 = (bf16[176,256]{1,0:T(8,128)(2,1)S(1)}, bf16[176,256]{1,0:T(8,128)(2,1)S(1)}, u32[]{:S(2)}, u32[]{:S(2)}) collective-permute-start(bf16[176,256]{1,0:T(8,128)(2,1)S(1)} %get-tuple-element.48), channel_id=1, source_target_pairs={{0,6},{2,4},{4,2},{6,0},{8,14},{10,12},{12,10},{14,8},{1,7},{3,5},... | collective-permute-start | bytes 270344 | tf_op jit(solution)/shard_map/ppermute | solution.py:372
  25.4 2.7 %collective-permute-done.3.left_ref.block_ref.refs_1_ = bf16[176,256]{1,0:T(8,128)(2,1)S(1)} collective-permute-done((bf16[176,256]{1,0:T(8,128)(2,1)S(1)}, bf16[176,256]{1,0:T(8,128)(2,1)S(1)}, u32[]{:S(2)}, u32[]{:S(2)}) %collective-permute-start.3) | collective-permute-done | bytes 90144 | tf_op jit(solution)/shard_map/ppermute | solution.py:365
  28.9 1.5 %collective-permute-start.5 = (bf16[160,512]{1,0:T(8,128)(2,1)S(1)}, bf16[160,512]{1,0:T(8,128)(2,1)S(1)}, u32[]{:S(2)}, u32[]{:S(2)}) collective-permute-start(bf16[160,512]{1,0:T(8,128)(2,1)S(1)} %shard_map.114.refs_0_), channel_id=1, source_target_pairs={{0,2},{2,0},{1,3},{3,1},{4,6},{6,4},{5,7},{7,5},{8,10},{10,8},{9,1... | collective-permute-start | bytes 491528 | tf_op jit(solution)/shard_map/ppermute | solution.py:368
  31.0 1.5 %collective-permute-done.9.refs_1_ = bf16[176,256]{1,0:T(8,128)(2,1)S(1)} collective-permute-done((bf16[176,256]{1,0:T(8,128)(2,1)S(1)}, bf16[176,256]{1,0:T(8,128)(2,1)S(1)}, u32[]{:S(2)}, u32[]{:S(2)}) %collective-permute-start.9) | collective-permute-done | bytes 90144 | tf_op jit(solution)/shard_map/ppermute | solution.py:372
  33.9 1.9 %shard_map.119.a_ref = bf16[160,2048]{1,0:T(8,128)(2,1)S(1)} custom-call(bf16[160,512]{1,0:T(8,128)(2,1)S(1)} %shard_map.114.refs_0_, bf16[176,256]{1,0:T(8,128)(2,1)S(1)} %collective-permute-done.6.block_ref.refs_1_.refs_3_, bf16[176,256]{1,0:T(8,128)(2,1)S(1)} %get-tuple-element.49.block_ref.refs_2_.refs_4_, ...), custom_call_target="tpu_custom_call" | custom-call | tf_op jit(solution)/shard_map/pallas_call | solution.py:447
  36.8 1.5 %shard_map.120 = (bf16[160,1024]{1,0:T(8,128)(2,1)S(1)}, bf16[80,1024]{1,0:T(8,128)(2,1)S(1)}, bf16[80,1024]{1,0:T(8,128)(2,1)S(1)}) custom-call(bf16[160,2048]{1,0:T(8,128)(2,1)S(1)} %shard_map.119.a_ref, bf16[2048,2048]{1,0:T(8,128)(2,1)S(1)} %get-tuple-element.44.w2_ref.w_ref), custom_call_target="tpu_custom_call" | custom-call | tf_op jit(solution)/shard_map/pallas_call | solution.py:469
  38.9 1.9 %shard_map.121.a_ref = bf16[160,2048]{1,0:T(8,128)(2,1)S(1)} custom-call(bf16[160,512]{1,0:T(8,128)(2,1)S(1)} %collective-permute-done.5.refs_0_, bf16[176,256]{1,0:T(8,128)(2,1)S(1)} %collective-permute-done.9.refs_1_, bf16[176,256]{1,0:T(8,128)(2,1)S(1)} %collective-permute-done.10.refs_2_.refs_7_, bf16[160,512]{1,0:T(8,128)(2,1)S(1)} %collective-permute-done.13.refs_3_, ...), custom_call_target="tpu_custom_call" | custom-call | flops 1342177280 | bytes 8388608 | tf_op jit(solution)/shard_map/pallas_call | solution.py:447
  40.8 0.9 %shard_map.123 = (bf16[80,1024]{1,0:T(8,128)(2,1)S(1)}, bf16[80,1024]{1,0:T(8,128)(2,1)S(1)}) custom-call(bf16[160,2048]{1,0:T(8,128)(2,1)S(1)} %shard_map.121.a_ref, bf16[2048,2048]{1,0:T(8,128)(2,1)S(1)} %get-tuple-element.44.w2_ref.w_ref), custom_call_target="tpu_custom_call" | custom-call | flops 671088640 | bytes 4194304 | tf_op jit(solution)/shard_map/pallas_call | solution.py:481
  42.6 0.9 %shard_map.122.kept_ref.refs_5_ = bf16[160,1024]{1,0:T(8,128)(2,1)S(1)} custom-call(bf16[160,2048]{1,0:T(8,128)(2,1)S(1)} %shard_map.121.a_ref, bf16[2048,2048]{1,0:T(8,128)(2,1)S(1)} %get-tuple-element.44.w2_ref.w_ref), custom_call_target="tpu_custom_call" | custom-call | flops 671088640 | bytes 4194304 | tf_op jit(solution)/shard_map/pallas_call | solution.py:481
  44.1 1.5 %collective-permute-start.21 = (bf16[40,1024]{1,0:T(8,128)(2,1)S(1)}, bf16[40,1024]{1,0:T(8,128)(2,1)S(1)}, u32[]{:S(2)}, u32[]{:S(2)}) collective-permute-start(bf16[40,1024]{1,0:T(8,128)(2,1)S(1)} %get-tuple-element.70.refs_8_), channel_id=1, source_target_pairs={{0,2},{2,0},{1,3},{3,1},{4,6},{6,4},{5,7},{7,5},{8,10},{10,8},{9,1... | collective-permute-start | bytes 245768 | tf_op jit(solution)/shard_map/ppermute | solution.py:368
  46.6 1.4 %collective-permute-start.25 = (bf16[40,1024]{1,0:T(8,128)(2,1)S(1)}, bf16[40,1024]{1,0:T(8,128)(2,1)S(1)}, u32[]{:S(2)}, u32[]{:S(2)}) collective-permute-start(bf16[40,1024]{1,0:T(8,128)(2,1)S(1)} %get-tuple-element.77), channel_id=1, source_target_pairs={{0,6},{2,4},{4,2},{6,0},{8,14},{10,12},{12,10},{14,8},{1,7},{3,5},... | collective-permute-start | bytes 245768 | tf_op jit(solution)/shard_map/ppermute | solution.py:372
  48.0 1.5 %collective-permute-start.26 = (bf16[40,1024]{1,0:T(8,128)(2,1)S(1)}, bf16[40,1024]{1,0:T(8,128)(2,1)S(1)}, u32[]{:S(2)}, u32[]{:S(2)}) collective-permute-start(bf16[40,1024]{1,0:T(8,128)(2,1)S(1)} %get-tuple-element.78), channel_id=1, source_target_pairs={{0,2},{2,0},{1,3},{3,1},{4,6},{6,4},{5,7},{7,5},{8,10},{10,8},{9,1... | collective-permute-start | bytes 245768 | tf_op jit(solution)/shard_map/ppermute | solution.py:368
  49.6 1.4 %collective-permute-start.20 = (bf16[40,1024]{1,0:T(8,128)(2,1)S(1)}, bf16[40,1024]{1,0:T(8,128)(2,1)S(1)}, u32[]{:S(2)}, u32[]{:S(2)}) collective-permute-start(bf16[40,1024]{1,0:T(8,128)(2,1)S(1)} %shard_map.126), channel_id=1, source_target_pairs={{0,8},{4,12},{8,0},{12,4},{1,9},{5,13},{9,1},{13,5},{2,10},{6,14},... | collective-permute-start | bytes 245768 | tf_op jit(solution)/shard_map/ppermute | solution.py:365
  51.0 4.0 %collective-permute-start.22 = (bf16[40,1024]{1,0:T(8,128)(2,1)S(1)}, bf16[40,1024]{1,0:T(8,128)(2,1)S(1)}, u32[]{:S(2)}, u32[]{:S(2)}) collective-permute-start(bf16[40,1024]{1,0:T(8,128)(2,1)S(1)} %shard_map.127), channel_id=1, source_target_pairs={{0,12},{4,8},{8,4},{12,0},{1,13},{5,9},{9,5},{13,1},{2,14},{6,10},... | collective-permute-start | bytes 245768 | tf_op jit(solution)/shard_map/ppermute | solution.py:365
  55.7 2.5 %collective-permute-done.20.refs_0_ = bf16[40,1024]{1,0:T(8,128)(2,1)S(1)} collective-permute-done((bf16[40,1024]{1,0:T(8,128)(2,1)S(1)}, bf16[40,1024]{1,0:T(8,128)(2,1)S(1)}, u32[]{:S(2)}, u32[]{:S(2)}) %collective-permute-start.20) | collective-permute-done | bytes 81952 | tf_op jit(solution)/shard_map/ppermute | solution.py:365
  58.1 1.2 %shard_map.130 = bf16[64,1024]{1,0:T(8,128)(2,1)} custom-call(s32[2,64]{1,0:T(2,128)S(1)} %bitcast.12, bf16[40,1024]{1,0:T(8,128)(2,1)S(1)} %collective-permute-done.20.refs_0_, bf16[40,1024]{1,0:T(8,128)(2,1)S(1)} %collective-permute-done.22.refs_1_, f32[64,1024]{1,0:T(8,128)S(1)} %shard_map.129.refs_2_), custom_call_target="tpu_custom_call" | custom-call | tf_op jit(solution)/shard_map/pallas_call | solution.py:517
  (54 shorter events, 9.5 us)
Async XLA Ops:
  1.1 14.5 %collective-permute-start = (bf16[272,256]{1,0:T(8,128)(2,1)S(1)}, bf16[272,256]{1,0:T(8,128)(2,1)S(1)}, u32[]{:S(2)}, u32[]{:S(2)}) collective-permute-start(bf16[272,256]{1,0:T(8,128)(2,1)S(1)} %shard_map.109.refs_0_), channel_id=1, source_target_pairs={{0,8},{4,12},{8,0},{12,4},{1,9},{5,13},{9,1},{13,5},{2,10},{6,14},... | collective-permute-start | bytes 417800 | tf_op jit(solution)/shard_map/ppermute | solution.py:365
  6.3 9.3 %collective-permute-start.2 = (bf16[272,256]{1,0:T(8,128)(2,1)S(1)}, bf16[272,256]{1,0:T(8,128)(2,1)S(1)}, u32[]{:S(2)}, u32[]{:S(2)}) collective-permute-start(bf16[272,256]{1,0:T(8,128)(2,1)S(1)} %shard_map.110.refs_0_), channel_id=1, source_target_pairs={{0,4},{4,0},{8,12},{12,8},{1,5},{5,1},{9,13},{13,9},{2,6},{6,2},{1... | collective-permute-start | bytes 417800 | tf_op jit(solution)/shard_map/ppermute | solution.py:365
  9.4 7.0 %collective-permute-start.1 = (bf16[272,256]{1,0:T(8,128)(2,1)S(1)}, bf16[272,256]{1,0:T(8,128)(2,1)S(1)}, u32[]{:S(2)}, u32[]{:S(2)}) collective-permute-start(bf16[272,256]{1,0:T(8,128)(2,1)S(1)} %get-tuple-element.45), channel_id=1, source_target_pairs={{0,12},{4,8},{8,4},{12,0},{1,13},{5,9},{9,5},{13,1},{2,14},{6,10},... | collective-permute-start | bytes 417800 | tf_op jit(solution)/shard_map/ppermute | solution.py:365
  17.3 10.8 %collective-permute-start.3 = (bf16[176,256]{1,0:T(8,128)(2,1)S(1)}, bf16[176,256]{1,0:T(8,128)(2,1)S(1)}, u32[]{:S(2)}, u32[]{:S(2)}) collective-permute-start(bf16[176,256]{1,0:T(8,128)(2,1)S(1)} %get-tuple-element.46), channel_id=1, source_target_pairs={{0,8},{4,12},{8,0},{12,4},{1,9},{5,13},{9,1},{13,5},{2,10},{6,14},... | collective-permute-start | bytes 270344 | tf_op jit(solution)/shard_map/ppermute | solution.py:365
  21.5 7.3 %collective-permute-start.4 = (bf16[176,256]{1,0:T(8,128)(2,1)S(1)}, bf16[176,256]{1,0:T(8,128)(2,1)S(1)}, u32[]{:S(2)}, u32[]{:S(2)}) collective-permute-start(bf16[176,256]{1,0:T(8,128)(2,1)S(1)} %get-tuple-element.47), channel_id=1, source_target_pairs={{0,12},{4,8},{8,4},{12,0},{1,13},{5,9},{9,5},{13,1},{2,14},{6,10},... | collective-permute-start | bytes 270344 | tf_op jit(solution)/shard_map/ppermute | solution.py:365
  22.0 8.5 %collective-permute-start.6 = (bf16[176,256]{1,0:T(8,128)(2,1)S(1)}, bf16[176,256]{1,0:T(8,128)(2,1)S(1)}, u32[]{:S(2)}, u32[]{:S(2)}) collective-permute-start(bf16[176,256]{1,0:T(8,128)(2,1)S(1)} %get-tuple-element.48), channel_id=1, source_target_pairs={{0,4},{4,0},{8,12},{12,8},{1,5},{5,1},{9,13},{13,9},{2,6},{6,2},{1... | collective-permute-start | bytes 270344 | tf_op jit(solution)/shard_map/ppermute | solution.py:365
  22.2 10.3 %collective-permute-start.9 = (bf16[176,256]{1,0:T(8,128)(2,1)S(1)}, bf16[176,256]{1,0:T(8,128)(2,1)S(1)}, u32[]{:S(2)}, u32[]{:S(2)}) collective-permute-start(bf16[176,256]{1,0:T(8,128)(2,1)S(1)} %get-tuple-element.48), channel_id=1, source_target_pairs={{0,6},{2,4},{4,2},{6,0},{8,14},{10,12},{12,10},{14,8},{1,7},{3,5},... | collective-permute-start | bytes 270344 | tf_op jit(solution)/shard_map/ppermute | solution.py:372
  24.9 7.6 %collective-permute-start.10 = (bf16[176,256]{1,0:T(8,128)(2,1)S(1)}, bf16[176,256]{1,0:T(8,128)(2,1)S(1)}, u32[]{:S(2)}, u32[]{:S(2)}) collective-permute-start(bf16[176,256]{1,0:T(8,128)(2,1)S(1)} %get-tuple-element.49.block_ref.refs_2_.refs_4_), channel_id=1, source_target_pairs={{0,2},{2,0},{1,3},{3,1},{4,6},{6,4},{5,7},{7,5},{8,10},{10,8},{9,1... | collective-permute-start | bytes 270344 | tf_op jit(solution)/shard_map/ppermute | solution.py:368
  28.9 7.0 %collective-permute-start.5 = (bf16[160,512]{1,0:T(8,128)(2,1)S(1)}, bf16[160,512]{1,0:T(8,128)(2,1)S(1)}, u32[]{:S(2)}, u32[]{:S(2)}) collective-permute-start(bf16[160,512]{1,0:T(8,128)(2,1)S(1)} %shard_map.114.refs_0_), channel_id=1, source_target_pairs={{0,2},{2,0},{1,3},{3,1},{4,6},{6,4},{5,7},{7,5},{8,10},{10,8},{9,1... | collective-permute-start | bytes 491528 | tf_op jit(solution)/shard_map/ppermute | solution.py:368
  30.4 2.6 %collective-permute-start.12 = (bf16[160,256]{1,0:T(8,128)(2,1)S(1)}, bf16[160,256]{1,0:T(8,128)(2,1)S(1)}, u32[]{:S(2)}, u32[]{:S(2)}) collective-permute-start(bf16[160,256]{1,0:T(8,128)(2,1)S(1)} %shard_map.118), channel_id=1, source_target_pairs={{0,1},{1,0},{2,3},{3,2},{4,5},{5,4},{6,7},{7,6},{8,9},{9,8},{10,11... | collective-permute-start | bytes 245768 | tf_op jit(solution)/shard_map/ppermute | solution.py:368
  30.5 2.6 %collective-permute-start.7 = (bf16[160,256]{1,0:T(8,128)(2,1)S(1)}, bf16[160,256]{1,0:T(8,128)(2,1)S(1)}, u32[]{:S(2)}, u32[]{:S(2)}) collective-permute-start(bf16[160,256]{1,0:T(8,128)(2,1)S(1)} %shard_map.115), channel_id=1, source_target_pairs={{0,1},{1,0},{2,3},{3,2},{4,5},{5,4},{6,7},{7,6},{8,9},{9,8},{10,11... | collective-permute-start | bytes 245768 | tf_op jit(solution)/shard_map/ppermute | solution.py:368
  35.8 3.1 %collective-permute-start.13 = (bf16[160,512]{1,0:T(8,128)(2,1)S(1)}, bf16[160,512]{1,0:T(8,128)(2,1)S(1)}, u32[]{:S(2)}, u32[]{:S(2)}) collective-permute-start(bf16[160,512]{1,0:T(8,128)(2,1)S(1)} %collective-permute-done.5.refs_0_), channel_id=1, source_target_pairs={{0,1},{1,0},{2,3},{3,2},{4,5},{5,4},{6,7},{7,6},{8,9},{9,8},{10,11... | collective-permute-start | bytes 491528 | tf_op jit(solution)/shard_map/ppermute | solution.py:368
  36.3 2.6 %collective-permute-start.14 = (bf16[176,256]{1,0:T(8,128)(2,1)S(1)}, bf16[176,256]{1,0:T(8,128)(2,1)S(1)}, u32[]{:S(2)}, u32[]{:S(2)}) collective-permute-start(bf16[176,256]{1,0:T(8,128)(2,1)S(1)} %collective-permute-done.9.refs_1_), channel_id=1, source_target_pairs={{0,1},{1,0},{2,3},{3,2},{4,5},{5,4},{6,7},{7,6},{8,9},{9,8},{10,11... | collective-permute-start | bytes 270344 | tf_op jit(solution)/shard_map/ppermute | solution.py:368
  36.4 2.5 %collective-permute-start.15 = (bf16[176,256]{1,0:T(8,128)(2,1)S(1)}, bf16[176,256]{1,0:T(8,128)(2,1)S(1)}, u32[]{:S(2)}, u32[]{:S(2)}) collective-permute-start(bf16[176,256]{1,0:T(8,128)(2,1)S(1)} %collective-permute-done.10.refs_2_.refs_7_), channel_id=1, source_target_pairs={{0,1},{1,0},{2,3},{3,2},{4,5},{5,4},{6,7},{7,6},{8,9},{9,8},{10,11... | collective-permute-start | bytes 270344 | tf_op jit(solution)/shard_map/ppermute | solution.py:368
  38.3 2.5 %collective-permute-start.16 = (bf16[80,1024]{1,0:T(8,128)(2,1)S(1)}, bf16[80,1024]{1,0:T(8,128)(2,1)S(1)}, u32[]{:S(2)}, u32[]{:S(2)}) collective-permute-start(bf16[80,1024]{1,0:T(8,128)(2,1)S(1)} %get-tuple-element.59), channel_id=1, source_target_pairs={{0,1},{1,0},{2,3},{3,2},{4,5},{5,4},{6,7},{7,6},{8,9},{9,8},{10,11... | collective-permute-start | bytes 491528 | tf_op jit(solution)/shard_map/ppermute | solution.py:368
  38.5 2.3 %collective-permute-start.17 = (bf16[80,1024]{1,0:T(8,128)(2,1)S(1)}, bf16[80,1024]{1,0:T(8,128)(2,1)S(1)}, u32[]{:S(2)}, u32[]{:S(2)}) collective-permute-start(bf16[80,1024]{1,0:T(8,128)(2,1)S(1)} %get-tuple-element.60), channel_id=1, source_target_pairs={{0,1},{1,0},{2,3},{3,2},{4,5},{5,4},{6,7},{7,6},{8,9},{9,8},{10,11... | collective-permute-start | bytes 491528 | tf_op jit(solution)/shard_map/ppermute | solution.py:368
  41.9 3.7 %collective-permute-start.23 = (bf16[80,1024]{1,0:T(8,128)(2,1)S(1)}, bf16[80,1024]{1,0:T(8,128)(2,1)S(1)}, u32[]{:S(2)}, u32[]{:S(2)}) collective-permute-start(bf16[80,1024]{1,0:T(8,128)(2,1)S(1)} %get-tuple-element.74), channel_id=1, source_target_pairs={{0,1},{1,0},{2,3},{3,2},{4,5},{5,4},{6,7},{7,6},{8,9},{9,8},{10,11... | collective-permute-start | bytes 491528 | tf_op jit(solution)/shard_map/ppermute | solution.py:368
  43.5 6.0 %collective-permute-start.19 = (bf16[40,1024]{1,0:T(8,128)(2,1)S(1)}, bf16[40,1024]{1,0:T(8,128)(2,1)S(1)}, u32[]{:S(2)}, u32[]{:S(2)}) collective-permute-start(bf16[40,1024]{1,0:T(8,128)(2,1)S(1)} %get-tuple-element.67), channel_id=1, source_target_pairs={{0,2},{2,0},{1,3},{3,1},{4,6},{6,4},{5,7},{7,5},{8,10},{10,8},{9,1... | collective-permute-start | bytes 245768 | tf_op jit(solution)/shard_map/ppermute | solution.py:368
  44.1 6.8 %collective-permute-start.21 = (bf16[40,1024]{1,0:T(8,128)(2,1)S(1)}, bf16[40,1024]{1,0:T(8,128)(2,1)S(1)}, u32[]{:S(2)}, u32[]{:S(2)}) collective-permute-start(bf16[40,1024]{1,0:T(8,128)(2,1)S(1)} %get-tuple-element.70.refs_8_), channel_id=1, source_target_pairs={{0,2},{2,0},{1,3},{3,1},{4,6},{6,4},{5,7},{7,5},{8,10},{10,8},{9,1... | collective-permute-start | bytes 245768 | tf_op jit(solution)/shard_map/ppermute | solution.py:368
  45.9 9.1 %collective-permute-start.24 = (bf16[40,1024]{1,0:T(8,128)(2,1)S(1)}, bf16[40,1024]{1,0:T(8,128)(2,1)S(1)}, u32[]{:S(2)}, u32[]{:S(2)}) collective-permute-start(bf16[40,1024]{1,0:T(8,128)(2,1)S(1)} %get-tuple-element.75), channel_id=1, source_target_pairs={{0,4},{4,0},{8,12},{12,8},{1,5},{5,1},{9,13},{13,9},{2,6},{6,2},{1... | collective-permute-start | bytes 245768 | tf_op jit(solution)/shard_map/ppermute | solution.py:365
  46.6 8.5 %collective-permute-start.25 = (bf16[40,1024]{1,0:T(8,128)(2,1)S(1)}, bf16[40,1024]{1,0:T(8,128)(2,1)S(1)}, u32[]{:S(2)}, u32[]{:S(2)}) collective-permute-start(bf16[40,1024]{1,0:T(8,128)(2,1)S(1)} %get-tuple-element.77), channel_id=1, source_target_pairs={{0,6},{2,4},{4,2},{6,0},{8,14},{10,12},{12,10},{14,8},{1,7},{3,5},... | collective-permute-start | bytes 245768 | tf_op jit(solution)/shard_map/ppermute | solution.py:372
  48.0 7.1 %collective-permute-start.26 = (bf16[40,1024]{1,0:T(8,128)(2,1)S(1)}, bf16[40,1024]{1,0:T(8,128)(2,1)S(1)}, u32[]{:S(2)}, u32[]{:S(2)}) collective-permute-start(bf16[40,1024]{1,0:T(8,128)(2,1)S(1)} %get-tuple-element.78), channel_id=1, source_target_pairs={{0,2},{2,0},{1,3},{3,1},{4,6},{6,4},{5,7},{7,5},{8,10},{10,8},{9,1... | collective-permute-start | bytes 245768 | tf_op jit(solution)/shard_map/ppermute | solution.py:368
  49.6 8.5 %collective-permute-start.20 = (bf16[40,1024]{1,0:T(8,128)(2,1)S(1)}, bf16[40,1024]{1,0:T(8,128)(2,1)S(1)}, u32[]{:S(2)}, u32[]{:S(2)}) collective-permute-start(bf16[40,1024]{1,0:T(8,128)(2,1)S(1)} %shard_map.126), channel_id=1, source_target_pairs={{0,8},{4,12},{8,0},{12,4},{1,9},{5,13},{9,1},{13,5},{2,10},{6,14},... | collective-permute-start | bytes 245768 | tf_op jit(solution)/shard_map/ppermute | solution.py:365
  51.0 7.1 %collective-permute-start.22 = (bf16[40,1024]{1,0:T(8,128)(2,1)S(1)}, bf16[40,1024]{1,0:T(8,128)(2,1)S(1)}, u32[]{:S(2)}, u32[]{:S(2)}) collective-permute-start(bf16[40,1024]{1,0:T(8,128)(2,1)S(1)} %shard_map.127), channel_id=1, source_target_pairs={{0,12},{4,8},{8,4},{12,0},{1,13},{5,9},{9,5},{13,1},{2,14},{6,10},... | collective-permute-start | bytes 245768 | tf_op jit(solution)/shard_map/ppermute | solution.py:365
  (4 other events, 17.9 us)

commit v5 on v4

--- a/solution.py
+++ b/solution.py
@@ -12,9 +12,11 @@
 EPSILON = 1e-05
 NEGATIVE = -1e30
 META = 16
+KINDS = 8
 LATER = 16 * 1024 * 1024
 MIB = 1024 * 1024
 ORDER = (2, 3, 1, 0)
+PAIRS = ((2, 3), (1, 0))
 VMEM_LIMIT = 12 * 1024 * 1024
 
 BF16 = jnp.bfloat16
@@ -68,11 +70,9 @@
     return pl.ds(pl.multiple_of(start * width, width), width)
 
 
-def thirds(array):
+def halves(array):
     high = array.astype(BF16).astype(F32)
-    middle = (array - high).astype(BF16).astype(F32)
-    low = (array - high - middle).astype(BF16).astype(F32)
-    return [high, middle, low]
+    return [high, (array - high).astype(BF16).astype(F32)]
 
 
 def pack_kernel(steps, q_hbm, m_hbm, h_hbm, tp_hbm, sp_hbm, r_hbm, rw_hbm, *refs):
@@ -108,14 +108,14 @@
     row = iota((META, rows), 0)
     lines = [tp_ref[...], sp_ref[...], r_ref[0:1, :], r_ref[1:2, :]]
     lines = [line.astype(F32) for line in lines]
-    lines += thirds(rw_ref[0:1, :]) + thirds(rw_ref[1:2, :])
+    lines += halves(rw_ref[0:1, :]) + halves(rw_ref[1:2, :])
     kinds = jnp.zeros((META, rows), F32)
     for k, line in enumerate(lines):
         kinds = jnp.where(row == k, line, kinds)
     kinds = kinds.astype(BF16)
     for step, out in zip(steps, outs):
         moved = (iota((rows, width), 1) == iota((rows, width), 0) + step * rows).astype(BF16)
-        out[4 * rows :, :] = dot(kinds, moved).astype(BF16)
+        out[4 * rows :, :] = dot(kinds, moved)[0:KINDS, :].astype(BF16)
     for k, out in enumerate(outs):
         large[k][0].wait()
         out[rows : 2 * rows, :] = m_ref[k, :, 0, :]
@@ -151,7 +151,7 @@
 
 
 def attend_kernel(experts, rows, cap, w1_ref, w2_ref, *refs):
-    arrived, compact = dict(zip(ORDER, refs[:experts])), refs[experts:]
+    arrived, compact, factor_ref = dict(zip(ORDER, refs[:experts])), refs[experts:-1], refs[-1]
     messages = [arrived[step] for step in range(experts)]
     width = messages[0].shape[1]
     count = experts * rows
@@ -190,29 +190,20 @@
     for step, out in zip(ORDER, compact):
         place = iota((experts * cap, count), 0) == spot[step : step + 1, :]
         place = place.astype(BF16)
-        out[0 : experts * cap, :] = dot(place, states).astype(BF16)
-        leads = first == (here ^ step)
-        values = [jnp.where(leads, meta[4 + k : 5 + k, :], meta[7 + k : 8 + k, :]) for k in range(3)]
-        values.append(leads.astype(F32))
-        lines = jnp.zeros((META, count), F32)
-        for k, value in enumerate(values):
-            lines = jnp.where(iota((META, count), 0) == k, value, lines)
-        out[experts * cap :, :] = jnp.zeros((META, width), BF16)
-        out[experts * cap :, 0 : experts * cap] = dot_nt(lines.astype(BF16), place).astype(BF16)
-
-
-def copy_kernel(block_ref, out_ref):
-    out_ref[...] = block_ref[...]
-
-
-def trim_kernel(block_ref, out_ref):
-    out_ref[...] = block_ref[0 : out_ref.shape[0], :]
+        out[...] = dot(place, states).astype(BF16)
+    leads = first == here
+    lines = jnp.where(iota((META, count), 0) == 3, leads.astype(F32), 0.0)
+    for k in range(2):
+        half = jnp.where(leads, meta[4 + k : 5 + k, :], meta[6 + k : 7 + k, :])
+        lines = jnp.where(iota((META, count), 0) == k, half, lines)
+    factor_ref[...] = jnp.zeros(factor_ref.shape, F32)
+    factor_ref[:, 0:META] = dot_nt(place, lines.astype(BF16))
 
 
 def pair_kernel(left_ref, right_ref, out_ref):
-    rows, width = slice(0, out_ref.shape[0]), left_ref.shape[1]
-    out_ref[:, 0:width] = left_ref[rows, :]
-    out_ref[:, width:] = right_ref[rows, :]
+    width = left_ref.shape[1]
+    out_ref[:, 0:width] = left_ref[...]
+    out_ref[:, width:] = right_ref[...]
 
 
 def first_kernel(tile, *refs):
@@ -260,56 +251,28 @@
             out_ref[:, at * tile : (at + 1) * tile] = part[k * rows : (k + 1) * rows, :].astype(BF16)
 
 
-def row_factors(lines_ref, count):
-    same = (iota((count, count), 0) == iota((count, count), 1)).astype(BF16)
-    columns = dot_nt(same, lines_ref[count:, 0:count])
-    return columns[:, 0:1] + columns[:, 1:2] + columns[:, 2:3], columns[:, 3:4]
-
-
-def plain_kernel(kept_ref, got_ref, *outs):
+def plain_kernel(start, kept_ref, got_ref, *outs):
     cap = outs[0].shape[0]
     for k, out_ref in enumerate(outs):
-        rows, half = slice((2 + k) * cap, (3 + k) * cap), slice(k * cap, (k + 1) * cap)
+        rows, half = slice(start + k * cap, start + (k + 1) * cap), slice(k * cap, (k + 1) * cap)
         total = kept_ref[rows, :].astype(F32) + got_ref[half, :].astype(F32)
         out_ref[...] = total.astype(BF16)
 
 
-def gather_states(blocks, states, rows):
+def base_kernel(start, kept_ref, got_ref, factor_ref, *refs):
+    blocks, bases, factors, states = refs[: len(PAIRS)], refs[-5:-3], refs[-3:-1], refs[-1]
     here = lax.axis_index("expert")
-    width = blocks[0].shape[1]
-    for step, block in zip(ORDER, blocks):
-        states[:, columns_at(here ^ step, width)] = block[rows, :].astype(F32)
-
-
-def base_kernel(experts, kept_ref, *refs):
-    got_ref, blocks, refs = refs[0], refs[1 : 1 + experts], refs[1 + experts :]
-    bases, factors, states = refs[:2], refs[2:4], refs[4]
-    count = kept_ref.shape[0]
-    cap = count // experts
-    weight, leads = row_factors(blocks[-1], count)
-    gather_states(blocks, states, slice(2 * cap, 4 * cap))
+    cap, width = bases[0].shape[0], blocks[0].shape[1] // 2
+    for steps, block in zip(PAIRS, blocks):
+        for k, step in enumerate(steps):
+            piece = block[start : start + 2 * cap, k * width : (k + 1) * width]
+            states[:, columns_at(here ^ step, width)] = piece.astype(F32)
     for k in range(2):
-        rows, half = slice((2 + k) * cap, (3 + k) * cap), slice(k * cap, (k + 1) * cap)
+        rows, half = slice(start + k * cap, start + (k + 1) * cap), slice(k * cap, (k + 1) * cap)
+        weight = factor_ref[rows, 0:1] + factor_ref[rows, 1:2]
         total = kept_ref[rows, :].astype(F32) + got_ref[half, :].astype(F32)
-        bases[k][...] = total * weight[rows, :] + leads[rows, :] * states[half, :]
-        factors[k][...] = jnp.broadcast_to(weight[rows, :], (cap, HEAD))
-
-
-def tail_kernel(experts, kept_ref, *refs):
-    got_ref, blocks, refs = refs[0], refs[1 : 1 + experts], refs[1 + experts :]
-    far_kept_ref, far_got_ref, lines_ref, _, near0, near1, far0, far1, states = refs
-    count = kept_ref.shape[0]
-    cap = count // experts
-    weight, leads = row_factors(blocks[-1], count)
-    far_weight, _ = row_factors(lines_ref, count)
-    gather_states(blocks, states, slice(0, 2 * cap))
-    for k, (near, far) in enumerate(((near0, far0), (near1, far1))):
-        rows = slice(k * cap, (k + 1) * cap)
-        total = kept_ref[rows, :].astype(F32) + got_ref[rows, :].astype(F32)
-        total = total * weight[rows, :] + leads[rows, :] * states[rows, :]
-        near[...] = total.astype(BF16)
-        total = far_kept_ref[rows, :].astype(F32) + far_got_ref[rows, :].astype(F32)
-        far[...] = (total * far_weight[rows, :]).astype(BF16)
+        bases[k][...] = total * weight + factor_ref[rows, 3:4] * states[half, :]
+        factors[k][...] = jnp.broadcast_to(weight, factors[k].shape)
 
 
 def join_kernel(came_ref, base_ref, factor_ref, out_ref):
@@ -318,9 +281,9 @@
 
 
 def mix_kernel(experts, cap, tile, steps, routes_ref, *refs):
-    returned, refs = refs[: len(steps)], refs[len(steps) :]
-    out_ref = refs[-1]
+    returned, (out_hbm, out_ref, sems) = refs[:-3], refs[-3:]
     rows = out_ref.shape[0]
+    copies = []
     expert = lax.axis_index("expert") ^ iota((META, rows), 0)
     named = (routes_ref[0:1, :] == expert) | (routes_ref[1:2, :] == expert)
     named = named & (iota((META, rows), 0) < experts)
@@ -333,10 +296,14 @@
     }
     for at in range(0, out_ref.shape[1], tile):
         cols = slice(at, at + tile)
-        share = refs[0][:, cols] if len(refs) > 1 else jnp.zeros((rows, tile), F32)
-        for step, block in zip(steps, returned):
-            share = share + dot(place[step], block[:, cols])
-        out_ref[:, cols] = share.astype(out_ref.dtype)
+        share = [dot(place[step], block[:, cols]) for step, block in zip(steps, returned)]
+        out_ref[:, cols] = sum(share).astype(BF16)
+        copies.append(
+            pltpu.make_async_copy(out_ref.at[:, cols], out_hbm.at[:, cols], sems.at[at // tile])
+        )
+        copies[-1].start()
+    for copy in copies:
+        copy.wait()
 
 
 def head_shards(
@@ -374,7 +341,7 @@
     def pack(steps, *after):
         return call(
             functools.partial(pack_kernel, steps),
-            [struct(4 * rows + META, width)] * len(steps),
+            [struct(4 * rows + KINDS, width)] * len(steps),
             [IN_HBM] * 7 + [IN_ANY] * len(after),
             scratch=[
                 pltpu.VMEM((len(steps), rows, 2, width), BF16),
@@ -425,23 +392,17 @@
         packed[0],
     )
 
-    compact = call(
+    *compact, factor = call(
         functools.partial(attend_kernel, experts, rows, cap),
-        [struct(experts * cap + META, width)] * experts,
+        [struct(experts * cap, width)] * experts + [struct(experts * cap, HEAD, F32)],
         [IN_VMEM] * (2 + experts),
         flops=8 * experts * experts * rows * rows * width,
         moved=16 * rows * columns,
     )(in_vmem(w_in), in_vmem(w_out), *messages)
 
-    def ahead(block, mib):
-        return call(copy_kernel, [struct(*block.shape)], [IN_VMEM], moved=mib * MIB)(block)[0]
-
     compact = dict(zip(ORDER, compact))
     own = {step: along(compact[step], step) for step in ORDER}
     count = experts * cap
-
-    def trim(block):
-        return call(trim_kernel, [struct(count, width)], [IN_VMEM])(block)[0]
 
     def first(blocks, known):
         return call(
@@ -456,25 +417,23 @@
     def pair(left, right):
         return call(pair_kernel, [struct(count, 2 * width)], [IN_VMEM] * 2)(left, right)[0]
 
-    trimmed = [trim(own[step]) for step in ORDER]
+    near = [pair(own[left], own[right]) for left, right in PAIRS]
     far1, far0 = across(compact[1]), swap(compact[0], "dp")
-    near = pair(own[2], own[3])
-    far = swap(near, "dp")
-    trimmed[2], far1, far0 = lax.optimization_barrier((trimmed[2], far1, far0))
-    near_other = [swap(block, "mp") for block in trimmed]
-    far1_other, far0_other = swap(far1, "mp"), swap(far0, "mp")
-    active = first([near, own[1], own[0], *near_other], 0)
-    far, active = lax.optimization_barrier((far, active))
-    far_other = swap(far, "mp")
+    held, far1, far0 = lax.optimization_barrier((own[1], far1, far0))
+    far = [swap(near[0], "dp"), pair(far1, far0)]
+    near_other = [swap(block, "mp") for block in (near[0], held, own[0])]
+    far_other = [swap(far[1], "mp")]
+
+    active = first([near[0], own[1], own[0]] + near_other, 0)
     kept, *sent = call(
         functools.partial(second_kernel, 512),
         [struct(count, columns)] + [struct(count // 2, columns)] * 2,
         [IN_VMEM, IN_VMEM],
     )(active, in_vmem(w_out))
+    far[0], kept = lax.optimization_barrier((far[0], kept))
+    far_other = [swap(far[0], "mp")] + far_other
     got = [swap(part, "mp") for part in sent]
-    far_other, kept = lax.optimization_barrier((far_other, kept))
-
-    active = first([far, far1, far0, far_other, far1_other, far0_other], 1)
+    active = first(far + far_other, 1)
     active, *got = lax.optimization_barrier((active, *got))
 
     def half(active, other, parts):
@@ -488,41 +447,46 @@
 
     theirs = [swap(part, "mp") for part in half(active, True, 2)]
     mine = half(active, False, 1)[0]
-    arrived = [own[step] for step in ORDER]
-    base2, base3, factor2, factor3 = call(
-        functools.partial(base_kernel, experts),
-        [struct(cap, columns, F32)] * 2 + [struct(cap, HEAD, F32)] * 2,
-        [IN_VMEM] * (2 + experts),
-        scratch=[pltpu.VMEM((2 * cap, columns), F32)],
-    )(kept, got[1], *arrived)
+
+    def base(start, part):
+        return call(
+            functools.partial(base_kernel, start),
+            [struct(cap, columns, F32)] * 2 + [struct(cap, HEAD, F32)] * 2,
+            [IN_VMEM] * (3 + len(PAIRS)),
+            scratch=[pltpu.VMEM((2 * cap, columns), F32)],
+        )(kept, part, factor, *near)
+
+    def plain(start, part):
+        return call(
+            functools.partial(plain_kernel, start), [struct(cap, columns)] * 2, [IN_VMEM] * 2
+        )(mine, part)
+
+    def join(came, base, factor):
+        return call(join_kernel, [struct(cap, columns)], [IN_VMEM] * 3)(came, base, factor)[0]
+
+    base2, base3, factor2, factor3 = base(2 * cap, got[1])
     theirs[1], base2 = lax.optimization_barrier((theirs[1], base2))
-    plain2, plain3 = call(plain_kernel, [struct(cap, columns)] * 2, [IN_VMEM] * 2)(mine, theirs[1])
-
-    def join(came, base, factor, mib):
-        return call(join_kernel, [struct(cap, columns)], [IN_VMEM] * 3, moved=mib * MIB)(
-            came, base, factor
-        )[0]
-
-    joined2 = join(swap(plain2, "dp"), base2, factor2, 4)
-    joined3 = join(swap(plain3, "dp"), base3, factor3, 0)
-    near0, near1, away0, away1 = call(
-        functools.partial(tail_kernel, experts),
-        [struct(cap, columns)] * 4,
-        [IN_VMEM] * (5 + experts) + [IN_ANY],
-        scratch=[pltpu.VMEM((2 * cap, columns), F32)],
-        moved=2 * LATER,
-    )(kept, got[0], *arrived, mine, theirs[0], far0, plain3)
-
-    def mix(steps, blocks, dtype, *before):
-        return call(
-            functools.partial(mix_kernel, experts, cap, 512, steps),
-            [struct(rows, columns, dtype)],
-            [IN_VMEM] * (1 + len(blocks) + len(before)),
-        )(routes.T, *blocks, *before)[0]
-
-    direct = [along(near1, 1), near0, across(away1), swap(away0, "dp")]
-    share = mix((1, 0, 1, 0), direct, F32)
-    return mix((2, 3), [along(joined2, 2), along(joined3, 3)], BF16, share)
+    base0, base1, factor0, factor1 = base(0, got[0])
+    plain2, plain3 = plain(2 * cap, theirs[1])
+    plain0, plain1 = plain(0, theirs[0])
+    returned = [
+        along(join(swap(plain2, "dp"), base2, factor2), 2),
+        along(join(swap(plain3, "dp"), base3, factor3), 3),
+        along(join(swap(plain1, "dp"), base1, factor1), 1),
+        join(swap(plain0, "dp"), base0, factor0),
+    ]
+    return pl.pallas_call(
+        functools.partial(mix_kernel, experts, cap, 256, ORDER),
+        out_shape=struct(rows, columns),
+        in_specs=[IN_VMEM] * (1 + experts),
+        out_specs=IN_HBM,
+        scratch_shapes=[
+            pltpu.VMEM((rows, columns), BF16),
+            pltpu.SemaphoreType.DMA((columns // 256,)),
+        ],
+        compiler_params=pltpu.CompilerParams(vmem_limit_bytes=VMEM_LIMIT),
+        cost_estimate=pl.CostEstimate(flops=1, bytes_accessed=1, transcendentals=0),
+    )(routes.T, *returned)
 
 
 def shards(

time: 59.6 us -> 57.6 us (0.966)
  starting transfers between devices: 29.7 us -> 25.2 us
  waiting for transfers between devices: 8.99 us -> 12.2 us
  Pallas kernels: 20.4 us -> 19.7 us
    ppermute x2 -> x1, starting transfers between devices: 4.18 us -> 1.13 us  [across(): return lax.ppermute(array, ('expert', 'dp'), pairs)]
    ppermute x9, waiting for transfers between devices: 6.55 us -> 9.09 us  [along(): lax.ppermute(array, 'expert', [(i, i ^ step) for i in range(experts)])]
    ppermute x16 -> x15, waiting for transfers between devices: 0.95 us -> 2.97 us  [swap(): return lax.ppermute(array, axis, [(0, 1), (1, 0)])]
    ppermute x2 -> x1, waiting for transfers between devices: 1.48 us -> 0.18 us  [across(): return lax.ppermute(array, ('expert', 'dp'), pairs)]
    ppermute x9, starting transfers between devices: 16.7 us -> 15.6 us  [along(): lax.ppermute(array, 'expert', [(i, i ^ step) for i in range(experts)])]
    pallas_call x14 -> x12, Pallas kernels: 6.21 us -> 5.6 us  [the longest x3 3.58 us: pack(): call(functools.partial(pack_kernel, steps), [struct(4 * rows + KINDS, wid...]
    ppermute x16 -> x15, starting transfers between devices: 8.81 us -> 8.47 us  [swap(): return lax.ppermute(array, axis, [(0, 1), (1, 0)])]
  transfers between devices with their start and end apart: 27 -> 25, of which waited for: 7 -> 13; matrix products, arithmetic and copies ran while one was open for 0% -> 0% of each run, Pallas kernels for 27% -> 27%
where the time goes in v5:
time: 57.6 us; the launch traced here: 57.4 us
  starting transfers between devices  25.2 us (44%)
  Pallas kernels  19.7 us (34%)
  waiting for transfers between devices  12.2 us (21%)
    ppermute x9, starting transfers between devices, along(): lax.ppermute(array, 'expert', [(i, i ^ step) for i in range(experts)])  15.6 us
    ppermute x9, waiting for transfers between devices, along(): lax.ppermute(array, 'expert', [(i, i ^ step) for i in range(experts)])  9.09 us
    ppermute x15, starting transfers between devices, swap(): return lax.ppermute(array, axis, [(0, 1), (1, 0)])  8.47 us
    pallas_call x1, Pallas kernels, head_shards(): pl.pallas_call(functools.partial(prefetch_kernel, experts), out_shape=[pl...  6.21 us
    pallas_call x2, Pallas kernels, first(): call(functools.partial(first_kernel, 512), [struct(count, hidden_units)],...  3.76 us
    pallas_call x3, Pallas kernels, pack(): call(functools.partial(pack_kernel, steps), [struct(4 * rows + KINDS, wid...  3.58 us
    ppermute x15, waiting for transfers between devices, swap(): return lax.ppermute(array, axis, [(0, 1), (1, 0)])  2.97 us
    pallas_call x2, Pallas kernels, half(): call(functools.partial(half_kernel, 512, other), [struct(count // parts,...  1.74 us
  transfers between devices with their start and end apart: 25, of which 13 were waited for; matrix products, arithmetic and copies ran while one was open for 0% of the time, Pallas kernels for 27%

profile of v5, /device:TPU:0, one launch (start us, length us, event | category | flops | bytes accessed | tf_op | source)
XLA Modules:
  0.0 57.4 jit_solution(17695356150956769034)
XLA Ops:
  0.0 1.1 %shard_map.109.refs_0_ = bf16[264,256]{1,0:T(8,128)(2,1)S(1)} custom-call(bf16[64,1024]{1,0:T(8,128)(2,1)} %q_hbm.5, bf16[64,2,1024]{2,1,0:T(2,128)(2,1)} %m_hbm.5, bf16[64,1024]{1,0:T(8,128)(2,1)} %h_hbm.5, s32[1,64]{1,0:T(1,128)} %bitcast.19, s32[1,64]{1,0:T(1,128)} %bitcast.22, s32[2,64]{1,0:T(2,128)} %bitcast.8, f32[2,64]{1,0:T(2,128)} %bitcast.14), custom_call_target="tpu_custom_call" | custom-call | tf_op jit(solution)/shard_map/pallas_call | solution.py:342
  1.1 4.1 %collective-permute-start = (bf16[264,256]{1,0:T(8,128)(2,1)S(1)}, bf16[264,256]{1,0:T(8,128)(2,1)S(1)}, u32[]{:S(2)}, u32[]{:S(2)}) collective-permute-start(bf16[264,256]{1,0:T(8,128)(2,1)S(1)} %shard_map.109.refs_0_), channel_id=1, source_target_pairs={{0,8},{4,12},{8,0},{12,4},{1,9},{5,13},{9,1},{13,5},{2,10},{6,14},... | collective-permute-start | bytes 405512 | tf_op jit(solution)/shard_map/ppermute | solution.py:332
  5.2 1.1 %shard_map.110.refs_0_ = bf16[264,256]{1,0:T(8,128)(2,1)S(1)} custom-call(bf16[64,1024]{1,0:T(8,128)(2,1)} %q_hbm.5, bf16[64,2,1024]{2,1,0:T(2,128)(2,1)} %m_hbm.5, bf16[64,1024]{1,0:T(8,128)(2,1)} %h_hbm.5, s32[1,64]{1,0:T(1,128)} %bitcast.20, s32[1,64]{1,0:T(1,128)} %bitcast.23, s32[2,64]{1,0:T(2,128)} %bitcast.9, f32[2,64]{1,0:T(2,128)} %bitcast.15, ...), custom_call_target="tpu_custom_call" | custom-call | bytes 16777216 | tf_op jit(solution)/shard_map/pallas_call | solution.py:342
  6.3 1.6 %collective-permute-start.2 = (bf16[264,256]{1,0:T(8,128)(2,1)S(1)}, bf16[264,256]{1,0:T(8,128)(2,1)S(1)}, u32[]{:S(2)}, u32[]{:S(2)}) collective-permute-start(bf16[264,256]{1,0:T(8,128)(2,1)S(1)} %shard_map.110.refs_0_), channel_id=1, source_target_pairs={{0,4},{4,0},{8,12},{12,8},{1,5},{5,1},{9,13},{13,9},{2,6},{6,2},{1... | collective-permute-start | bytes 405512 | tf_op jit(solution)/shard_map/ppermute | solution.py:332
  8.0 1.4 %shard_map.111 = (bf16[264,256]{1,0:T(8,128)(2,1)S(1)}, bf16[264,256]{1,0:T(8,128)(2,1)S(1)}) custom-call(bf16[64,1024]{1,0:T(8,128)(2,1)} %q_hbm.5, bf16[64,2,1024]{2,1,0:T(2,128)(2,1)} %m_hbm.5, bf16[64,1024]{1,0:T(8,128)(2,1)} %h_hbm.5, s32[1,64]{1,0:T(1,128)} %bitcast.21, s32[1,64]{1,0:T(1,128)} %bitcast.24, s32[2,64]{1,0:T(2,128)} %bitcast.10, ...), custom_call_target="tpu_custom_call" | custom-call | bytes 16777216 | tf_op jit(solution)/shard_map/pallas_call | solution.py:342
  9.4 6.2 %shard_map.112 = (bf16[2048,2048]{1,0:T(8,128)(2,1)S(1)}, bf16[2048,2048]{1,0:T(8,128)(2,1)S(1)}, f32[1,2048]{1,0:T(1,128)S(1)}, f32[1,2048]{1,0:T(1,128)S(1)}) custom-call(bf16[2048,2048]{1,0:T(8,128)(2,1)} %bitcast.12, bf16[2048,2048]{1,0:T(8,128)(2,1)} %bitcast.13, f32[1,2048]{1,0:T(1,128)} %bitcast.17, f32[1,2048]{1,0:T(1,128)} %bitcast.18, ...), custom_call_target="tpu_custom_call" | custom-call | bytes 33554432 | tf_op jit(solution)/shard_map/pallas_call | solution.py:372
  17.1 4.0 %collective-permute-start.3 = (bf16[160,256]{1,0:T(8,128)(2,1)S(1)}, bf16[160,256]{1,0:T(8,128)(2,1)S(1)}, u32[]{:S(2)}, u32[]{:S(2)}) collective-permute-start(bf16[160,256]{1,0:T(8,128)(2,1)S(1)} %get-tuple-element.47), channel_id=1, source_target_pairs={{0,8},{4,12},{8,0},{12,4},{1,9},{5,13},{9,1},{13,5},{2,10},{6,14},... | collective-permute-start | bytes 245768 | tf_op jit(solution)/shard_map/ppermute | solution.py:332
  21.6 1.1 %collective-permute-start.8 = (bf16[160,256]{1,0:T(8,128)(2,1)S(1)}, bf16[160,256]{1,0:T(8,128)(2,1)S(1)}, u32[]{:S(2)}, u32[]{:S(2)}) collective-permute-start(bf16[160,256]{1,0:T(8,128)(2,1)S(1)} %get-tuple-element.49), channel_id=1, source_target_pairs={{0,6},{2,4},{4,2},{6,0},{8,14},{10,12},{12,10},{14,8},{1,7},{3,5},... | collective-permute-start | bytes 245768 | tf_op jit(solution)/shard_map/ppermute | solution.py:339
  22.7 1.8 %collective-permute-start.6 = (bf16[160,256]{1,0:T(8,128)(2,1)S(1)}, bf16[160,256]{1,0:T(8,128)(2,1)S(1)}, u32[]{:S(2)}, u32[]{:S(2)}) collective-permute-start(bf16[160,256]{1,0:T(8,128)(2,1)S(1)} %get-tuple-element.49), channel_id=1, source_target_pairs={{0,4},{4,0},{8,12},{12,8},{1,5},{5,1},{9,13},{13,9},{2,6},{6,2},{1... | collective-permute-start | bytes 245768 | tf_op jit(solution)/shard_map/ppermute | solution.py:332
  25.0 1.7 %collective-permute-done.3.left_ref = bf16[160,256]{1,0:T(8,128)(2,1)S(1)} collective-permute-done((bf16[160,256]{1,0:T(8,128)(2,1)S(1)}, bf16[160,256]{1,0:T(8,128)(2,1)S(1)}, u32[]{:S(2)}, u32[]{:S(2)}) %collective-permute-start.3) | collective-permute-done | bytes 81952 | tf_op jit(solution)/shard_map/ppermute | solution.py:332
  26.7 1.3 %collective-permute-done.4.right_ref = bf16[160,256]{1,0:T(8,128)(2,1)S(1)} collective-permute-done((bf16[160,256]{1,0:T(8,128)(2,1)S(1)}, bf16[160,256]{1,0:T(8,128)(2,1)S(1)}, u32[]{:S(2)}, u32[]{:S(2)}) %collective-permute-start.4) | collective-permute-done | bytes 81952 | tf_op jit(solution)/shard_map/ppermute | solution.py:332
  28.2 1.7 %collective-permute-start.5 = (bf16[160,512]{1,0:T(8,128)(2,1)S(1)}, bf16[160,512]{1,0:T(8,128)(2,1)S(1)}, u32[]{:S(2)}, u32[]{:S(2)}) collective-permute-start(bf16[160,512]{1,0:T(8,128)(2,1)S(1)} %shard_map.114.refs_0_), channel_id=1, source_target_pairs={{0,2},{2,0},{1,3},{3,1},{4,6},{6,4},{5,7},{7,5},{8,10},{10,8},{9,1... | collective-permute-start | bytes 491528 | tf_op jit(solution)/shard_map/ppermute | solution.py:335
  32.0 1.9 %shard_map.115.a_ref = bf16[160,2048]{1,0:T(8,128)(2,1)S(1)} custom-call(bf16[160,512]{1,0:T(8,128)(2,1)S(1)} %shard_map.114.refs_0_, bf16[160,256]{1,0:T(8,128)(2,1)S(1)} %collective-permute-done.6.refs_1_.left_ref, bf16[160,256]{1,0:T(8,128)(2,1)S(1)} %get-tuple-element.50.refs_2_.right_ref, bf16[160,512]{1,0:T(8,128)(2,1)S(1)} %collective-permute-done.7.refs_3_, ...), custom_call_target="tpu_custom_call" | custom-call | tf_op jit(solution)/shard_map/pallas_call | solution.py:408
  33.9 1.5 %shard_map.116 = (bf16[160,1024]{1,0:T(8,128)(2,1)S(1)}, bf16[80,1024]{1,0:T(8,128)(2,1)S(1)}, bf16[80,1024]{1,0:T(8,128)(2,1)S(1)}) custom-call(bf16[160,2048]{1,0:T(8,128)(2,1)S(1)} %shard_map.115.a_ref, bf16[2048,2048]{1,0:T(8,128)(2,1)S(1)} %get-tuple-element.45.w2_ref.w_ref), custom_call_target="tpu_custom_call" | custom-call | tf_op jit(solution)/shard_map/pallas_call | solution.py:428
  37.0 1.9 %shard_map.118.a_ref = bf16[160,2048]{1,0:T(8,128)(2,1)S(1)} custom-call(bf16[160,512]{1,0:T(8,128)(2,1)S(1)} %collective-permute-done.5.refs_0_, bf16[160,512]{1,0:T(8,128)(2,1)S(1)} %shard_map.117.refs_1_, bf16[160,512]{1,0:T(8,128)(2,1)S(1)} %collective-permute-done.12.refs_2_, bf16[160,512]{1,0:T(8,128)(2,1)S(1)} %collective-permute-done.13.refs_3_, ...), custom_call_target="tpu_custom_call" | custom-call | flops 1342177280 | bytes 8388608 | tf_op jit(solution)/shard_map/pallas_call | solution.py:408
  41.5 1.1 %collective-permute-start.17 = (bf16[40,1024]{1,0:T(8,128)(2,1)S(1)}, bf16[40,1024]{1,0:T(8,128)(2,1)S(1)}, u32[]{:S(2)}, u32[]{:S(2)}) collective-permute-start(bf16[40,1024]{1,0:T(8,128)(2,1)S(1)} %get-tuple-element.67), channel_id=1, source_target_pairs={{0,2},{2,0},{1,3},{3,1},{4,6},{6,4},{5,7},{7,5},{8,10},{10,8},{9,1... | collective-permute-start | bytes 245768 | tf_op jit(solution)/shard_map/ppermute | solution.py:335
  42.6 1.0 %collective-permute-start.19 = (bf16[40,1024]{1,0:T(8,128)(2,1)S(1)}, bf16[40,1024]{1,0:T(8,128)(2,1)S(1)}, u32[]{:S(2)}, u32[]{:S(2)}) collective-permute-start(bf16[40,1024]{1,0:T(8,128)(2,1)S(1)} %get-tuple-element.70), channel_id=1, source_target_pairs={{0,2},{2,0},{1,3},{3,1},{4,6},{6,4},{5,7},{7,5},{8,10},{10,8},{9,1... | collective-permute-start | bytes 245768 | tf_op jit(solution)/shard_map/ppermute | solution.py:335
  43.6 1.1 %collective-permute-start.22 = (bf16[40,1024]{1,0:T(8,128)(2,1)S(1)}, bf16[40,1024]{1,0:T(8,128)(2,1)S(1)}, u32[]{:S(2)}, u32[]{:S(2)}) collective-permute-start(bf16[40,1024]{1,0:T(8,128)(2,1)S(1)} %get-tuple-element.74), channel_id=1, source_target_pairs={{0,2},{2,0},{1,3},{3,1},{4,6},{6,4},{5,7},{7,5},{8,10},{10,8},{9,1... | collective-permute-start | bytes 245768 | tf_op jit(solution)/shard_map/ppermute | solution.py:335
  44.9 1.0 %collective-permute-start.24 = (bf16[40,1024]{1,0:T(8,128)(2,1)S(1)}, bf16[40,1024]{1,0:T(8,128)(2,1)S(1)}, u32[]{:S(2)}, u32[]{:S(2)}) collective-permute-start(bf16[40,1024]{1,0:T(8,128)(2,1)S(1)} %get-tuple-element.78), channel_id=1, source_target_pairs={{0,2},{2,0},{1,3},{3,1},{4,6},{6,4},{5,7},{7,5},{8,10},{10,8},{9,1... | collective-permute-start | bytes 245768 | tf_op jit(solution)/shard_map/ppermute | solution.py:335
  45.9 0.9 %collective-permute-done.17.came_ref = bf16[40,1024]{1,0:T(8,128)(2,1)S(1)} collective-permute-done((bf16[40,1024]{1,0:T(8,128)(2,1)S(1)}, bf16[40,1024]{1,0:T(8,128)(2,1)S(1)}, u32[]{:S(2)}, u32[]{:S(2)}) %collective-permute-start.17) | collective-permute-done | bytes 81952 | tf_op jit(solution)/shard_map/ppermute | solution.py:335
  46.9 1.1 %collective-permute-start.18 = (bf16[40,1024]{1,0:T(8,128)(2,1)S(1)}, bf16[40,1024]{1,0:T(8,128)(2,1)S(1)}, u32[]{:S(2)}, u32[]{:S(2)}) collective-permute-start(bf16[40,1024]{1,0:T(8,128)(2,1)S(1)} %shard_map.124), channel_id=1, source_target_pairs={{0,8},{4,12},{8,0},{12,4},{1,9},{5,13},{9,1},{13,5},{2,10},{6,14},... | collective-permute-start | bytes 245768 | tf_op jit(solution)/shard_map/ppermute | solution.py:332
  48.7 2.2 %collective-permute-start.20 = (bf16[40,1024]{1,0:T(8,128)(2,1)S(1)}, bf16[40,1024]{1,0:T(8,128)(2,1)S(1)}, u32[]{:S(2)}, u32[]{:S(2)}) collective-permute-start(bf16[40,1024]{1,0:T(8,128)(2,1)S(1)} %shard_map.125), channel_id=1, source_target_pairs={{0,12},{4,8},{8,4},{12,0},{1,13},{5,9},{9,5},{13,1},{2,14},{6,10},... | collective-permute-start | bytes 245768 | tf_op jit(solution)/shard_map/ppermute | solution.py:332
  51.4 3.0 %collective-permute-done.18.refs_0_ = bf16[40,1024]{1,0:T(8,128)(2,1)S(1)} collective-permute-done((bf16[40,1024]{1,0:T(8,128)(2,1)S(1)}, bf16[40,1024]{1,0:T(8,128)(2,1)S(1)}, u32[]{:S(2)}, u32[]{:S(2)}) %collective-permute-start.18) | collective-permute-done | bytes 81952 | tf_op jit(solution)/shard_map/ppermute | solution.py:332
  56.1 1.2 %shard_map.130 = bf16[64,1024]{1,0:T(8,128)(2,1)} custom-call(s32[2,64]{1,0:T(2,128)S(1)} %bitcast.11, bf16[40,1024]{1,0:T(8,128)(2,1)S(1)} %collective-permute-done.18.refs_0_, bf16[40,1024]{1,0:T(8,128)(2,1)S(1)} %collective-permute-done.20.refs_1_, bf16[40,1024]{1,0:T(8,128)(2,1)S(1)} %collective-permute-done.23.refs_2_, ...), custom_call_target="tpu_custom_call" | custom-call | flops 1 | bytes 1 | tf_op jit(solution)/shard_map/pallas_call | solution.py:478
  (50 shorter events, 11.9 us)
Async XLA Ops:
  1.1 14.5 %collective-permute-start = (bf16[264,256]{1,0:T(8,128)(2,1)S(1)}, bf16[264,256]{1,0:T(8,128)(2,1)S(1)}, u32[]{:S(2)}, u32[]{:S(2)}) collective-permute-start(bf16[264,256]{1,0:T(8,128)(2,1)S(1)} %shard_map.109.refs_0_), channel_id=1, source_target_pairs={{0,8},{4,12},{8,0},{12,4},{1,9},{5,13},{9,1},{13,5},{2,10},{6,14},... | collective-permute-start | bytes 405512 | tf_op jit(solution)/shard_map/ppermute | solution.py:332
  6.3 9.3 %collective-permute-start.2 = (bf16[264,256]{1,0:T(8,128)(2,1)S(1)}, bf16[264,256]{1,0:T(8,128)(2,1)S(1)}, u32[]{:S(2)}, u32[]{:S(2)}) collective-permute-start(bf16[264,256]{1,0:T(8,128)(2,1)S(1)} %shard_map.110.refs_0_), channel_id=1, source_target_pairs={{0,4},{4,0},{8,12},{12,8},{1,5},{5,1},{9,13},{13,9},{2,6},{6,2},{1... | collective-permute-start | bytes 405512 | tf_op jit(solution)/shard_map/ppermute | solution.py:332
  9.3 6.9 %collective-permute-start.1 = (bf16[264,256]{1,0:T(8,128)(2,1)S(1)}, bf16[264,256]{1,0:T(8,128)(2,1)S(1)}, u32[]{:S(2)}, u32[]{:S(2)}) collective-permute-start(bf16[264,256]{1,0:T(8,128)(2,1)S(1)} %get-tuple-element.46), channel_id=1, source_target_pairs={{0,12},{4,8},{8,4},{12,0},{1,13},{5,9},{9,5},{13,1},{2,14},{6,10},... | collective-permute-start | bytes 405512 | tf_op jit(solution)/shard_map/ppermute | solution.py:332
  17.1 9.6 %collective-permute-start.3 = (bf16[160,256]{1,0:T(8,128)(2,1)S(1)}, bf16[160,256]{1,0:T(8,128)(2,1)S(1)}, u32[]{:S(2)}, u32[]{:S(2)}) collective-permute-start(bf16[160,256]{1,0:T(8,128)(2,1)S(1)} %get-tuple-element.47), channel_id=1, source_target_pairs={{0,8},{4,12},{8,0},{12,4},{1,9},{5,13},{9,1},{13,5},{2,10},{6,14},... | collective-permute-start | bytes 245768 | tf_op jit(solution)/shard_map/ppermute | solution.py:332
  21.1 7.0 %collective-permute-start.4 = (bf16[160,256]{1,0:T(8,128)(2,1)S(1)}, bf16[160,256]{1,0:T(8,128)(2,1)S(1)}, u32[]{:S(2)}, u32[]{:S(2)}) collective-permute-start(bf16[160,256]{1,0:T(8,128)(2,1)S(1)} %get-tuple-element.48), channel_id=1, source_target_pairs={{0,12},{4,8},{8,4},{12,0},{1,13},{5,9},{9,5},{13,1},{2,14},{6,10},... | collective-permute-start | bytes 245768 | tf_op jit(solution)/shard_map/ppermute | solution.py:332
  21.6 8.5 %collective-permute-start.8 = (bf16[160,256]{1,0:T(8,128)(2,1)S(1)}, bf16[160,256]{1,0:T(8,128)(2,1)S(1)}, u32[]{:S(2)}, u32[]{:S(2)}) collective-permute-start(bf16[160,256]{1,0:T(8,128)(2,1)S(1)} %get-tuple-element.49), channel_id=1, source_target_pairs={{0,6},{2,4},{4,2},{6,0},{8,14},{10,12},{12,10},{14,8},{1,7},{3,5},... | collective-permute-start | bytes 245768 | tf_op jit(solution)/shard_map/ppermute | solution.py:339
  22.7 8.1 %collective-permute-start.6 = (bf16[160,256]{1,0:T(8,128)(2,1)S(1)}, bf16[160,256]{1,0:T(8,128)(2,1)S(1)}, u32[]{:S(2)}, u32[]{:S(2)}) collective-permute-start(bf16[160,256]{1,0:T(8,128)(2,1)S(1)} %get-tuple-element.49), channel_id=1, source_target_pairs={{0,4},{4,0},{8,12},{12,8},{1,5},{5,1},{9,13},{13,9},{2,6},{6,2},{1... | collective-permute-start | bytes 245768 | tf_op jit(solution)/shard_map/ppermute | solution.py:332
  24.5 6.3 %collective-permute-start.9 = (bf16[160,256]{1,0:T(8,128)(2,1)S(1)}, bf16[160,256]{1,0:T(8,128)(2,1)S(1)}, u32[]{:S(2)}, u32[]{:S(2)}) collective-permute-start(bf16[160,256]{1,0:T(8,128)(2,1)S(1)} %get-tuple-element.50.refs_2_.right_ref), channel_id=1, source_target_pairs={{0,2},{2,0},{1,3},{3,1},{4,6},{6,4},{5,7},{7,5},{8,10},{10,8},{9,1... | collective-permute-start | bytes 245768 | tf_op jit(solution)/shard_map/ppermute | solution.py:335
  28.1 3.9 %collective-permute-start.7 = (bf16[160,512]{1,0:T(8,128)(2,1)S(1)}, bf16[160,512]{1,0:T(8,128)(2,1)S(1)}, u32[]{:S(2)}, u32[]{:S(2)}) collective-permute-start(bf16[160,512]{1,0:T(8,128)(2,1)S(1)} %shard_map.114.refs_0_), channel_id=1, source_target_pairs={{0,1},{1,0},{2,3},{3,2},{4,5},{5,4},{6,7},{7,6},{8,9},{9,8},{10,11... | collective-permute-start | bytes 491528 | tf_op jit(solution)/shard_map/ppermute | solution.py:335
  28.2 7.3 %collective-permute-start.5 = (bf16[160,512]{1,0:T(8,128)(2,1)S(1)}, bf16[160,512]{1,0:T(8,128)(2,1)S(1)}, u32[]{:S(2)}, u32[]{:S(2)}) collective-permute-start(bf16[160,512]{1,0:T(8,128)(2,1)S(1)} %shard_map.114.refs_0_), channel_id=1, source_target_pairs={{0,2},{2,0},{1,3},{3,1},{4,6},{6,4},{5,7},{7,5},{8,10},{10,8},{9,1... | collective-permute-start | bytes 491528 | tf_op jit(solution)/shard_map/ppermute | solution.py:335
  30.8 1.3 %collective-permute-start.10 = (bf16[160,256]{1,0:T(8,128)(2,1)S(1)}, bf16[160,256]{1,0:T(8,128)(2,1)S(1)}, u32[]{:S(2)}, u32[]{:S(2)}) collective-permute-start(bf16[160,256]{1,0:T(8,128)(2,1)S(1)} %collective-permute-done.6.refs_1_.left_ref), channel_id=1, source_target_pairs={{0,1},{1,0},{2,3},{3,2},{4,5},{5,4},{6,7},{7,6},{8,9},{9,8},{10,11... | collective-permute-start | bytes 245768 | tf_op jit(solution)/shard_map/ppermute | solution.py:335
  30.8 5.4 %collective-permute-start.13 = (bf16[160,512]{1,0:T(8,128)(2,1)S(1)}, bf16[160,512]{1,0:T(8,128)(2,1)S(1)}, u32[]{:S(2)}, u32[]{:S(2)}) collective-permute-start(bf16[160,512]{1,0:T(8,128)(2,1)S(1)} %shard_map.117.refs_1_), channel_id=1, source_target_pairs={{0,1},{1,0},{2,3},{3,2},{4,5},{5,4},{6,7},{7,6},{8,9},{9,8},{10,11... | collective-permute-start | bytes 491528 | tf_op jit(solution)/shard_map/ppermute | solution.py:335
  35.5 1.5 %collective-permute-start.12 = (bf16[160,512]{1,0:T(8,128)(2,1)S(1)}, bf16[160,512]{1,0:T(8,128)(2,1)S(1)}, u32[]{:S(2)}, u32[]{:S(2)}) collective-permute-start(bf16[160,512]{1,0:T(8,128)(2,1)S(1)} %collective-permute-done.5.refs_0_), channel_id=1, source_target_pairs={{0,1},{1,0},{2,3},{3,2},{4,5},{5,4},{6,7},{7,6},{8,9},{9,8},{10,11... | collective-permute-start | bytes 491528 | tf_op jit(solution)/shard_map/ppermute | solution.py:335
  35.7 3.1 %collective-permute-start.14 = (bf16[80,1024]{1,0:T(8,128)(2,1)S(1)}, bf16[80,1024]{1,0:T(8,128)(2,1)S(1)}, u32[]{:S(2)}, u32[]{:S(2)}) collective-permute-start(bf16[80,1024]{1,0:T(8,128)(2,1)S(1)} %get-tuple-element.58), channel_id=1, source_target_pairs={{0,1},{1,0},{2,3},{3,2},{4,5},{5,4},{6,7},{7,6},{8,9},{9,8},{10,11... | collective-permute-start | bytes 491528 | tf_op jit(solution)/shard_map/ppermute | solution.py:335
  36.1 2.8 %collective-permute-start.15 = (bf16[80,1024]{1,0:T(8,128)(2,1)S(1)}, bf16[80,1024]{1,0:T(8,128)(2,1)S(1)}, u32[]{:S(2)}, u32[]{:S(2)}) collective-permute-start(bf16[80,1024]{1,0:T(8,128)(2,1)S(1)} %get-tuple-element.59), channel_id=1, source_target_pairs={{0,1},{1,0},{2,3},{3,2},{4,5},{5,4},{6,7},{7,6},{8,9},{9,8},{10,11... | collective-permute-start | bytes 491528 | tf_op jit(solution)/shard_map/ppermute | solution.py:335
  39.8 1.6 %collective-permute-start.16 = (bf16[80,1024]{1,0:T(8,128)(2,1)S(1)}, bf16[80,1024]{1,0:T(8,128)(2,1)S(1)}, u32[]{:S(2)}, u32[]{:S(2)}) collective-permute-start(bf16[80,1024]{1,0:T(8,128)(2,1)S(1)} %get-tuple-element.61), channel_id=1, source_target_pairs={{0,1},{1,0},{2,3},{3,2},{4,5},{5,4},{6,7},{7,6},{8,9},{9,8},{10,11... | collective-permute-start | bytes 491528 | tf_op jit(solution)/shard_map/ppermute | solution.py:335
  40.0 3.6 %collective-permute-start.21 = (bf16[80,1024]{1,0:T(8,128)(2,1)S(1)}, bf16[80,1024]{1,0:T(8,128)(2,1)S(1)}, u32[]{:S(2)}, u32[]{:S(2)}) collective-permute-start(bf16[80,1024]{1,0:T(8,128)(2,1)S(1)} %get-tuple-element.73), channel_id=1, source_target_pairs={{0,1},{1,0},{2,3},{3,2},{4,5},{5,4},{6,7},{7,6},{8,9},{9,8},{10,11... | collective-permute-start | bytes 491528 | tf_op jit(solution)/shard_map/ppermute | solution.py:335
  41.5 5.4 %collective-permute-start.17 = (bf16[40,1024]{1,0:T(8,128)(2,1)S(1)}, bf16[40,1024]{1,0:T(8,128)(2,1)S(1)}, u32[]{:S(2)}, u32[]{:S(2)}) collective-permute-start(bf16[40,1024]{1,0:T(8,128)(2,1)S(1)} %get-tuple-element.67), channel_id=1, source_target_pairs={{0,2},{2,0},{1,3},{3,1},{4,6},{6,4},{5,7},{7,5},{8,10},{10,8},{9,1... | collective-permute-start | bytes 245768 | tf_op jit(solution)/shard_map/ppermute | solution.py:335
  42.6 6.0 %collective-permute-start.19 = (bf16[40,1024]{1,0:T(8,128)(2,1)S(1)}, bf16[40,1024]{1,0:T(8,128)(2,1)S(1)}, u32[]{:S(2)}, u32[]{:S(2)}) collective-permute-start(bf16[40,1024]{1,0:T(8,128)(2,1)S(1)} %get-tuple-element.70), channel_id=1, source_target_pairs={{0,2},{2,0},{1,3},{3,1},{4,6},{6,4},{5,7},{7,5},{8,10},{10,8},{9,1... | collective-permute-start | bytes 245768 | tf_op jit(solution)/shard_map/ppermute | solution.py:335
  43.6 7.3 %collective-permute-start.22 = (bf16[40,1024]{1,0:T(8,128)(2,1)S(1)}, bf16[40,1024]{1,0:T(8,128)(2,1)S(1)}, u32[]{:S(2)}, u32[]{:S(2)}) collective-permute-start(bf16[40,1024]{1,0:T(8,128)(2,1)S(1)} %get-tuple-element.74), channel_id=1, source_target_pairs={{0,2},{2,0},{1,3},{3,1},{4,6},{6,4},{5,7},{7,5},{8,10},{10,8},{9,1... | collective-permute-start | bytes 245768 | tf_op jit(solution)/shard_map/ppermute | solution.py:335
  44.9 6.4 %collective-permute-start.24 = (bf16[40,1024]{1,0:T(8,128)(2,1)S(1)}, bf16[40,1024]{1,0:T(8,128)(2,1)S(1)}, u32[]{:S(2)}, u32[]{:S(2)}) collective-permute-start(bf16[40,1024]{1,0:T(8,128)(2,1)S(1)} %get-tuple-element.78), channel_id=1, source_target_pairs={{0,2},{2,0},{1,3},{3,1},{4,6},{6,4},{5,7},{7,5},{8,10},{10,8},{9,1... | collective-permute-start | bytes 245768 | tf_op jit(solution)/shard_map/ppermute | solution.py:335
  46.9 7.5 %collective-permute-start.18 = (bf16[40,1024]{1,0:T(8,128)(2,1)S(1)}, bf16[40,1024]{1,0:T(8,128)(2,1)S(1)}, u32[]{:S(2)}, u32[]{:S(2)}) collective-permute-start(bf16[40,1024]{1,0:T(8,128)(2,1)S(1)} %shard_map.124), channel_id=1, source_target_pairs={{0,8},{4,12},{8,0},{12,4},{1,9},{5,13},{9,1},{13,5},{2,10},{6,14},... | collective-permute-start | bytes 245768 | tf_op jit(solution)/shard_map/ppermute | solution.py:332
  48.7 6.6 %collective-permute-start.20 = (bf16[40,1024]{1,0:T(8,128)(2,1)S(1)}, bf16[40,1024]{1,0:T(8,128)(2,1)S(1)}, u32[]{:S(2)}, u32[]{:S(2)}) collective-permute-start(bf16[40,1024]{1,0:T(8,128)(2,1)S(1)} %shard_map.125), channel_id=1, source_target_pairs={{0,12},{4,8},{8,4},{12,0},{1,13},{5,9},{9,5},{13,1},{2,14},{6,10},... | collective-permute-start | bytes 245768 | tf_op jit(solution)/shard_map/ppermute | solution.py:332
  51.0 5.1 %collective-permute-start.23 = (bf16[40,1024]{1,0:T(8,128)(2,1)S(1)}, bf16[40,1024]{1,0:T(8,128)(2,1)S(1)}, u32[]{:S(2)}, u32[]{:S(2)}) collective-permute-start(bf16[40,1024]{1,0:T(8,128)(2,1)S(1)} %shard_map.128), channel_id=1, source_target_pairs={{0,4},{4,0},{8,12},{12,8},{1,5},{5,1},{9,13},{13,9},{2,6},{6,2},{1... | collective-permute-start | bytes 245768 | tf_op jit(solution)/shard_map/ppermute | solution.py:332
  (2 other events, 17.7 us)

commit v6 on v5

--- a/solution.py
+++ b/solution.py
@@ -151,7 +151,8 @@
 
 
 def attend_kernel(experts, rows, cap, w1_ref, w2_ref, *refs):
-    arrived, compact, factor_ref = dict(zip(ORDER, refs[:experts])), refs[experts:-1], refs[-1]
+    arrived, compact = dict(zip(ORDER, refs[:experts])), refs[experts : 2 * experts]
+    factor_ref, home_ref = refs[2 * experts :]
     messages = [arrived[step] for step in range(experts)]
     width = messages[0].shape[1]
     count = experts * rows
@@ -187,6 +188,11 @@
     slot = dot(named.astype(BF16), before.astype(BF16)).astype(jnp.int32)
     block = (iota((META, count), 1) // rows) ^ iota((META, count), 0)
     spot = jnp.where(named, block * cap + slot, -1)
+    home = jnp.where(named, slot, -1)[:, 0:rows].astype(F32).astype(BF16)
+    home = dot_nt(same[0:rows, 0:rows], home).astype(jnp.int32)
+    for step in range(experts):
+        place = iota((rows, home_ref.shape[1]), 1) == home[:, step : step + 1]
+        home_ref[step * rows : (step + 1) * rows, :] = place.astype(BF16)
     for step, out in zip(ORDER, compact):
         place = iota((experts * cap, count), 0) == spot[step : step + 1, :]
         place = place.astype(BF16)
@@ -280,23 +286,16 @@
     out_ref[...] = total.astype(BF16)
 
 
-def mix_kernel(experts, cap, tile, steps, routes_ref, *refs):
+def mix_kernel(tile, steps, place_ref, *refs):
     returned, (out_hbm, out_ref, sems) = refs[:-3], refs[-3:]
-    rows = out_ref.shape[0]
+    rows, cap = out_ref.shape[0], returned[0].shape[0]
     copies = []
-    expert = lax.axis_index("expert") ^ iota((META, rows), 0)
-    named = (routes_ref[0:1, :] == expert) | (routes_ref[1:2, :] == expert)
-    named = named & (iota((META, rows), 0) < experts)
-    before = (iota((rows, rows), 0) < iota((rows, rows), 1)).astype(BF16)
-    slot = jnp.where(named, dot(named.astype(BF16), before), -1.0)
-    same = (iota((rows, rows), 0) == iota((rows, rows), 1)).astype(BF16)
-    slot = dot_nt(same, slot.astype(BF16)).astype(jnp.int32)
-    place = {
-        step: (iota((rows, cap), 1) == slot[:, step : step + 1]).astype(BF16) for step in set(steps)
-    }
     for at in range(0, out_ref.shape[1], tile):
         cols = slice(at, at + tile)
-        share = [dot(place[step], block[:, cols]) for step, block in zip(steps, returned)]
+        share = [
+            dot(place_ref[step * rows : (step + 1) * rows, 0:cap], block[:, cols])
+            for step, block in zip(steps, returned)
+        ]
         out_ref[:, cols] = sum(share).astype(BF16)
         copies.append(
             pltpu.make_async_copy(out_ref.at[:, cols], out_hbm.at[:, cols], sems.at[at // tile])
@@ -392,9 +391,10 @@
         packed[0],
     )
 
-    *compact, factor = call(
+    *compact, factor, home = call(
         functools.partial(attend_kernel, experts, rows, cap),
-        [struct(experts * cap, width)] * experts + [struct(experts * cap, HEAD, F32)],
+        [struct(experts * cap, width)] * experts
+        + [struct(experts * cap, HEAD, F32), struct(experts * rows, HEAD)],
         [IN_VMEM] * (2 + experts),
         flops=8 * experts * experts * rows * rows * width,
         moved=16 * rows * columns,
@@ -476,7 +476,7 @@
         join(swap(plain0, "dp"), base0, factor0),
     ]
     return pl.pallas_call(
-        functools.partial(mix_kernel, experts, cap, 256, ORDER),
+        functools.partial(mix_kernel, 256, ORDER),
         out_shape=struct(rows, columns),
         in_specs=[IN_VMEM] * (1 + experts),
         out_specs=IN_HBM,
@@ -486,7 +486,7 @@
         ],
         compiler_params=pltpu.CompilerParams(vmem_limit_bytes=VMEM_LIMIT),
         cost_estimate=pl.CostEstimate(flops=1, bytes_accessed=1, transcendentals=0),
-    )(routes.T, *returned)
+    )(home, *returned)
 
 
 def shards(

time: 57.6 us -> 57.4 us (level)
  no operation moved by 1% of the time
where the time goes in v6:
time: 57.4 us; the launch traced here: 57.1 us
  starting transfers between devices  25.2 us (44%)
  Pallas kernels  19.5 us (34%)
  waiting for transfers between devices  12.2 us (21%)
    ppermute x9, starting transfers between devices, along(): lax.ppermute(array, 'expert', [(i, i ^ step) for i in range(experts)])  15.6 us
    ppermute x9, waiting for transfers between devices, along(): lax.ppermute(array, 'expert', [(i, i ^ step) for i in range(experts)])  9.09 us
    ppermute x15, starting transfers between devices, swap(): return lax.ppermute(array, axis, [(0, 1), (1, 0)])  8.47 us
    pallas_call x1, Pallas kernels, head_shards(): pl.pallas_call(functools.partial(prefetch_kernel, experts), out_shape=[pl...  6.21 us
    pallas_call x2, Pallas kernels, first(): call(functools.partial(first_kernel, 512), [struct(count, hidden_units)],...  3.76 us
    pallas_call x3, Pallas kernels, pack(): call(functools.partial(pack_kernel, steps), [struct(4 * rows + KINDS, wid...  3.58 us
    ppermute x15, waiting for transfers between devices, swap(): return lax.ppermute(array, axis, [(0, 1), (1, 0)])  2.96 us
    pallas_call x2, Pallas kernels, half(): call(functools.partial(half_kernel, 512, other), [struct(count // parts,...  1.74 us
  transfers between devices with their start and end apart: 25, of which 13 were waited for; matrix products, arithmetic and copies ran while one was open for 0% of the time, Pallas kernels for 27%

profile of v6, /device:TPU:0, one launch (start us, length us, event | category | flops | bytes accessed | tf_op | source)
XLA Modules:
  0.0 57.1 jit_solution(14460281324214615196)
XLA Ops:
  0.0 1.1 %shard_map.109.refs_0_ = bf16[264,256]{1,0:T(8,128)(2,1)S(1)} custom-call(bf16[64,1024]{1,0:T(8,128)(2,1)} %q_hbm.5, bf16[64,2,1024]{2,1,0:T(2,128)(2,1)} %m_hbm.5, bf16[64,1024]{1,0:T(8,128)(2,1)} %h_hbm.5, s32[1,64]{1,0:T(1,128)} %bitcast.18, s32[1,64]{1,0:T(1,128)} %bitcast.21, s32[2,64]{1,0:T(2,128)} %bitcast.10, f32[2,64]{1,0:T(2,128)} %bitcast.13), custom_call_target="tpu_custom_call" | custom-call | tf_op jit(solution)/shard_map/pallas_call | solution.py:341
  1.1 4.1 %collective-permute-start = (bf16[264,256]{1,0:T(8,128)(2,1)S(1)}, bf16[264,256]{1,0:T(8,128)(2,1)S(1)}, u32[]{:S(2)}, u32[]{:S(2)}) collective-permute-start(bf16[264,256]{1,0:T(8,128)(2,1)S(1)} %shard_map.109.refs_0_), channel_id=1, source_target_pairs={{0,8},{4,12},{8,0},{12,4},{1,9},{5,13},{9,1},{13,5},{2,10},{6,14},... | collective-permute-start | bytes 405512 | tf_op jit(solution)/shard_map/ppermute | solution.py:331
  5.2 1.1 %shard_map.110.refs_0_ = bf16[264,256]{1,0:T(8,128)(2,1)S(1)} custom-call(bf16[64,1024]{1,0:T(8,128)(2,1)} %q_hbm.5, bf16[64,2,1024]{2,1,0:T(2,128)(2,1)} %m_hbm.5, bf16[64,1024]{1,0:T(8,128)(2,1)} %h_hbm.5, s32[1,64]{1,0:T(1,128)} %bitcast.19, s32[1,64]{1,0:T(1,128)} %bitcast.22, s32[2,64]{1,0:T(2,128)} %bitcast.11, f32[2,64]{1,0:T(2,128)} %bitcast.14, ...), custom_call_target="tpu_custom_call" | custom-call | bytes 16777216 | tf_op jit(solution)/shard_map/pallas_call | solution.py:341
  6.3 1.6 %collective-permute-start.2 = (bf16[264,256]{1,0:T(8,128)(2,1)S(1)}, bf16[264,256]{1,0:T(8,128)(2,1)S(1)}, u32[]{:S(2)}, u32[]{:S(2)}) collective-permute-start(bf16[264,256]{1,0:T(8,128)(2,1)S(1)} %shard_map.110.refs_0_), channel_id=1, source_target_pairs={{0,4},{4,0},{8,12},{12,8},{1,5},{5,1},{9,13},{13,9},{2,6},{6,2},{1... | collective-permute-start | bytes 405512 | tf_op jit(solution)/shard_map/ppermute | solution.py:331
  8.0 1.4 %shard_map.111 = (bf16[264,256]{1,0:T(8,128)(2,1)S(1)}, bf16[264,256]{1,0:T(8,128)(2,1)S(1)}) custom-call(bf16[64,1024]{1,0:T(8,128)(2,1)} %q_hbm.5, bf16[64,2,1024]{2,1,0:T(2,128)(2,1)} %m_hbm.5, bf16[64,1024]{1,0:T(8,128)(2,1)} %h_hbm.5, s32[1,64]{1,0:T(1,128)} %bitcast.20, s32[1,64]{1,0:T(1,128)} %bitcast.23, s32[2,64]{1,0:T(2,128)} %bitcast.12, ...), custom_call_target="tpu_custom_call" | custom-call | bytes 16777216 | tf_op jit(solution)/shard_map/pallas_call | solution.py:341
  9.4 6.2 %shard_map.112 = (bf16[2048,2048]{1,0:T(8,128)(2,1)S(1)}, bf16[2048,2048]{1,0:T(8,128)(2,1)S(1)}, f32[1,2048]{1,0:T(1,128)S(1)}, f32[1,2048]{1,0:T(1,128)S(1)}) custom-call(bf16[2048,2048]{1,0:T(8,128)(2,1)} %bitcast.8, bf16[2048,2048]{1,0:T(8,128)(2,1)} %bitcast.9, f32[1,2048]{1,0:T(1,128)} %bitcast.16, f32[1,2048]{1,0:T(1,128)} %bitcast.17, ...), custom_call_target="tpu_custom_call" | custom-call | bytes 33554432 | tf_op jit(solution)/shard_map/pallas_call | solution.py:371
  16.3 0.9 %shard_map.113 = (bf16[160,256]{1,0:T(8,128)(2,1)S(1)}, bf16[160,256]{1,0:T(8,128)(2,1)S(1)}, bf16[160,256]{1,0:T(8,128)(2,1)S(1)}, bf16[160,256]{1,0:T(8,128)(2...) custom-call(bf16[2048,2048]{1,0:T(8,128)(2,1)S(1)} %get-tuple-element.45.w1_ref.refs_8_.refs_6_, ...), custom_call_target="tpu_custom_call" | custom-call | flops 134217728 | bytes 1048576 | tf_op jit(solution)/shard_map/pallas_call | solution.py:394
  17.2 4.0 %collective-permute-start.3 = (bf16[160,256]{1,0:T(8,128)(2,1)S(1)}, bf16[160,256]{1,0:T(8,128)(2,1)S(1)}, u32[]{:S(2)}, u32[]{:S(2)}) collective-permute-start(bf16[160,256]{1,0:T(8,128)(2,1)S(1)} %get-tuple-element.49), channel_id=1, source_target_pairs={{0,8},{4,12},{8,0},{12,4},{1,9},{5,13},{9,1},{13,5},{2,10},{6,14},... | collective-permute-start | bytes 245768 | tf_op jit(solution)/shard_map/ppermute | solution.py:331
  21.6 1.1 %collective-permute-start.8 = (bf16[160,256]{1,0:T(8,128)(2,1)S(1)}, bf16[160,256]{1,0:T(8,128)(2,1)S(1)}, u32[]{:S(2)}, u32[]{:S(2)}) collective-permute-start(bf16[160,256]{1,0:T(8,128)(2,1)S(1)} %get-tuple-element.51), channel_id=1, source_target_pairs={{0,6},{2,4},{4,2},{6,0},{8,14},{10,12},{12,10},{14,8},{1,7},{3,5},... | collective-permute-start | bytes 245768 | tf_op jit(solution)/shard_map/ppermute | solution.py:338
  22.7 1.8 %collective-permute-start.6 = (bf16[160,256]{1,0:T(8,128)(2,1)S(1)}, bf16[160,256]{1,0:T(8,128)(2,1)S(1)}, u32[]{:S(2)}, u32[]{:S(2)}) collective-permute-start(bf16[160,256]{1,0:T(8,128)(2,1)S(1)} %get-tuple-element.51), channel_id=1, source_target_pairs={{0,4},{4,0},{8,12},{12,8},{1,5},{5,1},{9,13},{13,9},{2,6},{6,2},{1... | collective-permute-start | bytes 245768 | tf_op jit(solution)/shard_map/ppermute | solution.py:331
  25.1 1.7 %collective-permute-done.3.left_ref = bf16[160,256]{1,0:T(8,128)(2,1)S(1)} collective-permute-done((bf16[160,256]{1,0:T(8,128)(2,1)S(1)}, bf16[160,256]{1,0:T(8,128)(2,1)S(1)}, u32[]{:S(2)}, u32[]{:S(2)}) %collective-permute-start.3) | collective-permute-done | bytes 81952 | tf_op jit(solution)/shard_map/ppermute | solution.py:331
  26.8 1.4 %collective-permute-done.4.right_ref = bf16[160,256]{1,0:T(8,128)(2,1)S(1)} collective-permute-done((bf16[160,256]{1,0:T(8,128)(2,1)S(1)}, bf16[160,256]{1,0:T(8,128)(2,1)S(1)}, u32[]{:S(2)}, u32[]{:S(2)}) %collective-permute-start.4) | collective-permute-done | bytes 81952 | tf_op jit(solution)/shard_map/ppermute | solution.py:331
  28.2 1.7 %collective-permute-start.5 = (bf16[160,512]{1,0:T(8,128)(2,1)S(1)}, bf16[160,512]{1,0:T(8,128)(2,1)S(1)}, u32[]{:S(2)}, u32[]{:S(2)}) collective-permute-start(bf16[160,512]{1,0:T(8,128)(2,1)S(1)} %shard_map.114.refs_0_), channel_id=1, source_target_pairs={{0,2},{2,0},{1,3},{3,1},{4,6},{6,4},{5,7},{7,5},{8,10},{10,8},{9,1... | collective-permute-start | bytes 491528 | tf_op jit(solution)/shard_map/ppermute | solution.py:334
  32.1 1.9 %shard_map.115.a_ref = bf16[160,2048]{1,0:T(8,128)(2,1)S(1)} custom-call(bf16[160,512]{1,0:T(8,128)(2,1)S(1)} %shard_map.114.refs_0_, bf16[160,256]{1,0:T(8,128)(2,1)S(1)} %collective-permute-done.6.refs_1_.left_ref, bf16[160,256]{1,0:T(8,128)(2,1)S(1)} %get-tuple-element.52.refs_2_.right_ref, bf16[160,512]{1,0:T(8,128)(2,1)S(1)} %collective-permute-done.7.refs_3_, ...), custom_call_target="tpu_custom_call" | custom-call | tf_op jit(solution)/shard_map/pallas_call | solution.py:408
  34.0 1.5 %shard_map.116 = (bf16[160,1024]{1,0:T(8,128)(2,1)S(1)}, bf16[80,1024]{1,0:T(8,128)(2,1)S(1)}, bf16[80,1024]{1,0:T(8,128)(2,1)S(1)}) custom-call(bf16[160,2048]{1,0:T(8,128)(2,1)S(1)} %shard_map.115.a_ref, bf16[2048,2048]{1,0:T(8,128)(2,1)S(1)} %get-tuple-element.46.w2_ref.w_ref), custom_call_target="tpu_custom_call" | custom-call | tf_op jit(solution)/shard_map/pallas_call | solution.py:428
  37.0 1.9 %shard_map.118.a_ref = bf16[160,2048]{1,0:T(8,128)(2,1)S(1)} custom-call(bf16[160,512]{1,0:T(8,128)(2,1)S(1)} %collective-permute-done.5.refs_0_, bf16[160,512]{1,0:T(8,128)(2,1)S(1)} %shard_map.117.refs_1_, bf16[160,512]{1,0:T(8,128)(2,1)S(1)} %collective-permute-done.12.refs_2_, bf16[160,512]{1,0:T(8,128)(2,1)S(1)} %collective-permute-done.13.refs_3_, ...), custom_call_target="tpu_custom_call" | custom-call | flops 1342177280 | bytes 8388608 | tf_op jit(solution)/shard_map/pallas_call | solution.py:408
  41.5 1.1 %collective-permute-start.17 = (bf16[40,1024]{1,0:T(8,128)(2,1)S(1)}, bf16[40,1024]{1,0:T(8,128)(2,1)S(1)}, u32[]{:S(2)}, u32[]{:S(2)}) collective-permute-start(bf16[40,1024]{1,0:T(8,128)(2,1)S(1)} %get-tuple-element.69), channel_id=1, source_target_pairs={{0,2},{2,0},{1,3},{3,1},{4,6},{6,4},{5,7},{7,5},{8,10},{10,8},{9,1... | collective-permute-start | bytes 245768 | tf_op jit(solution)/shard_map/ppermute | solution.py:334
  42.6 1.0 %collective-permute-start.19 = (bf16[40,1024]{1,0:T(8,128)(2,1)S(1)}, bf16[40,1024]{1,0:T(8,128)(2,1)S(1)}, u32[]{:S(2)}, u32[]{:S(2)}) collective-permute-start(bf16[40,1024]{1,0:T(8,128)(2,1)S(1)} %get-tuple-element.72), channel_id=1, source_target_pairs={{0,2},{2,0},{1,3},{3,1},{4,6},{6,4},{5,7},{7,5},{8,10},{10,8},{9,1... | collective-permute-start | bytes 245768 | tf_op jit(solution)/shard_map/ppermute | solution.py:334
  43.6 1.1 %collective-permute-start.22 = (bf16[40,1024]{1,0:T(8,128)(2,1)S(1)}, bf16[40,1024]{1,0:T(8,128)(2,1)S(1)}, u32[]{:S(2)}, u32[]{:S(2)}) collective-permute-start(bf16[40,1024]{1,0:T(8,128)(2,1)S(1)} %get-tuple-element.76), channel_id=1, source_target_pairs={{0,2},{2,0},{1,3},{3,1},{4,6},{6,4},{5,7},{7,5},{8,10},{10,8},{9,1... | collective-permute-start | bytes 245768 | tf_op jit(solution)/shard_map/ppermute | solution.py:334
  44.9 1.0 %collective-permute-start.24 = (bf16[40,1024]{1,0:T(8,128)(2,1)S(1)}, bf16[40,1024]{1,0:T(8,128)(2,1)S(1)}, u32[]{:S(2)}, u32[]{:S(2)}) collective-permute-start(bf16[40,1024]{1,0:T(8,128)(2,1)S(1)} %get-tuple-element.80), channel_id=1, source_target_pairs={{0,2},{2,0},{1,3},{3,1},{4,6},{6,4},{5,7},{7,5},{8,10},{10,8},{9,1... | collective-permute-start | bytes 245768 | tf_op jit(solution)/shard_map/ppermute | solution.py:334
  46.9 1.1 %collective-permute-start.18 = (bf16[40,1024]{1,0:T(8,128)(2,1)S(1)}, bf16[40,1024]{1,0:T(8,128)(2,1)S(1)}, u32[]{:S(2)}, u32[]{:S(2)}) collective-permute-start(bf16[40,1024]{1,0:T(8,128)(2,1)S(1)} %shard_map.124), channel_id=1, source_target_pairs={{0,8},{4,12},{8,0},{12,4},{1,9},{5,13},{9,1},{13,5},{2,10},{6,14},... | collective-permute-start | bytes 245768 | tf_op jit(solution)/shard_map/ppermute | solution.py:331
  48.7 2.2 %collective-permute-start.20 = (bf16[40,1024]{1,0:T(8,128)(2,1)S(1)}, bf16[40,1024]{1,0:T(8,128)(2,1)S(1)}, u32[]{:S(2)}, u32[]{:S(2)}) collective-permute-start(bf16[40,1024]{1,0:T(8,128)(2,1)S(1)} %shard_map.125), channel_id=1, source_target_pairs={{0,12},{4,8},{8,4},{12,0},{1,13},{5,9},{9,5},{13,1},{2,14},{6,10},... | collective-permute-start | bytes 245768 | tf_op jit(solution)/shard_map/ppermute | solution.py:331
  51.4 3.0 %collective-permute-done.18.refs_0_ = bf16[40,1024]{1,0:T(8,128)(2,1)S(1)} collective-permute-done((bf16[40,1024]{1,0:T(8,128)(2,1)S(1)}, bf16[40,1024]{1,0:T(8,128)(2,1)S(1)}, u32[]{:S(2)}, u32[]{:S(2)}) %collective-permute-start.18) | collective-permute-done | bytes 81952 | tf_op jit(solution)/shard_map/ppermute | solution.py:331
  56.2 0.9 %shard_map.130 = bf16[64,1024]{1,0:T(8,128)(2,1)} custom-call(bf16[256,128]{1,0:T(8,128)(2,1)S(1)} %get-tuple-element.48.place_ref, bf16[40,1024]{1,0:T(8,128)(2,1)S(1)} %collective-permute-done.18.refs_0_, bf16[40,1024]{1,0:T(8,128)(2,1)S(1)} %collective-permute-done.20.refs_1_, bf16[40,1024]{1,0:T(8,128)(2,1)S(1)} %collective-permute-done.23.refs_2_, ...), custom_call_target="tpu_custom_call" | custom-call | flops 1 | bytes 1 | tf_op jit(solution)/shard_map/pallas_call | solution.py:478
  (48 shorter events, 11.8 us)
Async XLA Ops:
  1.1 14.5 %collective-permute-start = (bf16[264,256]{1,0:T(8,128)(2,1)S(1)}, bf16[264,256]{1,0:T(8,128)(2,1)S(1)}, u32[]{:S(2)}, u32[]{:S(2)}) collective-permute-start(bf16[264,256]{1,0:T(8,128)(2,1)S(1)} %shard_map.109.refs_0_), channel_id=1, source_target_pairs={{0,8},{4,12},{8,0},{12,4},{1,9},{5,13},{9,1},{13,5},{2,10},{6,14},... | collective-permute-start | bytes 405512 | tf_op jit(solution)/shard_map/ppermute | solution.py:331
  6.3 9.3 %collective-permute-start.2 = (bf16[264,256]{1,0:T(8,128)(2,1)S(1)}, bf16[264,256]{1,0:T(8,128)(2,1)S(1)}, u32[]{:S(2)}, u32[]{:S(2)}) collective-permute-start(bf16[264,256]{1,0:T(8,128)(2,1)S(1)} %shard_map.110.refs_0_), channel_id=1, source_target_pairs={{0,4},{4,0},{8,12},{12,8},{1,5},{5,1},{9,13},{13,9},{2,6},{6,2},{1... | collective-permute-start | bytes 405512 | tf_op jit(solution)/shard_map/ppermute | solution.py:331
  9.3 6.9 %collective-permute-start.1 = (bf16[264,256]{1,0:T(8,128)(2,1)S(1)}, bf16[264,256]{1,0:T(8,128)(2,1)S(1)}, u32[]{:S(2)}, u32[]{:S(2)}) collective-permute-start(bf16[264,256]{1,0:T(8,128)(2,1)S(1)} %get-tuple-element.47), channel_id=1, source_target_pairs={{0,12},{4,8},{8,4},{12,0},{1,13},{5,9},{9,5},{13,1},{2,14},{6,10},... | collective-permute-start | bytes 405512 | tf_op jit(solution)/shard_map/ppermute | solution.py:331
  17.2 9.6 %collective-permute-start.3 = (bf16[160,256]{1,0:T(8,128)(2,1)S(1)}, bf16[160,256]{1,0:T(8,128)(2,1)S(1)}, u32[]{:S(2)}, u32[]{:S(2)}) collective-permute-start(bf16[160,256]{1,0:T(8,128)(2,1)S(1)} %get-tuple-element.49), channel_id=1, source_target_pairs={{0,8},{4,12},{8,0},{12,4},{1,9},{5,13},{9,1},{13,5},{2,10},{6,14},... | collective-permute-start | bytes 245768 | tf_op jit(solution)/shard_map/ppermute | solution.py:331
  21.1 7.0 %collective-permute-start.4 = (bf16[160,256]{1,0:T(8,128)(2,1)S(1)}, bf16[160,256]{1,0:T(8,128)(2,1)S(1)}, u32[]{:S(2)}, u32[]{:S(2)}) collective-permute-start(bf16[160,256]{1,0:T(8,128)(2,1)S(1)} %get-tuple-element.50), channel_id=1, source_target_pairs={{0,12},{4,8},{8,4},{12,0},{1,13},{5,9},{9,5},{13,1},{2,14},{6,10},... | collective-permute-start | bytes 245768 | tf_op jit(solution)/shard_map/ppermute | solution.py:331
  21.6 8.5 %collective-permute-start.8 = (bf16[160,256]{1,0:T(8,128)(2,1)S(1)}, bf16[160,256]{1,0:T(8,128)(2,1)S(1)}, u32[]{:S(2)}, u32[]{:S(2)}) collective-permute-start(bf16[160,256]{1,0:T(8,128)(2,1)S(1)} %get-tuple-element.51), channel_id=1, source_target_pairs={{0,6},{2,4},{4,2},{6,0},{8,14},{10,12},{12,10},{14,8},{1,7},{3,5},... | collective-permute-start | bytes 245768 | tf_op jit(solution)/shard_map/ppermute | solution.py:338
  22.7 8.1 %collective-permute-start.6 = (bf16[160,256]{1,0:T(8,128)(2,1)S(1)}, bf16[160,256]{1,0:T(8,128)(2,1)S(1)}, u32[]{:S(2)}, u32[]{:S(2)}) collective-permute-start(bf16[160,256]{1,0:T(8,128)(2,1)S(1)} %get-tuple-element.51), channel_id=1, source_target_pairs={{0,4},{4,0},{8,12},{12,8},{1,5},{5,1},{9,13},{13,9},{2,6},{6,2},{1... | collective-permute-start | bytes 245768 | tf_op jit(solution)/shard_map/ppermute | solution.py:331
  24.5 6.3 %collective-permute-start.9 = (bf16[160,256]{1,0:T(8,128)(2,1)S(1)}, bf16[160,256]{1,0:T(8,128)(2,1)S(1)}, u32[]{:S(2)}, u32[]{:S(2)}) collective-permute-start(bf16[160,256]{1,0:T(8,128)(2,1)S(1)} %get-tuple-element.52.refs_2_.right_ref), channel_id=1, source_target_pairs={{0,2},{2,0},{1,3},{3,1},{4,6},{6,4},{5,7},{7,5},{8,10},{10,8},{9,1... | collective-permute-start | bytes 245768 | tf_op jit(solution)/shard_map/ppermute | solution.py:334
  28.1 3.9 %collective-permute-start.7 = (bf16[160,512]{1,0:T(8,128)(2,1)S(1)}, bf16[160,512]{1,0:T(8,128)(2,1)S(1)}, u32[]{:S(2)}, u32[]{:S(2)}) collective-permute-start(bf16[160,512]{1,0:T(8,128)(2,1)S(1)} %shard_map.114.refs_0_), channel_id=1, source_target_pairs={{0,1},{1,0},{2,3},{3,2},{4,5},{5,4},{6,7},{7,6},{8,9},{9,8},{10,11... | collective-permute-start | bytes 491528 | tf_op jit(solution)/shard_map/ppermute | solution.py:334
  28.2 7.3 %collective-permute-start.5 = (bf16[160,512]{1,0:T(8,128)(2,1)S(1)}, bf16[160,512]{1,0:T(8,128)(2,1)S(1)}, u32[]{:S(2)}, u32[]{:S(2)}) collective-permute-start(bf16[160,512]{1,0:T(8,128)(2,1)S(1)} %shard_map.114.refs_0_), channel_id=1, source_target_pairs={{0,2},{2,0},{1,3},{3,1},{4,6},{6,4},{5,7},{7,5},{8,10},{10,8},{9,1... | collective-permute-start | bytes 491528 | tf_op jit(solution)/shard_map/ppermute | solution.py:334
  30.8 1.3 %collective-permute-start.10 = (bf16[160,256]{1,0:T(8,128)(2,1)S(1)}, bf16[160,256]{1,0:T(8,128)(2,1)S(1)}, u32[]{:S(2)}, u32[]{:S(2)}) collective-permute-start(bf16[160,256]{1,0:T(8,128)(2,1)S(1)} %collective-permute-done.6.refs_1_.left_ref), channel_id=1, source_target_pairs={{0,1},{1,0},{2,3},{3,2},{4,5},{5,4},{6,7},{7,6},{8,9},{9,8},{10,11... | collective-permute-start | bytes 245768 | tf_op jit(solution)/shard_map/ppermute | solution.py:334
  30.8 5.4 %collective-permute-start.13 = (bf16[160,512]{1,0:T(8,128)(2,1)S(1)}, bf16[160,512]{1,0:T(8,128)(2,1)S(1)}, u32[]{:S(2)}, u32[]{:S(2)}) collective-permute-start(bf16[160,512]{1,0:T(8,128)(2,1)S(1)} %shard_map.117.refs_1_), channel_id=1, source_target_pairs={{0,1},{1,0},{2,3},{3,2},{4,5},{5,4},{6,7},{7,6},{8,9},{9,8},{10,11... | collective-permute-start | bytes 491528 | tf_op jit(solution)/shard_map/ppermute | solution.py:334
  35.5 1.5 %collective-permute-start.12 = (bf16[160,512]{1,0:T(8,128)(2,1)S(1)}, bf16[160,512]{1,0:T(8,128)(2,1)S(1)}, u32[]{:S(2)}, u32[]{:S(2)}) collective-permute-start(bf16[160,512]{1,0:T(8,128)(2,1)S(1)} %collective-permute-done.5.refs_0_), channel_id=1, source_target_pairs={{0,1},{1,0},{2,3},{3,2},{4,5},{5,4},{6,7},{7,6},{8,9},{9,8},{10,11... | collective-permute-start | bytes 491528 | tf_op jit(solution)/shard_map/ppermute | solution.py:334
  35.8 3.1 %collective-permute-start.14 = (bf16[80,1024]{1,0:T(8,128)(2,1)S(1)}, bf16[80,1024]{1,0:T(8,128)(2,1)S(1)}, u32[]{:S(2)}, u32[]{:S(2)}) collective-permute-start(bf16[80,1024]{1,0:T(8,128)(2,1)S(1)} %get-tuple-element.60), channel_id=1, source_target_pairs={{0,1},{1,0},{2,3},{3,2},{4,5},{5,4},{6,7},{7,6},{8,9},{9,8},{10,11... | collective-permute-start | bytes 491528 | tf_op jit(solution)/shard_map/ppermute | solution.py:334
  36.1 2.8 %collective-permute-start.15 = (bf16[80,1024]{1,0:T(8,128)(2,1)S(1)}, bf16[80,1024]{1,0:T(8,128)(2,1)S(1)}, u32[]{:S(2)}, u32[]{:S(2)}) collective-permute-start(bf16[80,1024]{1,0:T(8,128)(2,1)S(1)} %get-tuple-element.61), channel_id=1, source_target_pairs={{0,1},{1,0},{2,3},{3,2},{4,5},{5,4},{6,7},{7,6},{8,9},{9,8},{10,11... | collective-permute-start | bytes 491528 | tf_op jit(solution)/shard_map/ppermute | solution.py:334
  39.8 1.6 %collective-permute-start.16 = (bf16[80,1024]{1,0:T(8,128)(2,1)S(1)}, bf16[80,1024]{1,0:T(8,128)(2,1)S(1)}, u32[]{:S(2)}, u32[]{:S(2)}) collective-permute-start(bf16[80,1024]{1,0:T(8,128)(2,1)S(1)} %get-tuple-element.63), channel_id=1, source_target_pairs={{0,1},{1,0},{2,3},{3,2},{4,5},{5,4},{6,7},{7,6},{8,9},{9,8},{10,11... | collective-permute-start | bytes 491528 | tf_op jit(solution)/shard_map/ppermute | solution.py:334
  40.0 3.6 %collective-permute-start.21 = (bf16[80,1024]{1,0:T(8,128)(2,1)S(1)}, bf16[80,1024]{1,0:T(8,128)(2,1)S(1)}, u32[]{:S(2)}, u32[]{:S(2)}) collective-permute-start(bf16[80,1024]{1,0:T(8,128)(2,1)S(1)} %get-tuple-element.75), channel_id=1, source_target_pairs={{0,1},{1,0},{2,3},{3,2},{4,5},{5,4},{6,7},{7,6},{8,9},{9,8},{10,11... | collective-permute-start | bytes 491528 | tf_op jit(solution)/shard_map/ppermute | solution.py:334
  41.5 5.4 %collective-permute-start.17 = (bf16[40,1024]{1,0:T(8,128)(2,1)S(1)}, bf16[40,1024]{1,0:T(8,128)(2,1)S(1)}, u32[]{:S(2)}, u32[]{:S(2)}) collective-permute-start(bf16[40,1024]{1,0:T(8,128)(2,1)S(1)} %get-tuple-element.69), channel_id=1, source_target_pairs={{0,2},{2,0},{1,3},{3,1},{4,6},{6,4},{5,7},{7,5},{8,10},{10,8},{9,1... | collective-permute-start | bytes 245768 | tf_op jit(solution)/shard_map/ppermute | solution.py:334
  42.6 6.0 %collective-permute-start.19 = (bf16[40,1024]{1,0:T(8,128)(2,1)S(1)}, bf16[40,1024]{1,0:T(8,128)(2,1)S(1)}, u32[]{:S(2)}, u32[]{:S(2)}) collective-permute-start(bf16[40,1024]{1,0:T(8,128)(2,1)S(1)} %get-tuple-element.72), channel_id=1, source_target_pairs={{0,2},{2,0},{1,3},{3,1},{4,6},{6,4},{5,7},{7,5},{8,10},{10,8},{9,1... | collective-permute-start | bytes 245768 | tf_op jit(solution)/shard_map/ppermute | solution.py:334
  43.6 7.3 %collective-permute-start.22 = (bf16[40,1024]{1,0:T(8,128)(2,1)S(1)}, bf16[40,1024]{1,0:T(8,128)(2,1)S(1)}, u32[]{:S(2)}, u32[]{:S(2)}) collective-permute-start(bf16[40,1024]{1,0:T(8,128)(2,1)S(1)} %get-tuple-element.76), channel_id=1, source_target_pairs={{0,2},{2,0},{1,3},{3,1},{4,6},{6,4},{5,7},{7,5},{8,10},{10,8},{9,1... | collective-permute-start | bytes 245768 | tf_op jit(solution)/shard_map/ppermute | solution.py:334
  44.9 6.4 %collective-permute-start.24 = (bf16[40,1024]{1,0:T(8,128)(2,1)S(1)}, bf16[40,1024]{1,0:T(8,128)(2,1)S(1)}, u32[]{:S(2)}, u32[]{:S(2)}) collective-permute-start(bf16[40,1024]{1,0:T(8,128)(2,1)S(1)} %get-tuple-element.80), channel_id=1, source_target_pairs={{0,2},{2,0},{1,3},{3,1},{4,6},{6,4},{5,7},{7,5},{8,10},{10,8},{9,1... | collective-permute-start | bytes 245768 | tf_op jit(solution)/shard_map/ppermute | solution.py:334
  46.9 7.5 %collective-permute-start.18 = (bf16[40,1024]{1,0:T(8,128)(2,1)S(1)}, bf16[40,1024]{1,0:T(8,128)(2,1)S(1)}, u32[]{:S(2)}, u32[]{:S(2)}) collective-permute-start(bf16[40,1024]{1,0:T(8,128)(2,1)S(1)} %shard_map.124), channel_id=1, source_target_pairs={{0,8},{4,12},{8,0},{12,4},{1,9},{5,13},{9,1},{13,5},{2,10},{6,14},... | collective-permute-start | bytes 245768 | tf_op jit(solution)/shard_map/ppermute | solution.py:331
  48.7 6.6 %collective-permute-start.20 = (bf16[40,1024]{1,0:T(8,128)(2,1)S(1)}, bf16[40,1024]{1,0:T(8,128)(2,1)S(1)}, u32[]{:S(2)}, u32[]{:S(2)}) collective-permute-start(bf16[40,1024]{1,0:T(8,128)(2,1)S(1)} %shard_map.125), channel_id=1, source_target_pairs={{0,12},{4,8},{8,4},{12,0},{1,13},{5,9},{9,5},{13,1},{2,14},{6,10},... | collective-permute-start | bytes 245768 | tf_op jit(solution)/shard_map/ppermute | solution.py:331
  51.0 5.1 %collective-permute-start.23 = (bf16[40,1024]{1,0:T(8,128)(2,1)S(1)}, bf16[40,1024]{1,0:T(8,128)(2,1)S(1)}, u32[]{:S(2)}, u32[]{:S(2)}) collective-permute-start(bf16[40,1024]{1,0:T(8,128)(2,1)S(1)} %shard_map.128), channel_id=1, source_target_pairs={{0,4},{4,0},{8,12},{12,8},{1,5},{5,1},{9,13},{13,9},{2,6},{6,2},{1... | collective-permute-start | bytes 245768 | tf_op jit(solution)/shard_map/ppermute | solution.py:331
  (1 other events, 1.3 us)

commit v7 on v6

--- a/solution.py
+++ b/solution.py
@@ -193,6 +193,13 @@
     for step in range(experts):
         place = iota((rows, home_ref.shape[1]), 1) == home[:, step : step + 1]
         home_ref[step * rows : (step + 1) * rows, :] = place.astype(BF16)
+    kinds = dot_nt(same[0:rows, 0:rows], meta[:, 0:rows].astype(BF16))
+    leads = kinds[:, 2:3].astype(jnp.int32) == (here ^ 1)
+    place = iota((rows, home_ref.shape[1]), 1) == home[:, 1:2]
+    for k in range(2):
+        half = jnp.where(leads, kinds[:, 4 + k : 5 + k], kinds[:, 6 + k : 7 + k])
+        at = (experts + k) * rows
+        home_ref[at : at + rows, :] = jnp.where(place, half, 0.0).astype(BF16)
     for step, out in zip(ORDER, compact):
         place = iota((experts * cap, count), 0) == spot[step : step + 1, :]
         place = place.astype(BF16)
@@ -281,22 +288,49 @@
         factors[k][...] = jnp.broadcast_to(weight, factors[k].shape)
 
 
+def low_kernel(kept_ref, got_ref, factor_ref, *refs):
+    blocks, (base_ref, near_ref, weight_ref, states) = refs[: len(PAIRS)], refs[-4:]
+    here = lax.axis_index("expert")
+    cap, width = base_ref.shape[0], blocks[0].shape[1] // 2
+    for steps, block in zip(PAIRS, blocks):
+        for k, step in enumerate(steps):
+            piece = block[0 : 2 * cap, k * width : (k + 1) * width]
+            states[:, columns_at(here ^ step, width)] = piece.astype(F32)
+    weight = factor_ref[0 : 2 * cap, 0:1] + factor_ref[0 : 2 * cap, 1:2]
+    total = kept_ref[0 : 2 * cap, :].astype(F32) + got_ref[...].astype(F32)
+    total = total * weight + factor_ref[0 : 2 * cap, 3:4] * states[...]
+    base_ref[...] = total[0:cap, :]
+    near_ref[...] = total[cap:, :].astype(BF16)
+    weight_ref[...] = jnp.broadcast_to(weight[0:cap, :], weight_ref.shape)
+
+
 def join_kernel(came_ref, base_ref, factor_ref, out_ref):
     total = base_ref[...] + factor_ref[:, 0:1] * came_ref[...].astype(F32)
     out_ref[...] = total.astype(BF16)
 
 
-def mix_kernel(tile, steps, place_ref, *refs):
-    returned, (out_hbm, out_ref, sems) = refs[:-3], refs[-3:]
-    rows, cap = out_ref.shape[0], returned[0].shape[0]
-    copies = []
+def sum_kernel(tile, steps, place_ref, *refs):
+    returned, far_ref, out_ref = refs[:-2], refs[-2], refs[-1]
+    rows, cap = out_ref.shape[0], far_ref.shape[0]
+    last = place_ref.shape[0] // rows
+    terms = [*zip(steps, returned), (last - 2, far_ref), (last - 1, far_ref)]
     for at in range(0, out_ref.shape[1], tile):
         cols = slice(at, at + tile)
         share = [
             dot(place_ref[step * rows : (step + 1) * rows, 0:cap], block[:, cols])
-            for step, block in zip(steps, returned)
+            for step, block in terms
         ]
-        out_ref[:, cols] = sum(share).astype(BF16)
+        out_ref[:, cols] = sum(share)
+
+
+def mix_kernel(tile, place_ref, share_ref, came_ref, base_ref, factor_ref, out_hbm, out_ref, sems):
+    rows, cap = out_ref.shape[0], came_ref.shape[0]
+    copies = []
+    for at in range(0, out_ref.shape[1], tile):
+        cols = slice(at, at + tile)
+        own = base_ref[:, cols] + factor_ref[:, 0:1] * came_ref[:, cols].astype(F32)
+        own = dot(place_ref[0:rows, 0:cap], own.astype(BF16))
+        out_ref[:, cols] = (share_ref[:, cols] + own).astype(BF16)
         copies.append(
             pltpu.make_async_copy(out_ref.at[:, cols], out_hbm.at[:, cols], sems.at[at // tile])
         )
@@ -394,7 +428,7 @@
     *compact, factor, home = call(
         functools.partial(attend_kernel, experts, rows, cap),
         [struct(experts * cap, width)] * experts
-        + [struct(experts * cap, HEAD, F32), struct(experts * rows, HEAD)],
+        + [struct(experts * cap, HEAD, F32), struct((experts + 2) * rows, HEAD)],
         [IN_VMEM] * (2 + experts),
         flops=8 * experts * experts * rows * rows * width,
         moved=16 * rows * columns,
@@ -466,27 +500,38 @@
 
     base2, base3, factor2, factor3 = base(2 * cap, got[1])
     theirs[1], base2 = lax.optimization_barrier((theirs[1], base2))
-    base0, base1, factor0, factor1 = base(0, got[0])
+    base0, near1, factor0 = call(
+        low_kernel,
+        [struct(cap, columns, F32), struct(cap, columns), struct(cap, HEAD, F32)],
+        [IN_VMEM] * (3 + len(PAIRS)),
+        scratch=[pltpu.VMEM((2 * cap, columns), F32)],
+    )(kept, got[0], factor, *near)
     plain2, plain3 = plain(2 * cap, theirs[1])
     plain0, plain1 = plain(0, theirs[0])
     returned = [
         along(join(swap(plain2, "dp"), base2, factor2), 2),
         along(join(swap(plain3, "dp"), base3, factor3), 3),
-        along(join(swap(plain1, "dp"), base1, factor1), 1),
-        join(swap(plain0, "dp"), base0, factor0),
+        along(near1, 1),
+        across(plain1),
     ]
+    share = call(
+        functools.partial(sum_kernel, 512, ORDER[:-1]),
+        [struct(rows, columns, F32)],
+        [IN_VMEM] * (1 + experts),
+        moved=LATER,
+    )(home, *returned)[0]
     return pl.pallas_call(
-        functools.partial(mix_kernel, 256, ORDER),
+        functools.partial(mix_kernel, 512),
         out_shape=struct(rows, columns),
-        in_specs=[IN_VMEM] * (1 + experts),
+        in_specs=[IN_VMEM] * 5,
         out_specs=IN_HBM,
         scratch_shapes=[
             pltpu.VMEM((rows, columns), BF16),
-            pltpu.SemaphoreType.DMA((columns // 256,)),
+            pltpu.SemaphoreType.DMA((columns // 512,)),
         ],
         compiler_params=pltpu.CompilerParams(vmem_limit_bytes=VMEM_LIMIT),
         cost_estimate=pl.CostEstimate(flops=1, bytes_accessed=1, transcendentals=0),
-    )(home, *returned)
+    )(home, share, swap(plain0, "dp"), base0, factor0)
 
 
 def shards(

time: 57.4 us -> 56.7 us (0.988)
  waiting for transfers between devices: 12.2 us -> 9.99 us
  starting transfers between devices: 25.2 us -> 26.8 us
    ppermute x1 -> x2, starting transfers between devices: 1.13 us -> 3.01 us  [across(): return lax.ppermute(array, ('expert', 'dp'), pairs)]
    ppermute x15 -> x14, starting transfers between devices: 8.47 us -> 7.06 us  [swap(): return lax.ppermute(array, axis, [(0, 1), (1, 0)])]
    ppermute x9, waiting for transfers between devices: 9.09 us -> 7.85 us  [along(): lax.ppermute(array, 'expert', [(i, i ^ step) for i in range(experts)])]
    ppermute x9, starting transfers between devices: 15.6 us -> 16.7 us  [along(): lax.ppermute(array, 'expert', [(i, i ^ step) for i in range(experts)])]
    ppermute x15 -> x14, waiting for transfers between devices: 2.96 us -> 1.95 us  [swap(): return lax.ppermute(array, axis, [(0, 1), (1, 0)])]
    pallas_call x1 -> x3, Pallas kernels: 0.94 us -> 1.36 us  [the longest x1 0.9 us: head_shards(): pl.pallas_call(functools.partial(mix_kernel, 512), out_shape=struct(rows,...]
  transfers between devices with their start and end apart: 25 -> 25, of which waited for: 13 -> 10; matrix products, arithmetic and copies ran while one was open for 0% -> 0% of each run, Pallas kernels for 27% -> 28%
where the time goes in v7:
time: 56.7 us; the launch traced here: 56.5 us
  starting transfers between devices  26.8 us (47%)
  Pallas kernels  19.5 us (34%)
  waiting for transfers between devices  9.99 us (18%)
    ppermute x9, starting transfers between devices, along(): lax.ppermute(array, 'expert', [(i, i ^ step) for i in range(experts)])  16.7 us
    ppermute x9, waiting for transfers between devices, along(): lax.ppermute(array, 'expert', [(i, i ^ step) for i in range(experts)])  7.85 us
    ppermute x14, starting transfers between devices, swap(): return lax.ppermute(array, axis, [(0, 1), (1, 0)])  7.06 us
    pallas_call x1, Pallas kernels, head_shards(): pl.pallas_call(functools.partial(prefetch_kernel, experts), out_shape=[pl...  6.21 us
    pallas_call x2, Pallas kernels, first(): call(functools.partial(first_kernel, 512), [struct(count, hidden_units)],...  3.76 us
    pallas_call x3, Pallas kernels, pack(): call(functools.partial(pack_kernel, steps), [struct(4 * rows + KINDS, wid...  3.58 us
    ppermute x2, starting transfers between devices, across(): return lax.ppermute(array, ('expert', 'dp'), pairs)  3.01 us
    ppermute x14, waiting for transfers between devices, swap(): return lax.ppermute(array, axis, [(0, 1), (1, 0)])  1.95 us
  transfers between devices with their start and end apart: 25, of which 10 were waited for; matrix products, arithmetic and copies ran while one was open for 0% of the time, Pallas kernels for 28%

profile of v7, /device:TPU:0, one launch (start us, length us, event | category | flops | bytes accessed | tf_op | source)
XLA Modules:
  0.0 56.5 jit_solution(13078919717929748381)
XLA Ops:
  0.0 1.1 %shard_map.109.refs_0_ = bf16[264,256]{1,0:T(8,128)(2,1)S(1)} custom-call(bf16[64,1024]{1,0:T(8,128)(2,1)} %q_hbm.5, bf16[64,2,1024]{2,1,0:T(2,128)(2,1)} %m_hbm.5, bf16[64,1024]{1,0:T(8,128)(2,1)} %h_hbm.5, s32[1,64]{1,0:T(1,128)} %bitcast.18, s32[1,64]{1,0:T(1,128)} %bitcast.21, s32[2,64]{1,0:T(2,128)} %bitcast.10, f32[2,64]{1,0:T(2,128)} %bitcast.13), custom_call_target="tpu_custom_call" | custom-call | tf_op jit(solution)/shard_map/pallas_call | solution.py:375
  1.1 4.1 %collective-permute-start = (bf16[264,256]{1,0:T(8,128)(2,1)S(1)}, bf16[264,256]{1,0:T(8,128)(2,1)S(1)}, u32[]{:S(2)}, u32[]{:S(2)}) collective-permute-start(bf16[264,256]{1,0:T(8,128)(2,1)S(1)} %shard_map.109.refs_0_), channel_id=1, source_target_pairs={{0,8},{4,12},{8,0},{12,4},{1,9},{5,13},{9,1},{13,5},{2,10},{6,14},... | collective-permute-start | bytes 405512 | tf_op jit(solution)/shard_map/ppermute | solution.py:365
  5.2 1.1 %shard_map.110.refs_0_ = bf16[264,256]{1,0:T(8,128)(2,1)S(1)} custom-call(bf16[64,1024]{1,0:T(8,128)(2,1)} %q_hbm.5, bf16[64,2,1024]{2,1,0:T(2,128)(2,1)} %m_hbm.5, bf16[64,1024]{1,0:T(8,128)(2,1)} %h_hbm.5, s32[1,64]{1,0:T(1,128)} %bitcast.19, s32[1,64]{1,0:T(1,128)} %bitcast.22, s32[2,64]{1,0:T(2,128)} %bitcast.11, f32[2,64]{1,0:T(2,128)} %bitcast.14, ...), custom_call_target="tpu_custom_call" | custom-call | bytes 16777216 | tf_op jit(solution)/shard_map/pallas_call | solution.py:375
  6.3 1.6 %collective-permute-start.2 = (bf16[264,256]{1,0:T(8,128)(2,1)S(1)}, bf16[264,256]{1,0:T(8,128)(2,1)S(1)}, u32[]{:S(2)}, u32[]{:S(2)}) collective-permute-start(bf16[264,256]{1,0:T(8,128)(2,1)S(1)} %shard_map.110.refs_0_), channel_id=1, source_target_pairs={{0,4},{4,0},{8,12},{12,8},{1,5},{5,1},{9,13},{13,9},{2,6},{6,2},{1... | collective-permute-start | bytes 405512 | tf_op jit(solution)/shard_map/ppermute | solution.py:365
  8.0 1.4 %shard_map.111 = (bf16[264,256]{1,0:T(8,128)(2,1)S(1)}, bf16[264,256]{1,0:T(8,128)(2,1)S(1)}) custom-call(bf16[64,1024]{1,0:T(8,128)(2,1)} %q_hbm.5, bf16[64,2,1024]{2,1,0:T(2,128)(2,1)} %m_hbm.5, bf16[64,1024]{1,0:T(8,128)(2,1)} %h_hbm.5, s32[1,64]{1,0:T(1,128)} %bitcast.20, s32[1,64]{1,0:T(1,128)} %bitcast.23, s32[2,64]{1,0:T(2,128)} %bitcast.12, ...), custom_call_target="tpu_custom_call" | custom-call | bytes 16777216 | tf_op jit(solution)/shard_map/pallas_call | solution.py:375
  9.4 6.2 %shard_map.112 = (bf16[2048,2048]{1,0:T(8,128)(2,1)S(1)}, bf16[2048,2048]{1,0:T(8,128)(2,1)S(1)}, f32[1,2048]{1,0:T(1,128)S(1)}, f32[1,2048]{1,0:T(1,128)S(1)}) custom-call(bf16[2048,2048]{1,0:T(8,128)(2,1)} %bitcast.8, bf16[2048,2048]{1,0:T(8,128)(2,1)} %bitcast.9, f32[1,2048]{1,0:T(1,128)} %bitcast.16, f32[1,2048]{1,0:T(1,128)} %bitcast.17, ...), custom_call_target="tpu_custom_call" | custom-call | bytes 33554432 | tf_op jit(solution)/shard_map/pallas_call | solution.py:405
  17.1 4.0 %collective-permute-start.3 = (bf16[160,256]{1,0:T(8,128)(2,1)S(1)}, bf16[160,256]{1,0:T(8,128)(2,1)S(1)}, u32[]{:S(2)}, u32[]{:S(2)}) collective-permute-start(bf16[160,256]{1,0:T(8,128)(2,1)S(1)} %get-tuple-element.48), channel_id=1, source_target_pairs={{0,8},{4,12},{8,0},{12,4},{1,9},{5,13},{9,1},{13,5},{2,10},{6,14},... | collective-permute-start | bytes 245768 | tf_op jit(solution)/shard_map/ppermute | solution.py:365
  21.6 1.1 %collective-permute-start.8 = (bf16[160,256]{1,0:T(8,128)(2,1)S(1)}, bf16[160,256]{1,0:T(8,128)(2,1)S(1)}, u32[]{:S(2)}, u32[]{:S(2)}) collective-permute-start(bf16[160,256]{1,0:T(8,128)(2,1)S(1)} %get-tuple-element.50), channel_id=1, source_target_pairs={{0,6},{2,4},{4,2},{6,0},{8,14},{10,12},{12,10},{14,8},{1,7},{3,5},... | collective-permute-start | bytes 245768 | tf_op jit(solution)/shard_map/ppermute | solution.py:372
  22.7 1.8 %collective-permute-start.6 = (bf16[160,256]{1,0:T(8,128)(2,1)S(1)}, bf16[160,256]{1,0:T(8,128)(2,1)S(1)}, u32[]{:S(2)}, u32[]{:S(2)}) collective-permute-start(bf16[160,256]{1,0:T(8,128)(2,1)S(1)} %get-tuple-element.50), channel_id=1, source_target_pairs={{0,4},{4,0},{8,12},{12,8},{1,5},{5,1},{9,13},{13,9},{2,6},{6,2},{1... | collective-permute-start | bytes 245768 | tf_op jit(solution)/shard_map/ppermute | solution.py:365
  25.0 1.7 %collective-permute-done.3.left_ref = bf16[160,256]{1,0:T(8,128)(2,1)S(1)} collective-permute-done((bf16[160,256]{1,0:T(8,128)(2,1)S(1)}, bf16[160,256]{1,0:T(8,128)(2,1)S(1)}, u32[]{:S(2)}, u32[]{:S(2)}) %collective-permute-start.3) | collective-permute-done | bytes 81952 | tf_op jit(solution)/shard_map/ppermute | solution.py:365
  26.7 1.3 %collective-permute-done.4.right_ref = bf16[160,256]{1,0:T(8,128)(2,1)S(1)} collective-permute-done((bf16[160,256]{1,0:T(8,128)(2,1)S(1)}, bf16[160,256]{1,0:T(8,128)(2,1)S(1)}, u32[]{:S(2)}, u32[]{:S(2)}) %collective-permute-start.4) | collective-permute-done | bytes 81952 | tf_op jit(solution)/shard_map/ppermute | solution.py:365
  28.2 1.7 %collective-permute-start.5 = (bf16[160,512]{1,0:T(8,128)(2,1)S(1)}, bf16[160,512]{1,0:T(8,128)(2,1)S(1)}, u32[]{:S(2)}, u32[]{:S(2)}) collective-permute-start(bf16[160,512]{1,0:T(8,128)(2,1)S(1)} %shard_map.114.refs_0_), channel_id=1, source_target_pairs={{0,2},{2,0},{1,3},{3,1},{4,6},{6,4},{5,7},{7,5},{8,10},{10,8},{9,1... | collective-permute-start | bytes 491528 | tf_op jit(solution)/shard_map/ppermute | solution.py:368
  32.0 1.9 %shard_map.115.a_ref = bf16[160,2048]{1,0:T(8,128)(2,1)S(1)} custom-call(bf16[160,512]{1,0:T(8,128)(2,1)S(1)} %shard_map.114.refs_0_, bf16[160,256]{1,0:T(8,128)(2,1)S(1)} %collective-permute-done.6.refs_1_.left_ref, bf16[160,256]{1,0:T(8,128)(2,1)S(1)} %get-tuple-element.51.refs_2_.right_ref, bf16[160,512]{1,0:T(8,128)(2,1)S(1)} %collective-permute-done.7.refs_3_, ...), custom_call_target="tpu_custom_call" | custom-call | tf_op jit(solution)/shard_map/pallas_call | solution.py:442
  33.9 1.5 %shard_map.116 = (bf16[160,1024]{1,0:T(8,128)(2,1)S(1)}, bf16[80,1024]{1,0:T(8,128)(2,1)S(1)}, bf16[80,1024]{1,0:T(8,128)(2,1)S(1)}) custom-call(bf16[160,2048]{1,0:T(8,128)(2,1)S(1)} %shard_map.115.a_ref, bf16[2048,2048]{1,0:T(8,128)(2,1)S(1)} %get-tuple-element.45.w2_ref.w_ref), custom_call_target="tpu_custom_call" | custom-call | tf_op jit(solution)/shard_map/pallas_call | solution.py:462
  37.0 1.9 %shard_map.118.a_ref = bf16[160,2048]{1,0:T(8,128)(2,1)S(1)} custom-call(bf16[160,512]{1,0:T(8,128)(2,1)S(1)} %collective-permute-done.5.refs_0_, bf16[160,512]{1,0:T(8,128)(2,1)S(1)} %shard_map.117.refs_1_, bf16[160,512]{1,0:T(8,128)(2,1)S(1)} %collective-permute-done.12.refs_2_, bf16[160,512]{1,0:T(8,128)(2,1)S(1)} %collective-permute-done.13.refs_3_, ...), custom_call_target="tpu_custom_call" | custom-call | flops 1342177280 | bytes 8388608 | tf_op jit(solution)/shard_map/pallas_call | solution.py:442
  38.9 0.9 %shard_map.120 = (bf16[80,1024]{1,0:T(8,128)(2,1)S(1)}, bf16[80,1024]{1,0:T(8,128)(2,1)S(1)}) custom-call(bf16[160,2048]{1,0:T(8,128)(2,1)S(1)} %shard_map.118.a_ref, bf16[2048,2048]{1,0:T(8,128)(2,1)S(1)} %get-tuple-element.45.w2_ref.w_ref), custom_call_target="tpu_custom_call" | custom-call | flops 671088640 | bytes 4194304 | tf_op jit(solution)/shard_map/pallas_call | solution.py:474
  40.5 0.9 %shard_map.119.kept_ref = bf16[160,1024]{1,0:T(8,128)(2,1)S(1)} custom-call(bf16[160,2048]{1,0:T(8,128)(2,1)S(1)} %shard_map.118.a_ref, bf16[2048,2048]{1,0:T(8,128)(2,1)S(1)} %get-tuple-element.45.w2_ref.w_ref), custom_call_target="tpu_custom_call" | custom-call | flops 671088640 | bytes 4194304 | tf_op jit(solution)/shard_map/pallas_call | solution.py:474
  41.4 1.1 %collective-permute-start.17 = (bf16[40,1024]{1,0:T(8,128)(2,1)S(1)}, bf16[40,1024]{1,0:T(8,128)(2,1)S(1)}, u32[]{:S(2)}, u32[]{:S(2)}) collective-permute-start(bf16[40,1024]{1,0:T(8,128)(2,1)S(1)} %get-tuple-element.68), channel_id=1, source_target_pairs={{0,2},{2,0},{1,3},{3,1},{4,6},{6,4},{5,7},{7,5},{8,10},{10,8},{9,1... | collective-permute-start | bytes 245768 | tf_op jit(solution)/shard_map/ppermute | solution.py:368
  42.6 1.0 %collective-permute-start.19 = (bf16[40,1024]{1,0:T(8,128)(2,1)S(1)}, bf16[40,1024]{1,0:T(8,128)(2,1)S(1)}, u32[]{:S(2)}, u32[]{:S(2)}) collective-permute-start(bf16[40,1024]{1,0:T(8,128)(2,1)S(1)} %get-tuple-element.71), channel_id=1, source_target_pairs={{0,2},{2,0},{1,3},{3,1},{4,6},{6,4},{5,7},{7,5},{8,10},{10,8},{9,1... | collective-permute-start | bytes 245768 | tf_op jit(solution)/shard_map/ppermute | solution.py:368
  44.5 1.9 %collective-permute-start.23 = (bf16[40,1024]{1,0:T(8,128)(2,1)S(1)}, bf16[40,1024]{1,0:T(8,128)(2,1)S(1)}, u32[]{:S(2)}, u32[]{:S(2)}) collective-permute-start(bf16[40,1024]{1,0:T(8,128)(2,1)S(1)} %get-tuple-element.77), channel_id=1, source_target_pairs={{0,6},{2,4},{4,2},{6,0},{8,14},{10,12},{12,10},{14,8},{1,7},{3,5},... | collective-permute-start | bytes 245768 | tf_op jit(solution)/shard_map/ppermute | solution.py:372
  46.9 1.2 %collective-permute-start.18 = (bf16[40,1024]{1,0:T(8,128)(2,1)S(1)}, bf16[40,1024]{1,0:T(8,128)(2,1)S(1)}, u32[]{:S(2)}, u32[]{:S(2)}) collective-permute-start(bf16[40,1024]{1,0:T(8,128)(2,1)S(1)} %shard_map.124), channel_id=1, source_target_pairs={{0,8},{4,12},{8,0},{12,4},{1,9},{5,13},{9,1},{13,5},{2,10},{6,14},... | collective-permute-start | bytes 245768 | tf_op jit(solution)/shard_map/ppermute | solution.py:365
  48.3 2.6 %collective-permute-start.20 = (bf16[40,1024]{1,0:T(8,128)(2,1)S(1)}, bf16[40,1024]{1,0:T(8,128)(2,1)S(1)}, u32[]{:S(2)}, u32[]{:S(2)}) collective-permute-start(bf16[40,1024]{1,0:T(8,128)(2,1)S(1)} %shard_map.125), channel_id=1, source_target_pairs={{0,12},{4,8},{8,4},{12,0},{1,13},{5,9},{9,5},{13,1},{2,14},{6,10},... | collective-permute-start | bytes 245768 | tf_op jit(solution)/shard_map/ppermute | solution.py:365
  51.7 3.5 %collective-permute-done.18.refs_0_ = bf16[40,1024]{1,0:T(8,128)(2,1)S(1)} collective-permute-done((bf16[40,1024]{1,0:T(8,128)(2,1)S(1)}, bf16[40,1024]{1,0:T(8,128)(2,1)S(1)}, u32[]{:S(2)}, u32[]{:S(2)}) %collective-permute-start.18) | collective-permute-done | bytes 81952 | tf_op jit(solution)/shard_map/ppermute | solution.py:365
  55.6 0.9 %shard_map.129 = bf16[64,1024]{1,0:T(8,128)(2,1)} custom-call(bf16[384,128]{1,0:T(8,128)(2,1)S(1)} %get-tuple-element.47.place_ref, f32[64,1024]{1,0:T(8,128)S(1)} %shard_map.128.share_ref, bf16[40,1024]{1,0:T(8,128)(2,1)S(1)} %collective-permute-done.24.came_ref, f32[40,1024]{1,0:T(8,128)S(1)} %get-tuple-element.79.base_ref, ...), custom_call_target="tpu_custom_call" | custom-call | flops 1 | bytes 1 | tf_op jit(solution)/shard_map/pallas_call | solution.py:523
  (47 shorter events, 9.7 us)
Async XLA Ops:
  1.1 14.5 %collective-permute-start = (bf16[264,256]{1,0:T(8,128)(2,1)S(1)}, bf16[264,256]{1,0:T(8,128)(2,1)S(1)}, u32[]{:S(2)}, u32[]{:S(2)}) collective-permute-start(bf16[264,256]{1,0:T(8,128)(2,1)S(1)} %shard_map.109.refs_0_), channel_id=1, source_target_pairs={{0,8},{4,12},{8,0},{12,4},{1,9},{5,13},{9,1},{13,5},{2,10},{6,14},... | collective-permute-start | bytes 405512 | tf_op jit(solution)/shard_map/ppermute | solution.py:365
  6.3 9.3 %collective-permute-start.2 = (bf16[264,256]{1,0:T(8,128)(2,1)S(1)}, bf16[264,256]{1,0:T(8,128)(2,1)S(1)}, u32[]{:S(2)}, u32[]{:S(2)}) collective-permute-start(bf16[264,256]{1,0:T(8,128)(2,1)S(1)} %shard_map.110.refs_0_), channel_id=1, source_target_pairs={{0,4},{4,0},{8,12},{12,8},{1,5},{5,1},{9,13},{13,9},{2,6},{6,2},{1... | collective-permute-start | bytes 405512 | tf_op jit(solution)/shard_map/ppermute | solution.py:365
  9.3 6.9 %collective-permute-start.1 = (bf16[264,256]{1,0:T(8,128)(2,1)S(1)}, bf16[264,256]{1,0:T(8,128)(2,1)S(1)}, u32[]{:S(2)}, u32[]{:S(2)}) collective-permute-start(bf16[264,256]{1,0:T(8,128)(2,1)S(1)} %get-tuple-element.46), channel_id=1, source_target_pairs={{0,12},{4,8},{8,4},{12,0},{1,13},{5,9},{9,5},{13,1},{2,14},{6,10},... | collective-permute-start | bytes 405512 | tf_op jit(solution)/shard_map/ppermute | solution.py:365
  17.1 9.6 %collective-permute-start.3 = (bf16[160,256]{1,0:T(8,128)(2,1)S(1)}, bf16[160,256]{1,0:T(8,128)(2,1)S(1)}, u32[]{:S(2)}, u32[]{:S(2)}) collective-permute-start(bf16[160,256]{1,0:T(8,128)(2,1)S(1)} %get-tuple-element.48), channel_id=1, source_target_pairs={{0,8},{4,12},{8,0},{12,4},{1,9},{5,13},{9,1},{13,5},{2,10},{6,14},... | collective-permute-start | bytes 245768 | tf_op jit(solution)/shard_map/ppermute | solution.py:365
  21.1 7.0 %collective-permute-start.4 = (bf16[160,256]{1,0:T(8,128)(2,1)S(1)}, bf16[160,256]{1,0:T(8,128)(2,1)S(1)}, u32[]{:S(2)}, u32[]{:S(2)}) collective-permute-start(bf16[160,256]{1,0:T(8,128)(2,1)S(1)} %get-tuple-element.49), channel_id=1, source_target_pairs={{0,12},{4,8},{8,4},{12,0},{1,13},{5,9},{9,5},{13,1},{2,14},{6,10},... | collective-permute-start | bytes 245768 | tf_op jit(solution)/shard_map/ppermute | solution.py:365
  21.6 8.5 %collective-permute-start.8 = (bf16[160,256]{1,0:T(8,128)(2,1)S(1)}, bf16[160,256]{1,0:T(8,128)(2,1)S(1)}, u32[]{:S(2)}, u32[]{:S(2)}) collective-permute-start(bf16[160,256]{1,0:T(8,128)(2,1)S(1)} %get-tuple-element.50), channel_id=1, source_target_pairs={{0,6},{2,4},{4,2},{6,0},{8,14},{10,12},{12,10},{14,8},{1,7},{3,5},... | collective-permute-start | bytes 245768 | tf_op jit(solution)/shard_map/ppermute | solution.py:372
  22.7 8.1 %collective-permute-start.6 = (bf16[160,256]{1,0:T(8,128)(2,1)S(1)}, bf16[160,256]{1,0:T(8,128)(2,1)S(1)}, u32[]{:S(2)}, u32[]{:S(2)}) collective-permute-start(bf16[160,256]{1,0:T(8,128)(2,1)S(1)} %get-tuple-element.50), channel_id=1, source_target_pairs={{0,4},{4,0},{8,12},{12,8},{1,5},{5,1},{9,13},{13,9},{2,6},{6,2},{1... | collective-permute-start | bytes 245768 | tf_op jit(solution)/shard_map/ppermute | solution.py:365
  24.5 6.3 %collective-permute-start.9 = (bf16[160,256]{1,0:T(8,128)(2,1)S(1)}, bf16[160,256]{1,0:T(8,128)(2,1)S(1)}, u32[]{:S(2)}, u32[]{:S(2)}) collective-permute-start(bf16[160,256]{1,0:T(8,128)(2,1)S(1)} %get-tuple-element.51.refs_2_.right_ref), channel_id=1, source_target_pairs={{0,2},{2,0},{1,3},{3,1},{4,6},{6,4},{5,7},{7,5},{8,10},{10,8},{9,1... | collective-permute-start | bytes 245768 | tf_op jit(solution)/shard_map/ppermute | solution.py:368
  28.1 3.9 %collective-permute-start.7 = (bf16[160,512]{1,0:T(8,128)(2,1)S(1)}, bf16[160,512]{1,0:T(8,128)(2,1)S(1)}, u32[]{:S(2)}, u32[]{:S(2)}) collective-permute-start(bf16[160,512]{1,0:T(8,128)(2,1)S(1)} %shard_map.114.refs_0_), channel_id=1, source_target_pairs={{0,1},{1,0},{2,3},{3,2},{4,5},{5,4},{6,7},{7,6},{8,9},{9,8},{10,11... | collective-permute-start | bytes 491528 | tf_op jit(solution)/shard_map/ppermute | solution.py:368
  28.2 7.3 %collective-permute-start.5 = (bf16[160,512]{1,0:T(8,128)(2,1)S(1)}, bf16[160,512]{1,0:T(8,128)(2,1)S(1)}, u32[]{:S(2)}, u32[]{:S(2)}) collective-permute-start(bf16[160,512]{1,0:T(8,128)(2,1)S(1)} %shard_map.114.refs_0_), channel_id=1, source_target_pairs={{0,2},{2,0},{1,3},{3,1},{4,6},{6,4},{5,7},{7,5},{8,10},{10,8},{9,1... | collective-permute-start | bytes 491528 | tf_op jit(solution)/shard_map/ppermute | solution.py:368
  30.8 1.3 %collective-permute-start.10 = (bf16[160,256]{1,0:T(8,128)(2,1)S(1)}, bf16[160,256]{1,0:T(8,128)(2,1)S(1)}, u32[]{:S(2)}, u32[]{:S(2)}) collective-permute-start(bf16[160,256]{1,0:T(8,128)(2,1)S(1)} %collective-permute-done.6.refs_1_.left_ref), channel_id=1, source_target_pairs={{0,1},{1,0},{2,3},{3,2},{4,5},{5,4},{6,7},{7,6},{8,9},{9,8},{10,11... | collective-permute-start | bytes 245768 | tf_op jit(solution)/shard_map/ppermute | solution.py:368
  30.8 5.4 %collective-permute-start.13 = (bf16[160,512]{1,0:T(8,128)(2,1)S(1)}, bf16[160,512]{1,0:T(8,128)(2,1)S(1)}, u32[]{:S(2)}, u32[]{:S(2)}) collective-permute-start(bf16[160,512]{1,0:T(8,128)(2,1)S(1)} %shard_map.117.refs_1_), channel_id=1, source_target_pairs={{0,1},{1,0},{2,3},{3,2},{4,5},{5,4},{6,7},{7,6},{8,9},{9,8},{10,11... | collective-permute-start | bytes 491528 | tf_op jit(solution)/shard_map/ppermute | solution.py:368
  35.5 1.5 %collective-permute-start.12 = (bf16[160,512]{1,0:T(8,128)(2,1)S(1)}, bf16[160,512]{1,0:T(8,128)(2,1)S(1)}, u32[]{:S(2)}, u32[]{:S(2)}) collective-permute-start(bf16[160,512]{1,0:T(8,128)(2,1)S(1)} %collective-permute-done.5.refs_0_), channel_id=1, source_target_pairs={{0,1},{1,0},{2,3},{3,2},{4,5},{5,4},{6,7},{7,6},{8,9},{9,8},{10,11... | collective-permute-start | bytes 491528 | tf_op jit(solution)/shard_map/ppermute | solution.py:368
  35.7 3.1 %collective-permute-start.14 = (bf16[80,1024]{1,0:T(8,128)(2,1)S(1)}, bf16[80,1024]{1,0:T(8,128)(2,1)S(1)}, u32[]{:S(2)}, u32[]{:S(2)}) collective-permute-start(bf16[80,1024]{1,0:T(8,128)(2,1)S(1)} %get-tuple-element.59), channel_id=1, source_target_pairs={{0,1},{1,0},{2,3},{3,2},{4,5},{5,4},{6,7},{7,6},{8,9},{9,8},{10,11... | collective-permute-start | bytes 491528 | tf_op jit(solution)/shard_map/ppermute | solution.py:368
  36.1 2.8 %collective-permute-start.15 = (bf16[80,1024]{1,0:T(8,128)(2,1)S(1)}, bf16[80,1024]{1,0:T(8,128)(2,1)S(1)}, u32[]{:S(2)}, u32[]{:S(2)}) collective-permute-start(bf16[80,1024]{1,0:T(8,128)(2,1)S(1)} %get-tuple-element.60), channel_id=1, source_target_pairs={{0,1},{1,0},{2,3},{3,2},{4,5},{5,4},{6,7},{7,6},{8,9},{9,8},{10,11... | collective-permute-start | bytes 491528 | tf_op jit(solution)/shard_map/ppermute | solution.py:368
  39.7 1.6 %collective-permute-start.16 = (bf16[80,1024]{1,0:T(8,128)(2,1)S(1)}, bf16[80,1024]{1,0:T(8,128)(2,1)S(1)}, u32[]{:S(2)}, u32[]{:S(2)}) collective-permute-start(bf16[80,1024]{1,0:T(8,128)(2,1)S(1)} %get-tuple-element.62), channel_id=1, source_target_pairs={{0,1},{1,0},{2,3},{3,2},{4,5},{5,4},{6,7},{7,6},{8,9},{9,8},{10,11... | collective-permute-start | bytes 491528 | tf_op jit(solution)/shard_map/ppermute | solution.py:368
  40.0 4.5 %collective-permute-start.22 = (bf16[80,1024]{1,0:T(8,128)(2,1)S(1)}, bf16[80,1024]{1,0:T(8,128)(2,1)S(1)}, u32[]{:S(2)}, u32[]{:S(2)}) collective-permute-start(bf16[80,1024]{1,0:T(8,128)(2,1)S(1)} %get-tuple-element.76), channel_id=1, source_target_pairs={{0,1},{1,0},{2,3},{3,2},{4,5},{5,4},{6,7},{7,6},{8,9},{9,8},{10,11... | collective-permute-start | bytes 491528 | tf_op jit(solution)/shard_map/ppermute | solution.py:368
  41.4 5.4 %collective-permute-start.17 = (bf16[40,1024]{1,0:T(8,128)(2,1)S(1)}, bf16[40,1024]{1,0:T(8,128)(2,1)S(1)}, u32[]{:S(2)}, u32[]{:S(2)}) collective-permute-start(bf16[40,1024]{1,0:T(8,128)(2,1)S(1)} %get-tuple-element.68), channel_id=1, source_target_pairs={{0,2},{2,0},{1,3},{3,1},{4,6},{6,4},{5,7},{7,5},{8,10},{10,8},{9,1... | collective-permute-start | bytes 245768 | tf_op jit(solution)/shard_map/ppermute | solution.py:368
  42.6 5.7 %collective-permute-start.19 = (bf16[40,1024]{1,0:T(8,128)(2,1)S(1)}, bf16[40,1024]{1,0:T(8,128)(2,1)S(1)}, u32[]{:S(2)}, u32[]{:S(2)}) collective-permute-start(bf16[40,1024]{1,0:T(8,128)(2,1)S(1)} %get-tuple-element.71), channel_id=1, source_target_pairs={{0,2},{2,0},{1,3},{3,1},{4,6},{6,4},{5,7},{7,5},{8,10},{10,8},{9,1... | collective-permute-start | bytes 245768 | tf_op jit(solution)/shard_map/ppermute | solution.py:368
  43.7 8.0 %collective-permute-start.21 = (bf16[40,1024]{1,0:T(8,128)(2,1)S(1)}, bf16[40,1024]{1,0:T(8,128)(2,1)S(1)}, u32[]{:S(2)}, u32[]{:S(2)}) collective-permute-start(bf16[40,1024]{1,0:T(8,128)(2,1)S(1)} %get-tuple-element.75), channel_id=1, source_target_pairs={{0,4},{4,0},{8,12},{12,8},{1,5},{5,1},{9,13},{13,9},{2,6},{6,2},{1... | collective-permute-start | bytes 245768 | tf_op jit(solution)/shard_map/ppermute | solution.py:365
  44.5 7.2 %collective-permute-start.23 = (bf16[40,1024]{1,0:T(8,128)(2,1)S(1)}, bf16[40,1024]{1,0:T(8,128)(2,1)S(1)}, u32[]{:S(2)}, u32[]{:S(2)}) collective-permute-start(bf16[40,1024]{1,0:T(8,128)(2,1)S(1)} %get-tuple-element.77), channel_id=1, source_target_pairs={{0,6},{2,4},{4,2},{6,0},{8,14},{10,12},{12,10},{14,8},{1,7},{3,5},... | collective-permute-start | bytes 245768 | tf_op jit(solution)/shard_map/ppermute | solution.py:372
  46.9 8.4 %collective-permute-start.18 = (bf16[40,1024]{1,0:T(8,128)(2,1)S(1)}, bf16[40,1024]{1,0:T(8,128)(2,1)S(1)}, u32[]{:S(2)}, u32[]{:S(2)}) collective-permute-start(bf16[40,1024]{1,0:T(8,128)(2,1)S(1)} %shard_map.124), channel_id=1, source_target_pairs={{0,8},{4,12},{8,0},{12,4},{1,9},{5,13},{9,1},{13,5},{2,10},{6,14},... | collective-permute-start | bytes 245768 | tf_op jit(solution)/shard_map/ppermute | solution.py:365
  48.3 6.9 %collective-permute-start.20 = (bf16[40,1024]{1,0:T(8,128)(2,1)S(1)}, bf16[40,1024]{1,0:T(8,128)(2,1)S(1)}, u32[]{:S(2)}, u32[]{:S(2)}) collective-permute-start(bf16[40,1024]{1,0:T(8,128)(2,1)S(1)} %shard_map.125), channel_id=1, source_target_pairs={{0,12},{4,8},{8,4},{12,0},{1,13},{5,9},{9,5},{13,1},{2,14},{6,10},... | collective-permute-start | bytes 245768 | tf_op jit(solution)/shard_map/ppermute | solution.py:365
  51.0 4.6 %collective-permute-start.24 = (bf16[40,1024]{1,0:T(8,128)(2,1)S(1)}, bf16[40,1024]{1,0:T(8,128)(2,1)S(1)}, u32[]{:S(2)}, u32[]{:S(2)}) collective-permute-start(bf16[40,1024]{1,0:T(8,128)(2,1)S(1)} %get-tuple-element.78), channel_id=1, source_target_pairs={{0,2},{2,0},{1,3},{3,1},{4,6},{6,4},{5,7},{7,5},{8,10},{10,8},{9,1... | collective-permute-start | bytes 245768 | tf_op jit(solution)/shard_map/ppermute | solution.py:368
  (1 other events, 1.3 us)

commit v8 on v7

--- a/solution.py
+++ b/solution.py
@@ -183,10 +183,10 @@
     expert = here ^ iota((META, count), 0)
     named = ((first == expert) | (second == expert)) & (iota((META, count), 0) < experts)
     before = (iota((count, count), 0) < iota((count, count), 1)) & (
-        iota((count, count), 0) // rows == iota((count, count), 1) // rows
+        iota((count, 1), 0) // rows == iota((1, count), 1) // rows
     )
     slot = dot(named.astype(BF16), before.astype(BF16)).astype(jnp.int32)
-    block = (iota((META, count), 1) // rows) ^ iota((META, count), 0)
+    block = (iota((1, count), 1) // rows) ^ iota((META, 1), 0)
     spot = jnp.where(named, block * cap + slot, -1)
     home = jnp.where(named, slot, -1)[:, 0:rows].astype(F32).astype(BF16)
     home = dot_nt(same[0:rows, 0:rows], home).astype(jnp.int32)
@@ -499,7 +499,6 @@
         return call(join_kernel, [struct(cap, columns)], [IN_VMEM] * 3)(came, base, factor)[0]
 
     base2, base3, factor2, factor3 = base(2 * cap, got[1])
-    theirs[1], base2 = lax.optimization_barrier((theirs[1], base2))
     base0, near1, factor0 = call(
         low_kernel,
         [struct(cap, columns, F32), struct(cap, columns), struct(cap, HEAD, F32)],
@@ -515,7 +514,7 @@
         across(plain1),
     ]
     share = call(
-        functools.partial(sum_kernel, 512, ORDER[:-1]),
+        functools.partial(sum_kernel, 1024, ORDER[:-1]),
         [struct(rows, columns, F32)],
         [IN_VMEM] * (1 + experts),
         moved=LATER,

time: 56.7 us -> 56.7 us (level)
  transfers between devices with their start and end apart: 25 -> 25, of which waited for: 10 -> 9; matrix products, arithmetic and copies ran while one was open for 0% -> 0% of each run, Pallas kernels for 28% -> 28%
where the time goes in v8:
time: 56.7 us; the launch traced here: 56.5 us
  starting transfers between devices  26.9 us (47%)
  Pallas kernels  19.5 us (34%)
  waiting for transfers between devices  9.85 us (17%)
    ppermute x9, starting transfers between devices, along(): lax.ppermute(array, 'expert', [(i, i ^ step) for i in range(experts)])  16.8 us
    ppermute x9, waiting for transfers between devices, along(): lax.ppermute(array, 'expert', [(i, i ^ step) for i in range(experts)])  8.05 us
    ppermute x14, starting transfers between devices, swap(): return lax.ppermute(array, axis, [(0, 1), (1, 0)])  7.13 us
    pallas_call x1, Pallas kernels, head_shards(): pl.pallas_call(functools.partial(prefetch_kernel, experts), out_shape=[pl...  6.21 us
    pallas_call x2, Pallas kernels, first(): call(functools.partial(first_kernel, 512), [struct(count, hidden_units)],...  3.76 us
    pallas_call x3, Pallas kernels, pack(): call(functools.partial(pack_kernel, steps), [struct(4 * rows + KINDS, wid...  3.58 us
    ppermute x2, starting transfers between devices, across(): return lax.ppermute(array, ('expert', 'dp'), pairs)  3 us
    pallas_call x2, Pallas kernels, half(): call(functools.partial(half_kernel, 512, other), [struct(count // parts,...  1.74 us
  transfers between devices with their start and end apart: 25, of which 9 were waited for; matrix products, arithmetic and copies ran while one was open for 0% of the time, Pallas kernels for 28%

profile of v8, /device:TPU:0, one launch (start us, length us, event | category | flops | bytes accessed | tf_op | source)
XLA Modules:
  0.0 56.5 jit_solution(8680484502973215472)
XLA Ops:
  0.0 1.1 %shard_map.109.refs_0_ = bf16[264,256]{1,0:T(8,128)(2,1)S(1)} custom-call(bf16[64,1024]{1,0:T(8,128)(2,1)} %q_hbm.5, bf16[64,2,1024]{2,1,0:T(2,128)(2,1)} %m_hbm.5, bf16[64,1024]{1,0:T(8,128)(2,1)} %h_hbm.5, s32[1,64]{1,0:T(1,128)} %bitcast.18, s32[1,64]{1,0:T(1,128)} %bitcast.21, s32[2,64]{1,0:T(2,128)} %bitcast.10, f32[2,64]{1,0:T(2,128)} %bitcast.13), custom_call_target="tpu_custom_call" | custom-call | tf_op jit(solution)/shard_map/pallas_call | solution.py:375
  1.1 4.1 %collective-permute-start = (bf16[264,256]{1,0:T(8,128)(2,1)S(1)}, bf16[264,256]{1,0:T(8,128)(2,1)S(1)}, u32[]{:S(2)}, u32[]{:S(2)}) collective-permute-start(bf16[264,256]{1,0:T(8,128)(2,1)S(1)} %shard_map.109.refs_0_), channel_id=1, source_target_pairs={{0,8},{4,12},{8,0},{12,4},{1,9},{5,13},{9,1},{13,5},{2,10},{6,14},... | collective-permute-start | bytes 405512 | tf_op jit(solution)/shard_map/ppermute | solution.py:365
  5.2 1.1 %shard_map.110.refs_0_ = bf16[264,256]{1,0:T(8,128)(2,1)S(1)} custom-call(bf16[64,1024]{1,0:T(8,128)(2,1)} %q_hbm.5, bf16[64,2,1024]{2,1,0:T(2,128)(2,1)} %m_hbm.5, bf16[64,1024]{1,0:T(8,128)(2,1)} %h_hbm.5, s32[1,64]{1,0:T(1,128)} %bitcast.19, s32[1,64]{1,0:T(1,128)} %bitcast.22, s32[2,64]{1,0:T(2,128)} %bitcast.11, f32[2,64]{1,0:T(2,128)} %bitcast.14, ...), custom_call_target="tpu_custom_call" | custom-call | bytes 16777216 | tf_op jit(solution)/shard_map/pallas_call | solution.py:375
  6.3 1.6 %collective-permute-start.2 = (bf16[264,256]{1,0:T(8,128)(2,1)S(1)}, bf16[264,256]{1,0:T(8,128)(2,1)S(1)}, u32[]{:S(2)}, u32[]{:S(2)}) collective-permute-start(bf16[264,256]{1,0:T(8,128)(2,1)S(1)} %shard_map.110.refs_0_), channel_id=1, source_target_pairs={{0,4},{4,0},{8,12},{12,8},{1,5},{5,1},{9,13},{13,9},{2,6},{6,2},{1... | collective-permute-start | bytes 405512 | tf_op jit(solution)/shard_map/ppermute | solution.py:365
  8.0 1.4 %shard_map.111 = (bf16[264,256]{1,0:T(8,128)(2,1)S(1)}, bf16[264,256]{1,0:T(8,128)(2,1)S(1)}) custom-call(bf16[64,1024]{1,0:T(8,128)(2,1)} %q_hbm.5, bf16[64,2,1024]{2,1,0:T(2,128)(2,1)} %m_hbm.5, bf16[64,1024]{1,0:T(8,128)(2,1)} %h_hbm.5, s32[1,64]{1,0:T(1,128)} %bitcast.20, s32[1,64]{1,0:T(1,128)} %bitcast.23, s32[2,64]{1,0:T(2,128)} %bitcast.12, ...), custom_call_target="tpu_custom_call" | custom-call | bytes 16777216 | tf_op jit(solution)/shard_map/pallas_call | solution.py:375
  9.4 6.2 %shard_map.112 = (bf16[2048,2048]{1,0:T(8,128)(2,1)S(1)}, bf16[2048,2048]{1,0:T(8,128)(2,1)S(1)}, f32[1,2048]{1,0:T(1,128)S(1)}, f32[1,2048]{1,0:T(1,128)S(1)}) custom-call(bf16[2048,2048]{1,0:T(8,128)(2,1)} %bitcast.8, bf16[2048,2048]{1,0:T(8,128)(2,1)} %bitcast.9, f32[1,2048]{1,0:T(1,128)} %bitcast.16, f32[1,2048]{1,0:T(1,128)} %bitcast.17, ...), custom_call_target="tpu_custom_call" | custom-call | bytes 33554432 | tf_op jit(solution)/shard_map/pallas_call | solution.py:405
  17.1 4.0 %collective-permute-start.3 = (bf16[160,256]{1,0:T(8,128)(2,1)S(1)}, bf16[160,256]{1,0:T(8,128)(2,1)S(1)}, u32[]{:S(2)}, u32[]{:S(2)}) collective-permute-start(bf16[160,256]{1,0:T(8,128)(2,1)S(1)} %get-tuple-element.46), channel_id=1, source_target_pairs={{0,8},{4,12},{8,0},{12,4},{1,9},{5,13},{9,1},{13,5},{2,10},{6,14},... | collective-permute-start | bytes 245768 | tf_op jit(solution)/shard_map/ppermute | solution.py:365
  21.6 1.1 %collective-permute-start.8 = (bf16[160,256]{1,0:T(8,128)(2,1)S(1)}, bf16[160,256]{1,0:T(8,128)(2,1)S(1)}, u32[]{:S(2)}, u32[]{:S(2)}) collective-permute-start(bf16[160,256]{1,0:T(8,128)(2,1)S(1)} %get-tuple-element.48), channel_id=1, source_target_pairs={{0,6},{2,4},{4,2},{6,0},{8,14},{10,12},{12,10},{14,8},{1,7},{3,5},... | collective-permute-start | bytes 245768 | tf_op jit(solution)/shard_map/ppermute | solution.py:372
  22.7 1.8 %collective-permute-start.6 = (bf16[160,256]{1,0:T(8,128)(2,1)S(1)}, bf16[160,256]{1,0:T(8,128)(2,1)S(1)}, u32[]{:S(2)}, u32[]{:S(2)}) collective-permute-start(bf16[160,256]{1,0:T(8,128)(2,1)S(1)} %get-tuple-element.48), channel_id=1, source_target_pairs={{0,4},{4,0},{8,12},{12,8},{1,5},{5,1},{9,13},{13,9},{2,6},{6,2},{1... | collective-permute-start | bytes 245768 | tf_op jit(solution)/shard_map/ppermute | solution.py:365
  25.0 1.7 %collective-permute-done.3.left_ref = bf16[160,256]{1,0:T(8,128)(2,1)S(1)} collective-permute-done((bf16[160,256]{1,0:T(8,128)(2,1)S(1)}, bf16[160,256]{1,0:T(8,128)(2,1)S(1)}, u32[]{:S(2)}, u32[]{:S(2)}) %collective-permute-start.3) | collective-permute-done | bytes 81952 | tf_op jit(solution)/shard_map/ppermute | solution.py:365
  26.7 1.3 %collective-permute-done.4.right_ref = bf16[160,256]{1,0:T(8,128)(2,1)S(1)} collective-permute-done((bf16[160,256]{1,0:T(8,128)(2,1)S(1)}, bf16[160,256]{1,0:T(8,128)(2,1)S(1)}, u32[]{:S(2)}, u32[]{:S(2)}) %collective-permute-start.4) | collective-permute-done | bytes 81952 | tf_op jit(solution)/shard_map/ppermute | solution.py:365
  28.2 1.7 %collective-permute-start.5 = (bf16[160,512]{1,0:T(8,128)(2,1)S(1)}, bf16[160,512]{1,0:T(8,128)(2,1)S(1)}, u32[]{:S(2)}, u32[]{:S(2)}) collective-permute-start(bf16[160,512]{1,0:T(8,128)(2,1)S(1)} %shard_map.114.refs_0_), channel_id=1, source_target_pairs={{0,2},{2,0},{1,3},{3,1},{4,6},{6,4},{5,7},{7,5},{8,10},{10,8},{9,1... | collective-permute-start | bytes 491528 | tf_op jit(solution)/shard_map/ppermute | solution.py:368
  32.0 1.9 %shard_map.115.a_ref = bf16[160,2048]{1,0:T(8,128)(2,1)S(1)} custom-call(bf16[160,512]{1,0:T(8,128)(2,1)S(1)} %shard_map.114.refs_0_, bf16[160,256]{1,0:T(8,128)(2,1)S(1)} %collective-permute-done.6.refs_1_.left_ref, bf16[160,256]{1,0:T(8,128)(2,1)S(1)} %get-tuple-element.49.refs_2_.right_ref, bf16[160,512]{1,0:T(8,128)(2,1)S(1)} %collective-permute-done.7.refs_3_, ...), custom_call_target="tpu_custom_call" | custom-call | tf_op jit(solution)/shard_map/pallas_call | solution.py:442
  33.9 1.5 %shard_map.116 = (bf16[160,1024]{1,0:T(8,128)(2,1)S(1)}, bf16[80,1024]{1,0:T(8,128)(2,1)S(1)}, bf16[80,1024]{1,0:T(8,128)(2,1)S(1)}) custom-call(bf16[160,2048]{1,0:T(8,128)(2,1)S(1)} %shard_map.115.a_ref, bf16[2048,2048]{1,0:T(8,128)(2,1)S(1)} %get-tuple-element.43.w2_ref.w_ref), custom_call_target="tpu_custom_call" | custom-call | tf_op jit(solution)/shard_map/pallas_call | solution.py:462
  37.0 1.9 %shard_map.118.a_ref = bf16[160,2048]{1,0:T(8,128)(2,1)S(1)} custom-call(bf16[160,512]{1,0:T(8,128)(2,1)S(1)} %collective-permute-done.5.refs_0_, bf16[160,512]{1,0:T(8,128)(2,1)S(1)} %shard_map.117.refs_1_, bf16[160,512]{1,0:T(8,128)(2,1)S(1)} %collective-permute-done.12.refs_2_, bf16[160,512]{1,0:T(8,128)(2,1)S(1)} %collective-permute-done.13.refs_3_, ...), custom_call_target="tpu_custom_call" | custom-call | flops 1342177280 | bytes 8388608 | tf_op jit(solution)/shard_map/pallas_call | solution.py:442
  38.9 0.9 %shard_map.120 = (bf16[80,1024]{1,0:T(8,128)(2,1)S(1)}, bf16[80,1024]{1,0:T(8,128)(2,1)S(1)}) custom-call(bf16[160,2048]{1,0:T(8,128)(2,1)S(1)} %shard_map.118.a_ref, bf16[2048,2048]{1,0:T(8,128)(2,1)S(1)} %get-tuple-element.43.w2_ref.w_ref), custom_call_target="tpu_custom_call" | custom-call | flops 671088640 | bytes 4194304 | tf_op jit(solution)/shard_map/pallas_call | solution.py:474
  40.3 0.9 %shard_map.119.kept_ref = bf16[160,1024]{1,0:T(8,128)(2,1)S(1)} custom-call(bf16[160,2048]{1,0:T(8,128)(2,1)S(1)} %shard_map.118.a_ref, bf16[2048,2048]{1,0:T(8,128)(2,1)S(1)} %get-tuple-element.43.w2_ref.w_ref), custom_call_target="tpu_custom_call" | custom-call | flops 671088640 | bytes 4194304 | tf_op jit(solution)/shard_map/pallas_call | solution.py:474
  41.3 1.1 %collective-permute-start.17 = (bf16[40,1024]{1,0:T(8,128)(2,1)S(1)}, bf16[40,1024]{1,0:T(8,128)(2,1)S(1)}, u32[]{:S(2)}, u32[]{:S(2)}) collective-permute-start(bf16[40,1024]{1,0:T(8,128)(2,1)S(1)} %get-tuple-element.61), channel_id=1, source_target_pairs={{0,2},{2,0},{1,3},{3,1},{4,6},{6,4},{5,7},{7,5},{8,10},{10,8},{9,1... | collective-permute-start | bytes 245768 | tf_op jit(solution)/shard_map/ppermute | solution.py:368
  42.4 1.0 %collective-permute-start.19 = (bf16[40,1024]{1,0:T(8,128)(2,1)S(1)}, bf16[40,1024]{1,0:T(8,128)(2,1)S(1)}, u32[]{:S(2)}, u32[]{:S(2)}) collective-permute-start(bf16[40,1024]{1,0:T(8,128)(2,1)S(1)} %get-tuple-element.67), channel_id=1, source_target_pairs={{0,2},{2,0},{1,3},{3,1},{4,6},{6,4},{5,7},{7,5},{8,10},{10,8},{9,1... | collective-permute-start | bytes 245768 | tf_op jit(solution)/shard_map/ppermute | solution.py:368
  44.5 1.9 %collective-permute-start.23 = (bf16[40,1024]{1,0:T(8,128)(2,1)S(1)}, bf16[40,1024]{1,0:T(8,128)(2,1)S(1)}, u32[]{:S(2)}, u32[]{:S(2)}) collective-permute-start(bf16[40,1024]{1,0:T(8,128)(2,1)S(1)} %get-tuple-element.73), channel_id=1, source_target_pairs={{0,6},{2,4},{4,2},{6,0},{8,14},{10,12},{12,10},{14,8},{1,7},{3,5},... | collective-permute-start | bytes 245768 | tf_op jit(solution)/shard_map/ppermute | solution.py:372
  46.7 1.4 %collective-permute-start.18 = (bf16[40,1024]{1,0:T(8,128)(2,1)S(1)}, bf16[40,1024]{1,0:T(8,128)(2,1)S(1)}, u32[]{:S(2)}, u32[]{:S(2)}) collective-permute-start(bf16[40,1024]{1,0:T(8,128)(2,1)S(1)} %shard_map.124), channel_id=1, source_target_pairs={{0,8},{4,12},{8,0},{12,4},{1,9},{5,13},{9,1},{13,5},{2,10},{6,14},... | collective-permute-start | bytes 245768 | tf_op jit(solution)/shard_map/ppermute | solution.py:365
  48.2 2.5 %collective-permute-start.20 = (bf16[40,1024]{1,0:T(8,128)(2,1)S(1)}, bf16[40,1024]{1,0:T(8,128)(2,1)S(1)}, u32[]{:S(2)}, u32[]{:S(2)}) collective-permute-start(bf16[40,1024]{1,0:T(8,128)(2,1)S(1)} %shard_map.125), channel_id=1, source_target_pairs={{0,12},{4,8},{8,4},{12,0},{1,13},{5,9},{9,5},{13,1},{2,14},{6,10},... | collective-permute-start | bytes 245768 | tf_op jit(solution)/shard_map/ppermute | solution.py:365
  51.5 3.7 %collective-permute-done.18.refs_0_ = bf16[40,1024]{1,0:T(8,128)(2,1)S(1)} collective-permute-done((bf16[40,1024]{1,0:T(8,128)(2,1)S(1)}, bf16[40,1024]{1,0:T(8,128)(2,1)S(1)}, u32[]{:S(2)}, u32[]{:S(2)}) %collective-permute-start.18) | collective-permute-done | bytes 81952 | tf_op jit(solution)/shard_map/ppermute | solution.py:365
  55.6 0.9 %shard_map.129 = bf16[64,1024]{1,0:T(8,128)(2,1)} custom-call(bf16[384,128]{1,0:T(8,128)(2,1)S(1)} %get-tuple-element.45.place_ref, f32[64,1024]{1,0:T(8,128)S(1)} %shard_map.128.share_ref, bf16[40,1024]{1,0:T(8,128)(2,1)S(1)} %collective-permute-done.24.came_ref, f32[40,1024]{1,0:T(8,128)S(1)} %get-tuple-element.75.base_ref, ...), custom_call_target="tpu_custom_call" | custom-call | flops 1 | bytes 1 | tf_op jit(solution)/shard_map/pallas_call | solution.py:522
  (47 shorter events, 9.5 us)
Async XLA Ops:
  1.1 14.5 %collective-permute-start = (bf16[264,256]{1,0:T(8,128)(2,1)S(1)}, bf16[264,256]{1,0:T(8,128)(2,1)S(1)}, u32[]{:S(2)}, u32[]{:S(2)}) collective-permute-start(bf16[264,256]{1,0:T(8,128)(2,1)S(1)} %shard_map.109.refs_0_), channel_id=1, source_target_pairs={{0,8},{4,12},{8,0},{12,4},{1,9},{5,13},{9,1},{13,5},{2,10},{6,14},... | collective-permute-start | bytes 405512 | tf_op jit(solution)/shard_map/ppermute | solution.py:365
  6.3 9.3 %collective-permute-start.2 = (bf16[264,256]{1,0:T(8,128)(2,1)S(1)}, bf16[264,256]{1,0:T(8,128)(2,1)S(1)}, u32[]{:S(2)}, u32[]{:S(2)}) collective-permute-start(bf16[264,256]{1,0:T(8,128)(2,1)S(1)} %shard_map.110.refs_0_), channel_id=1, source_target_pairs={{0,4},{4,0},{8,12},{12,8},{1,5},{5,1},{9,13},{13,9},{2,6},{6,2},{1... | collective-permute-start | bytes 405512 | tf_op jit(solution)/shard_map/ppermute | solution.py:365
  9.3 6.9 %collective-permute-start.1 = (bf16[264,256]{1,0:T(8,128)(2,1)S(1)}, bf16[264,256]{1,0:T(8,128)(2,1)S(1)}, u32[]{:S(2)}, u32[]{:S(2)}) collective-permute-start(bf16[264,256]{1,0:T(8,128)(2,1)S(1)} %get-tuple-element.44), channel_id=1, source_target_pairs={{0,12},{4,8},{8,4},{12,0},{1,13},{5,9},{9,5},{13,1},{2,14},{6,10},... | collective-permute-start | bytes 405512 | tf_op jit(solution)/shard_map/ppermute | solution.py:365
  17.1 9.6 %collective-permute-start.3 = (bf16[160,256]{1,0:T(8,128)(2,1)S(1)}, bf16[160,256]{1,0:T(8,128)(2,1)S(1)}, u32[]{:S(2)}, u32[]{:S(2)}) collective-permute-start(bf16[160,256]{1,0:T(8,128)(2,1)S(1)} %get-tuple-element.46), channel_id=1, source_target_pairs={{0,8},{4,12},{8,0},{12,4},{1,9},{5,13},{9,1},{13,5},{2,10},{6,14},... | collective-permute-start | bytes 245768 | tf_op jit(solution)/shard_map/ppermute | solution.py:365
  21.1 7.0 %collective-permute-start.4 = (bf16[160,256]{1,0:T(8,128)(2,1)S(1)}, bf16[160,256]{1,0:T(8,128)(2,1)S(1)}, u32[]{:S(2)}, u32[]{:S(2)}) collective-permute-start(bf16[160,256]{1,0:T(8,128)(2,1)S(1)} %get-tuple-element.47), channel_id=1, source_target_pairs={{0,12},{4,8},{8,4},{12,0},{1,13},{5,9},{9,5},{13,1},{2,14},{6,10},... | collective-permute-start | bytes 245768 | tf_op jit(solution)/shard_map/ppermute | solution.py:365
  21.6 8.5 %collective-permute-start.8 = (bf16[160,256]{1,0:T(8,128)(2,1)S(1)}, bf16[160,256]{1,0:T(8,128)(2,1)S(1)}, u32[]{:S(2)}, u32[]{:S(2)}) collective-permute-start(bf16[160,256]{1,0:T(8,128)(2,1)S(1)} %get-tuple-element.48), channel_id=1, source_target_pairs={{0,6},{2,4},{4,2},{6,0},{8,14},{10,12},{12,10},{14,8},{1,7},{3,5},... | collective-permute-start | bytes 245768 | tf_op jit(solution)/shard_map/ppermute | solution.py:372
  22.7 8.1 %collective-permute-start.6 = (bf16[160,256]{1,0:T(8,128)(2,1)S(1)}, bf16[160,256]{1,0:T(8,128)(2,1)S(1)}, u32[]{:S(2)}, u32[]{:S(2)}) collective-permute-start(bf16[160,256]{1,0:T(8,128)(2,1)S(1)} %get-tuple-element.48), channel_id=1, source_target_pairs={{0,4},{4,0},{8,12},{12,8},{1,5},{5,1},{9,13},{13,9},{2,6},{6,2},{1... | collective-permute-start | bytes 245768 | tf_op jit(solution)/shard_map/ppermute | solution.py:365
  24.5 6.3 %collective-permute-start.9 = (bf16[160,256]{1,0:T(8,128)(2,1)S(1)}, bf16[160,256]{1,0:T(8,128)(2,1)S(1)}, u32[]{:S(2)}, u32[]{:S(2)}) collective-permute-start(bf16[160,256]{1,0:T(8,128)(2,1)S(1)} %get-tuple-element.49.refs_2_.right_ref), channel_id=1, source_target_pairs={{0,2},{2,0},{1,3},{3,1},{4,6},{6,4},{5,7},{7,5},{8,10},{10,8},{9,1... | collective-permute-start | bytes 245768 | tf_op jit(solution)/shard_map/ppermute | solution.py:368
  28.1 3.9 %collective-permute-start.7 = (bf16[160,512]{1,0:T(8,128)(2,1)S(1)}, bf16[160,512]{1,0:T(8,128)(2,1)S(1)}, u32[]{:S(2)}, u32[]{:S(2)}) collective-permute-start(bf16[160,512]{1,0:T(8,128)(2,1)S(1)} %shard_map.114.refs_0_), channel_id=1, source_target_pairs={{0,1},{1,0},{2,3},{3,2},{4,5},{5,4},{6,7},{7,6},{8,9},{9,8},{10,11... | collective-permute-start | bytes 491528 | tf_op jit(solution)/shard_map/ppermute | solution.py:368
  28.2 7.3 %collective-permute-start.5 = (bf16[160,512]{1,0:T(8,128)(2,1)S(1)}, bf16[160,512]{1,0:T(8,128)(2,1)S(1)}, u32[]{:S(2)}, u32[]{:S(2)}) collective-permute-start(bf16[160,512]{1,0:T(8,128)(2,1)S(1)} %shard_map.114.refs_0_), channel_id=1, source_target_pairs={{0,2},{2,0},{1,3},{3,1},{4,6},{6,4},{5,7},{7,5},{8,10},{10,8},{9,1... | collective-permute-start | bytes 491528 | tf_op jit(solution)/shard_map/ppermute | solution.py:368
  30.8 1.3 %collective-permute-start.10 = (bf16[160,256]{1,0:T(8,128)(2,1)S(1)}, bf16[160,256]{1,0:T(8,128)(2,1)S(1)}, u32[]{:S(2)}, u32[]{:S(2)}) collective-permute-start(bf16[160,256]{1,0:T(8,128)(2,1)S(1)} %collective-permute-done.6.refs_1_.left_ref), channel_id=1, source_target_pairs={{0,1},{1,0},{2,3},{3,2},{4,5},{5,4},{6,7},{7,6},{8,9},{9,8},{10,11... | collective-permute-start | bytes 245768 | tf_op jit(solution)/shard_map/ppermute | solution.py:368
  30.8 5.4 %collective-permute-start.13 = (bf16[160,512]{1,0:T(8,128)(2,1)S(1)}, bf16[160,512]{1,0:T(8,128)(2,1)S(1)}, u32[]{:S(2)}, u32[]{:S(2)}) collective-permute-start(bf16[160,512]{1,0:T(8,128)(2,1)S(1)} %shard_map.117.refs_1_), channel_id=1, source_target_pairs={{0,1},{1,0},{2,3},{3,2},{4,5},{5,4},{6,7},{7,6},{8,9},{9,8},{10,11... | collective-permute-start | bytes 491528 | tf_op jit(solution)/shard_map/ppermute | solution.py:368
  35.5 1.5 %collective-permute-start.12 = (bf16[160,512]{1,0:T(8,128)(2,1)S(1)}, bf16[160,512]{1,0:T(8,128)(2,1)S(1)}, u32[]{:S(2)}, u32[]{:S(2)}) collective-permute-start(bf16[160,512]{1,0:T(8,128)(2,1)S(1)} %collective-permute-done.5.refs_0_), channel_id=1, source_target_pairs={{0,1},{1,0},{2,3},{3,2},{4,5},{5,4},{6,7},{7,6},{8,9},{9,8},{10,11... | collective-permute-start | bytes 491528 | tf_op jit(solution)/shard_map/ppermute | solution.py:368
  35.7 3.1 %collective-permute-start.14 = (bf16[80,1024]{1,0:T(8,128)(2,1)S(1)}, bf16[80,1024]{1,0:T(8,128)(2,1)S(1)}, u32[]{:S(2)}, u32[]{:S(2)}) collective-permute-start(bf16[80,1024]{1,0:T(8,128)(2,1)S(1)} %get-tuple-element.57), channel_id=1, source_target_pairs={{0,1},{1,0},{2,3},{3,2},{4,5},{5,4},{6,7},{7,6},{8,9},{9,8},{10,11... | collective-permute-start | bytes 491528 | tf_op jit(solution)/shard_map/ppermute | solution.py:368
  36.1 2.8 %collective-permute-start.15 = (bf16[80,1024]{1,0:T(8,128)(2,1)S(1)}, bf16[80,1024]{1,0:T(8,128)(2,1)S(1)}, u32[]{:S(2)}, u32[]{:S(2)}) collective-permute-start(bf16[80,1024]{1,0:T(8,128)(2,1)S(1)} %get-tuple-element.58), channel_id=1, source_target_pairs={{0,1},{1,0},{2,3},{3,2},{4,5},{5,4},{6,7},{7,6},{8,9},{9,8},{10,11... | collective-permute-start | bytes 491528 | tf_op jit(solution)/shard_map/ppermute | solution.py:368
  39.7 1.5 %collective-permute-start.16 = (bf16[80,1024]{1,0:T(8,128)(2,1)S(1)}, bf16[80,1024]{1,0:T(8,128)(2,1)S(1)}, u32[]{:S(2)}, u32[]{:S(2)}) collective-permute-start(bf16[80,1024]{1,0:T(8,128)(2,1)S(1)} %get-tuple-element.60), channel_id=1, source_target_pairs={{0,1},{1,0},{2,3},{3,2},{4,5},{5,4},{6,7},{7,6},{8,9},{9,8},{10,11... | collective-permute-start | bytes 491528 | tf_op jit(solution)/shard_map/ppermute | solution.py:368
  40.0 4.5 %collective-permute-start.22 = (bf16[80,1024]{1,0:T(8,128)(2,1)S(1)}, bf16[80,1024]{1,0:T(8,128)(2,1)S(1)}, u32[]{:S(2)}, u32[]{:S(2)}) collective-permute-start(bf16[80,1024]{1,0:T(8,128)(2,1)S(1)} %get-tuple-element.72), channel_id=1, source_target_pairs={{0,1},{1,0},{2,3},{3,2},{4,5},{5,4},{6,7},{7,6},{8,9},{9,8},{10,11... | collective-permute-start | bytes 491528 | tf_op jit(solution)/shard_map/ppermute | solution.py:368
  41.3 5.4 %collective-permute-start.17 = (bf16[40,1024]{1,0:T(8,128)(2,1)S(1)}, bf16[40,1024]{1,0:T(8,128)(2,1)S(1)}, u32[]{:S(2)}, u32[]{:S(2)}) collective-permute-start(bf16[40,1024]{1,0:T(8,128)(2,1)S(1)} %get-tuple-element.61), channel_id=1, source_target_pairs={{0,2},{2,0},{1,3},{3,1},{4,6},{6,4},{5,7},{7,5},{8,10},{10,8},{9,1... | collective-permute-start | bytes 245768 | tf_op jit(solution)/shard_map/ppermute | solution.py:368
  42.4 5.7 %collective-permute-start.19 = (bf16[40,1024]{1,0:T(8,128)(2,1)S(1)}, bf16[40,1024]{1,0:T(8,128)(2,1)S(1)}, u32[]{:S(2)}, u32[]{:S(2)}) collective-permute-start(bf16[40,1024]{1,0:T(8,128)(2,1)S(1)} %get-tuple-element.67), channel_id=1, source_target_pairs={{0,2},{2,0},{1,3},{3,1},{4,6},{6,4},{5,7},{7,5},{8,10},{10,8},{9,1... | collective-permute-start | bytes 245768 | tf_op jit(solution)/shard_map/ppermute | solution.py:368
  43.7 7.8 %collective-permute-start.21 = (bf16[40,1024]{1,0:T(8,128)(2,1)S(1)}, bf16[40,1024]{1,0:T(8,128)(2,1)S(1)}, u32[]{:S(2)}, u32[]{:S(2)}) collective-permute-start(bf16[40,1024]{1,0:T(8,128)(2,1)S(1)} %get-tuple-element.71), channel_id=1, source_target_pairs={{0,4},{4,0},{8,12},{12,8},{1,5},{5,1},{9,13},{13,9},{2,6},{6,2},{1... | collective-permute-start | bytes 245768 | tf_op jit(solution)/shard_map/ppermute | solution.py:365
  44.5 7.0 %collective-permute-start.23 = (bf16[40,1024]{1,0:T(8,128)(2,1)S(1)}, bf16[40,1024]{1,0:T(8,128)(2,1)S(1)}, u32[]{:S(2)}, u32[]{:S(2)}) collective-permute-start(bf16[40,1024]{1,0:T(8,128)(2,1)S(1)} %get-tuple-element.73), channel_id=1, source_target_pairs={{0,6},{2,4},{4,2},{6,0},{8,14},{10,12},{12,10},{14,8},{1,7},{3,5},... | collective-permute-start | bytes 245768 | tf_op jit(solution)/shard_map/ppermute | solution.py:372
  46.7 8.6 %collective-permute-start.18 = (bf16[40,1024]{1,0:T(8,128)(2,1)S(1)}, bf16[40,1024]{1,0:T(8,128)(2,1)S(1)}, u32[]{:S(2)}, u32[]{:S(2)}) collective-permute-start(bf16[40,1024]{1,0:T(8,128)(2,1)S(1)} %shard_map.124), channel_id=1, source_target_pairs={{0,8},{4,12},{8,0},{12,4},{1,9},{5,13},{9,1},{13,5},{2,10},{6,14},... | collective-permute-start | bytes 245768 | tf_op jit(solution)/shard_map/ppermute | solution.py:365
  48.2 7.1 %collective-permute-start.20 = (bf16[40,1024]{1,0:T(8,128)(2,1)S(1)}, bf16[40,1024]{1,0:T(8,128)(2,1)S(1)}, u32[]{:S(2)}, u32[]{:S(2)}) collective-permute-start(bf16[40,1024]{1,0:T(8,128)(2,1)S(1)} %shard_map.125), channel_id=1, source_target_pairs={{0,12},{4,8},{8,4},{12,0},{1,13},{5,9},{9,5},{13,1},{2,14},{6,10},... | collective-permute-start | bytes 245768 | tf_op jit(solution)/shard_map/ppermute | solution.py:365
  50.7 4.8 %collective-permute-start.24 = (bf16[40,1024]{1,0:T(8,128)(2,1)S(1)}, bf16[40,1024]{1,0:T(8,128)(2,1)S(1)}, u32[]{:S(2)}, u32[]{:S(2)}) collective-permute-start(bf16[40,1024]{1,0:T(8,128)(2,1)S(1)} %get-tuple-element.74), channel_id=1, source_target_pairs={{0,2},{2,0},{1,3},{3,1},{4,6},{6,4},{5,7},{7,5},{8,10},{10,8},{9,1... | collective-permute-start | bytes 245768 | tf_op jit(solution)/shard_map/ppermute | solution.py:368
  (1 other events, 1.3 us)

commit v9 on v7

--- a/solution.py
+++ b/solution.py
@@ -472,7 +472,7 @@
 
     def half(active, other, parts):
         return call(
-            functools.partial(half_kernel, 512, other),
+            functools.partial(half_kernel, 1024, other),
             [struct(count // parts, columns)] * parts,
             [IN_VMEM, IN_VMEM],
             flops=count * model * hidden_units,

time: 56.7 us -> 56.7 us (level)
  no operation moved by 1% of the time
where the time goes in v9:
time: 56.7 us; the launch traced here: 56.5 us
  starting transfers between devices  26.7 us (47%)
  Pallas kernels  19.5 us (34%)
  waiting for transfers between devices  10 us (18%)
    ppermute x9, starting transfers between devices, along(): lax.ppermute(array, 'expert', [(i, i ^ step) for i in range(experts)])  16.6 us
    ppermute x9, waiting for transfers between devices, along(): lax.ppermute(array, 'expert', [(i, i ^ step) for i in range(experts)])  7.85 us
    ppermute x14, starting transfers between devices, swap(): return lax.ppermute(array, axis, [(0, 1), (1, 0)])  7.07 us
    pallas_call x1, Pallas kernels, head_shards(): pl.pallas_call(functools.partial(prefetch_kernel, experts), out_shape=[pl...  6.21 us
    pallas_call x2, Pallas kernels, first(): call(functools.partial(first_kernel, 512), [struct(count, hidden_units)],...  3.76 us
    pallas_call x3, Pallas kernels, pack(): call(functools.partial(pack_kernel, steps), [struct(4 * rows + KINDS, wid...  3.58 us
    ppermute x2, starting transfers between devices, across(): return lax.ppermute(array, ('expert', 'dp'), pairs)  3.01 us
    ppermute x14, waiting for transfers between devices, swap(): return lax.ppermute(array, axis, [(0, 1), (1, 0)])  1.97 us
  transfers between devices with their start and end apart: 25, of which 10 were waited for; matrix products, arithmetic and copies ran while one was open for 0% of the time, Pallas kernels for 28%

profile of v9, /device:TPU:0, one launch (start us, length us, event | category | flops | bytes accessed | tf_op | source)
XLA Modules:
  0.0 56.5 jit_solution(13194786323936614898)
XLA Ops:
  0.0 1.1 %shard_map.109.refs_0_ = bf16[264,256]{1,0:T(8,128)(2,1)S(1)} custom-call(bf16[64,1024]{1,0:T(8,128)(2,1)} %q_hbm.5, bf16[64,2,1024]{2,1,0:T(2,128)(2,1)} %m_hbm.5, bf16[64,1024]{1,0:T(8,128)(2,1)} %h_hbm.5, s32[1,64]{1,0:T(1,128)} %bitcast.18, s32[1,64]{1,0:T(1,128)} %bitcast.21, s32[2,64]{1,0:T(2,128)} %bitcast.10, f32[2,64]{1,0:T(2,128)} %bitcast.13), custom_call_target="tpu_custom_call" | custom-call | tf_op jit(solution)/shard_map/pallas_call | solution.py:375
  1.1 4.1 %collective-permute-start = (bf16[264,256]{1,0:T(8,128)(2,1)S(1)}, bf16[264,256]{1,0:T(8,128)(2,1)S(1)}, u32[]{:S(2)}, u32[]{:S(2)}) collective-permute-start(bf16[264,256]{1,0:T(8,128)(2,1)S(1)} %shard_map.109.refs_0_), channel_id=1, source_target_pairs={{0,8},{4,12},{8,0},{12,4},{1,9},{5,13},{9,1},{13,5},{2,10},{6,14},... | collective-permute-start | bytes 405512 | tf_op jit(solution)/shard_map/ppermute | solution.py:365
  5.2 1.1 %shard_map.110.refs_0_ = bf16[264,256]{1,0:T(8,128)(2,1)S(1)} custom-call(bf16[64,1024]{1,0:T(8,128)(2,1)} %q_hbm.5, bf16[64,2,1024]{2,1,0:T(2,128)(2,1)} %m_hbm.5, bf16[64,1024]{1,0:T(8,128)(2,1)} %h_hbm.5, s32[1,64]{1,0:T(1,128)} %bitcast.19, s32[1,64]{1,0:T(1,128)} %bitcast.22, s32[2,64]{1,0:T(2,128)} %bitcast.11, f32[2,64]{1,0:T(2,128)} %bitcast.14, ...), custom_call_target="tpu_custom_call" | custom-call | bytes 16777216 | tf_op jit(solution)/shard_map/pallas_call | solution.py:375
  6.3 1.6 %collective-permute-start.2 = (bf16[264,256]{1,0:T(8,128)(2,1)S(1)}, bf16[264,256]{1,0:T(8,128)(2,1)S(1)}, u32[]{:S(2)}, u32[]{:S(2)}) collective-permute-start(bf16[264,256]{1,0:T(8,128)(2,1)S(1)} %shard_map.110.refs_0_), channel_id=1, source_target_pairs={{0,4},{4,0},{8,12},{12,8},{1,5},{5,1},{9,13},{13,9},{2,6},{6,2},{1... | collective-permute-start | bytes 405512 | tf_op jit(solution)/shard_map/ppermute | solution.py:365
  8.0 1.4 %shard_map.111 = (bf16[264,256]{1,0:T(8,128)(2,1)S(1)}, bf16[264,256]{1,0:T(8,128)(2,1)S(1)}) custom-call(bf16[64,1024]{1,0:T(8,128)(2,1)} %q_hbm.5, bf16[64,2,1024]{2,1,0:T(2,128)(2,1)} %m_hbm.5, bf16[64,1024]{1,0:T(8,128)(2,1)} %h_hbm.5, s32[1,64]{1,0:T(1,128)} %bitcast.20, s32[1,64]{1,0:T(1,128)} %bitcast.23, s32[2,64]{1,0:T(2,128)} %bitcast.12, ...), custom_call_target="tpu_custom_call" | custom-call | bytes 16777216 | tf_op jit(solution)/shard_map/pallas_call | solution.py:375
  9.4 6.2 %shard_map.112 = (bf16[2048,2048]{1,0:T(8,128)(2,1)S(1)}, bf16[2048,2048]{1,0:T(8,128)(2,1)S(1)}, f32[1,2048]{1,0:T(1,128)S(1)}, f32[1,2048]{1,0:T(1,128)S(1)}) custom-call(bf16[2048,2048]{1,0:T(8,128)(2,1)} %bitcast.8, bf16[2048,2048]{1,0:T(8,128)(2,1)} %bitcast.9, f32[1,2048]{1,0:T(1,128)} %bitcast.16, f32[1,2048]{1,0:T(1,128)} %bitcast.17, ...), custom_call_target="tpu_custom_call" | custom-call | bytes 33554432 | tf_op jit(solution)/shard_map/pallas_call | solution.py:405
  17.1 4.0 %collective-permute-start.3 = (bf16[160,256]{1,0:T(8,128)(2,1)S(1)}, bf16[160,256]{1,0:T(8,128)(2,1)S(1)}, u32[]{:S(2)}, u32[]{:S(2)}) collective-permute-start(bf16[160,256]{1,0:T(8,128)(2,1)S(1)} %get-tuple-element.48), channel_id=1, source_target_pairs={{0,8},{4,12},{8,0},{12,4},{1,9},{5,13},{9,1},{13,5},{2,10},{6,14},... | collective-permute-start | bytes 245768 | tf_op jit(solution)/shard_map/ppermute | solution.py:365
  21.6 1.1 %collective-permute-start.8 = (bf16[160,256]{1,0:T(8,128)(2,1)S(1)}, bf16[160,256]{1,0:T(8,128)(2,1)S(1)}, u32[]{:S(2)}, u32[]{:S(2)}) collective-permute-start(bf16[160,256]{1,0:T(8,128)(2,1)S(1)} %get-tuple-element.50), channel_id=1, source_target_pairs={{0,6},{2,4},{4,2},{6,0},{8,14},{10,12},{12,10},{14,8},{1,7},{3,5},... | collective-permute-start | bytes 245768 | tf_op jit(solution)/shard_map/ppermute | solution.py:372
  22.7 1.8 %collective-permute-start.6 = (bf16[160,256]{1,0:T(8,128)(2,1)S(1)}, bf16[160,256]{1,0:T(8,128)(2,1)S(1)}, u32[]{:S(2)}, u32[]{:S(2)}) collective-permute-start(bf16[160,256]{1,0:T(8,128)(2,1)S(1)} %get-tuple-element.50), channel_id=1, source_target_pairs={{0,4},{4,0},{8,12},{12,8},{1,5},{5,1},{9,13},{13,9},{2,6},{6,2},{1... | collective-permute-start | bytes 245768 | tf_op jit(solution)/shard_map/ppermute | solution.py:365
  25.0 1.7 %collective-permute-done.3.left_ref = bf16[160,256]{1,0:T(8,128)(2,1)S(1)} collective-permute-done((bf16[160,256]{1,0:T(8,128)(2,1)S(1)}, bf16[160,256]{1,0:T(8,128)(2,1)S(1)}, u32[]{:S(2)}, u32[]{:S(2)}) %collective-permute-start.3) | collective-permute-done | bytes 81952 | tf_op jit(solution)/shard_map/ppermute | solution.py:365
  26.7 1.3 %collective-permute-done.4.right_ref = bf16[160,256]{1,0:T(8,128)(2,1)S(1)} collective-permute-done((bf16[160,256]{1,0:T(8,128)(2,1)S(1)}, bf16[160,256]{1,0:T(8,128)(2,1)S(1)}, u32[]{:S(2)}, u32[]{:S(2)}) %collective-permute-start.4) | collective-permute-done | bytes 81952 | tf_op jit(solution)/shard_map/ppermute | solution.py:365
  28.2 1.7 %collective-permute-start.5 = (bf16[160,512]{1,0:T(8,128)(2,1)S(1)}, bf16[160,512]{1,0:T(8,128)(2,1)S(1)}, u32[]{:S(2)}, u32[]{:S(2)}) collective-permute-start(bf16[160,512]{1,0:T(8,128)(2,1)S(1)} %shard_map.114.refs_0_), channel_id=1, source_target_pairs={{0,2},{2,0},{1,3},{3,1},{4,6},{6,4},{5,7},{7,5},{8,10},{10,8},{9,1... | collective-permute-start | bytes 491528 | tf_op jit(solution)/shard_map/ppermute | solution.py:368
  32.0 1.9 %shard_map.115.a_ref = bf16[160,2048]{1,0:T(8,128)(2,1)S(1)} custom-call(bf16[160,512]{1,0:T(8,128)(2,1)S(1)} %shard_map.114.refs_0_, bf16[160,256]{1,0:T(8,128)(2,1)S(1)} %collective-permute-done.6.refs_1_.left_ref, bf16[160,256]{1,0:T(8,128)(2,1)S(1)} %get-tuple-element.51.refs_2_.right_ref, bf16[160,512]{1,0:T(8,128)(2,1)S(1)} %collective-permute-done.7.refs_3_, ...), custom_call_target="tpu_custom_call" | custom-call | tf_op jit(solution)/shard_map/pallas_call | solution.py:442
  33.9 1.5 %shard_map.116 = (bf16[160,1024]{1,0:T(8,128)(2,1)S(1)}, bf16[80,1024]{1,0:T(8,128)(2,1)S(1)}, bf16[80,1024]{1,0:T(8,128)(2,1)S(1)}) custom-call(bf16[160,2048]{1,0:T(8,128)(2,1)S(1)} %shard_map.115.a_ref, bf16[2048,2048]{1,0:T(8,128)(2,1)S(1)} %get-tuple-element.45.w2_ref.w_ref), custom_call_target="tpu_custom_call" | custom-call | tf_op jit(solution)/shard_map/pallas_call | solution.py:462
  37.0 1.9 %shard_map.118.a_ref = bf16[160,2048]{1,0:T(8,128)(2,1)S(1)} custom-call(bf16[160,512]{1,0:T(8,128)(2,1)S(1)} %collective-permute-done.5.refs_0_, bf16[160,512]{1,0:T(8,128)(2,1)S(1)} %shard_map.117.refs_1_, bf16[160,512]{1,0:T(8,128)(2,1)S(1)} %collective-permute-done.12.refs_2_, bf16[160,512]{1,0:T(8,128)(2,1)S(1)} %collective-permute-done.13.refs_3_, ...), custom_call_target="tpu_custom_call" | custom-call | flops 1342177280 | bytes 8388608 | tf_op jit(solution)/shard_map/pallas_call | solution.py:442
  38.9 0.9 %shard_map.120 = (bf16[80,1024]{1,0:T(8,128)(2,1)S(1)}, bf16[80,1024]{1,0:T(8,128)(2,1)S(1)}) custom-call(bf16[160,2048]{1,0:T(8,128)(2,1)S(1)} %shard_map.118.a_ref, bf16[2048,2048]{1,0:T(8,128)(2,1)S(1)} %get-tuple-element.45.w2_ref.w_ref), custom_call_target="tpu_custom_call" | custom-call | flops 671088640 | bytes 4194304 | tf_op jit(solution)/shard_map/pallas_call | solution.py:474
  40.5 0.9 %shard_map.119.kept_ref = bf16[160,1024]{1,0:T(8,128)(2,1)S(1)} custom-call(bf16[160,2048]{1,0:T(8,128)(2,1)S(1)} %shard_map.118.a_ref, bf16[2048,2048]{1,0:T(8,128)(2,1)S(1)} %get-tuple-element.45.w2_ref.w_ref), custom_call_target="tpu_custom_call" | custom-call | flops 671088640 | bytes 4194304 | tf_op jit(solution)/shard_map/pallas_call | solution.py:474
  41.4 1.1 %collective-permute-start.17 = (bf16[40,1024]{1,0:T(8,128)(2,1)S(1)}, bf16[40,1024]{1,0:T(8,128)(2,1)S(1)}, u32[]{:S(2)}, u32[]{:S(2)}) collective-permute-start(bf16[40,1024]{1,0:T(8,128)(2,1)S(1)} %get-tuple-element.68), channel_id=1, source_target_pairs={{0,2},{2,0},{1,3},{3,1},{4,6},{6,4},{5,7},{7,5},{8,10},{10,8},{9,1... | collective-permute-start | bytes 245768 | tf_op jit(solution)/shard_map/ppermute | solution.py:368
  42.6 1.0 %collective-permute-start.19 = (bf16[40,1024]{1,0:T(8,128)(2,1)S(1)}, bf16[40,1024]{1,0:T(8,128)(2,1)S(1)}, u32[]{:S(2)}, u32[]{:S(2)}) collective-permute-start(bf16[40,1024]{1,0:T(8,128)(2,1)S(1)} %get-tuple-element.71), channel_id=1, source_target_pairs={{0,2},{2,0},{1,3},{3,1},{4,6},{6,4},{5,7},{7,5},{8,10},{10,8},{9,1... | collective-permute-start | bytes 245768 | tf_op jit(solution)/shard_map/ppermute | solution.py:368
  44.5 1.9 %collective-permute-start.23 = (bf16[40,1024]{1,0:T(8,128)(2,1)S(1)}, bf16[40,1024]{1,0:T(8,128)(2,1)S(1)}, u32[]{:S(2)}, u32[]{:S(2)}) collective-permute-start(bf16[40,1024]{1,0:T(8,128)(2,1)S(1)} %get-tuple-element.77), channel_id=1, source_target_pairs={{0,6},{2,4},{4,2},{6,0},{8,14},{10,12},{12,10},{14,8},{1,7},{3,5},... | collective-permute-start | bytes 245768 | tf_op jit(solution)/shard_map/ppermute | solution.py:372
  46.9 1.2 %collective-permute-start.18 = (bf16[40,1024]{1,0:T(8,128)(2,1)S(1)}, bf16[40,1024]{1,0:T(8,128)(2,1)S(1)}, u32[]{:S(2)}, u32[]{:S(2)}) collective-permute-start(bf16[40,1024]{1,0:T(8,128)(2,1)S(1)} %shard_map.124), channel_id=1, source_target_pairs={{0,8},{4,12},{8,0},{12,4},{1,9},{5,13},{9,1},{13,5},{2,10},{6,14},... | collective-permute-start | bytes 245768 | tf_op jit(solution)/shard_map/ppermute | solution.py:365
  48.3 2.6 %collective-permute-start.20 = (bf16[40,1024]{1,0:T(8,128)(2,1)S(1)}, bf16[40,1024]{1,0:T(8,128)(2,1)S(1)}, u32[]{:S(2)}, u32[]{:S(2)}) collective-permute-start(bf16[40,1024]{1,0:T(8,128)(2,1)S(1)} %shard_map.125), channel_id=1, source_target_pairs={{0,12},{4,8},{8,4},{12,0},{1,13},{5,9},{9,5},{13,1},{2,14},{6,10},... | collective-permute-start | bytes 245768 | tf_op jit(solution)/shard_map/ppermute | solution.py:365
  51.7 3.5 %collective-permute-done.18.refs_0_ = bf16[40,1024]{1,0:T(8,128)(2,1)S(1)} collective-permute-done((bf16[40,1024]{1,0:T(8,128)(2,1)S(1)}, bf16[40,1024]{1,0:T(8,128)(2,1)S(1)}, u32[]{:S(2)}, u32[]{:S(2)}) %collective-permute-start.18) | collective-permute-done | bytes 81952 | tf_op jit(solution)/shard_map/ppermute | solution.py:365
  55.6 0.9 %shard_map.129 = bf16[64,1024]{1,0:T(8,128)(2,1)} custom-call(bf16[384,128]{1,0:T(8,128)(2,1)S(1)} %get-tuple-element.47.place_ref, f32[64,1024]{1,0:T(8,128)S(1)} %shard_map.128.share_ref, bf16[40,1024]{1,0:T(8,128)(2,1)S(1)} %collective-permute-done.24.came_ref, f32[40,1024]{1,0:T(8,128)S(1)} %get-tuple-element.79.base_ref, ...), custom_call_target="tpu_custom_call" | custom-call | flops 1 | bytes 1 | tf_op jit(solution)/shard_map/pallas_call | solution.py:523
  (47 shorter events, 9.8 us)
Async XLA Ops:
  1.1 14.5 %collective-permute-start = (bf16[264,256]{1,0:T(8,128)(2,1)S(1)}, bf16[264,256]{1,0:T(8,128)(2,1)S(1)}, u32[]{:S(2)}, u32[]{:S(2)}) collective-permute-start(bf16[264,256]{1,0:T(8,128)(2,1)S(1)} %shard_map.109.refs_0_), channel_id=1, source_target_pairs={{0,8},{4,12},{8,0},{12,4},{1,9},{5,13},{9,1},{13,5},{2,10},{6,14},... | collective-permute-start | bytes 405512 | tf_op jit(solution)/shard_map/ppermute | solution.py:365
  6.3 9.3 %collective-permute-start.2 = (bf16[264,256]{1,0:T(8,128)(2,1)S(1)}, bf16[264,256]{1,0:T(8,128)(2,1)S(1)}, u32[]{:S(2)}, u32[]{:S(2)}) collective-permute-start(bf16[264,256]{1,0:T(8,128)(2,1)S(1)} %shard_map.110.refs_0_), channel_id=1, source_target_pairs={{0,4},{4,0},{8,12},{12,8},{1,5},{5,1},{9,13},{13,9},{2,6},{6,2},{1... | collective-permute-start | bytes 405512 | tf_op jit(solution)/shard_map/ppermute | solution.py:365
  9.3 6.9 %collective-permute-start.1 = (bf16[264,256]{1,0:T(8,128)(2,1)S(1)}, bf16[264,256]{1,0:T(8,128)(2,1)S(1)}, u32[]{:S(2)}, u32[]{:S(2)}) collective-permute-start(bf16[264,256]{1,0:T(8,128)(2,1)S(1)} %get-tuple-element.46), channel_id=1, source_target_pairs={{0,12},{4,8},{8,4},{12,0},{1,13},{5,9},{9,5},{13,1},{2,14},{6,10},... | collective-permute-start | bytes 405512 | tf_op jit(solution)/shard_map/ppermute | solution.py:365
  17.1 9.6 %collective-permute-start.3 = (bf16[160,256]{1,0:T(8,128)(2,1)S(1)}, bf16[160,256]{1,0:T(8,128)(2,1)S(1)}, u32[]{:S(2)}, u32[]{:S(2)}) collective-permute-start(bf16[160,256]{1,0:T(8,128)(2,1)S(1)} %get-tuple-element.48), channel_id=1, source_target_pairs={{0,8},{4,12},{8,0},{12,4},{1,9},{5,13},{9,1},{13,5},{2,10},{6,14},... | collective-permute-start | bytes 245768 | tf_op jit(solution)/shard_map/ppermute | solution.py:365
  21.1 7.0 %collective-permute-start.4 = (bf16[160,256]{1,0:T(8,128)(2,1)S(1)}, bf16[160,256]{1,0:T(8,128)(2,1)S(1)}, u32[]{:S(2)}, u32[]{:S(2)}) collective-permute-start(bf16[160,256]{1,0:T(8,128)(2,1)S(1)} %get-tuple-element.49), channel_id=1, source_target_pairs={{0,12},{4,8},{8,4},{12,0},{1,13},{5,9},{9,5},{13,1},{2,14},{6,10},... | collective-permute-start | bytes 245768 | tf_op jit(solution)/shard_map/ppermute | solution.py:365
  21.6 8.5 %collective-permute-start.8 = (bf16[160,256]{1,0:T(8,128)(2,1)S(1)}, bf16[160,256]{1,0:T(8,128)(2,1)S(1)}, u32[]{:S(2)}, u32[]{:S(2)}) collective-permute-start(bf16[160,256]{1,0:T(8,128)(2,1)S(1)} %get-tuple-element.50), channel_id=1, source_target_pairs={{0,6},{2,4},{4,2},{6,0},{8,14},{10,12},{12,10},{14,8},{1,7},{3,5},... | collective-permute-start | bytes 245768 | tf_op jit(solution)/shard_map/ppermute | solution.py:372
  22.7 8.1 %collective-permute-start.6 = (bf16[160,256]{1,0:T(8,128)(2,1)S(1)}, bf16[160,256]{1,0:T(8,128)(2,1)S(1)}, u32[]{:S(2)}, u32[]{:S(2)}) collective-permute-start(bf16[160,256]{1,0:T(8,128)(2,1)S(1)} %get-tuple-element.50), channel_id=1, source_target_pairs={{0,4},{4,0},{8,12},{12,8},{1,5},{5,1},{9,13},{13,9},{2,6},{6,2},{1... | collective-permute-start | bytes 245768 | tf_op jit(solution)/shard_map/ppermute | solution.py:365
  24.5 6.3 %collective-permute-start.9 = (bf16[160,256]{1,0:T(8,128)(2,1)S(1)}, bf16[160,256]{1,0:T(8,128)(2,1)S(1)}, u32[]{:S(2)}, u32[]{:S(2)}) collective-permute-start(bf16[160,256]{1,0:T(8,128)(2,1)S(1)} %get-tuple-element.51.refs_2_.right_ref), channel_id=1, source_target_pairs={{0,2},{2,0},{1,3},{3,1},{4,6},{6,4},{5,7},{7,5},{8,10},{10,8},{9,1... | collective-permute-start | bytes 245768 | tf_op jit(solution)/shard_map/ppermute | solution.py:368
  28.1 3.9 %collective-permute-start.7 = (bf16[160,512]{1,0:T(8,128)(2,1)S(1)}, bf16[160,512]{1,0:T(8,128)(2,1)S(1)}, u32[]{:S(2)}, u32[]{:S(2)}) collective-permute-start(bf16[160,512]{1,0:T(8,128)(2,1)S(1)} %shard_map.114.refs_0_), channel_id=1, source_target_pairs={{0,1},{1,0},{2,3},{3,2},{4,5},{5,4},{6,7},{7,6},{8,9},{9,8},{10,11... | collective-permute-start | bytes 491528 | tf_op jit(solution)/shard_map/ppermute | solution.py:368
  28.2 7.3 %collective-permute-start.5 = (bf16[160,512]{1,0:T(8,128)(2,1)S(1)}, bf16[160,512]{1,0:T(8,128)(2,1)S(1)}, u32[]{:S(2)}, u32[]{:S(2)}) collective-permute-start(bf16[160,512]{1,0:T(8,128)(2,1)S(1)} %shard_map.114.refs_0_), channel_id=1, source_target_pairs={{0,2},{2,0},{1,3},{3,1},{4,6},{6,4},{5,7},{7,5},{8,10},{10,8},{9,1... | collective-permute-start | bytes 491528 | tf_op jit(solution)/shard_map/ppermute | solution.py:368
  30.8 1.3 %collective-permute-start.10 = (bf16[160,256]{1,0:T(8,128)(2,1)S(1)}, bf16[160,256]{1,0:T(8,128)(2,1)S(1)}, u32[]{:S(2)}, u32[]{:S(2)}) collective-permute-start(bf16[160,256]{1,0:T(8,128)(2,1)S(1)} %collective-permute-done.6.refs_1_.left_ref), channel_id=1, source_target_pairs={{0,1},{1,0},{2,3},{3,2},{4,5},{5,4},{6,7},{7,6},{8,9},{9,8},{10,11... | collective-permute-start | bytes 245768 | tf_op jit(solution)/shard_map/ppermute | solution.py:368
  30.8 5.4 %collective-permute-start.13 = (bf16[160,512]{1,0:T(8,128)(2,1)S(1)}, bf16[160,512]{1,0:T(8,128)(2,1)S(1)}, u32[]{:S(2)}, u32[]{:S(2)}) collective-permute-start(bf16[160,512]{1,0:T(8,128)(2,1)S(1)} %shard_map.117.refs_1_), channel_id=1, source_target_pairs={{0,1},{1,0},{2,3},{3,2},{4,5},{5,4},{6,7},{7,6},{8,9},{9,8},{10,11... | collective-permute-start | bytes 491528 | tf_op jit(solution)/shard_map/ppermute | solution.py:368
  35.5 1.5 %collective-permute-start.12 = (bf16[160,512]{1,0:T(8,128)(2,1)S(1)}, bf16[160,512]{1,0:T(8,128)(2,1)S(1)}, u32[]{:S(2)}, u32[]{:S(2)}) collective-permute-start(bf16[160,512]{1,0:T(8,128)(2,1)S(1)} %collective-permute-done.5.refs_0_), channel_id=1, source_target_pairs={{0,1},{1,0},{2,3},{3,2},{4,5},{5,4},{6,7},{7,6},{8,9},{9,8},{10,11... | collective-permute-start | bytes 491528 | tf_op jit(solution)/shard_map/ppermute | solution.py:368
  35.7 3.1 %collective-permute-start.14 = (bf16[80,1024]{1,0:T(8,128)(2,1)S(1)}, bf16[80,1024]{1,0:T(8,128)(2,1)S(1)}, u32[]{:S(2)}, u32[]{:S(2)}) collective-permute-start(bf16[80,1024]{1,0:T(8,128)(2,1)S(1)} %get-tuple-element.59), channel_id=1, source_target_pairs={{0,1},{1,0},{2,3},{3,2},{4,5},{5,4},{6,7},{7,6},{8,9},{9,8},{10,11... | collective-permute-start | bytes 491528 | tf_op jit(solution)/shard_map/ppermute | solution.py:368
  36.1 2.8 %collective-permute-start.15 = (bf16[80,1024]{1,0:T(8,128)(2,1)S(1)}, bf16[80,1024]{1,0:T(8,128)(2,1)S(1)}, u32[]{:S(2)}, u32[]{:S(2)}) collective-permute-start(bf16[80,1024]{1,0:T(8,128)(2,1)S(1)} %get-tuple-element.60), channel_id=1, source_target_pairs={{0,1},{1,0},{2,3},{3,2},{4,5},{5,4},{6,7},{7,6},{8,9},{9,8},{10,11... | collective-permute-start | bytes 491528 | tf_op jit(solution)/shard_map/ppermute | solution.py:368
  39.7 1.7 %collective-permute-start.16 = (bf16[80,1024]{1,0:T(8,128)(2,1)S(1)}, bf16[80,1024]{1,0:T(8,128)(2,1)S(1)}, u32[]{:S(2)}, u32[]{:S(2)}) collective-permute-start(bf16[80,1024]{1,0:T(8,128)(2,1)S(1)} %get-tuple-element.62), channel_id=1, source_target_pairs={{0,1},{1,0},{2,3},{3,2},{4,5},{5,4},{6,7},{7,6},{8,9},{9,8},{10,11... | collective-permute-start | bytes 491528 | tf_op jit(solution)/shard_map/ppermute | solution.py:368
  40.0 4.5 %collective-permute-start.22 = (bf16[80,1024]{1,0:T(8,128)(2,1)S(1)}, bf16[80,1024]{1,0:T(8,128)(2,1)S(1)}, u32[]{:S(2)}, u32[]{:S(2)}) collective-permute-start(bf16[80,1024]{1,0:T(8,128)(2,1)S(1)} %get-tuple-element.76), channel_id=1, source_target_pairs={{0,1},{1,0},{2,3},{3,2},{4,5},{5,4},{6,7},{7,6},{8,9},{9,8},{10,11... | collective-permute-start | bytes 491528 | tf_op jit(solution)/shard_map/ppermute | solution.py:368
  41.4 5.4 %collective-permute-start.17 = (bf16[40,1024]{1,0:T(8,128)(2,1)S(1)}, bf16[40,1024]{1,0:T(8,128)(2,1)S(1)}, u32[]{:S(2)}, u32[]{:S(2)}) collective-permute-start(bf16[40,1024]{1,0:T(8,128)(2,1)S(1)} %get-tuple-element.68), channel_id=1, source_target_pairs={{0,2},{2,0},{1,3},{3,1},{4,6},{6,4},{5,7},{7,5},{8,10},{10,8},{9,1... | collective-permute-start | bytes 245768 | tf_op jit(solution)/shard_map/ppermute | solution.py:368
  42.6 5.7 %collective-permute-start.19 = (bf16[40,1024]{1,0:T(8,128)(2,1)S(1)}, bf16[40,1024]{1,0:T(8,128)(2,1)S(1)}, u32[]{:S(2)}, u32[]{:S(2)}) collective-permute-start(bf16[40,1024]{1,0:T(8,128)(2,1)S(1)} %get-tuple-element.71), channel_id=1, source_target_pairs={{0,2},{2,0},{1,3},{3,1},{4,6},{6,4},{5,7},{7,5},{8,10},{10,8},{9,1... | collective-permute-start | bytes 245768 | tf_op jit(solution)/shard_map/ppermute | solution.py:368
  43.7 8.0 %collective-permute-start.21 = (bf16[40,1024]{1,0:T(8,128)(2,1)S(1)}, bf16[40,1024]{1,0:T(8,128)(2,1)S(1)}, u32[]{:S(2)}, u32[]{:S(2)}) collective-permute-start(bf16[40,1024]{1,0:T(8,128)(2,1)S(1)} %get-tuple-element.75), channel_id=1, source_target_pairs={{0,4},{4,0},{8,12},{12,8},{1,5},{5,1},{9,13},{13,9},{2,6},{6,2},{1... | collective-permute-start | bytes 245768 | tf_op jit(solution)/shard_map/ppermute | solution.py:365
  44.5 7.2 %collective-permute-start.23 = (bf16[40,1024]{1,0:T(8,128)(2,1)S(1)}, bf16[40,1024]{1,0:T(8,128)(2,1)S(1)}, u32[]{:S(2)}, u32[]{:S(2)}) collective-permute-start(bf16[40,1024]{1,0:T(8,128)(2,1)S(1)} %get-tuple-element.77), channel_id=1, source_target_pairs={{0,6},{2,4},{4,2},{6,0},{8,14},{10,12},{12,10},{14,8},{1,7},{3,5},... | collective-permute-start | bytes 245768 | tf_op jit(solution)/shard_map/ppermute | solution.py:372
  46.9 8.4 %collective-permute-start.18 = (bf16[40,1024]{1,0:T(8,128)(2,1)S(1)}, bf16[40,1024]{1,0:T(8,128)(2,1)S(1)}, u32[]{:S(2)}, u32[]{:S(2)}) collective-permute-start(bf16[40,1024]{1,0:T(8,128)(2,1)S(1)} %shard_map.124), channel_id=1, source_target_pairs={{0,8},{4,12},{8,0},{12,4},{1,9},{5,13},{9,1},{13,5},{2,10},{6,14},... | collective-permute-start | bytes 245768 | tf_op jit(solution)/shard_map/ppermute | solution.py:365
  48.3 6.9 %collective-permute-start.20 = (bf16[40,1024]{1,0:T(8,128)(2,1)S(1)}, bf16[40,1024]{1,0:T(8,128)(2,1)S(1)}, u32[]{:S(2)}, u32[]{:S(2)}) collective-permute-start(bf16[40,1024]{1,0:T(8,128)(2,1)S(1)} %shard_map.125), channel_id=1, source_target_pairs={{0,12},{4,8},{8,4},{12,0},{1,13},{5,9},{9,5},{13,1},{2,14},{6,10},... | collective-permute-start | bytes 245768 | tf_op jit(solution)/shard_map/ppermute | solution.py:365
  51.0 4.6 %collective-permute-start.24 = (bf16[40,1024]{1,0:T(8,128)(2,1)S(1)}, bf16[40,1024]{1,0:T(8,128)(2,1)S(1)}, u32[]{:S(2)}, u32[]{:S(2)}) collective-permute-start(bf16[40,1024]{1,0:T(8,128)(2,1)S(1)} %get-tuple-element.78), channel_id=1, source_target_pairs={{0,2},{2,0},{1,3},{3,1},{4,6},{6,4},{5,7},{7,5},{8,10},{10,8},{9,1... | collective-permute-start | bytes 245768 | tf_op jit(solution)/shard_map/ppermute | solution.py:368
  (1 other events, 1.3 us)
